TPU v7x, 32 devices: a whole 2x2x4 slice. The times are simulated.
32 devices in a mesh: seq: 8 (over y, x, core), dp: 4 (over z).
Axes of the slice: x: 2, y: 2, z: 4, core: 2. Of those that a mesh axis runs over, the one named last changes fastest.
Arguments:
- tokens: bfloat16 [4, 2, 1024, 2048], P('dp', None, 'seq'), may hold values from -6 to 6
- lengths: int32 [4, 2], P('dp'), may hold values from 1024 to 1024, as said below
- attn_gain: bfloat16 [2048], P(('seq', 'dp')), may hold values from 0.25 to 1.75
- w_qdown: bfloat16 [2048, 1024], P(('seq', 'dp')), may hold values from -0.125 to 0.125
- q_gain: bfloat16 [1024], P(('seq', 'dp')), may hold values from 0.25 to 1.75
- w_qup: bfloat16 [1024, 4096], P(('seq', 'dp')), may hold values from -0.1875 to 0.1875
- w_key: bfloat16 [2048, 256], P(('seq', 'dp')), may hold values from -0.125 to 0.125
- w_value: bfloat16 [2048, 256], P(('seq', 'dp')), may hold values from -0.125 to 0.125
- w_out: bfloat16 [4096, 2048], P(('seq', 'dp')), may hold values from -1.5 to 1.5
- ffn_gain: bfloat16 [2048], P(('seq', 'dp')), may hold values from 0.25 to 1.75
- w_gate: bfloat16 [2048, 5632], P(('seq', 'dp')), may hold values from -0.125 to 0.125
- w_up: bfloat16 [2048, 5632], P(('seq', 'dp')), may hold values from -0.125 to 0.125
- w_down: bfloat16 [5632, 2048], P(('seq', 'dp')), may hold values from -0.078125 to 0.078125
- cotangent: bfloat16 [4, 2, 1024, 2048], P('dp', None, 'seq'), may hold values from -6 to 6
Outputs:
- out_tokens: bfloat16 [4, 2, 1024, 2048], P('dp', None, 'seq')
- grad_tokens: float32 [4, 2, 1024, 2048], P('dp', None, 'seq')
- grad_attn_gain: float32 [2048], P(('seq', 'dp'))
- grad_w_qdown: float32 [2048, 1024], P(('seq', 'dp'))
- grad_q_gain: float32 [1024], P(('seq', 'dp'))
- grad_w_qup: float32 [1024, 4096], P(('seq', 'dp'))
- grad_w_key: float32 [2048, 256], P(('seq', 'dp'))
- grad_w_value: float32 [2048, 256], P(('seq', 'dp'))
- grad_w_out: float32 [4096, 2048], P(('seq', 'dp'))
- grad_ffn_gain: float32 [2048], P(('seq', 'dp'))
- grad_w_gate: float32 [2048, 5632], P(('seq', 'dp'))
- grad_w_up: float32 [2048, 5632], P(('seq', 'dp'))
- grad_w_down: float32 [5632, 2048], P(('seq', 'dp'))
Inputs may be any that keep to these rules, and one draw needn't show every extreme that they name: `lengths`: in every group, one sequence, chosen by the draw, has the full length 1024; positions at or past a sequence's length are padding.
All inputs are finite; a program needn't handle non-finite values.
Results may differ from a plain program's by a relative error of at most 0.015.
Values may be sent and summed in bfloat16 or wider, within the bound.
A program may use at most 512 MiB of HBM per device.

v0:
```python
import math

import jax
import jax.numpy as jnp
from jax import lax
from jax.sharding import PartitionSpec as P

epsilon = 1e-06


def rms_scale(values):
    return lax.rsqrt(jnp.mean(values * values, axis=-1, keepdims=True) + epsilon)


def rotate_half(values):
    half_width = values.shape[-1] // 2
    return jnp.concatenate([-values[..., half_width:], values[..., :half_width]], axis=-1)


def rotary(positions, head_width):
    half_width = head_width // 2
    frequency = jnp.exp(
        jnp.arange(half_width, dtype=jnp.float32) * (-2.0 * math.log(10000.0) / head_width)
    )
    angles = positions.astype(jnp.float32)[:, None] * frequency[None, :]
    cos_table = jnp.cos(angles)
    sin_table = jnp.sin(angles)
    return (
        jnp.concatenate([cos_table, cos_table], -1),
        jnp.concatenate([sin_table, sin_table], -1),
    )


def matmul(left, right):
    return jnp.dot(left, right, preferred_element_type=jnp.float32)


def inner_rows(left, right):
    return lax.dot_general(
        left, right, (((0,), (0,)), ((), ())), preferred_element_type=jnp.float32
    )


def outer_cols(left, right):
    return lax.dot_general(
        left, right, (((1,), (1,)), ((), ())), preferred_element_type=jnp.float32
    )


def norm_back(grad_in, inputs, scale_rows, gain):
    weighted = grad_in * gain
    return scale_rows * weighted - inputs * scale_rows**3 * jnp.mean(
        weighted * inputs, axis=-1, keepdims=True
    )


def slot_scores(query_block, key_block, query_pos, length, score_scale):
    key_pos = jnp.arange(key_block.shape[0], dtype=jnp.int32)
    visible = (key_pos[None, :] <= query_pos[:, None]) & (key_pos[None, :] < length)
    return jnp.where(visible, outer_cols(query_block, key_block) * score_scale, -1e30)


def per_device(
    tokens,
    lengths,
    attn_gain,
    w_qdown,
    q_gain,
    w_qup,
    w_key,
    w_value,
    w_out,
    ffn_gain,
    w_gate,
    w_up,
    w_down,
    cotangent,
):
    slot_count, seq_span, model_width = (tokens.shape[1], tokens.shape[2], tokens.shape[3])
    row_count = slot_count * seq_span
    seq_rank = lax.axis_index("seq")
    grad_scale = 1.0 / math.sqrt(row_count * lax.axis_size("seq") * lax.axis_size("dp"))
    gain_one, down_q, gain_q, up_q, key_proj, value_proj, out_proj = (
        lax.all_gather(attn_gain, ("seq", "dp"), axis=0, tiled=True),
        lax.all_gather(w_qdown, ("seq", "dp"), axis=0, tiled=True),
        lax.all_gather(q_gain, ("seq", "dp"), axis=0, tiled=True),
        lax.all_gather(w_qup, ("seq", "dp"), axis=0, tiled=True),
        lax.all_gather(w_key, ("seq", "dp"), axis=0, tiled=True),
        lax.all_gather(w_value, ("seq", "dp"), axis=0, tiled=True),
        lax.all_gather(w_out, ("seq", "dp"), axis=0, tiled=True),
    )
    gain_two, gate_proj, up_proj, down_proj = (
        lax.all_gather(ffn_gain, ("seq", "dp"), axis=0, tiled=True),
        lax.all_gather(w_gate, ("seq", "dp"), axis=0, tiled=True),
        lax.all_gather(w_up, ("seq", "dp"), axis=0, tiled=True),
        lax.all_gather(w_down, ("seq", "dp"), axis=0, tiled=True),
    )
    gain_one = gain_one.astype(jnp.float32)
    gain_q = gain_q.astype(jnp.float32)
    gain_two = gain_two.astype(jnp.float32)
    head_width = key_proj.shape[1]
    head_count = up_q.shape[1] // head_width
    score_scale = 1.0 / math.sqrt(head_width)
    inputs = tokens[0].reshape(row_count, model_width).astype(jnp.float32)
    positions = seq_rank * seq_span + jnp.arange(seq_span, dtype=jnp.int32)
    cos_table, sin_table = rotary(positions, head_width)
    valid_mask = (
        (positions[None, :] < lengths[0][:, None]).astype(jnp.float32).reshape(row_count, 1)
    )
    scale_one = rms_scale(inputs)
    normed = (inputs * scale_one * gain_one).astype(jnp.bfloat16)
    q_down = matmul(normed, down_q)
    scale_q = rms_scale(q_down)
    q_normed = (q_down * scale_q * gain_q).astype(jnp.bfloat16)
    q_raw = matmul(q_normed, up_q).reshape(slot_count, seq_span, head_count, head_width)
    queries = (
        q_raw * cos_table[None, :, None, :] + rotate_half(q_raw) * sin_table[None, :, None, :]
    ).astype(jnp.bfloat16)
    k_raw = matmul(normed, key_proj).reshape(slot_count, seq_span, head_width)
    key_rows = (k_raw * cos_table + rotate_half(k_raw) * sin_table).astype(jnp.bfloat16)
    value_rows = (
        matmul(normed, value_proj).astype(jnp.bfloat16).reshape(slot_count, seq_span, head_width)
    )
    all_keys, all_values = (
        lax.all_gather(key_rows, "seq", axis=1, tiled=True),
        lax.all_gather(value_rows, "seq", axis=1, tiled=True),
    )
    query_pos = jnp.repeat(positions, head_count)
    outputs = []
    totals = []
    for slot_index in range(slot_count):
        query_block = queries[slot_index].reshape(seq_span * head_count, head_width)
        scores = slot_scores(
            query_block, all_keys[slot_index], query_pos, lengths[0, slot_index], score_scale
        )
        row_top = jnp.max(scores, axis=-1, keepdims=True)
        log_total = row_top + jnp.log(jnp.sum(jnp.exp(scores - row_top), axis=-1, keepdims=True))
        attn_probs = jnp.exp(scores - log_total).astype(jnp.bfloat16)
        outputs.append(
            matmul(attn_probs, all_values[slot_index]).reshape(seq_span, head_count * head_width)
        )
        totals.append(log_total)
    mixed = jnp.concatenate(outputs, 0).astype(jnp.bfloat16)
    middle = inputs + matmul(mixed, out_proj)
    scale_two = rms_scale(middle)
    normed2 = (middle * scale_two * gain_two).astype(jnp.bfloat16)
    gate_val = matmul(normed2, gate_proj)
    up_val = matmul(normed2, up_proj)
    sigma = jax.nn.sigmoid(gate_val)
    activated = (gate_val * sigma * up_val).astype(jnp.bfloat16)
    output = middle + matmul(activated, down_proj)
    out_tokens = output.astype(jnp.bfloat16).reshape(1, slot_count, seq_span, model_width)
    seed_grad = (
        cotangent[0].reshape(row_count, model_width).astype(jnp.float32) * valid_mask
    ).astype(jnp.bfloat16)
    grad_act = outer_cols(seed_grad, down_proj)
    gate_grad = (grad_act * up_val * sigma * (1.0 + gate_val * (1.0 - sigma))).astype(jnp.bfloat16)
    up_grad = (grad_act * gate_val * sigma).astype(jnp.bfloat16)
    grad_normed2 = outer_cols(gate_grad, gate_proj) + outer_cols(up_grad, up_proj)
    ffn_terms = (
        jnp.sum(grad_normed2 * middle * scale_two, axis=0) * grad_scale,
        inner_rows(normed2, gate_grad) * grad_scale,
        inner_rows(normed2, up_grad) * grad_scale,
        inner_rows(activated, seed_grad) * grad_scale,
    )
    grad_ffn_gain, grad_w_gate, grad_w_up, grad_w_down = (
        lax.psum_scatter(ffn_terms[0], ("seq", "dp"), scatter_dimension=0, tiled=True),
        lax.psum_scatter(ffn_terms[1], ("seq", "dp"), scatter_dimension=0, tiled=True),
        lax.psum_scatter(ffn_terms[2], ("seq", "dp"), scatter_dimension=0, tiled=True),
        lax.psum_scatter(ffn_terms[3], ("seq", "dp"), scatter_dimension=0, tiled=True),
    )
    grad_middle = seed_grad.astype(jnp.float32) + norm_back(
        grad_normed2, middle, scale_two, gain_two
    )
    grad_branch = grad_middle.astype(jnp.bfloat16)
    grad_mixed = outer_cols(grad_branch, out_proj).astype(jnp.bfloat16)
    grad_queries = []
    grad_keys = []
    grad_values = []
    for slot_index in range(slot_count):
        query_block = queries[slot_index].reshape(seq_span * head_count, head_width)
        scores = slot_scores(
            query_block, all_keys[slot_index], query_pos, lengths[0, slot_index], score_scale
        )
        attn_probs = jnp.exp(scores - totals[slot_index])
        grad_block = grad_mixed[slot_index * seq_span : (slot_index + 1) * seq_span].reshape(
            seq_span * head_count, head_width
        )
        grad_probs = outer_cols(grad_block, all_values[slot_index])
        grad_scores = (
            attn_probs * (grad_probs - jnp.sum(attn_probs * grad_probs, axis=-1, keepdims=True))
        ).astype(jnp.bfloat16)
        grad_queries.append(matmul(grad_scores, all_keys[slot_index]) * score_scale)
        grad_keys.append(inner_rows(grad_scores, query_block) * score_scale)
        grad_values.append(inner_rows(attn_probs.astype(jnp.bfloat16), grad_block))
    key_sum, value_sum = (
        lax.psum_scatter(jnp.stack(grad_keys), "seq", scatter_dimension=1, tiled=True),
        lax.psum_scatter(jnp.stack(grad_values), "seq", scatter_dimension=1, tiled=True),
    )
    grad_k = (
        (key_sum * cos_table - rotate_half(key_sum * sin_table))
        .astype(jnp.bfloat16)
        .reshape(row_count, head_width)
    )
    grad_v = value_sum.astype(jnp.bfloat16).reshape(row_count, head_width)
    grad_q_rot = jnp.stack(grad_queries).reshape(slot_count, seq_span, head_count, head_width)
    grad_q = grad_q_rot * cos_table[None, :, None, :] - rotate_half(
        grad_q_rot * sin_table[None, :, None, :]
    )
    grad_q = grad_q.astype(jnp.bfloat16).reshape(row_count, head_count * head_width)
    grad_q_normed = outer_cols(grad_q, up_q)
    grad_q_down = norm_back(grad_q_normed, q_down, scale_q, gain_q).astype(jnp.bfloat16)
    grad_normed = (
        outer_cols(grad_q_down, down_q)
        + outer_cols(grad_k, key_proj)
        + outer_cols(grad_v, value_proj)
    )
    grad_inputs = grad_middle + norm_back(grad_normed, inputs, scale_one, gain_one)
    attn_terms = (
        jnp.sum(grad_normed * inputs * scale_one, axis=0) * grad_scale,
        inner_rows(normed, grad_q_down) * grad_scale,
        jnp.sum(grad_q_normed * q_down * scale_q, axis=0) * grad_scale,
        inner_rows(q_normed, grad_q) * grad_scale,
        inner_rows(normed, grad_k) * grad_scale,
        inner_rows(normed, grad_v) * grad_scale,
        inner_rows(mixed, grad_branch) * grad_scale,
    )
    grad_attn_gain, grad_w_qdown, grad_q_gain, grad_w_qup, grad_w_key, grad_w_value, grad_w_out = (
        lax.psum_scatter(attn_terms[0], ("seq", "dp"), scatter_dimension=0, tiled=True),
        lax.psum_scatter(attn_terms[1], ("seq", "dp"), scatter_dimension=0, tiled=True),
        lax.psum_scatter(attn_terms[2], ("seq", "dp"), scatter_dimension=0, tiled=True),
        lax.psum_scatter(attn_terms[3], ("seq", "dp"), scatter_dimension=0, tiled=True),
        lax.psum_scatter(attn_terms[4], ("seq", "dp"), scatter_dimension=0, tiled=True),
        lax.psum_scatter(attn_terms[5], ("seq", "dp"), scatter_dimension=0, tiled=True),
        lax.psum_scatter(attn_terms[6], ("seq", "dp"), scatter_dimension=0, tiled=True),
    )
    grad_tokens = grad_inputs.reshape(1, slot_count, seq_span, model_width)
    return (
        out_tokens,
        grad_tokens,
        grad_attn_gain,
        grad_w_qdown,
        grad_q_gain,
        grad_w_qup,
        grad_w_key,
        grad_w_value,
        grad_w_out,
        grad_ffn_gain,
        grad_w_gate,
        grad_w_up,
        grad_w_down,
    )


def solution(mesh):
    placed = (
        P("dp", None, "seq", None),
        P("dp", None),
        P(("seq", "dp")),
        P(("seq", "dp"), None),
        P(("seq", "dp")),
        P(("seq", "dp"), None),
        P(("seq", "dp"), None),
        P(("seq", "dp"), None),
        P(("seq", "dp"), None),
        P(("seq", "dp")),
        P(("seq", "dp"), None),
        P(("seq", "dp"), None),
        P(("seq", "dp"), None),
        P("dp", None, "seq", None),
    )
    return jax.shard_map(
        per_device,
        mesh=mesh,
        in_specs=placed,
        out_specs=(
            P("dp", None, "seq", None),
            P("dp", None, "seq", None),
            P(("seq", "dp")),
            P(("seq", "dp"), None),
            P(("seq", "dp")),
            P(("seq", "dp"), None),
            P(("seq", "dp"), None),
            P(("seq", "dp"), None),
            P(("seq", "dp"), None),
            P(("seq", "dp")),
            P(("seq", "dp"), None),
            P(("seq", "dp"), None),
            P(("seq", "dp"), None),
        ),
        check_vma=False,
    )
```

profile of v0, /device:TPU:0, one launch (start us, length us, event | category | flops | bytes accessed | tf_op | source)
XLA Modules:
  0.0 5540.4 jit_solution(16407929339614672599)
XLA Ops:
  12.6 42.2 all-reduce.7
  57.3 10.2 all-gather.15.cloned.1.call-done
  70.8 52.5 all-gather.19.cloned.1.call-done
  131.9 55.5 %all-gather.11.cloned.1.call-done = bf16[2048,1024]{1,0:T(8,128)(2,1)} async-done(((bf16[64,1024]{1,0:T(8,128)(2,1)}), bf16[2048,1024]{1,0:T(8,128)(2,1)}) %all-gather.11.cloned.1.call-update) | async-done | bytes 4194320 | tf_op jit(solution)/shard_map/all_gather | solution.py:85
  187.4 3.5 multiply_reduce_fusion.7
  191.6 74.6 %all-gather.13.cloned.1.call-done = bf16[1024,4096]{1,0:T(8,128)(2,1)} async-done(((bf16[32,4096]{1,0:T(8,128)(2,1)}), bf16[1024,4096]{1,0:T(8,128)(2,1)}) %all-gather.13.cloned.1.call-update) | async-done | bytes 8388624 | tf_op jit(solution)/shard_map/all_gather | solution.py:87
  266.2 5.8 fusion.44
  275.4 15.2 all-gather.17.cloned.1.call-done
  290.6 4.3 fusion.48
  298.3 18.2 all-gather.21.cloned.1.call-done
  316.5 5.1 convolution_convert_fusion.2
  322.9 3.8 fusion.49
  335.7 98.6 %all-gather.23.cloned.1.call-done = bf16[4096,2048]{1,0:T(8,128)(2,1)} async-done(((bf16[128,2048]{1,0:T(8,128)(2,1)}), bf16[4096,2048]{1,0:T(8,128)(2,1)}) %all-gather.23.cloned.1.call-update) | async-done | bytes 16777232 | tf_op jit(solution)/shard_map/all_gather | solution.py:90
  434.4 8.3 multiply_reduce_fusion.4
  444.2 135.8 %all-gather.25.cloned.1.call-done = bf16[2048,5632]{1,0:T(8,128)(2,1)} async-done(((bf16[64,5632]{1,0:T(8,128)(2,1)}), bf16[2048,5632]{1,0:T(8,128)(2,1)}) %all-gather.25.cloned.1.call-update) | async-done | bytes 23068688 | tf_op jit(solution)/shard_map/all_gather | solution.py:94
  580.0 13.3 fusion.50
  593.4 132.4 %all-gather.27.cloned.1.call-done = bf16[2048,5632]{1,0:T(8,128)(2,1)} async-done(((bf16[64,5632]{1,0:T(8,128)(2,1)}), bf16[2048,5632]{1,0:T(8,128)(2,1)}) %all-gather.27.cloned.1.call-update) | async-done | bytes 23068688 | tf_op jit(solution)/shard_map/all_gather | solution.py:95
  725.8 13.2 fusion.51
  739.0 132.3 %all-gather.29.cloned.1.call-done = bf16[5632,2048]{1,0:T(8,128)(2,1)} async-done(((bf16[176,2048]{1,0:T(8,128)(2,1)}), bf16[5632,2048]{1,0:T(8,128)(2,1)}) %all-gather.29.cloned.1.call-update) | async-done | bytes 23068688 | tf_op jit(solution)/shard_map/all_gather | solution.py:96
  871.3 25.8 multiply_convert_fusion.2
  897.0 12.7 fusion.52
  909.8 14.0 multiply_reduce_fusion.2
  927.0 18.1 convolution_convert_fusion
  952.8 5.7 multiply_reduce_fusion
  958.4 5.1 multiply_convert_fusion
  967.1 5.5 multiply_reduce_fusion.1
  979.8 5.0 convolution_bitcast_fusion
  984.8 5.1 convolution_bitcast_fusion.1
  992.8 26.4 reduce-scatter.11.cloned.1.call-done
  1025.0 39.0 reduce-scatter.13.cloned.1.call-done
  1067.8 3.8 convolution_multiply_fusion.5
  1082.0 4.6 convolution_multiply_fusion.4
  1086.9 9.9 convolution_multiply_fusion.3
  1096.8 14.9 broadcast_multiply_fusion
  1113.0 19.7 convolution_multiply_fusion.1
  1132.8 19.7 convolution_multiply_fusion
  1153.7 19.7 convolution_multiply_fusion.2
  1174.5 3.7 fusion.53
  1178.2 12.3 fusion.8
  1194.2 40.0 all-reduce.6
  1235.9 3.5 fusion.19
  1239.4 104.6 %reduce-scatter.21.cloned.1.call-done = f32[64,256]{1,0:T(8,128)} async-done(((f32[2048,256]{1,0:T(8,128)}), f32[64,256]{1,0:T(8,128)}) %reduce-scatter.21.cloned.1.call-update) | async-done | bytes 65552 | tf_op jit(solution)/shard_map/reduce_scatter | solution.py:234
  1344.1 186.2 %reduce-scatter.15.cloned.1.call-done = f32[64,1024]{1,0:T(8,128)} async-done(((f32[2048,1024]{1,0:T(8,128)}), f32[64,1024]{1,0:T(8,128)}) %reduce-scatter.15.cloned.1.call-update) | async-done | bytes 262160 | tf_op jit(solution)/shard_map/reduce_scatter | solution.py:230
  1530.3 364.6 %reduce-scatter.17.cloned.1.call-done = f32[32,4096]{1,0:T(8,128)} async-done(((f32[1024,4096]{1,0:T(8,128)}), f32[32,4096]{1,0:T(8,128)}) %reduce-scatter.17.cloned.1.call-update) | async-done | bytes 524304 | tf_op jit(solution)/shard_map/reduce_scatter | solution.py:232
  1894.9 712.6 %reduce-scatter.23.cloned.1.call-done = f32[128,2048]{1,0:T(8,128)} async-done(((f32[4096,2048]{1,0:T(8,128)}), f32[128,2048]{1,0:T(8,128)}) %reduce-scatter.23.cloned.1.call-update) | async-done | bytes 1048592 | tf_op jit(solution)/shard_map/reduce_scatter | solution.py:235
  2607.5 974.5 %reduce-scatter.25.cloned.1.call-done = f32[64,5632]{1,0:T(8,128)} async-done(((f32[2048,5632]{1,0:T(8,128)}), f32[64,5632]{1,0:T(8,128)}) %reduce-scatter.25.cloned.1.call-update) | async-done | bytes 1441808 | tf_op jit(solution)/shard_map/reduce_scatter | solution.py:168
  3582.0 975.6 %reduce-scatter.27.cloned.1.call-done = f32[64,5632]{1,0:T(8,128)} async-done(((f32[2048,5632]{1,0:T(8,128)}), f32[64,5632]{1,0:T(8,128)}) %reduce-scatter.27.cloned.1.call-update) | async-done | bytes 1441808 | tf_op jit(solution)/shard_map/reduce_scatter | solution.py:169
  4557.6 975.5 %reduce-scatter.29.cloned.1.call-done = f32[176,2048]{1,0:T(8,128)} async-done(((f32[5632,2048]{1,0:T(8,128)}), f32[176,2048]{1,0:T(8,128)}) %reduce-scatter.29.cloned.1.call-update) | async-done | bytes 1441808 | tf_op jit(solution)/shard_map/reduce_scatter | solution.py:170
  (250 shorter events, 92.1 us)
Async XLA Ops:
  7.2 63.3 %copy-start.2 = (bf16[1,2,128,2048]{3,2,1,0:T(8,128)(2,1)S(1)}, bf16[1,2,128,2048]{3,2,1,0:T(8,128)(2,1)}, u32[]{:S(2)}) copy-start(bf16[1,2,128,2048]{3,2,1,0:T(8,128)(2,1)} %param.14) | copy-start | bytes 3145732
  7.2 60.4 %all-gather.15.cloned.1.call-start = ((), (), s32[]{:S(2)}) async-start(), calls=%async_computation.12 | async-start | bytes 1081344 | tf_op jit(solution)/shard_map/all_gather | solution.py:88
  7.9 115.4 %all-gather.19.cloned.1.call-start = ((), (), s32[]{:S(2)}) async-start(), calls=%async_computation.14 | async-start | bytes 1081344 | tf_op jit(solution)/shard_map/all_gather | solution.py:89
  8.7 178.8 %all-gather.11.cloned.1.call-start = ((), (), s32[]{:S(2)}) async-start(), calls=%async_computation.10 | async-start | bytes 4325376 | tf_op jit(solution)/shard_map/all_gather | solution.py:85
  9.4 256.8 %all-gather.13.cloned.1.call-start = ((), (), s32[]{:S(2)}) async-start(), calls=%async_computation.11 | async-start | bytes 8650752 | tf_op jit(solution)/shard_map/all_gather | solution.py:87
  10.0 280.6 %all-gather.17.cloned.1.call-start = ((), (), s32[]{:S(2)}) async-start(), calls=%async_computation.13 | async-start | bytes 1179648 | tf_op jit(solution)/shard_map/all_gather | solution.py:125
  54.8 16.0 copy-start.45
  55.2 218.9 %copy-start.26 = (f32[128,256]{1,0:T(8,128)}, f32[128,256]{1,0:T(8,128)S(1)}, u32[]{:S(2)}) copy-start(f32[128,256]{1,0:T(8,128)S(1)} %pad_maximum_fusion.4) | copy-start | bytes 393220
  55.2 218.9 %copy-start.28 = (f32[128,256]{1,0:T(8,128)}, f32[128,256]{1,0:T(8,128)S(1)}, u32[]{:S(2)}) copy-start(f32[128,256]{1,0:T(8,128)S(1)} %pad_maximum_fusion.3) | copy-start | bytes 393220
  57.3 13.1 copy-start.56
  57.3 68.3 %copy-start.50 = (f32[256]{0:T(256)}, f32[256]{0:T(256)S(1)}, u32[]{:S(2)}) copy-start(f32[256]{0:T(256)S(1)} %get-tuple-element.45) | copy-start | bytes 3076
  69.6 59.1 %copy-start.55 = (s32[1,2]{1,0:T(1,128)S(1)}, s32[1,2]{1,0:T(1,128)}, u32[]{:S(2)}) copy-start(s32[1,2]{1,0:T(1,128)} %param.15) | copy-start | bytes 28
  69.6 61.1 %copy-start.20 = (bf16[1,2,128,2048]{3,2,1,0:T(8,128)(2,1)S(1)}, bf16[1,2,128,2048]{3,2,1,0:T(8,128)(2,1)}, u32[]{:S(2)}) copy-start(bf16[1,2,128,2048]{3,2,1,0:T(8,128)(2,1)} %param.27) | copy-start | bytes 3145732
  70.4 246.1 %all-gather.21.cloned.1.call-start = ((), (), s32[]{:S(2)}) async-start(), calls=%async_computation.15 | async-start | bytes 1179648 | tf_op jit(solution)/shard_map/all_gather | solution.py:126
  70.8 120.2 %copy-start.8 = (bf16[256,2048]{1,0:T(8,128)(2,1)}, bf16[256,2048]{1,0:T(8,128)(2,1)S(1)}, u32[]{:S(2)}) copy-start(bf16[256,2048]{1,0:T(8,128)(2,1)S(1)} %fusion.16) | copy-start | bytes 3145732
  125.6 308.8 %all-gather.23.cloned.1.call-start = ((), (), s32[]{:S(2)}) async-start(), calls=%async_computation.16 | async-start | bytes 17301504 | tf_op jit(solution)/shard_map/all_gather | solution.py:90
  126.4 453.6 %all-gather.25.cloned.1.call-start = ((), (), s32[]{:S(2)}) async-start(), calls=%async_computation.17 | async-start | bytes 23789568 | tf_op jit(solution)/shard_map/all_gather | solution.py:94
  127.1 598.6 %all-gather.27.cloned.1.call-start = ((), (), s32[]{:S(2)}) async-start(), calls=%async_computation.18 | async-start | bytes 23789568 | tf_op jit(solution)/shard_map/all_gather | solution.py:95
  127.9 743.4 %all-gather.29.cloned.1.call-start = ((), (), s32[]{:S(2)}) async-start(), calls=%async_computation.19 | async-start | bytes 23789568 | tf_op jit(solution)/shard_map/all_gather | solution.py:96
  128.5 890.8 %reduce-scatter.11.cloned.1.call-start = ((), (), s32[]{:S(2)}) async-start(), calls=%async_computation.20 | async-start | bytes 2359296 | tf_op jit(solution)/shard_map/reduce_scatter | solution.py:197
  128.5 137.7 %copy-start.43 = (f32[1024]{0:T(1024)}, f32[1024]{0:T(1024)S(1)}, u32[]{:S(2)}) copy-start(f32[1024]{0:T(1024)S(1)} %convert_element_type.136) | copy-start | bytes 12292
  191.0 81.0 %copy-start.6 = (f32[256,1024]{1,0:T(8,128)}, f32[256,1024]{1,0:T(8,128)S(1)}, u32[]{:S(2)}) copy-start(f32[256,1024]{1,0:T(8,128)S(1)} %get-tuple-element.51) | copy-start | bytes 3145732
  191.6 80.4 %copy-start.48 = (f32[256]{0:T(256)}, f32[256]{0:T(256)S(1)}, u32[]{:S(2)}) copy-start(f32[256]{0:T(256)S(1)} %get-tuple-element.41) | copy-start | bytes 3076
  275.4 19.5 copy-start.39
  275.4 47.5 copy-start.41
  335.7 106.9 %copy-start.17 = (bf16[256,4096]{1,0:T(8,128)(2,1)}, bf16[256,4096]{1,0:T(8,128)(2,1)S(1)}, u32[]{:S(2)}) copy-start(bf16[256,4096]{1,0:T(8,128)(2,1)S(1)} %constant_dynamic-update-slice_fusion) | copy-start | bytes 6291460
  444.2 281.5 %copy-start.4 = (bf16[256,2048]{1,0:T(8,128)(2,1)}, bf16[256,2048]{1,0:T(8,128)(2,1)S(1)}, u32[]{:S(2)}) copy-start(bf16[256,2048]{1,0:T(8,128)(2,1)S(1)} %multiply_convert_fusion.5) | copy-start | bytes 3145732
  593.4 277.9 %copy-start.24 = (bf16[256,2048]{1,0:T(8,128)(2,1)S(1)}, bf16[256,2048]{1,0:T(8,128)(2,1)}, u32[]{:S(2)}) copy-start(bf16[256,2048]{1,0:T(8,128)(2,1)} %fusion.9) | copy-start | bytes 3145732
  897.0 12.7 copy-start.13
  958.4 7.1 copy-start.42
  965.5 7.0 slice-start
  967.1 5.5 slice-start.1
  979.7 84.3 %reduce-scatter.13.cloned.1.call-start = ((), (), s32[]{:S(2)}) async-start(), calls=%async_computation.21 | async-start | bytes 2359296 | tf_op jit(solution)/shard_map/reduce_scatter | solution.py:198
  979.8 5.0 copy-start.16
  989.9 29.3 copy-start.27
  989.9 30.3 copy-start.29
  991.4 248.0 %reduce-scatter.19.cloned.1.call-start = ((), (), s32[]{:S(2)}) async-start(), calls=%async_computation.24 | async-start | bytes 2162688 | tf_op jit(solution)/shard_map/reduce_scatter | solution.py:233
  992.8 72.8 %copy-start.10 = (bf16[1,2,128,2048]{3,2,1,0:T(8,128)(2,1)S(1)}, bf16[1,2,128,2048]{3,2,1,0:T(8,128)(2,1)}, u32[]{:S(2)}) copy-start(bf16[1,2,128,2048]{3,2,1,0:T(8,128)(2,1)} %fusion.14) | copy-start | bytes 3145732
  1025.0 319.1 %reduce-scatter.21.cloned.1.call-start = ((), (), s32[]{:S(2)}) async-start(), calls=%async_computation.25 | async-start | bytes 2162688 | tf_op jit(solution)/shard_map/reduce_scatter | solution.py:234
  1067.5 462.7 %reduce-scatter.15.cloned.1.call-start = ((), (), s32[]{:S(2)}) async-start(), calls=%async_computation.22 | async-start | bytes 8650752 | tf_op jit(solution)/shard_map/reduce_scatter | solution.py:230
  1076.0 4.8 copy-start.11
  1086.6 808.2 %reduce-scatter.17.cloned.1.call-start = ((), (), s32[]{:S(2)}) async-start(), calls=%async_computation.23 | async-start | bytes 17301504 | tf_op jit(solution)/shard_map/reduce_scatter | solution.py:232
  1096.8 1510.7 %reduce-scatter.23.cloned.1.call-start = ((), (), s32[]{:S(2)}) async-start(), calls=%async_computation.26 | async-start | bytes 34603008 | tf_op jit(solution)/shard_map/reduce_scatter | solution.py:235
  1111.8 2470.2 %reduce-scatter.25.cloned.1.call-start = ((), (), s32[]{:S(2)}) async-start(), calls=%async_computation.27 | async-start | bytes 47579136 | tf_op jit(solution)/shard_map/reduce_scatter | solution.py:168
  1132.7 3424.9 %reduce-scatter.27.cloned.1.call-start = ((), (), s32[]{:S(2)}) async-start(), calls=%async_computation.28 | async-start | bytes 47579136 | tf_op jit(solution)/shard_map/reduce_scatter | solution.py:169
  1152.5 4380.7 %reduce-scatter.29.cloned.1.call-start = ((), (), s32[]{:S(2)}) async-start(), calls=%async_computation.29 | async-start | bytes 47579136 | tf_op jit(solution)/shard_map/reduce_scatter | solution.py:170
  1178.2 12.3 copy-start.35
  1178.2 12.3 copy-start.38
  (36 other events, 78.6 us)
Sparse Core Ops, SparseCore 0:
  11.0 56.5 all-gather.14
  70.5 52.7 all-gather.18
  126.3 61.0 all-gather.10
  190.2 75.9 all-gather.12
  268.5 22.0 all-gather.16
  293.0 23.4 all-gather.20
  319.5 114.8 all-gather.22
  437.2 142.7 all-gather.24
  582.9 142.8 all-gather.26
  728.4 142.7 all-gather.28
  979.8 39.3 reduce-scatter.10
  1022.7 41.2 reduce-scatter.12
  1066.8 138.0 reduce-scatter.18
  1207.7 136.3 reduce-scatter.20
  1346.8 183.4 reduce-scatter.14
  1533.0 361.8 reduce-scatter.16
  1897.6 709.8 reduce-scatter.22
  2610.2 971.7 reduce-scatter.24
  3584.9 972.7 reduce-scatter.26
  4560.4 972.7 reduce-scatter.28
where the time goes:
time: 5550 us; the launch traced here: 5540 us
  waiting for transfers between devices  5090 us (92%)
  matrix products  277 us (5%)
  blocking collectives  82.2 us (1%)
    reduce_scatter x1, waiting for transfers between devices, per_device(): lax.psum_scatter(ffn_terms[2], ('seq', 'dp'), scatter_dimension=0, tiled=...  976 us
    reduce_scatter x1, waiting for transfers between devices, per_device(): lax.psum_scatter(ffn_terms[3], ('seq', 'dp'), scatter_dimension=0, tiled=...  976 us
    reduce_scatter x1, waiting for transfers between devices, per_device(): lax.psum_scatter(ffn_terms[1], ('seq', 'dp'), scatter_dimension=0, tiled=...  974 us
    reduce_scatter x1, waiting for transfers between devices, per_device(): lax.psum_scatter(attn_terms[6], ('seq', 'dp'), scatter_dimension=0, tiled...  713 us
    reduce_scatter x1, waiting for transfers between devices, per_device(): lax.psum_scatter(attn_terms[3], ('seq', 'dp'), scatter_dimension=0, tiled...  365 us
    reduce_scatter x1, waiting for transfers between devices, per_device(): lax.psum_scatter(attn_terms[1], ('seq', 'dp'), scatter_dimension=0, tiled...  186 us
    all_gather x1, waiting for transfers between devices, per_device(): lax.all_gather(w_gate, ('seq', 'dp'), axis=0, tiled=True)  136 us
    all_gather x1, waiting for transfers between devices, per_device(): lax.all_gather(w_up, ('seq', 'dp'), axis=0, tiled=True)  132 us
  transfers between devices with their start and end apart: 20, of which 19 were waited for; matrix products, arithmetic and copies ran while one was open for 4% of the time, Pallas kernels for 0%

commit v1 on v0

v1 whole, which is shorter than its diff:
```python
import math

import jax
import jax.numpy as jnp
import numpy as np
from jax import lax
from jax.sharding import Mesh
from jax.sharding import PartitionSpec as P

epsilon = 1e-06
CORES = 2
f32, bf16 = jnp.float32, jnp.bfloat16


def rms_scale(values):
    return lax.rsqrt(jnp.mean(values * values, axis=-1, keepdims=True) + epsilon)


def rotate_half(values):
    half_width = values.shape[-1] // 2
    return jnp.concatenate([-values[..., half_width:], values[..., :half_width]], axis=-1)


def rotary(positions, head_width):
    half_width = head_width // 2
    frequency = jnp.exp(
        jnp.arange(half_width, dtype=f32) * (-2.0 * math.log(10000.0) / head_width)
    )
    angles = positions.astype(f32)[:, None] * frequency[None, :]
    cos_table = jnp.cos(angles)
    sin_table = jnp.sin(angles)
    return (
        jnp.concatenate([cos_table, cos_table], -1),
        jnp.concatenate([sin_table, sin_table], -1),
    )


def matmul(left, right):
    return jnp.dot(left, right, preferred_element_type=f32)


def inner_rows(left, right):
    return lax.dot_general(left, right, (((0,), (0,)), ((), ())), preferred_element_type=f32)


def outer_cols(left, right):
    return lax.dot_general(left, right, (((1,), (1,)), ((), ())), preferred_element_type=f32)


def norm_back(grad_in, inputs, scale_rows, gain):
    weighted = grad_in * gain
    return scale_rows * weighted - inputs * scale_rows**3 * jnp.mean(
        weighted * inputs, axis=-1, keepdims=True
    )


def take(blocks, index):
    return lax.dynamic_index_in_dim(blocks, index, 0, keepdims=False)


def swap_cores(block):
    return lax.ppermute(block, "core", [(0, 1), (1, 0)])


def to_chip(block, bits):
    count = lax.axis_size("chip")
    return lax.ppermute(block, "chip", [(i, i ^ bits) for i in range(count)])


def placed_blocks(pairs, count):
    result = jnp.zeros((count,) + pairs[0][1].shape, pairs[0][1].dtype)
    for index, block in pairs:
        result = lax.dynamic_update_index_in_dim(result, block, index, 0)
    return result


def gather_chips(block):
    count, me = lax.axis_size("chip"), lax.axis_index("chip")
    rows = block.shape[0]
    if count != 4:
        return lax.all_gather(block, "chip", axis=0, tiled=True)
    top, low = block[: rows // 2], block[rows // 2 :]
    top_x, low_y = to_chip(top, 1), to_chip(low, 2)
    top_y, low_x = to_chip(top, 2), to_chip(low, 1)
    top_d, low_d = to_chip(top_x, 2), to_chip(low_y, 1)
    pairs = [
        (2 * me, top),
        (2 * me + 1, low),
        (2 * (me ^ 1), top_x),
        (2 * (me ^ 1) + 1, low_x),
        (2 * (me ^ 2), top_y),
        (2 * (me ^ 2) + 1, low_y),
        (2 * (me ^ 3), top_d),
        (2 * (me ^ 3) + 1, low_d),
    ]
    return placed_blocks(pairs, 2 * count).reshape(count * rows, block.shape[1])


def add(left, right):
    return left.astype(f32) + right.astype(f32)


def scatter_chips(terms):
    count, me = lax.axis_size("chip"), lax.axis_index("chip")
    if count != 4:
        return lax.psum_scatter(terms, "chip", scatter_dimension=0, tiled=True).astype(f32)
    rows = terms.shape[0] // count
    blocks = terms.reshape(2 * count, rows // 2, terms.shape[1])
    top = [take(blocks, 2 * (me ^ k)) for k in range(4)]
    low = [take(blocks, 2 * (me ^ k) + 1) for k in range(4)]
    top_far = add(top[2], to_chip(top[3], 1)).astype(bf16)
    low_far = add(low[1], to_chip(low[3], 2)).astype(bf16)
    top_near = add(top[0], to_chip(top[1], 1))
    low_near = add(low[0], to_chip(low[2], 2))
    top_sum = top_near + to_chip(top_far, 2).astype(f32)
    low_sum = low_near + to_chip(low_far, 1).astype(f32)
    return jnp.concatenate([top_sum, low_sum], 0)


def exchange_chips(blocks):
    count, me = lax.axis_size("chip"), lax.axis_index("chip")
    pairs = [(me, take(blocks, me))]
    for bits in range(1, count):
        pairs.append((me ^ bits, to_chip(take(blocks, me ^ bits), bits)))
    return placed_blocks(pairs, count)


def by_columns(weight):
    count = lax.axis_size("chip")
    rows, width = weight.shape
    return weight.reshape(rows, count, width // count).transpose(1, 0, 2)


def gather_columns(weight):
    mine = exchange_chips(by_columns(weight))
    whole = lax.all_gather(mine, ("core", "dp"), axis=1, tiled=False)
    return whole.reshape(-1, mine.shape[-1])


def gather_rows(weight):
    return lax.all_gather(weight, ("core", "dp"), axis=0, tiled=True)


def sum_cores(terms):
    me = lax.axis_index("core")
    return add(take(terms, me), swap_cores(take(terms, 1 - me))).astype(bf16)


def scatter_rows(terms):
    rows, width = terms.shape
    half = sum_cores(terms.reshape(CORES, rows // CORES, width))
    return lax.psum_scatter(half, "dp", scatter_dimension=0, tiled=True)


def scatter_columns(terms):
    chips, dp = lax.axis_size("chip"), lax.axis_size("dp")
    width = terms.shape[1]
    split = terms.reshape(chips, CORES, dp, -1, width).transpose(1, 2, 0, 3, 4)
    half = sum_cores(split.reshape(CORES, dp, -1, width))
    mine = lax.psum_scatter(half, "dp", scatter_dimension=0, tiled=True)
    mine = exchange_chips(mine.reshape(chips, -1, width))
    return mine.transpose(1, 0, 2).reshape(-1, chips * width)


def pair_in(block):
    me = lax.axis_index("core")
    kept, got = take(block, me), swap_cores(take(block, 1 - me))
    return jnp.where(
        me == 0, jnp.concatenate([kept, got], 0), jnp.concatenate([got, kept], 0)
    )


def pair_out(rows):
    me = lax.axis_index("core")
    blocks = rows.reshape(CORES, -1, rows.shape[1])
    kept, got = take(blocks, me), swap_cores(take(blocks, 1 - me))
    return jnp.where(me == 0, jnp.stack([kept, got]), jnp.stack([got, kept]))


def attention_scores(queries, keys, length, score_scale):
    span = keys.shape[0]
    pos = jnp.arange(span, dtype=jnp.int32)
    visible = (pos[None, :] <= pos[:, None]) & (pos[None, :] < length)
    scores = jnp.einsum("hqd,kd->hqk", queries, keys, preferred_element_type=f32)
    return jnp.where(visible[None], scores * score_scale, -1e30)


def per_device(
    tokens,
    lengths,
    attn_gain,
    w_qdown,
    q_gain,
    w_qup,
    w_key,
    w_value,
    w_out,
    ffn_gain,
    w_gate,
    w_up,
    w_down,
    cotangent,
):
    slot_count, seq_span, width = tokens.shape[1:]
    assert slot_count == CORES
    chips, dp = lax.axis_size("chip"), lax.axis_size("dp")
    chip, core = lax.axis_index("chip"), lax.axis_index("core")
    devices = chips * CORES * dp
    row_count = CORES * seq_span
    span = chips * row_count
    head_width = w_key.shape[1]
    q_width = w_qdown.shape[1]
    heads = w_qup.shape[1] // head_width // chips
    score_scale = 1.0 / math.sqrt(head_width)
    grad_scale = 1.0 / math.sqrt(slot_count * seq_span * devices)

    own_rows, own_q = attn_gain.shape[0], q_gain.shape[0]
    gains = jnp.stack([attn_gain, ffn_gain, jnp.pad(q_gain, (0, own_rows - own_q))], 1)
    small = jnp.concatenate([w_qdown, w_key, w_value, jnp.pad(gains, ((0, 0), (0, 125)))], 1)
    small = lax.all_gather(small, ("chip", "core", "dp"), axis=0, tiled=True)
    down_q = small[:, :q_width]
    key_value = small[:, q_width : q_width + 2 * head_width]
    gains = small[:, q_width + 2 * head_width :][:, :3].astype(f32)
    gain_one, gain_two = gains[:, 0], gains[:, 1]
    gain_q = gains[:, 2].reshape(devices, own_rows)[:, :own_q].reshape(-1)
    up_q = gather_columns(w_qup)
    out_proj = gather_rows(w_out)
    gate_proj = gather_columns(w_gate)
    up_proj = gather_columns(w_up)
    down_proj = gather_rows(w_down)

    length = lengths[0, core]
    positions = chip * row_count + jnp.arange(row_count, dtype=jnp.int32)
    cos_own, sin_own = rotary(positions, head_width)
    cos_all, sin_all = rotary(jnp.arange(span, dtype=jnp.int32), head_width)
    valid_mask = (positions < length).astype(f32)[:, None]

    inputs = pair_in(tokens[0]).astype(f32)
    seed_grad = (pair_in(cotangent[0]).astype(f32) * valid_mask).astype(bf16)
    seed_all = gather_chips(seed_grad)

    scale_one = rms_scale(inputs)
    normed = (inputs * scale_one * gain_one).astype(bf16)
    normed_cols = exchange_chips(by_columns(normed)).reshape(span, -1)
    q_down = matmul(normed, down_q)
    scale_q = rms_scale(q_down)
    q_normed = (q_down * scale_q * gain_q).astype(bf16)
    kv_raw = matmul(normed, key_value)
    k_raw, v_raw = kv_raw[:, :head_width], kv_raw[:, head_width:]
    key_rows = (k_raw * cos_own + rotate_half(k_raw) * sin_own).astype(bf16)
    shared = gather_chips(jnp.concatenate([q_normed, key_rows, v_raw.astype(bf16)], 1))
    q_normed_all = shared[:, :q_width]
    keys = shared[:, q_width : q_width + head_width]
    values = shared[:, q_width + head_width :]

    q_raw = matmul(q_normed_all, up_q).reshape(span, heads, head_width)
    queries = (q_raw * cos_all[:, None] + rotate_half(q_raw) * sin_all[:, None]).astype(bf16)
    queries = queries.transpose(1, 0, 2)
    scores = attention_scores(queries, keys, length, score_scale)
    row_top = jnp.max(scores, axis=-1, keepdims=True)
    log_total = row_top + jnp.log(jnp.sum(jnp.exp(scores - row_top), axis=-1, keepdims=True))
    probs = jnp.exp(scores - log_total).astype(bf16)
    mixed = jnp.einsum("hqk,kd->hqd", probs, values, preferred_element_type=f32)
    mixed = mixed.astype(bf16).transpose(1, 0, 2).reshape(span, heads * head_width)
    middle = inputs + scatter_chips(matmul(mixed, out_proj).astype(bf16))
    scale_two = rms_scale(middle)
    normed2 = gather_chips((middle * scale_two * gain_two).astype(bf16))

    gate_val = matmul(normed2, gate_proj)
    up_val = matmul(normed2, up_proj)
    sigma = jax.nn.sigmoid(gate_val)
    activated = (gate_val * sigma * up_val).astype(bf16)
    output = middle + scatter_chips(matmul(activated, down_proj).astype(bf16))
    out_tokens = pair_out(output.astype(bf16))[None]

    grad_act = outer_cols(seed_all, down_proj)
    gate_grad = (grad_act * up_val * sigma * (1.0 + gate_val * (1.0 - sigma))).astype(bf16)
    up_grad = (grad_act * gate_val * sigma).astype(bf16)
    grad_normed2 = scatter_chips(
        (outer_cols(gate_grad, gate_proj) + outer_cols(up_grad, up_proj)).astype(bf16)
    )
    grad_w_down = scatter_rows((inner_rows(activated, seed_all) * grad_scale).astype(bf16))
    grad_w_gate = scatter_columns((inner_rows(normed2, gate_grad) * grad_scale).astype(bf16))
    grad_w_up = scatter_columns((inner_rows(normed2, up_grad) * grad_scale).astype(bf16))
    gain_two_terms = jnp.sum(grad_normed2 * middle * scale_two, axis=0) * grad_scale
    grad_middle = seed_grad.astype(f32) + norm_back(grad_normed2, middle, scale_two, gain_two)
    grad_branch = gather_chips(grad_middle.astype(bf16))
    grad_mixed = outer_cols(grad_branch, out_proj).astype(bf16)
    grad_w_out = scatter_rows((inner_rows(mixed, grad_branch) * grad_scale).astype(bf16))

    grad_mixed = grad_mixed.reshape(span, heads, head_width).transpose(1, 0, 2)
    scores = attention_scores(queries, keys, length, score_scale)
    exact = jnp.exp(scores - log_total)
    grad_probs = jnp.einsum("hqd,kd->hqk", grad_mixed, values, preferred_element_type=f32)
    grad_scores = (
        exact * (grad_probs - jnp.sum(exact * grad_probs, axis=-1, keepdims=True))
    ).astype(bf16)
    grad_q = jnp.einsum("hqk,kd->qhd", grad_scores, keys, preferred_element_type=f32)
    grad_q = grad_q * score_scale
    grad_k = jnp.einsum("hqk,hqd->kd", grad_scores, queries, preferred_element_type=f32)
    grad_v = jnp.einsum(
        "hqk,hqd->kd", exact.astype(bf16), grad_mixed, preferred_element_type=f32
    )
    grad_q = grad_q * cos_all[:, None] - rotate_half(grad_q * sin_all[:, None])
    grad_q = grad_q.astype(bf16).reshape(span, heads * head_width)
    grad_w_qup = scatter_columns((inner_rows(q_normed_all, grad_q) * grad_scale).astype(bf16))
    back = jnp.concatenate([outer_cols(grad_q, up_q), grad_k * score_scale, grad_v], 1)
    back = scatter_chips(back.astype(bf16))
    grad_q_normed = back[:, :q_width]
    key_sum = back[:, q_width : q_width + head_width]
    value_sum = back[:, q_width + head_width :]
    grad_k = key_sum * cos_own - rotate_half(key_sum * sin_own)
    grad_q_down = norm_back(grad_q_normed, q_down, scale_q, gain_q)
    gain_q_terms = jnp.sum(grad_q_normed * q_down * scale_q, axis=0) * grad_scale
    back = jnp.concatenate([grad_q_down, grad_k, value_sum], 1).astype(bf16)
    grad_normed = outer_cols(back, small[:, : q_width + 2 * head_width])
    grad_inputs = grad_middle + norm_back(grad_normed, inputs, scale_one, gain_one)
    grad_tokens = pair_out(grad_inputs)[None]
    gain_one_terms = jnp.sum(grad_normed * inputs * scale_one, axis=0) * grad_scale

    grad_small = (inner_rows(normed_cols, gather_chips(back)) * grad_scale).astype(bf16)
    grad_small = scatter_rows(grad_small).astype(f32)
    grad_gains = jnp.concatenate(
        [
            gain_one_terms.reshape(devices, own_rows),
            gain_two_terms.reshape(devices, own_rows),
            gain_q_terms.reshape(devices, own_q),
        ],
        1,
    )
    grad_gains = lax.psum_scatter(
        grad_gains, ("chip", "core", "dp"), scatter_dimension=0, tiled=True
    )[0]
    return (
        out_tokens,
        grad_tokens,
        grad_gains[:own_rows],
        grad_small[:, :q_width],
        grad_gains[2 * own_rows :],
        grad_w_qup.astype(f32),
        grad_small[:, q_width : q_width + head_width],
        grad_small[:, q_width + head_width :],
        grad_w_out.astype(f32),
        grad_gains[own_rows : 2 * own_rows],
        grad_w_gate.astype(f32),
        grad_w_up.astype(f32),
        grad_w_down.astype(f32),
    )


def solution(mesh):
    seq, dp = mesh.shape["seq"], mesh.shape["dp"]
    chips = Mesh(
        np.asarray(mesh.devices).reshape(seq // CORES, CORES, dp), ("chip", "core", "dp")
    )
    every = ("chip", "core", "dp")
    rows, vector = P(every, None), P(every)
    block = P("dp", None, ("chip", "core"), None)
    weights = (vector, rows, vector, rows, rows, rows, rows, vector, rows, rows, rows)
    return jax.shard_map(
        per_device,
        mesh=chips,
        in_specs=(block, P("dp", None)) + weights + (block,),
        out_specs=(block, block) + weights,
        check_vma=False,
    )
```

time: 5550 us -> 925 us (0.17)
  waiting for transfers between devices: 5090 us -> 378 us
  local copies, waits for them, and re-layouts: 39.9 us -> 143 us
  matrix products: 277 us -> 176 us
  starting transfers between devices: 1.44 us -> 89.8 us
    reduce_scatter x10 -> x6, waiting for transfers between devices: 4360 us -> 59.4 us  [the longest x3 50.4 us: scatter_rows(): return lax.psum_scatter(half, 'dp', scatter_dimension=0, tiled=True)]
    all_gather x10 -> x6, waiting for transfers between devices: 725 us -> 68 us  [the longest x3 29 us: gather_columns(): whole = lax.all_gather(mine, ('core', 'dp'), axis=1, tiled=False)]
    ppermute x0 -> x85, waiting for transfers between devices: none -> 249 us  [the longest x75 232 us: to_chip(): return lax.ppermute(block, 'chip', [(i, i ^ bits) for i in range(count)])]
    ppermute x0 -> x85, starting transfers between devices: none -> 89.1 us  [the longest x75 87.7 us: to_chip(): return lax.ppermute(block, 'chip', [(i, i ^ bits) for i in range(count)])]
    dynamic_update_slice x0 -> x68, local copies, waits for them, and re-layouts: none -> 67.2 us  [placed_blocks(): result = lax.dynamic_update_index_in_dim(result, block, index, 0)]
    dot_general x12 -> x6, matrix products: 106 us -> 39.4 us  [inner_rows(): lax.dot_general(left, right, (((0,), (0,)), ((), ())), preferred_element_...]
  transfers between devices with their start and end apart: 20 -> 97, of which waited for: 19 -> 48; matrix products, arithmetic and copies ran while one was open for 4% -> 35% of each run, Pallas kernels for 0% -> 0%
where the time goes in v1:
time: 925 us; the launch traced here: 915 us
  waiting for transfers between devices  378 us (41%)
  matrix products  176 us (19%)
  local copies, waits for them, and re-layouts  143 us (15%)
  starting transfers between devices  89.8 us (10%)
  other arithmetic  71.4 us (8%)
  blocking collectives  40.1 us (4%)
  between operations  16.6 us (2%)
    ppermute x75, waiting for transfers between devices, to_chip(): return lax.ppermute(block, 'chip', [(i, i ^ bits) for i in range(count)])  232 us
    ppermute x75, starting transfers between devices, to_chip(): return lax.ppermute(block, 'chip', [(i, i ^ bits) for i in range(count)])  87.7 us
    dynamic_update_slice x68, local copies, waits for them, and re-layouts, placed_blocks(): result = lax.dynamic_update_index_in_dim(result, block, index, 0)  67.2 us
    reduce_scatter x3, waiting for transfers between devices, scatter_rows(): return lax.psum_scatter(half, 'dp', scatter_dimension=0, tiled=True)  50.4 us
    dot_general x7, matrix products, matmul(): return jnp.dot(left, right, preferred_element_type=f32)  49.8 us
    dot_general x6, matrix products, outer_cols(): lax.dot_general(left, right, (((1,), (1,)), ((), ())), preferred_element_...  45.4 us
    unnamed x1, blocking collectives  40.1 us
    dot_general x6, matrix products, inner_rows(): lax.dot_general(left, right, (((0,), (0,)), ((), ())), preferred_element_...  39.4 us
  transfers between devices with their start and end apart: 97, of which 48 were waited for; matrix products, arithmetic and copies ran while one was open for 35% of the time, Pallas kernels for 0%

profile of v1, /device:TPU:0, one launch (start us, length us, event | category | flops | bytes accessed | tf_op | source)
XLA Modules:
  0.0 914.7 jit_solution(1379419088847872943)
XLA Ops:
  78.6 9.8 %collective-permute-done.36 = bf16[128,2048]{1,0:T(8,128)(2,1)} collective-permute-done((bf16[128,2048]{1,0:T(8,128)(2,1)}, bf16[128,2048]{1,0:T(8,128)(2,1)}, u32[]{:S(2)}, u32[]{:S(2)}) %collective-permute-start.36) | collective-permute-done | bytes 524320 | tf_op jit(solution)/shard_map/ppermute | solution.py:67
  88.4 11.0 %collective-permute-done.39 = bf16[128,2048]{1,0:T(8,128)(2,1)} collective-permute-done((bf16[128,2048]{1,0:T(8,128)(2,1)}, bf16[128,2048]{1,0:T(8,128)(2,1)}, u32[]{:S(2)}, u32[]{:S(2)}) %collective-permute-start.39) | collective-permute-done | bytes 524320 | tf_op jit(solution)/shard_map/ppermute | solution.py:67
  109.3 24.7 %all-gather.7.cloned.1.call-done = bf16[2048,1664]{1,0:T(8,128)(2,1)} async-done(((bf16[64,1664]{1,0:T(8,128)(2,1)}), bf16[2048,1664]{1,0:T(8,128)(2,1)}) %all-gather.7.cloned.1.call-update) | async-done | bytes 6815760 | tf_op jit(solution)/shard_map/all_gather | solution.py:220
  149.3 8.4 collective-permute-done.1
  158.8 6.7 collective-permute-done.2
  169.2 6.9 collective-permute-done.5
  195.8 7.1 convolution_convert_fusion.2
  202.9 7.5 convolution_convert_fusion.1
  218.7 7.8 collective-permute-done.11
  228.7 14.3 %all-gather.17.cloned.1.call-done = bf16[1408,2048]{1,0:T(8,128)(2,1)} async-done(((bf16[176,2048]{1,0:T(8,128)(2,1)}), bf16[1408,2048]{1,0:T(8,128)(2,1)}) %all-gather.17.cloned.1.call-update) | async-done | bytes 5767184 | tf_op jit(solution)/shard_map/all_gather | solution.py:141
  243.0 12.0 %fusion.93 = f32[1024,1408]{1,0:T(8,128)} fusion(bf16[1024,2048]{1,0:T(8,128)(2,1)} %bitcast.76, bf16[1408,2048]{1,0:T(8,128)(2,1)} %all-gather.17.cloned.1.call-done), kind=kOutput, calls=%fused_computation.336 | convolution fusion | flops 5905580032 | bytes 15728640 | tf_op jit(solution)/shard_map/dot_general | solution.py:47
  266.1 6.9 collective-permute-done.62
  273.1 10.2 %collective-permute-done.13 = bf16[128,2048]{1,0:T(8,128)(2,1)S(1)} collective-permute-done((bf16[128,2048]{1,0:T(8,128)(2,1)}, bf16[128,2048]{1,0:T(8,128)(2,1)S(1)}, u32[]{:S(2)}, u32[]{:S(2)}) %collective-permute-start.13) | collective-permute-done | bytes 524320 | tf_op jit(solution)/shard_map/ppermute | solution.py:67
  294.1 6.5 collective-permute-done.16
  302.9 9.5 %collective-permute-done.19 = bf16[128,2048]{1,0:T(8,128)(2,1)S(1)} collective-permute-done((bf16[128,2048]{1,0:T(8,128)(2,1)S(1)}, bf16[128,2048]{1,0:T(8,128)(2,1)S(1)}, u32[]{:S(2)}, u32[]{:S(2)}) %collective-permute-start.19) | collective-permute-done | bytes 524320 | tf_op jit(solution)/shard_map/ppermute | solution.py:67
  316.4 5.2 collective-permute-done.20
  323.3 11.8 %fusion.92 = f32[1024,1408]{1,0:T(8,128)} fusion(bf16[1024,2048]{1,0:T(8,128)(2,1)} %bitcast.44, bf16[2048,1408]{1,0:T(8,128)(2,1)} %bitcast.540), kind=kOutput, calls=%fused_computation.335 | convolution fusion | flops 5905580032 | bytes 15728640 | tf_op jit(solution)/shard_map/dot_general | solution.py:39
  335.1 29.0 %all-gather.13.cloned.1.call-done = bf16[4,8,64,1408]{3,2,1,0:T(8,128)(2,1)} async-done(((bf16[4,1,64,1408]{3,2,1,0:T(8,128)(2,1)}), bf16[4,8,64,1408]{3,2,1,0:T(8,128)(2,1)}) %all-gather.13.cloned.1.call-update) | async-done | bytes 5767184 | tf_op jit(solution)/shard_map/all_gather | solution.py:136
  364.1 17.0 %multiply_convert_fusion.6 = (bf16[1024,1408]{1,0:T(8,128)(2,1)}, bf16[1024,1408]{1,0:T(8,128)(2,1)}, bf16[1024,1408]{1,0:T(8,128)(2,1)}) fusion(f32[1024,1408]{1,0:T(8,128)} %fusion.93, f32[1024,1408]{1,0:T(8,128)} %fusion.92, bf16[1024,2048]{1,0:T(8,128)(2,1)} %bitcast.44, bf16[2048,1408]{1,0:T(8,128)(2,1)} %bitcast.542), kind=kOutput, calls=%fused_computation.21 | convolution fusion | flops 5928648704 | bytes 30146560 | tf_op jit(solution)/shard_map/dot_general | solution.py:39
  381.2 10.5 %fusion.94 = f32[1024,2048]{1,0:T(8,128)} fusion(bf16[1024,1408]{1,0:T(8,128)(2,1)} %get-tuple-element.28, bf16[2048,1408]{1,0:T(8,128)(2,1)S(1)} %bitcast.541), kind=kOutput, calls=%fused_computation.337 | convolution fusion | flops 5905580032 | bytes 17039360 | tf_op jit(solution)/shard_map/dot_general | solution.py:47
  391.7 10.4 %add_convert_fusion = bf16[1024,2048]{1,0:T(8,128)(2,1)S(1)} fusion(f32[1024,2048]{1,0:T(8,128)} %fusion.94, bf16[1024,1408]{1,0:T(8,128)(2,1)} %get-tuple-element.26, bf16[2048,1408]{1,0:T(8,128)(2,1)S(1)} %bitcast.543), kind=kOutput, calls=%fused_computation.11 | convolution fusion | flops 5909774336 | bytes 21233664 | tf_op jit(solution)/shard_map/dot_general | solution.py:47
  403.9 6.9 convolution_convert_fusion
  421.9 6.4 collective-permute-done.29
  429.9 9.6 %collective-permute-done.42 = bf16[128,2048]{1,0:T(8,128)(2,1)S(1)} collective-permute-done((bf16[128,2048]{1,0:T(8,128)(2,1)S(1)}, bf16[128,2048]{1,0:T(8,128)(2,1)S(1)}, u32[]{:S(2)}, u32[]{:S(2)}) %collective-permute-start.42) | collective-permute-done | bytes 524320 | tf_op jit(solution)/shard_map/ppermute | solution.py:67
  443.5 6.6 collective-permute-done.28
  451.6 31.3 %collective-permute-done.30 = bf16[128,2048]{1,0:T(8,128)(2,1)S(1)} collective-permute-done((bf16[128,2048]{1,0:T(8,128)(2,1)S(1)}, bf16[128,2048]{1,0:T(8,128)(2,1)S(1)}, u32[]{:S(2)}, u32[]{:S(2)}) %collective-permute-start.30) | collective-permute-done | bytes 524320 | tf_op jit(solution)/shard_map/ppermute | solution.py:67
  486.3 9.6 %collective-permute-done.33 = bf16[128,2048]{1,0:T(8,128)(2,1)S(1)} collective-permute-done((bf16[128,2048]{1,0:T(8,128)(2,1)S(1)}, bf16[128,2048]{1,0:T(8,128)(2,1)S(1)}, u32[]{:S(2)}, u32[]{:S(2)}) %collective-permute-start.33) | collective-permute-done | bytes 524320 | tf_op jit(solution)/shard_map/ppermute | solution.py:67
  503.6 10.2 %collective-permute-done.48 = bf16[128,2048]{1,0:T(8,128)(2,1)S(1)} collective-permute-done((bf16[128,2048]{1,0:T(8,128)(2,1)S(1)}, bf16[128,2048]{1,0:T(8,128)(2,1)S(1)}, u32[]{:S(2)}, u32[]{:S(2)}) %collective-permute-start.48) | collective-permute-done | bytes 524320 | tf_op jit(solution)/shard_map/ppermute | solution.py:67
  515.3 11.2 %collective-permute-done.51 = bf16[128,2048]{1,0:T(8,128)(2,1)S(1)} collective-permute-done((bf16[128,2048]{1,0:T(8,128)(2,1)S(1)}, bf16[128,2048]{1,0:T(8,128)(2,1)S(1)}, u32[]{:S(2)}, u32[]{:S(2)}) %collective-permute-start.51) | collective-permute-done | bytes 524320 | tf_op jit(solution)/shard_map/ppermute | solution.py:67
  527.2 7.0 collective-permute-done.52
  535.7 5.8 convolution_convert_fusion.3
  544.4 14.3 %multiply_reduce_fusion = (f32[4,1024]{1,0:T(4,128)S(1)}, f32[4,1024,1024]{1,2,0:T(8,128)}) fusion(f32[4,1024,1024]{1,2,0:T(8,128)} %copy-done.2, f32[4,1024]{1,0:T(4,128)S(1)} %copy-done.46, pred[1024,1024]{0,1:T(8,128)(4,1)S(1)} %fusion.13, bf16[1024,1536]{1,0:T(8,128)(2,1)} %bitcast.474, bf16[1024,4,256]{2,0,1:T(8,128)(2,1)S(1)} %copy.118), kind=kOutput, calls=%fused_computation.1 | convolution fusion | flops 2168451072 | bytes 37257216 | tf_op jit(solution)/shard_map/hqd,kd->hqk/dot_general | solution.py:294
  558.6 10.6 %fusion.48 = bf16[1024,256]{1,0:T(8,128)(2,1)} fusion(bf16[1024,4,256]{2,0,1:T(8,128)(2,1)S(1)} %copy.118, f32[4,1024,1024]{1,2,0:T(8,128)} %copy-done.2, f32[4,1024]{1,0:T(4,128)S(1)} %copy-done.46, pred[1024,1024]{0,1:T(8,128)(4,1)S(1)} %fusion.13), kind=kOutput, calls=%fused_computation.103 | convolution fusion | flops 2164523008 | bytes 20463616 | tf_op jit(solution)/shard_map/hqk,hqd->kd/dot_general | solution.py:301
  569.3 8.5 multiply_convert_fusion
  600.8 9.4 %multiply_convert_fusion.2 = bf16[2048,1408]{1,0:T(8,128)(2,1)S(1)} fusion(bf16[1024,2048]{1,0:T(8,128)(2,1)} %bitcast.44, bf16[1024,1408]{1,0:T(8,128)(2,1)S(1)} %copy-done.72), kind=kOutput, calls=%fused_computation.7 | convolution fusion | flops 5911347200 | bytes 12845056 | tf_op jit(solution)/shard_map/dot_general | solution.py:43
  632.5 7.6 collective-permute-done.64
  641.6 7.5 collective-permute-done.67
  667.5 9.9 %multiply_convert_fusion.3 = bf16[2048,1408]{1,0:T(8,128)(2,1)S(1)} fusion(bf16[1024,2048]{1,0:T(8,128)(2,1)} %bitcast.44, bf16[1024,1408]{1,0:T(8,128)(2,1)} %get-tuple-element.26), kind=kOutput, calls=%fused_computation.8 | convolution fusion | flops 5911347200 | bytes 12845056 | tf_op jit(solution)/shard_map/dot_general | solution.py:43
  678.4 5.1 collective-permute-done.76
  685.9 8.9 multiply_convert_fusion.1
  695.3 5.1 collective-permute-done.84
  703.3 7.0 multiply_convert_fusion.4
  730.8 40.1 %all-reduce.2 = f32[32,160]{1,0:T(8,128)S(1)} all-reduce(f32[32,160]{1,0:T(8,128)S(1)} %pad_maximum_fusion.9), channel_id=2, replica_groups=mesh['chip'=4,'core'=2,'dp'=4] {'chip','core','dp'}, use_global_device_ids=true, to_apply=%region_12.13.clone | all-reduce | flops 5120 | bytes 40960
  792.1 9.0 reduce-scatter.13.cloned.1.call-done
  808.0 5.0 dynamic_update_slice.285
  813.2 5.0 dynamic_update_slice.281
  818.2 41.3 %reduce-scatter.17.cloned.1.call-done = bf16[176,2048]{1,0:T(8,128)(2,1)} async-done(((bf16[704,2048]{1,0:T(8,128)(2,1)}), bf16[176,2048]{1,0:T(8,128)(2,1)}) %reduce-scatter.17.cloned.1.call-update) | async-done | bytes 720912 | tf_op jit(solution)/shard_map/reduce_scatter | solution.py:152
  896.5 9.0 reduce-scatter.11.cloned.1.call-done
  (587 shorter events, 356.8 us)
Async XLA Ops:
  7.3 98.1 %all-gather.9.cloned.1.call-start = ((), (), s32[]{:S(2)}) async-start(), calls=%async_computation.7 | async-start | bytes 2359296 | tf_op jit(solution)/shard_map/all_gather | solution.py:136
  19.8 114.2 %all-gather.7.cloned.1.call-start = ((), (), s32[]{:S(2)}) async-start(), calls=%async_computation.6 | async-start | bytes 7028736 | tf_op jit(solution)/shard_map/all_gather | solution.py:220
  20.8 182.1 %all-gather.11.cloned.1.call-start = ((), (), s32[]{:S(2)}) async-start(), calls=%async_computation.8 | async-start | bytes 4718592 | tf_op jit(solution)/shard_map/all_gather | solution.py:141
  21.5 221.5 %all-gather.17.cloned.1.call-start = ((), (), s32[]{:S(2)}) async-start(), calls=%async_computation.11 | async-start | bytes 6488064 | tf_op jit(solution)/shard_map/all_gather | solution.py:141
  22.1 301.2 %all-gather.15.cloned.1.call-start = ((), (), s32[]{:S(2)}) async-start(), calls=%async_computation.10 | async-start | bytes 6488064 | tf_op jit(solution)/shard_map/all_gather | solution.py:136
  33.9 330.2 %all-gather.13.cloned.1.call-start = ((), (), s32[]{:S(2)}) async-start(), calls=%async_computation.9 | async-start | bytes 6488064 | tf_op jit(solution)/shard_map/all_gather | solution.py:136
  34.9 41.8 %collective-permute-start = (bf16[128,2048]{1,0:T(8,128)(2,1)}, bf16[128,2048]{1,0:T(8,128)(2,1)S(1)}, u32[]{:S(2)}, u32[]{:S(2)}) collective-permute-start(bf16[128,2048]{1,0:T(8,128)(2,1)} %get-tuple-element.74), channel_id=1, source_target_pairs={{0,4},{4,0},{1,5},{5,1},{2,6},{6,2},{3,7},{7,3},{8,12},{12,8},{9,1... | collective-permute-start | bytes 1572872 | tf_op jit(solution)/shard_map/ppermute | solution.py:62
  36.1 29.3 %collective-permute-start.35 = (bf16[128,2048]{1,0:T(8,128)(2,1)}, bf16[128,2048]{1,0:T(8,128)(2,1)}, u32[]{:S(2)}, u32[]{:S(2)}) collective-permute-start(bf16[128,2048]{1,0:T(8,128)(2,1)} %get-tuple-element.69), channel_id=1, source_target_pairs={{0,4},{4,0},{1,5},{5,1},{2,6},{6,2},{3,7},{7,3},{8,12},{12,8},{9,1... | collective-permute-start | bytes 1572872 | tf_op jit(solution)/shard_map/ppermute | solution.py:62
  65.1 706.9 %reduce-scatter.9.cloned.1.call-start = ((), (), s32[]{:S(2)}) async-start(), calls=%async_computation.13 | async-start | bytes 1310720 | tf_op jit(solution)/shard_map/reduce_scatter | solution.py:160
  69.9 32.7 %collective-permute-start.38 = (bf16[128,2048]{1,0:T(8,128)(2,1)}, bf16[128,2048]{1,0:T(8,128)(2,1)S(1)}, u32[]{:S(2)}, u32[]{:S(2)}) collective-permute-start(bf16[128,2048]{1,0:T(8,128)(2,1)} %get-tuple-element.67), channel_id=1, source_target_pairs={{0,16},{8,24},{16,0},{24,8},{1,17},{9,25},{17,1},{25,9},{2,18},{10... | collective-permute-start | bytes 1572872 | tf_op jit(solution)/shard_map/ppermute | solution.py:67
  70.8 31.0 %collective-permute-start.37 = (bf16[128,2048]{1,0:T(8,128)(2,1)}, bf16[128,2048]{1,0:T(8,128)(2,1)S(1)}, u32[]{:S(2)}, u32[]{:S(2)}) collective-permute-start(bf16[128,2048]{1,0:T(8,128)(2,1)} %get-tuple-element.66), channel_id=1, source_target_pairs={{0,8},{8,0},{16,24},{24,16},{1,9},{9,1},{17,25},{25,17},{2,10},{10... | collective-permute-start | bytes 1572872 | tf_op jit(solution)/shard_map/ppermute | solution.py:67
  71.3 28.1 %collective-permute-start.39 = (bf16[128,2048]{1,0:T(8,128)(2,1)}, bf16[128,2048]{1,0:T(8,128)(2,1)}, u32[]{:S(2)}, u32[]{:S(2)}) collective-permute-start(bf16[128,2048]{1,0:T(8,128)(2,1)} %get-tuple-element.66), channel_id=1, source_target_pairs={{0,16},{8,24},{16,0},{24,8},{1,17},{9,25},{17,1},{25,9},{2,18},{10... | collective-permute-start | bytes 1572872 | tf_op jit(solution)/shard_map/ppermute | solution.py:67
  88.4 124.8 %collective-permute-start.40 = (bf16[128,2048]{1,0:T(8,128)(2,1)}, bf16[128,2048]{1,0:T(8,128)(2,1)}, u32[]{:S(2)}, u32[]{:S(2)}) collective-permute-start(bf16[128,2048]{1,0:T(8,128)(2,1)} %collective-permute-done.36), channel_id=1, source_target_pairs={{0,16},{8,24},{16,0},{24,8},{1,17},{9,25},{17,1},{25,9},{2,18},{10... | collective-permute-start | bytes 1572872 | tf_op jit(solution)/shard_map/ppermute | solution.py:67
  99.4 115.7 %collective-permute-start.41 = (bf16[128,2048]{1,0:T(8,128)(2,1)}, bf16[128,2048]{1,0:T(8,128)(2,1)}, u32[]{:S(2)}, u32[]{:S(2)}) collective-permute-start(bf16[128,2048]{1,0:T(8,128)(2,1)} %collective-permute-done.39), channel_id=1, source_target_pairs={{0,8},{8,0},{16,24},{24,16},{1,9},{9,1},{17,25},{25,17},{2,10},{10... | collective-permute-start | bytes 1572872 | tf_op jit(solution)/shard_map/ppermute | solution.py:67
  217.0 43.6 %collective-permute-start.10 = (bf16[128,2048]{1,0:T(8,128)(2,1)}, bf16[128,2048]{1,0:T(8,128)(2,1)S(1)}, u32[]{:S(2)}, u32[]{:S(2)}) collective-permute-start(bf16[128,2048]{1,0:T(8,128)(2,1)} %get-tuple-element.45), channel_id=1, source_target_pairs={{0,8},{8,0},{16,24},{24,16},{1,9},{9,1},{17,25},{25,17},{2,10},{10... | collective-permute-start | bytes 1572872 | tf_op jit(solution)/shard_map/ppermute | solution.py:67
  217.7 43.4 %collective-permute-start.14 = (bf16[128,2048]{1,0:T(8,128)(2,1)}, bf16[128,2048]{1,0:T(8,128)(2,1)S(1)}, u32[]{:S(2)}, u32[]{:S(2)}) collective-permute-start(bf16[128,2048]{1,0:T(8,128)(2,1)} %get-tuple-element.46), channel_id=1, source_target_pairs={{0,16},{8,24},{16,0},{24,8},{1,17},{9,25},{17,1},{25,9},{2,18},{10... | collective-permute-start | bytes 1572872 | tf_op jit(solution)/shard_map/ppermute | solution.py:67
  227.5 35.1 %collective-permute-start.12 = (bf16[128,2048]{1,0:T(8,128)(2,1)}, bf16[128,2048]{1,0:T(8,128)(2,1)}, u32[]{:S(2)}, u32[]{:S(2)}) collective-permute-start(bf16[128,2048]{1,0:T(8,128)(2,1)} %fusion.62), channel_id=1, source_target_pairs={{0,16},{8,24},{16,0},{24,8},{1,17},{9,25},{17,1},{25,9},{2,18},{10... | collective-permute-start | bytes 1572872 | tf_op jit(solution)/shard_map/ppermute | solution.py:67
  260.6 158.2 %collective-permute-start.63 = (bf16[256,512]{1,0:T(8,128)(2,1)}, bf16[256,512]{1,0:T(8,128)(2,1)}, u32[]{:S(2)}, u32[]{:S(2)}) collective-permute-start(bf16[256,512]{1,0:T(8,128)(2,1)} %bitcast.124), channel_id=1, source_target_pairs={{0,24},{8,16},{16,8},{24,0},{1,25},{9,17},{17,9},{25,1},{2,26},{10... | collective-permute-start | bytes 786440 | tf_op jit(solution)/shard_map/ppermute | solution.py:67
  261.1 22.2 %collective-permute-start.13 = (bf16[128,2048]{1,0:T(8,128)(2,1)}, bf16[128,2048]{1,0:T(8,128)(2,1)S(1)}, u32[]{:S(2)}, u32[]{:S(2)}) collective-permute-start(bf16[128,2048]{1,0:T(8,128)(2,1)} %get-tuple-element.47), channel_id=1, source_target_pairs={{0,16},{8,24},{16,0},{24,8},{1,17},{9,25},{17,1},{25,9},{2,18},{10... | collective-permute-start | bytes 1572872 | tf_op jit(solution)/shard_map/ppermute | solution.py:67
  286.3 28.4 %collective-permute-start.18 = (bf16[128,2048]{1,0:T(8,128)(2,1)S(1)}, bf16[128,2048]{1,0:T(8,128)(2,1)S(1)}, u32[]{:S(2)}, u32[]{:S(2)}) collective-permute-start(bf16[128,2048]{1,0:T(8,128)(2,1)S(1)} %get-tuple-element.73), channel_id=1, source_target_pairs={{0,16},{8,24},{16,0},{24,8},{1,17},{9,25},{17,1},{25,9},{2,18},{10... | collective-permute-start | bytes 1572872 | tf_op jit(solution)/shard_map/ppermute | solution.py:67
  287.8 26.1 %collective-permute-start.17 = (bf16[128,2048]{1,0:T(8,128)(2,1)S(1)}, bf16[128,2048]{1,0:T(8,128)(2,1)S(1)}, u32[]{:S(2)}, u32[]{:S(2)}) collective-permute-start(bf16[128,2048]{1,0:T(8,128)(2,1)S(1)} %get-tuple-element.72), channel_id=1, source_target_pairs={{0,8},{8,0},{16,24},{24,16},{1,9},{9,1},{17,25},{25,17},{2,10},{10... | collective-permute-start | bytes 1572872 | tf_op jit(solution)/shard_map/ppermute | solution.py:67
  289.2 23.1 %collective-permute-start.19 = (bf16[128,2048]{1,0:T(8,128)(2,1)S(1)}, bf16[128,2048]{1,0:T(8,128)(2,1)S(1)}, u32[]{:S(2)}, u32[]{:S(2)}) collective-permute-start(bf16[128,2048]{1,0:T(8,128)(2,1)S(1)} %get-tuple-element.72), channel_id=1, source_target_pairs={{0,16},{8,24},{16,0},{24,8},{1,17},{9,25},{17,1},{25,9},{2,18},{10... | collective-permute-start | bytes 1572872 | tf_op jit(solution)/shard_map/ppermute | solution.py:67
  412.6 27.0 %collective-permute-start.42 = (bf16[128,2048]{1,0:T(8,128)(2,1)S(1)}, bf16[128,2048]{1,0:T(8,128)(2,1)S(1)}, u32[]{:S(2)}, u32[]{:S(2)}) collective-permute-start(bf16[128,2048]{1,0:T(8,128)(2,1)S(1)} %get-tuple-element.33), channel_id=1, source_target_pairs={{0,8},{8,0},{16,24},{24,16},{1,9},{9,1},{17,25},{25,17},{2,10},{10... | collective-permute-start | bytes 1572872 | tf_op jit(solution)/shard_map/ppermute | solution.py:67
  413.1 27.9 %collective-permute-start.46 = (bf16[128,2048]{1,0:T(8,128)(2,1)S(1)}, bf16[128,2048]{1,0:T(8,128)(2,1)S(1)}, u32[]{:S(2)}, u32[]{:S(2)}) collective-permute-start(bf16[128,2048]{1,0:T(8,128)(2,1)S(1)} %get-tuple-element.34), channel_id=1, source_target_pairs={{0,16},{8,24},{16,0},{24,8},{1,17},{9,25},{17,1},{25,9},{2,18},{10... | collective-permute-start | bytes 1572872 | tf_op jit(solution)/shard_map/ppermute | solution.py:67
  417.2 24.4 %collective-permute-start.44 = (bf16[128,2048]{1,0:T(8,128)(2,1)S(1)}, bf16[128,2048]{1,0:T(8,128)(2,1)S(1)}, u32[]{:S(2)}, u32[]{:S(2)}) collective-permute-start(bf16[128,2048]{1,0:T(8,128)(2,1)S(1)} %fusion.54), channel_id=1, source_target_pairs={{0,16},{8,24},{16,0},{24,8},{1,17},{9,25},{17,1},{25,9},{2,18},{10... | collective-permute-start | bytes 1572872 | tf_op jit(solution)/shard_map/ppermute | solution.py:67
  420.4 29.7 %collective-permute-start.28 = (bf16[128,2048]{1,0:T(8,128)(2,1)S(1)}, bf16[128,2048]{1,0:T(8,128)(2,1)S(1)}, u32[]{:S(2)}, u32[]{:S(2)}) collective-permute-start(bf16[128,2048]{1,0:T(8,128)(2,1)S(1)} %get-tuple-element.39), channel_id=1, source_target_pairs={{0,8},{8,0},{16,24},{24,16},{1,9},{9,1},{17,25},{25,17},{2,10},{10... | collective-permute-start | bytes 1572872 | tf_op jit(solution)/shard_map/ppermute | solution.py:67
  428.3 23.3 %collective-permute-start.32 = (bf16[128,2048]{1,0:T(8,128)(2,1)S(1)}, bf16[128,2048]{1,0:T(8,128)(2,1)S(1)}, u32[]{:S(2)}, u32[]{:S(2)}) collective-permute-start(bf16[128,2048]{1,0:T(8,128)(2,1)S(1)} %get-tuple-element.40), channel_id=1, source_target_pairs={{0,16},{8,24},{16,0},{24,8},{1,17},{9,25},{17,1},{25,9},{2,18},{10... | collective-permute-start | bytes 1572872 | tf_op jit(solution)/shard_map/ppermute | solution.py:67
  439.5 46.8 %collective-permute-start.31 = (bf16[128,2048]{1,0:T(8,128)(2,1)S(1)}, bf16[128,2048]{1,0:T(8,128)(2,1)S(1)}, u32[]{:S(2)}, u32[]{:S(2)}) collective-permute-start(bf16[128,2048]{1,0:T(8,128)(2,1)S(1)} %get-tuple-element.41), channel_id=1, source_target_pairs={{0,16},{8,24},{16,0},{24,8},{1,17},{9,25},{17,1},{25,9},{2,18},{10... | collective-permute-start | bytes 1572872 | tf_op jit(solution)/shard_map/ppermute | solution.py:67
  441.0 43.8 %collective-permute-start.45 = (bf16[128,2048]{1,0:T(8,128)(2,1)S(1)}, bf16[128,2048]{1,0:T(8,128)(2,1)S(1)}, u32[]{:S(2)}, u32[]{:S(2)}) collective-permute-start(bf16[128,2048]{1,0:T(8,128)(2,1)S(1)} %get-tuple-element.35), channel_id=1, source_target_pairs={{0,16},{8,24},{16,0},{24,8},{1,17},{9,25},{17,1},{25,9},{2,18},{10... | collective-permute-start | bytes 1572872 | tf_op jit(solution)/shard_map/ppermute | solution.py:67
  441.6 41.2 %collective-permute-start.30 = (bf16[128,2048]{1,0:T(8,128)(2,1)S(1)}, bf16[128,2048]{1,0:T(8,128)(2,1)S(1)}, u32[]{:S(2)}, u32[]{:S(2)}) collective-permute-start(bf16[128,2048]{1,0:T(8,128)(2,1)S(1)} %fusion.58), channel_id=1, source_target_pairs={{0,16},{8,24},{16,0},{24,8},{1,17},{9,25},{17,1},{25,9},{2,18},{10... | collective-permute-start | bytes 1572872 | tf_op jit(solution)/shard_map/ppermute | solution.py:67
  450.1 34.7 %collective-permute-start.47 = (bf16[128,2048]{1,0:T(8,128)(2,1)S(1)}, bf16[128,2048]{1,0:T(8,128)(2,1)S(1)}, u32[]{:S(2)}, u32[]{:S(2)}) collective-permute-start(bf16[128,2048]{1,0:T(8,128)(2,1)S(1)} %get-tuple-element.32), channel_id=1, source_target_pairs={{0,8},{8,0},{16,24},{24,16},{1,9},{9,1},{17,25},{25,17},{2,10},{10... | collective-permute-start | bytes 1572872 | tf_op jit(solution)/shard_map/ppermute | solution.py:67
  500.4 26.7 %collective-permute-start.50 = (bf16[128,2048]{1,0:T(8,128)(2,1)S(1)}, bf16[128,2048]{1,0:T(8,128)(2,1)S(1)}, u32[]{:S(2)}, u32[]{:S(2)}) collective-permute-start(bf16[128,2048]{1,0:T(8,128)(2,1)S(1)} %get-tuple-element.65), channel_id=1, source_target_pairs={{0,16},{8,24},{16,0},{24,8},{1,17},{9,25},{17,1},{25,9},{2,18},{10... | collective-permute-start | bytes 1572872 | tf_op jit(solution)/shard_map/ppermute | solution.py:67
  501.8 25.2 %collective-permute-start.49 = (bf16[128,2048]{1,0:T(8,128)(2,1)S(1)}, bf16[128,2048]{1,0:T(8,128)(2,1)S(1)}, u32[]{:S(2)}, u32[]{:S(2)}) collective-permute-start(bf16[128,2048]{1,0:T(8,128)(2,1)S(1)} %get-tuple-element.64), channel_id=1, source_target_pairs={{0,8},{8,0},{16,24},{24,16},{1,9},{9,1},{17,25},{25,17},{2,10},{10... | collective-permute-start | bytes 1572872 | tf_op jit(solution)/shard_map/ppermute | solution.py:67
  502.4 24.1 %collective-permute-start.51 = (bf16[128,2048]{1,0:T(8,128)(2,1)S(1)}, bf16[128,2048]{1,0:T(8,128)(2,1)S(1)}, u32[]{:S(2)}, u32[]{:S(2)}) collective-permute-start(bf16[128,2048]{1,0:T(8,128)(2,1)S(1)} %get-tuple-element.64), channel_id=1, source_target_pairs={{0,16},{8,24},{16,0},{24,8},{1,17},{9,25},{17,1},{25,9},{2,18},{10... | collective-permute-start | bytes 1572872 | tf_op jit(solution)/shard_map/ppermute | solution.py:67
  593.4 24.7 %collective-permute-start.71 = (bf16[4,128,1024]{2,1,0:T(8,128)(2,1)S(1)}, bf16[4,128,1024]{2,1,0:T(8,128)(2,1)S(1)}, u32[]{:S(2)}, u32[]{:S(2)}) collective-permute-start(bf16[4,128,1024]{2,1,0:T(8,128)(2,1)S(1)} %dynamic-slice_bitcast_fusion.4), channel_id=1, source_target_pairs={{0,4},{4,0},{1,5},{5,1},{2,6},{6,2},{3,7},{7,3},{8,12},{12,8},{9,1... | collective-permute-start | bytes 3145736 | tf_op jit(solution)/shard_map/ppermute | solution.py:62
  618.1 44.3 %collective-permute-start.80 = (bf16[4,256,1408]{2,1,0:T(8,128)(2,1)}, bf16[4,256,1408]{2,1,0:T(8,128)(2,1)}, u32[]{:S(2)}, u32[]{:S(2)}) collective-permute-start(bf16[4,256,1408]{2,1,0:T(8,128)(2,1)} %dynamic-slice_bitcast_fusion.1), channel_id=1, source_target_pairs={{0,4},{4,0},{1,5},{5,1},{2,6},{6,2},{3,7},{7,3},{8,12},{12,8},{9,1... | collective-permute-start | bytes 8650760 | tf_op jit(solution)/shard_map/ppermute | solution.py:62
  619.5 165.5 %reduce-scatter.7.cloned.1.call-start = ((), (), s32[]{:S(2)}) async-start(), calls=%async_computation.12 | async-start | bytes 983040 | tf_op jit(solution)/shard_map/reduce_scatter | solution.py:152
  628.7 22.0 %collective-permute-start.66 = (bf16[128,1536]{1,0:T(8,128)(2,1)S(1)}, bf16[128,1536]{1,0:T(8,128)(2,1)S(1)}, u32[]{:S(2)}, u32[]{:S(2)}) collective-permute-start(bf16[128,1536]{1,0:T(8,128)(2,1)S(1)} %get-tuple-element.77), channel_id=1, source_target_pairs={{0,16},{8,24},{16,0},{24,8},{1,17},{9,25},{17,1},{25,9},{2,18},{10... | collective-permute-start | bytes 1179656 | tf_op jit(solution)/shard_map/ppermute | solution.py:67
  662.4 124.3 %reduce-scatter.15.cloned.1.call-start = ((), (), s32[]{:S(2)}) async-start(), calls=%async_computation.16 | async-start | bytes 3604480 | tf_op jit(solution)/shard_map/reduce_scatter | solution.py:160
  667.4 133.7 %reduce-scatter.13.cloned.1.call-start = ((), (), s32[]{:S(2)}) async-start(), calls=%async_computation.15 | async-start | bytes 3604480 | tf_op jit(solution)/shard_map/reduce_scatter | solution.py:160
  685.9 173.7 %reduce-scatter.17.cloned.1.call-start = ((), (), s32[]{:S(2)}) async-start(), calls=%async_computation.17 | async-start | bytes 3604480 | tf_op jit(solution)/shard_map/reduce_scatter | solution.py:152
  703.2 202.3 %reduce-scatter.11.cloned.1.call-start = ((), (), s32[]{:S(2)}) async-start(), calls=%async_computation.14 | async-start | bytes 2621440 | tf_op jit(solution)/shard_map/reduce_scatter | solution.py:152
  729.3 47.6 %collective-permute-start.60 = (f32[128,2048]{1,0:T(8,128)S(1)}, f32[128,2048]{1,0:T(8,128)S(1)}, u32[]{:S(2)}, u32[]{:S(2)}) collective-permute-start(f32[128,2048]{1,0:T(8,128)S(1)} %get-tuple-element.58), channel_id=1, source_target_pairs={{0,4},{4,0},{1,5},{5,1},{2,6},{6,2},{3,7},{7,3},{8,12},{12,8},{9,1... | collective-permute-start | bytes 3145736 | tf_op jit(solution)/shard_map/ppermute | solution.py:62
  790.1 72.1 %collective-permute-start.82 = (bf16[64,1408]{1,0:T(8,128)(2,1)S(1)}, bf16[64,1408]{1,0:T(8,128)(2,1)S(1)}, u32[]{:S(2)}, u32[]{:S(2)}) collective-permute-start(bf16[64,1408]{1,0:T(8,128)(2,1)S(1)} %get-tuple-element.81), channel_id=1, source_target_pairs={{0,16},{8,24},{16,0},{24,8},{1,17},{9,25},{17,1},{25,9},{2,18},{10... | collective-permute-start | bytes 540680 | tf_op jit(solution)/shard_map/ppermute | solution.py:67
  790.2 72.3 %collective-permute-start.83 = (bf16[64,1408]{1,0:T(8,128)(2,1)}, bf16[64,1408]{1,0:T(8,128)(2,1)S(1)}, u32[]{:S(2)}, u32[]{:S(2)}) collective-permute-start(bf16[64,1408]{1,0:T(8,128)(2,1)} %get-tuple-element.80), channel_id=1, source_target_pairs={{0,24},{8,16},{16,8},{24,0},{1,25},{9,17},{17,9},{25,1},{2,26},{10... | collective-permute-start | bytes 540680 | tf_op jit(solution)/shard_map/ppermute | solution.py:67
  803.1 76.2 %collective-permute-start.77 = (bf16[64,1408]{1,0:T(8,128)(2,1)}, bf16[64,1408]{1,0:T(8,128)(2,1)S(1)}, u32[]{:S(2)}, u32[]{:S(2)}) collective-permute-start(bf16[64,1408]{1,0:T(8,128)(2,1)} %get-tuple-element.86), channel_id=1, source_target_pairs={{0,8},{8,0},{16,24},{24,16},{1,9},{9,1},{17,25},{25,17},{2,10},{10... | collective-permute-start | bytes 540680 | tf_op jit(solution)/shard_map/ppermute | solution.py:67
  804.6 74.9 %collective-permute-start.78 = (bf16[64,1408]{1,0:T(8,128)(2,1)}, bf16[64,1408]{1,0:T(8,128)(2,1)S(1)}, u32[]{:S(2)}, u32[]{:S(2)}) collective-permute-start(bf16[64,1408]{1,0:T(8,128)(2,1)} %get-tuple-element.85), channel_id=1, source_target_pairs={{0,16},{8,24},{16,0},{24,8},{1,17},{9,25},{17,1},{25,9},{2,18},{10... | collective-permute-start | bytes 540680 | tf_op jit(solution)/shard_map/ppermute | solution.py:67
  806.0 73.8 %collective-permute-start.79 = (bf16[64,1408]{1,0:T(8,128)(2,1)S(1)}, bf16[64,1408]{1,0:T(8,128)(2,1)S(1)}, u32[]{:S(2)}, u32[]{:S(2)}) collective-permute-start(bf16[64,1408]{1,0:T(8,128)(2,1)S(1)} %get-tuple-element.84), channel_id=1, source_target_pairs={{0,24},{8,16},{16,8},{24,0},{1,25},{9,17},{17,9},{25,1},{2,26},{10... | collective-permute-start | bytes 540680 | tf_op jit(solution)/shard_map/ppermute | solution.py:67
  (130 other events, 1752.1 us)
Sparse Core Ops, SparseCore 0:
  19.9 28.4 all-gather.8
  51.2 82.7 all-gather.6
  135.6 46.2 all-gather.10
  183.4 59.5 all-gather.16
  244.4 59.0 all-gather.14
  305.0 59.0 all-gather.12
  619.6 25.9 reduce-scatter.8
  662.5 22.0 reduce-scatter.6
  687.0 55.4 reduce-scatter.14
  744.7 56.3 reduce-scatter.12
  803.5 56.0 reduce-scatter.16
  861.8 43.6 reduce-scatter.10

commit v2 on v1

v2 whole, which is shorter than its diff:
```python
import functools
import math

import jax
import jax.numpy as jnp
import numpy as np
from jax import lax
from jax.experimental import pallas as pl
from jax.experimental.pallas import tpu as pltpu
from jax.sharding import Mesh
from jax.sharding import PartitionSpec as P

epsilon = 1e-06
CORES = 2
TILE = 256
f32, bf16 = jnp.float32, jnp.bfloat16
BESIDE = pl.CostEstimate(flops=1, bytes_accessed=1, transcendentals=0)


def rms_scale(values):
    return lax.rsqrt(jnp.mean(values * values, axis=-1, keepdims=True) + epsilon)


def rotate_half(values):
    half_width = values.shape[-1] // 2
    return jnp.concatenate([-values[..., half_width:], values[..., :half_width]], axis=-1)


def rotary(positions, head_width):
    half_width = head_width // 2
    frequency = jnp.exp(
        jnp.arange(half_width, dtype=f32) * (-2.0 * math.log(10000.0) / head_width)
    )
    angles = positions.astype(f32)[:, None] * frequency[None, :]
    cos_table = jnp.cos(angles)
    sin_table = jnp.sin(angles)
    return (
        jnp.concatenate([cos_table, cos_table], -1),
        jnp.concatenate([sin_table, sin_table], -1),
    )


def matmul(left, right):
    return jnp.dot(left, right, preferred_element_type=f32)


def inner_rows(left, right):
    return lax.dot_general(left, right, (((0,), (0,)), ((), ())), preferred_element_type=f32)


def outer_cols(left, right):
    return lax.dot_general(left, right, (((1,), (1,)), ((), ())), preferred_element_type=f32)


def norm_back(grad_in, inputs, scale_rows, gain):
    weighted = grad_in * gain
    return scale_rows * weighted - inputs * scale_rows**3 * jnp.mean(
        weighted * inputs, axis=-1, keepdims=True
    )


def take(blocks, index):
    return lax.dynamic_index_in_dim(blocks, index, 0, keepdims=False)


def swap_cores(block):
    return lax.ppermute(block, "core", [(0, 1), (1, 0)])


def to_chip(block, bits):
    count = lax.axis_size("chip")
    return lax.ppermute(block, "chip", [(i, i ^ bits) for i in range(count)])


def gather_near(block):
    rows = block.shape[0]
    if lax.axis_size("chip") != 4:
        return (block,)
    top, low = block[: rows // 2], block[rows // 2 :]
    return top, low, to_chip(top, 1), to_chip(low, 1), to_chip(top, 2), to_chip(low, 2)


def join_kernel(*refs):
    *piece_refs, out_ref = refs
    for k, ref in enumerate(piece_refs):

        @pl.when(pl.program_id(0) == k)
        def _():
            out_ref[...] = ref[...]


def join_rows(pieces):
    rows, width = pieces[0].shape
    count = len(pieces)
    return pl.pallas_call(
        join_kernel,
        grid=(count,),
        in_specs=[pl.BlockSpec((rows, width), lambda k: (0, 0))] * count,
        out_specs=pl.BlockSpec((rows, width), lambda k: (k, 0)),
        out_shape=jax.ShapeDtypeStruct((count * rows, width), pieces[0].dtype),
        compiler_params=pltpu.CompilerParams(vmem_limit_bytes=24 << 20),
        cost_estimate=BESIDE,
    )(*pieces)


def gather_far(near):
    if lax.axis_size("chip") != 4:
        return lax.all_gather(near[0], "chip", axis=0, tiled=True)
    return join_rows(list(near) + list(far_halves(near)))


def far_halves(near):
    return to_chip(near[2], 2), to_chip(near[5], 1)


def chip_flip():
    return lax.axis_index("chip") if lax.axis_size("chip") == 4 else jnp.int32(0)


def reordered(blocks, flip):
    bits = 1
    while bits < len(blocks):
        swapped = [blocks[k ^ bits] for k in range(len(blocks))]
        blocks = [jnp.where(flip & bits > 0, b, a) for a, b in zip(blocks, swapped)]
        bits *= 2
    return blocks


def gather_chips(block):
    return gather_far(gather_near(block))


def add(left, right):
    return left.astype(f32) + right.astype(f32)


def scatter_near(pieces):
    if lax.axis_size("chip") != 4:
        return tuple(pieces)
    top, low = pieces[::2], pieces[1::2]
    top_far = add(top[2], to_chip(top[3], 1)).astype(bf16)
    low_far = add(low[1], to_chip(low[3], 2)).astype(bf16)
    return top_far, low_far, top[0], to_chip(top[1], 1), low[0], to_chip(low[2], 2)


def scatter_far(near):
    if lax.axis_size("chip") != 4:
        return lax.psum_scatter(near[0], "chip", scatter_dimension=0, tiled=True).astype(f32)
    top_far, low_far, top, top_x, low, low_y = near
    top = add(top, top_x) + to_chip(top_far, 2).astype(f32)
    low = add(low, low_y) + to_chip(low_far, 1).astype(f32)
    return jnp.concatenate([top, low], 0)


def scatter_chips(pieces, beside=()):
    near, beside = tie(scatter_near(pieces), tuple(beside))
    total = scatter_far(near)
    return (total,) + beside if beside else total


def exchange(parts):
    count = lax.axis_size("chip")
    if count != 4:
        blocks = lax.all_to_all(jnp.stack(parts), "chip", 0, 0, tiled=True)
        return [blocks[k] for k in range(count)]
    return [parts[0]] + [to_chip(parts[k], k) for k in range(1, count)]


def tie(*values):
    return lax.optimization_barrier(values)


def by_columns(weight):
    count = lax.axis_size("chip")
    rows, width = weight.shape
    return weight.reshape(rows, count, width // count).transpose(1, 0, 2)


def gather_columns(parts):
    mine = jnp.stack(exchange(parts))[:, None]
    whole = lax.all_gather(mine, ("core", "dp"), axis=1, tiled=True)
    return whole


def gather_rows(weight):
    return lax.all_gather(weight, ("core", "dp"), axis=0, tiled=True)


def sum_cores(terms):
    me = lax.axis_index("core")
    return add(take(terms, me), swap_cores(take(terms, 1 - me))).astype(bf16)


def halve_rows(terms):
    rows, width = terms.shape
    return sum_cores(terms.reshape(CORES, rows // CORES, width))


def scatter_dp(half):
    return lax.psum_scatter(half, "dp", scatter_dimension=0, tiled=True)


def halve_columns(terms):
    cores, dp, chips, own, width = terms.shape
    return sum_cores(terms.reshape(cores, dp, chips * own, width))


def join_blocks(mine):
    blocks = exchange(jnp.split(mine.reshape(-1, mine.shape[-1]), lax.axis_size("chip"), 0))
    return reordered(blocks, chip_flip())


def join_columns(mine):
    return jnp.concatenate(join_blocks(mine), 1).astype(f32)


def sum_chips(values):
    count, bits = lax.axis_size("chip"), 1
    while bits < count:
        values = values + to_chip(values, bits)
        bits *= 2
    return values


def row_sums(values):
    sums = jnp.sum(values, axis=-1).reshape(-1, 128)
    return sum_chips(sums).reshape(-1, 1)


def pair_in(block):
    me = lax.axis_index("core")
    kept, got = take(block, me), swap_cores(take(block, 1 - me))
    return jnp.where(
        me == 0, jnp.concatenate([kept, got], 0), jnp.concatenate([got, kept], 0)
    )


def pair_out(rows):
    me = lax.axis_index("core")
    blocks = rows.reshape(CORES, -1, rows.shape[1])
    kept, got = take(blocks, me), swap_cores(take(blocks, 1 - me))
    return jnp.where(me == 0, jnp.stack([kept, got]), jnp.stack([got, kept]))


def visible_scores(keys, queries, first, length, score_scale):
    scores = outer_cols(keys, queries) * score_scale
    key_pos = lax.broadcasted_iota(jnp.int32, scores.shape, 0)
    query_pos = lax.broadcasted_iota(jnp.int32, scores.shape, 1) + first
    return jnp.where((key_pos <= query_pos) & (key_pos < length), scores, -1e30)


def flipped(start, flip):
    return pl.ds(pl.multiple_of(((start // TILE) ^ flip) * TILE, TILE), TILE)


def attend_kernel(
    score_scale,
    length_ref,
    flip_ref,
    rows_ref,
    up_ref,
    keys_ref,
    values_t_ref,
    cos_ref,
    sin_ref,
    queries_ref,
    mixed_ref,
    total_ref,
):
    length, flip = length_ref[0], flip_ref[0]
    chips = lax.axis_size("chip")
    depth = up_ref.shape[1]
    for start in range(0, keys_ref.shape[0], TILE):
        stop = start + TILE
        raw = 0.0
        for part in range(chips):
            raw = raw + matmul(rows_ref[part, start:stop, :depth], up_ref[part])
        raw = raw * cos_ref[start:stop, :] + rotate_half(raw) * sin_ref[start:stop, :]
        queries = raw.astype(bf16)
        queries_ref[start:stop, :] = queries
        scores = visible_scores(keys_ref[:stop, :], queries, start, length, score_scale)
        top = jnp.max(scores, axis=0, keepdims=True)
        powers = jnp.exp(scores - top)
        total = jnp.sum(powers, axis=0, keepdims=True)
        total_ref[0, :, start:stop] = top + jnp.log(total)
        probs = (powers * (1.0 / total)).astype(bf16)
        mixed = matmul(values_t_ref[:, :stop], probs)
        mixed_ref[flipped(start, flip), :] = mixed.T.astype(bf16)


def attend(length, flip, rows, up, keys, values, cos_table, sin_table, score_scale):
    span, head_width = keys.shape
    heads = up.shape[2] // head_width
    whole = lambda array: pl.BlockSpec(array.shape, lambda h: (0, 0))
    head = lambda height: pl.BlockSpec((height, head_width), lambda h: (0, h))
    values_t = values.T
    return pl.pallas_call(
        functools.partial(attend_kernel, score_scale),
        grid=(heads,),
        in_specs=[
            pl.BlockSpec(memory_space=pltpu.SMEM),
            pl.BlockSpec(memory_space=pltpu.SMEM),
            pl.BlockSpec(rows.shape, lambda h: (0, 0, 0)),
            pl.BlockSpec(up.shape[:2] + (head_width,), lambda h: (0, 0, h)),
            whole(keys),
            whole(values_t),
            whole(cos_table),
            whole(sin_table),
        ],
        out_specs=[
            head(span),
            head(span),
            pl.BlockSpec((1, 1, span), lambda h: (h, 0, 0)),
        ],
        out_shape=[
            jax.ShapeDtypeStruct((span, heads * head_width), bf16),
            jax.ShapeDtypeStruct((span, heads * head_width), bf16),
            jax.ShapeDtypeStruct((heads, 1, span), f32),
        ],
        compiler_params=pltpu.CompilerParams(vmem_limit_bytes=48 << 20),
        cost_estimate=BESIDE,
    )(length, flip, rows, up, keys, values_t, cos_table, sin_table)


def attend_back_kernel(
    score_scale,
    length_ref,
    flip_ref,
    queries_ref,
    grad_ref,
    total_ref,
    keys_ref,
    keys_t_ref,
    values_ref,
    cos_ref,
    sin_ref,
    grad_q_ref,
    grad_k_ref,
    grad_v_ref,
):
    length, flip = length_ref[0], flip_ref[0]

    @pl.when(pl.program_id(0) == 0)
    def _():
        grad_k_ref[...] = jnp.zeros_like(grad_k_ref)
        grad_v_ref[...] = jnp.zeros_like(grad_v_ref)

    for start in range(0, queries_ref.shape[0], TILE):
        stop = start + TILE
        queries, grads = queries_ref[start:stop, :], grad_ref[flipped(start, flip), :]
        scores = visible_scores(keys_ref[:stop, :], queries, start, length, score_scale)
        probs = jnp.exp(scores - total_ref[0, :, start:stop])
        grad_probs = outer_cols(values_ref[:stop, :], grads)
        mean = jnp.sum(probs * grad_probs, axis=0, keepdims=True)
        grad_scores = (probs * (grad_probs - mean)).astype(bf16)
        grad_v_ref[:stop, :] += matmul(probs.astype(bf16), grads)
        grad_k_ref[:stop, :] += matmul(grad_scores, queries) * score_scale
        grad_q = matmul(keys_t_ref[:, :stop], grad_scores).T * score_scale
        grad_q = grad_q * cos_ref[start:stop, :] - rotate_half(
            grad_q * sin_ref[start:stop, :]
        )
        grad_q_ref[start:stop, :] = grad_q.astype(bf16)


def attend_back(
    length, flip, queries, grads, total, keys, values, cos_table, sin_table, score_scale
):
    span, head_width = keys.shape
    heads = queries.shape[1] // head_width
    whole = lambda array: pl.BlockSpec(array.shape, lambda h: (0, 0))
    head = pl.BlockSpec((span, head_width), lambda h: (0, h))
    keys_t = keys.T
    summed = jax.ShapeDtypeStruct((span, head_width), f32)
    return pl.pallas_call(
        functools.partial(attend_back_kernel, score_scale),
        grid=(heads,),
        in_specs=[
            pl.BlockSpec(memory_space=pltpu.SMEM),
            pl.BlockSpec(memory_space=pltpu.SMEM),
            head,
            head,
            pl.BlockSpec((1, 1, span), lambda h: (h, 0, 0)),
            whole(keys),
            whole(keys_t),
            whole(values),
            whole(cos_table),
            whole(sin_table),
        ],
        out_specs=[head, whole(keys), whole(keys)],
        out_shape=[jax.ShapeDtypeStruct(queries.shape, bf16), summed, summed],
        compiler_params=pltpu.CompilerParams(vmem_limit_bytes=48 << 20),
        cost_estimate=BESIDE,
    )(length, flip, queries, grads, total, keys, keys_t, values, cos_table, sin_table)


CONTRACT = {"nn": ((1,), (0,)), "nt": ((1,), (1,)), "tn": ((0,), (0,))}


def write_halves(out_refs, block, value):
    rows = value.shape[0] // 2
    for k in range(len(out_refs) // 2):

        @pl.when(block == k)
        def _():
            out_refs[2 * k][...] = value[:rows]
            out_refs[2 * k + 1][...] = value[rows:]


def product_kernel(kind, scale, layout, count, _, *refs):
    inputs, out_refs = refs[: 2 * count], refs[2 * count :]
    total = 0.0
    for left, right in zip(inputs[::2], inputs[1::2]):
        total = total + lax.dot_general(
            left[...], right[...], (CONTRACT[kind], ((), ())), preferred_element_type=f32
        )
    out_ref = out_refs[0]
    total = (total * scale).astype(bf16)
    if layout == "split":
        out_ref[0, :, 0] = total.reshape(out_ref.shape[1], out_ref.shape[3], out_ref.shape[4])
    elif layout == "pieces":
        write_halves(out_refs, pl.program_id(0), total)
    else:
        out_ref[...] = total


def product(kind, *pairs, scale=1.0, layout=None, plain=False):
    left, right = pairs[0]
    rows = left.shape[1] if kind == "tn" else left.shape[0]
    width = right.shape[0] if kind == "nt" else right.shape[1]
    chips, dp = lax.axis_size("chip"), lax.axis_size("dp")
    own = rows // (chips * CORES * dp)
    tiles = [t for t in (256, 128) if rows % t == 0]
    if layout == "split":
        tiles = [dp * own]
    elif layout == "pieces":
        tiles = [rows // chips] if chips == 4 else []
    if not tiles or tiles[0] % 128 or width % 128:
        total = sum(
            lax.dot_general(a, b, (CONTRACT[kind], ((), ())), preferred_element_type=f32)
            for a, b in pairs
        )
        total = (total * scale).astype(bf16)
        if layout == "split":
            total = total.reshape(chips, CORES, dp, own, width).transpose(1, 2, 0, 3, 4)
        return as_pieces(total) if layout == "pieces" else total
    tile = tiles[0]
    inputs, specs = [], []
    for left, right in pairs:
        inputs += [left, right]
        if kind == "tn":
            specs.append(pl.BlockSpec((left.shape[0], tile), lambda i, f: (0, i)))
        else:
            specs.append(pl.BlockSpec((tile, left.shape[1]), lambda i, f: (i, 0)))
        specs.append(pl.BlockSpec(right.shape, lambda i, f: (0, 0)))
    if layout == "split":
        shapes = [(CORES, dp, chips, own, width)]
        outs = [
            pl.BlockSpec(
                (1, dp, 1, own, width), lambda i, f: (i % CORES, 0, (i // CORES) ^ f[0], 0, 0)
            )
        ]
    elif layout == "pieces":
        shapes = [(tile // 2, width)] * (2 * chips)
        outs = [pl.BlockSpec(shape, lambda i, f: (0, 0)) for shape in shapes]
    else:
        shapes = [(rows, width)]
        outs = [pl.BlockSpec((tile, width), lambda i, f: (i, 0))]
    results = pl.pallas_call(
        functools.partial(product_kernel, kind, scale, layout, len(pairs)),
        grid_spec=pltpu.PrefetchScalarGridSpec(
            num_scalar_prefetch=1, grid=(rows // tile,), in_specs=specs, out_specs=outs
        ),
        out_shape=[jax.ShapeDtypeStruct(shape, bf16) for shape in shapes],
        compiler_params=pltpu.CompilerParams(vmem_limit_bytes=56 << 20),
        cost_estimate=BESIDE,
    )(jnp.zeros(1, jnp.int32) if plain else chip_flip()[None], *inputs)
    return results if layout == "pieces" else results[0]


def as_pieces(terms):
    return jnp.split(terms, 8, 0) if lax.axis_size("chip") == 4 else [terms]


def back_kernel(grad_ref, up_ref, grad_k_ref, grad_v_ref, place_ref, *out_refs):
    grads = outer_cols(grad_ref[...], up_ref[0]).astype(bf16)
    parts = jnp.concatenate([grad_k_ref[...], grad_v_ref[...]], 1).astype(bf16)
    parts = outer_cols(parts, place_ref[0]).astype(bf16)
    write_halves(out_refs, pl.program_id(0), jnp.concatenate([grads, parts], 1))


def back_terms(grad_q, up_q, grad_k, grad_v, place):
    chips, depth, width = up_q.shape
    span = grad_q.shape[0]
    if chips != 4:
        grads = jnp.einsum("tn,kin->kti", grad_q, up_q, preferred_element_type=f32)
        parts = jnp.concatenate([grad_k, grad_v], 1).astype(bf16)
        parts = jnp.einsum("sn,kcn->ksc", parts, place, preferred_element_type=f32)
        terms = jnp.concatenate([grads, parts], 2).astype(bf16)
        return [terms.reshape(chips * span, -1)]
    whole = lambda array: pl.BlockSpec(array.shape, lambda k: (0, 0))
    block = lambda array: pl.BlockSpec((1,) + array.shape[1:], lambda k: (k, 0, 0))
    shape = (span // 2, depth + place.shape[1])
    return pl.pallas_call(
        back_kernel,
        grid=(chips,),
        in_specs=[whole(grad_q), block(up_q), whole(grad_k), whole(grad_v), block(place)],
        out_specs=[pl.BlockSpec(shape, lambda k: (0, 0))] * (2 * chips),
        out_shape=[jax.ShapeDtypeStruct(shape, bf16)] * (2 * chips),
        compiler_params=pltpu.CompilerParams(vmem_limit_bytes=48 << 20),
        cost_estimate=BESIDE,
    )(grad_q, up_q, grad_k, grad_v, place)


def spread_kernel(flip_rows, count, flip_ref, *refs):
    left_refs, weight_ref, out_refs = refs[:count], refs[count], refs[count + 1 :]
    chips, groups, _, own, _ = weight_ref.shape
    depth = groups * own
    columns = []
    for place in range(chips):
        total = 0.0
        for j, left_ref in enumerate(left_refs):
            block = weight_ref[place ^ flip_ref[0], :, j].reshape(depth, weight_ref.shape[4])
            total = total + outer_cols(left_ref[...], block[:, : left_ref.shape[1]])
        columns.append(total.astype(bf16))
    block = pl.program_id(0) ^ flip_ref[0] if flip_rows else pl.program_id(0)
    write_halves(out_refs, block, jnp.concatenate(columns, 1))


def spread(lefts, weight, flip_rows=False):
    chips, groups, _, own, width = weight.shape
    rows, depth = lefts[0].shape[0], chips * groups * own
    if chips != 4 or lefts[0].shape[1] % 128:
        total = sum(
            outer_cols(left, weight[:, :, j].reshape(depth, width)[:, : left.shape[1]])
            for j, left in enumerate(lefts)
        )
        return as_pieces(total.astype(bf16))
    tile = rows // chips
    shape = (tile // 2, depth)
    return pl.pallas_call(
        functools.partial(spread_kernel, flip_rows, len(lefts)),
        grid_spec=pltpu.PrefetchScalarGridSpec(
            num_scalar_prefetch=1,
            grid=(chips,),
            in_specs=[pl.BlockSpec((tile, left.shape[1]), lambda i, f: (i, 0)) for left in lefts]
            + [pl.BlockSpec(weight.shape, lambda i, f: (0, 0, 0, 0, 0))],
            out_specs=[pl.BlockSpec(shape, lambda i, f: (0, 0))] * (2 * chips),
        ),
        out_shape=[jax.ShapeDtypeStruct(shape, bf16)] * (2 * chips),
        compiler_params=pltpu.CompilerParams(vmem_limit_bytes=56 << 20),
        cost_estimate=BESIDE,
    )(chip_flip()[None], *lefts, weight)


def split_kernel(_, small_ref, qup_ref, gate_ref, up_ref, *out_refs):
    chips = len(out_refs) // 3
    own = gate_ref.shape[0]
    for k in range(chips):

        @pl.when(pl.program_id(0) == k)
        def _():
            out_refs[k][...] = small_ref[0]
            out_refs[chips + k][...] = qup_ref[...]
            out_refs[2 * chips + k][:own, :] = gate_ref[...]
            out_refs[2 * chips + k][own:, :] = up_ref[...]


def split_columns(small, w_qup, w_gate, w_up):
    chips = lax.axis_size("chip")
    own, width = w_gate.shape
    width = width // chips
    if chips != 4 or width % 128:
        gate_up = jnp.concatenate([by_columns(w_gate), by_columns(w_up)], 1)
        return list(small), list(by_columns(w_qup)), list(gate_up)
    own_q, q_width = w_qup.shape[0], w_qup.shape[1] // chips
    shapes = [small.shape[1:], (own_q, q_width), (2 * own, width)]
    columns = lambda rows, size: pl.BlockSpec((rows, size), lambda k, f: (0, k ^ f[0]))
    outs = pl.pallas_call(
        split_kernel,
        grid_spec=pltpu.PrefetchScalarGridSpec(
            num_scalar_prefetch=1,
            grid=(chips,),
            in_specs=[
                pl.BlockSpec((1,) + small.shape[1:], lambda k, f: (k ^ f[0], 0, 0)),
                columns(own_q, q_width),
                columns(own, width),
                columns(own, width),
            ],
            out_specs=[
                pl.BlockSpec(shape, lambda k, f: (0, 0)) for shape in shapes for _ in range(chips)
            ],
        ),
        out_shape=[jax.ShapeDtypeStruct(shape, bf16) for shape in shapes for _ in range(chips)],
        cost_estimate=BESIDE,
    )(chip_flip()[None], small, w_qup, w_gate, w_up)
    return outs[:chips], outs[chips : 2 * chips], outs[2 * chips :]


def normed_kernel(flip_ref, *refs):
    *piece_refs, gain_ref, small_ref, normed_ref, raw_ref = refs
    per_step = len(piece_refs) // pl.num_programs(0)
    for k in range(pl.num_programs(0)):

        @pl.when(pl.program_id(0) == k)
        def _():
            pieces = [ref[...] for ref in piece_refs[k * per_step : (k + 1) * per_step]]
            rows = jnp.concatenate(pieces, 0).astype(f32)
            normed = (rows * rms_scale(rows) * gain_ref[...]).astype(bf16)
            normed_ref[...] = normed
            depth = small_ref.shape[1]
            raw = 0.0
            for place in range(small_ref.shape[0]):
                weight = small_ref[place ^ flip_ref[0]][:, : raw_ref.shape[1]]
                columns = normed[:, place * depth : (place + 1) * depth]
                raw = raw + matmul(columns, weight)
            raw_ref[...] = raw


def normed_rows(near, gain, small, width_out):
    chips = lax.axis_size("chip")
    if chips != 4:
        rows = lax.all_gather(near[0], "chip", axis=0, tiled=True).astype(f32)
        normed = (rows * rms_scale(rows) * gain).astype(bf16)
        small = small.reshape(normed.shape[1], -1)[:, :width_out]
        return normed, matmul(normed, small)
    pieces = list(near) + list(far_halves(near))
    half, width = pieces[0].shape
    whole = lambda array: pl.BlockSpec(array.shape, lambda k, f: (0,) * array.ndim)
    block = lambda size: pl.BlockSpec((2 * half, size), lambda k, f: (k ^ f[0], 0))
    gain = gain[None, :]
    rows = chips * 2 * half
    return pl.pallas_call(
        normed_kernel,
        grid_spec=pltpu.PrefetchScalarGridSpec(
            num_scalar_prefetch=1,
            grid=(chips,),
            in_specs=[whole(piece) for piece in pieces] + [whole(gain), whole(small)],
            out_specs=[block(width), block(width_out)],
        ),
        out_shape=[
            jax.ShapeDtypeStruct((rows, width), bf16),
            jax.ShapeDtypeStruct((rows, width_out), f32),
        ],
        compiler_params=pltpu.CompilerParams(vmem_limit_bytes=48 << 20),
        cost_estimate=BESIDE,
    )(chip_flip()[None], *pieces, gain, small)


def gate_terms(gate, up):
    sigma = jax.nn.sigmoid(gate)
    silu = gate * sigma
    return (
        (silu * up).astype(bf16),
        silu.astype(bf16),
        (up * sigma * (1.0 + gate * (1.0 - sigma))).astype(bf16),
    )


def gate_kernel(flip_ref, rows_ref, weight_ref, active_ref, silu_ref, slope_ref):
    chips, groups, _, own, width = weight_ref.shape
    depth = groups * own
    both = 0.0
    for place in range(chips):
        block = weight_ref[place ^ flip_ref[0]]
        block = jnp.concatenate([block[:, j].reshape(depth, width) for j in range(2)], 1)
        both = both + matmul(rows_ref[:, place * depth : (place + 1) * depth], block)
    active_ref[...], silu_ref[...], slope_ref[...] = gate_terms(both[:, :width], both[:, width:])


def gated(rows, gate_up):
    chips, groups, _, own, width = gate_up.shape
    if width % 128:
        gate, up = [gate_up[:, :, j].reshape(rows.shape[1], width) for j in range(2)]
        return gate_terms(matmul(rows, gate), matmul(rows, up))
    out = pl.BlockSpec((rows.shape[0], 128), lambda i, f: (0, i))
    return pl.pallas_call(
        gate_kernel,
        grid_spec=pltpu.PrefetchScalarGridSpec(
            num_scalar_prefetch=1,
            grid=(width // 128,),
            in_specs=[
                pl.BlockSpec(rows.shape, lambda i, f: (0, 0)),
                pl.BlockSpec((chips, groups, 2, own, 128), lambda i, f: (0, 0, 0, 0, i)),
            ],
            out_specs=[out] * 3,
        ),
        out_shape=[jax.ShapeDtypeStruct((rows.shape[0], width), bf16)] * 3,
        compiler_params=pltpu.CompilerParams(vmem_limit_bytes=48 << 20),
        cost_estimate=BESIDE,
    )(chip_flip()[None], rows, gate_up)


def gate_back_kernel(seed_ref, down_ref, silu_ref, slope_ref, gate_ref, up_ref):
    grads = outer_cols(seed_ref[...], down_ref[...])
    gate_ref[...] = (grads * slope_ref[...].astype(f32)).astype(bf16)
    up_ref[...] = (grads * silu_ref[...].astype(f32)).astype(bf16)


def gated_back(seed, down_proj, silu, slope):
    width, depth = down_proj.shape
    if width % 128:
        grads = outer_cols(seed, down_proj)
        return (grads * slope.astype(f32)).astype(bf16), (grads * silu.astype(f32)).astype(bf16)
    rows = lambda size: pl.BlockSpec((TILE, size), lambda i: (i, 0))
    return pl.pallas_call(
        gate_back_kernel,
        grid=(seed.shape[0] // TILE,),
        in_specs=[
            rows(depth),
            pl.BlockSpec(down_proj.shape, lambda i: (0, 0)),
            rows(width),
            rows(width),
        ],
        out_specs=[rows(width)] * 2,
        out_shape=[jax.ShapeDtypeStruct(silu.shape, bf16)] * 2,
        compiler_params=pltpu.CompilerParams(vmem_limit_bytes=48 << 20),
        cost_estimate=BESIDE,
    )(seed, down_proj, silu, slope)


def per_device(
    tokens,
    lengths,
    attn_gain,
    w_qdown,
    q_gain,
    w_qup,
    w_key,
    w_value,
    w_out,
    ffn_gain,
    w_gate,
    w_up,
    w_down,
    cotangent,
):
    slot_count, seq_span, width = tokens.shape[1:]
    assert slot_count == CORES
    chips, dp = lax.axis_size("chip"), lax.axis_size("dp")
    chip, core = lax.axis_index("chip"), lax.axis_index("core")
    devices = chips * CORES * dp
    row_count = CORES * seq_span
    span = chips * row_count
    head_width = w_key.shape[1]
    q_width = w_qdown.shape[1]
    score_scale = 1.0 / math.sqrt(head_width)
    grad_scale = 1.0 / math.sqrt(slot_count * seq_span * devices)

    half = head_width // 2
    own_rows, own_q = attn_gain.shape[0], q_gain.shape[0]
    q_cols, v_cols, k_cols = q_width // chips, head_width // chips, half // chips
    small_cols = q_cols + 2 * v_cols
    length = lengths[0, core]
    positions = chip * row_count + jnp.arange(row_count, dtype=jnp.int32)
    valid_mask = (positions < length).astype(f32)[:, None]
    tokens_own = pair_in(tokens[0])
    inputs = tokens_own.astype(f32)
    flip = chip_flip()[None]

    gains = jnp.stack([attn_gain, ffn_gain, jnp.pad(q_gain, (0, own_rows - own_q))], 1)
    gains = jnp.pad(gains, ((0, 0), (0, 125)))
    key_pairs = w_key.reshape(own_rows, 2, chips, k_cols).transpose(2, 0, 1, 3)
    small = jnp.concatenate(
        [
            by_columns(w_qdown),
            key_pairs.reshape(chips, own_rows, 2 * k_cols),
            by_columns(w_value),
            jnp.broadcast_to(gains, (chips,) + gains.shape),
        ],
        2,
    )
    small, up_q, gate_up = split_columns(small, w_qup, w_gate, w_up)
    tokens_own, small = tie(tokens_own, small)
    tokens_near = gather_near(tokens_own)
    small = gather_columns(small)
    small, w_out, cotangent, tokens_near, gate_up = tie(
        small, w_out, cotangent, tokens_near, gate_up
    )
    up_q, gate_up = gather_columns(up_q), gather_columns(gate_up)
    seed_grad = (pair_in(cotangent[0]).astype(f32) * valid_mask).astype(bf16)
    gains = small.reshape(chips, -1, small.shape[-1])[:, :, small_cols : small_cols + 3]
    gains = jnp.concatenate(reordered(list(gains.astype(f32)), flip[0]), 0)
    gain_one, gain_two = gains[:, 0], gains[:, 1]
    gain_q = gains[:, 2].reshape(devices, own_rows)[:, :own_q].reshape(-1)
    gain_q = lax.dynamic_slice_in_dim(gain_q, chip * q_cols, q_cols, 0)
    out_proj = gather_rows(w_out)
    up_q = up_q.reshape(chips, q_cols, -1)
    gate_up = gate_up.reshape(chips, CORES * dp, 2, own_rows, -1)
    down_proj = gather_rows(w_down)

    cos_all, sin_all = rotary(jnp.arange(span, dtype=jnp.int32), head_width)
    cos_own = lax.dynamic_slice_in_dim(cos_all, chip * k_cols, k_cols, 1)
    sin_own = lax.dynamic_slice_in_dim(sin_all, chip * k_cols, k_cols, 1)
    normed_all, raw = normed_rows(
        tokens_near, gain_one, small.reshape(chips, -1, small.shape[-1]), small_cols
    )
    q_down = raw[:, :q_cols]
    scale_q = lax.rsqrt(row_sums(q_down * q_down) / q_width + epsilon)
    q_normed = (q_down * scale_q * gain_q).astype(bf16)
    k_one, k_two = raw[:, q_cols : q_cols + k_cols], raw[:, q_cols + k_cols : q_cols + 2 * k_cols]
    key_cols = [k_one * cos_own - k_two * sin_own, k_two * cos_own + k_one * sin_own]
    shared = jnp.concatenate(key_cols + [raw[:, q_cols + v_cols :]], 1).astype(bf16)
    shared = gather_chips(jnp.concatenate([q_normed, shared], 1))
    shared, seed_tied = tie(shared, seed_grad)
    seed_near = gather_near(seed_tied)
    shared = shared.reshape(chips, span, small_cols)
    local, sender = jnp.arange(2 * v_cols), (jnp.arange(chips) ^ flip[0])[:, None]
    target = jnp.where(
        local < v_cols,
        local // k_cols * half + sender * k_cols + local % k_cols,
        head_width + sender * v_cols + local - v_cols,
    )
    place = (target[:, :, None] == jnp.arange(2 * head_width)).astype(bf16)
    key_values = jnp.einsum(
        "ksc,kcn->sn", shared[:, :, q_cols:], place, preferred_element_type=f32
    ).astype(bf16)
    keys, values = key_values[:, :head_width], key_values[:, head_width:]

    queries, mixed, log_total = attend(
        length[None], flip, shared, up_q, keys, values, cos_all, sin_all, score_scale
    )
    part, *seed_near = tie(product("nn", (mixed, out_proj), layout="pieces"), *seed_near)
    middle = inputs + scatter_chips(part)
    scale_two = rms_scale(middle)
    normed2 = gather_chips((middle * scale_two * gain_two).astype(bf16))

    normed2, *seed_near = tie(normed2, *seed_near)
    seed_all = gather_far(seed_near)
    activated, silu, slope = gated(normed2, gate_up)
    down_terms = product("tn", (activated, seed_all), scale=grad_scale)
    down_terms, down_proj = tie(down_terms, down_proj)
    down_half = halve_rows(down_terms)
    gate_grad, up_grad = gated_back(seed_all, down_proj, silu, slope)
    gate_tied, up_tied, down_half = tie(gate_grad, up_grad, down_half)
    grad_w_down = scatter_dp(down_half)
    part = spread([gate_tied, up_tied], gate_up)
    part, gate_grad, up_grad = tie(part, gate_grad, up_grad)
    gate_part, up_part = [
        product("tn", (normed2, grad), scale=grad_scale, layout="split")
        for grad in (gate_grad, up_grad)
    ]
    grad_normed2, gate_sum, up_sum = scatter_chips(part, (gate_part, up_part))
    gate_half, up_half = halve_columns(gate_sum), halve_columns(up_sum)
    grad_w_gate = scatter_dp(gate_half)
    grad_normed2, grad_w_down, up_half = tie(grad_normed2, grad_w_down, up_half)
    grad_w_up = scatter_dp(up_half)
    grad_middle = seed_grad.astype(f32) + norm_back(grad_normed2, middle, scale_two, gain_two)
    grad_branch, activated = tie(grad_middle.astype(bf16), activated)
    grad_branch, grad_w_gate, out_part = tie(
        gather_chips(grad_branch), grad_w_gate, product("nn", (activated, down_proj), layout="pieces")
    )
    out_near = scatter_near(out_part)
    grad_mixed = product("nt", (grad_branch, out_proj))
    grad_q, grad_k, grad_v = attend_back(
        length[None], flip, queries, grad_mixed, log_total, keys, values, cos_all, sin_all, score_scale
    )
    grad_q, out_near = tie(grad_q, out_near)
    back = back_terms(grad_q, up_q, grad_k, grad_v, place)
    back, mixed, grad_q = tie(back, mixed, grad_q)
    out_half = halve_rows(product("tn", (mixed, grad_branch), scale=grad_scale))
    back, grad_q, out_half, grad_w_up = scatter_chips(back, (grad_q, out_half, grad_w_up))
    grad_w_out = scatter_dp(out_half)
    q_rows = shared[:, :, :q_cols].transpose(1, 0, 2).reshape(span, q_width)
    qup_half = halve_columns(
        product("tn", (q_rows, grad_q), scale=grad_scale, layout="split", plain=True)
    )
    back, qup_half, out_near = tie(back, qup_half, out_near)
    grad_w_qup = scatter_dp(qup_half)
    weighted = back[:, :q_cols] * gain_q
    mean = row_sums(weighted * q_down) / q_width
    grad_q_down = scale_q * weighted - q_down * scale_q**3 * mean
    k_one, k_two = back[:, q_cols : q_cols + k_cols], back[:, q_cols + k_cols : q_cols + 2 * k_cols]
    back = jnp.concatenate(
        [
            grad_q_down,
            k_one * cos_own + k_two * sin_own,
            k_two * cos_own - k_one * sin_own,
            back[:, q_cols + v_cols :],
        ],
        1,
    ).astype(bf16)
    output = middle + scatter_far(out_near)
    terms, back, grad_w_out, output = tie(
        spread([back], small[:, :, None], flip_rows=True), back, grad_w_out, output
    )
    small_sum = product("tn", (normed_all, back), scale=grad_scale, layout="split")
    grad_normed, small_sum, grad_w_gate, grad_w_up = scatter_chips(
        terms, (small_sum, grad_w_gate, grad_w_up)
    )
    small_half, grad_w_qup = tie(halve_columns(small_sum), grad_w_qup)
    grad_small = scatter_dp(small_half)
    out_tokens = pair_out(output.astype(bf16))[None]
    grad_inputs = grad_middle + norm_back(grad_normed, inputs, rms_scale(inputs), gain_one)
    grad_tokens = pair_out(grad_inputs)[None]
    grad_w_qup = join_columns(grad_w_qup)
    parts = jnp.stack(join_blocks(grad_small), 1).astype(f32)
    grad_w_key = parts[:, :, q_cols : q_cols + v_cols].reshape(own_rows, chips, 2, k_cols)
    grad_w_key = grad_w_key.transpose(0, 2, 1, 3).reshape(own_rows, head_width)
    grad_w_gate, grad_w_up = join_columns(grad_w_gate), join_columns(grad_w_up)
    grad_w_qdown = parts[:, :, :q_cols].reshape(own_rows, q_width)
    grad_w_value = parts[:, :, q_cols + v_cols :].reshape(own_rows, head_width)
    overlap = lambda weight, grad: jnp.sum(weight.astype(f32) * grad, axis=1)
    attn_terms = overlap(w_qdown, grad_w_qdown) + overlap(w_key, grad_w_key)
    attn_terms = attn_terms + overlap(w_value, grad_w_value)
    ffn_terms = overlap(w_gate, grad_w_gate) + overlap(w_up, grad_w_up)
    return (
        out_tokens,
        grad_tokens,
        attn_terms / attn_gain.astype(f32),
        grad_w_qdown,
        overlap(w_qup, grad_w_qup) / q_gain.astype(f32),
        grad_w_qup,
        grad_w_key,
        grad_w_value,
        grad_w_out.astype(f32),
        ffn_terms / ffn_gain.astype(f32),
        grad_w_gate,
        grad_w_up,
        grad_w_down.astype(f32),
    )


def solution(mesh):
    seq, dp = mesh.shape["seq"], mesh.shape["dp"]
    chips = Mesh(
        np.asarray(mesh.devices).reshape(seq // CORES, CORES, dp), ("chip", "core", "dp")
    )
    every = ("chip", "core", "dp")
    rows, vector = P(every, None), P(every)
    block = P("dp", None, ("chip", "core"), None)
    weights = (vector, rows, vector, rows, rows, rows, rows, vector, rows, rows, rows)
    return jax.shard_map(
        per_device,
        mesh=chips,
        in_specs=(block, P("dp", None)) + weights + (block,),
        out_specs=(block, block) + weights,
        check_vma=False,
    )
```

time: 925 us -> 701 us (0.76)
  Pallas kernels: 0 us -> 208 us
  matrix products: 176 us -> 0.83 us
  waiting for transfers between devices: 378 us -> 239 us
  local copies, waits for them, and re-layouts: 143 us -> 62 us
  blocking collectives: 40.1 us -> 0 us
    pallas_call x0 -> x22, Pallas kernels: none -> 208 us  [the longest x9 94.1 us: product(): pl.pallas_call(functools.partial(product_kernel, kind, scale, layout, len...]
    dot_general x25 -> x1, matrix products: 176 us -> 0.83 us  [per_device(): jnp.einsum('ksc,kcn->sn', shared[:, :, q_cols:], place, preferred_element...]
    dynamic_update_slice x68 -> x0, local copies, waits for them, and re-layouts: 67.2 us -> none  [placed_blocks(): result = lax.dynamic_update_index_in_dim(result, block, index, 0)]
    all_gather x4 -> x3, waiting for transfers between devices: 53.7 us -> 0.01 us  [gather_columns(): whole = lax.all_gather(mine, ('core', 'dp'), axis=1, tiled=True)]
    reduce_scatter x6, waiting for transfers between devices: 59.4 us -> 17.5 us  [scatter_dp(): return lax.psum_scatter(half, 'dp', scatter_dimension=0, tiled=True)]
    unnamed x1 -> x0, blocking collectives: 40.1 us -> none
    ppermute x75 -> x85, waiting for transfers between devices: 232 us -> 216 us  [to_chip(): return lax.ppermute(block, 'chip', [(i, i ^ bits) for i in range(count)])]
    all_gather x2, waiting for transfers between devices: 14.3 us -> 0.01 us  [gather_rows(): return lax.all_gather(weight, ('core', 'dp'), axis=0, tiled=True)]
  transfers between devices with their start and end apart: 97 -> 106, of which waited for: 48 -> 57; matrix products, arithmetic and copies ran while one was open for 35% -> 15% of each run, Pallas kernels for 0% -> 30%
where the time goes in v2:
time: 701 us; the launch traced here: 695 us
  waiting for transfers between devices  239 us (34%)
  Pallas kernels  208 us (30%)
  starting transfers between devices  91.4 us (13%)
  other arithmetic  78.5 us (11%)
  local copies, waits for them, and re-layouts  62 us (9%)
  between operations  15.7 us (2%)
    ppermute x85, waiting for transfers between devices, to_chip(): return lax.ppermute(block, 'chip', [(i, i ^ bits) for i in range(count)])  216 us
    pallas_call x9, Pallas kernels, product(): pl.pallas_call(functools.partial(product_kernel, kind, scale, layout, len...  94.1 us
    ppermute x85, starting transfers between devices, to_chip(): return lax.ppermute(block, 'chip', [(i, i ^ bits) for i in range(count)])  89.6 us
    pallas_call x2, Pallas kernels, spread(): pl.pallas_call(functools.partial(spread_kernel, flip_rows, len(lefts)), g...  28.9 us
    unnamed x225, local copies, waits for them, and re-layouts  28.4 us
    pallas_call x1, Pallas kernels, attend(): pl.pallas_call(functools.partial(attend_kernel, score_scale), grid=(heads...  18.5 us
    pallas_call x1, Pallas kernels, gated(): pl.pallas_call(gate_kernel, grid_spec=pltpu.PrefetchScalarGridSpec(num_sc...  18.4 us
    reduce_scatter x6, waiting for transfers between devices, scatter_dp(): return lax.psum_scatter(half, 'dp', scatter_dimension=0, tiled=True)  17.5 us
  transfers between devices with their start and end apart: 106, of which 57 were waited for; matrix products, arithmetic and copies ran while one was open for 15% of the time, Pallas kernels for 30%

profile of v2, /device:TPU:0, one launch (start us, length us, event | category | flops | bytes accessed | tf_op | source)
XLA Modules:
  0.0 695.4 jit_solution(1720585792330685970)
XLA Ops:
  10.5 3.8 shard_map.237
  36.5 10.8 %collective-permute-done.7.refs_5_ = bf16[128,2048]{1,0:T(8,128)(2,1)S(1)} collective-permute-done((bf16[128,2048]{1,0:T(8,128)(2,1)S(1)}, bf16[128,2048]{1,0:T(8,128)(2,1)S(1)}, u32[]{:S(2)}, u32[]{:S(2)}) %collective-permute-start.7) | collective-permute-done | bytes 524320 | tf_op jit(solution)/shard_map/ppermute | solution.py:72
  48.9 6.4 collective-permute-done.6.refs_4_
  59.9 8.1 %collective-permute-done.40 = bf16[128,1408]{1,0:T(8,128)(2,1)S(1)} collective-permute-done((bf16[128,1408]{1,0:T(8,128)(2,1)}, bf16[128,1408]{1,0:T(8,128)(2,1)S(1)}, u32[]{:S(2)}, u32[]{:S(2)}) %collective-permute-start.40) | collective-permute-done | bytes 360480 | tf_op jit(solution)/shard_map/ppermute | solution.py:72
  68.0 5.6 collective-permute-done.41
  87.6 4.3 collective-permute-done.8.refs_6_
  97.7 6.8 shard_map.238
  118.1 6.8 collective-permute-done.15.refs_5_
  127.5 4.6 collective-permute-done.13.refs_3_
  132.1 4.3 collective-permute-done.17.refs_7_
  148.9 18.5 %shard_map.240 = (bf16[1024,1024]{1,0:T(8,128)(2,1)S(1)}, bf16[1024,1024]{1,0:T(8,128)(2,1)}, f32[4,1,1024]{2,1,0:T(1,128)S(1)}) custom-call(s32[1]{0:T(128)} %bitcast.24.length_ref, s32[1]{0:T(128)} %bitcast._.flip_ref, bf16[4,1024,384]{2,1,0:T(8,128)(2,1)} %bitcast.215, bf16[4,256,1024]{2,1,0:T(8,128)(2,1)} %all-gather.15.cloned.1.call-done.up_ref, ...), custom_call_target="tpu_custom_call" | custom-call | flops 1 | bytes 1 | tf_op jit(solution)/shard_map/pallas_call | solution.py:297
  168.7 9.9 %shard_map.241 = (bf16[128,2048]{1,0:T(8,128)(2,1)}, bf16[128,2048]{1,0:T(8,128)(2,1)}, bf16[128,2048]{1,0:T(8,128)(2,1)}, bf16[128,2048]{1,0:T(8,128)(2,1)}, bf...) custom-call(s32[1]{0:T(128)} %bitcast._.flip_ref, ...), custom_call_target="tpu_custom_call" | custom-call | flops 1 | bytes 1 | tf_op jit(solution)/shard_map/pallas_call | solution.py:468
  182.8 9.4 %collective-permute-done.26 = bf16[128,2048]{1,0:T(8,128)(2,1)S(1)} collective-permute-done((bf16[128,2048]{1,0:T(8,128)(2,1)}, bf16[128,2048]{1,0:T(8,128)(2,1)S(1)}, u32[]{:S(2)}, u32[]{:S(2)}) %collective-permute-start.26) | collective-permute-done | bytes 524320 | tf_op jit(solution)/shard_map/ppermute | solution.py:72
  194.8 5.9 collective-permute-done.28
  205.8 10.9 %collective-permute-done.30 = bf16[128,2048]{1,0:T(8,128)(2,1)S(1)} collective-permute-done((bf16[128,2048]{1,0:T(8,128)(2,1)S(1)}, bf16[128,2048]{1,0:T(8,128)(2,1)S(1)}, u32[]{:S(2)}, u32[]{:S(2)}) %collective-permute-start.30) | collective-permute-done | bytes 524320 | tf_op jit(solution)/shard_map/ppermute | solution.py:72
  224.7 10.8 %collective-permute-done.35.refs_5_ = bf16[128,2048]{1,0:T(8,128)(2,1)S(1)} collective-permute-done((bf16[128,2048]{1,0:T(8,128)(2,1)S(1)}, bf16[128,2048]{1,0:T(8,128)(2,1)S(1)}, u32[]{:S(2)}, u32[]{:S(2)}) %collective-permute-start.35) | collective-permute-done | bytes 524320 | tf_op jit(solution)/shard_map/ppermute | solution.py:72
  237.5 5.4 collective-permute-done.33.refs_3_
  242.9 9.5 %collective-permute-done.37.refs_7_ = bf16[128,2048]{1,0:T(8,128)(2,1)S(1)} collective-permute-done((bf16[128,2048]{1,0:T(8,128)(2,1)S(1)}, bf16[128,2048]{1,0:T(8,128)(2,1)S(1)}, u32[]{:S(2)}, u32[]{:S(2)}) %collective-permute-start.37) | collective-permute-done | bytes 524320 | tf_op jit(solution)/shard_map/ppermute | solution.py:72
  255.0 9.4 %collective-permute-done.38.refs_6_ = bf16[128,2048]{1,0:T(8,128)(2,1)S(1)} collective-permute-done((bf16[128,2048]{1,0:T(8,128)(2,1)}, bf16[128,2048]{1,0:T(8,128)(2,1)S(1)}, u32[]{:S(2)}, u32[]{:S(2)}) %collective-permute-start.38) | collective-permute-done | bytes 524320 | tf_op jit(solution)/shard_map/ppermute | solution.py:72
  268.9 18.4 %shard_map.244 = (bf16[1024,1408]{1,0:T(8,128)(2,1)S(1)}, bf16[1024,1408]{1,0:T(8,128)(2,1)S(1)}, bf16[1024,1408]{1,0:T(8,128)(2,1)}) custom-call(s32[1]{0:T(128)} %bitcast._.flip_ref, bf16[1024,2048]{1,0:T(8,128)(2,1)} %copy-done.2, bf16[4,8,2,64,1408]{4,3,2,1,0:T(8,128)(2,1)} %bitcast.220), custom_call_target="tpu_custom_call" | custom-call | flops 1 | bytes 1 | tf_op jit(solution)/shard_map/pallas_call | solution.py:676
  290.5 13.4 %shard_map.245 = bf16[1408,2048]{1,0:T(8,128)(2,1)} custom-call(s32[1]{0:T(128)} %bitcast._.flip_ref, bf16[1024,1408]{1,0:T(8,128)(2,1)} %copy-done.9, bf16[1024,2048]{1,0:T(8,128)(2,1)} %copy-done.4), custom_call_target="tpu_custom_call" | custom-call | flops 1 | bytes 1 | tf_op jit(solution)/shard_map/pallas_call | solution.py:468
  303.8 3.9 dynamic-slice_bitcast_fusion.2
  307.8 11.4 %shard_map.246 = (bf16[1024,1408]{1,0:T(8,128)(2,1)S(1)}, bf16[1024,1408]{1,0:T(8,128)(2,1)S(1)}) custom-call(bf16[1024,2048]{1,0:T(8,128)(2,1)} %copy-done.4, bf16[1408,2048]{1,0:T(8,128)(2,1)} %all-gather.11.cloned.1.call-done.down_ref.refs_1_, bf16[1024,1408]{1,0:T(8,128)(2,1)} %copy-done.12, bf16[1024,1408]{1,0:T(8,128)(2,1)} %get-tuple-element.292.slope_ref), custom_call_target="tpu_custom_call" | custom-call | flops 1 | bytes 1 | tf_op jit(solution)/shard_map/pallas_call | solution.py:705
  322.4 4.8 fusion.2
  327.4 21.5 %shard_map.247 = (bf16[128,2048]{1,0:T(8,128)(2,1)}, bf16[128,2048]{1,0:T(8,128)(2,1)}, bf16[128,2048]{1,0:T(8,128)(2,1)}, bf16[128,2048]{1,0:T(8,128)(2,1)}, bf...) custom-call(s32[1]{0:T(128)} %bitcast._.flip_ref, ...), custom_call_target="tpu_custom_call" | custom-call | flops 1 | bytes 1 | tf_op jit(solution)/shard_map/pallas_call | solution.py:540
  352.9 12.1 %shard_map.248 = bf16[2,4,4,64,1408]{4,3,2,1,0:T(8,128)(2,1)} custom-call(s32[1]{0:T(128)} %bitcast._.flip_ref, bf16[1024,2048]{1,0:T(8,128)(2,1)} %copy-done.2, bf16[1024,1408]{1,0:T(8,128)(2,1)} %copy-done.8), custom_call_target="tpu_custom_call" | custom-call | flops 1 | bytes 1 | tf_op jit(solution)/shard_map/pallas_call | solution.py:468
  365.0 12.2 %shard_map.249 = bf16[2,4,4,64,1408]{4,3,2,1,0:T(8,128)(2,1)} custom-call(s32[1]{0:T(128)} %bitcast._.flip_ref, bf16[1024,2048]{1,0:T(8,128)(2,1)} %copy-done.2, bf16[1024,1408]{1,0:T(8,128)(2,1)} %copy-done.7), custom_call_target="tpu_custom_call" | custom-call | flops 1 | bytes 1 | tf_op jit(solution)/shard_map/pallas_call | solution.py:468
  381.7 5.3 collective-permute-done.57
  393.9 12.6 %collective-permute-done.48 = bf16[128,2048]{1,0:T(8,128)(2,1)S(1)} collective-permute-done((bf16[128,2048]{1,0:T(8,128)(2,1)}, bf16[128,2048]{1,0:T(8,128)(2,1)S(1)}, u32[]{:S(2)}, u32[]{:S(2)}) %collective-permute-start.48) | collective-permute-done | bytes 524320 | tf_op jit(solution)/shard_map/ppermute | solution.py:72
  411.8 3.3 fusion.4
  415.9 3.7 fusion.18
  425.1 10.8 %collective-permute-done.54.refs_5_ = bf16[128,2048]{1,0:T(8,128)(2,1)S(1)} collective-permute-done((bf16[128,2048]{1,0:T(8,128)(2,1)S(1)}, bf16[128,2048]{1,0:T(8,128)(2,1)S(1)}, u32[]{:S(2)}, u32[]{:S(2)}) %collective-permute-start.54) | collective-permute-done | bytes 524320 | tf_op jit(solution)/shard_map/ppermute | solution.py:72
  438.0 12.8 %shard_map.251 = (bf16[128,2048]{1,0:T(8,128)(2,1)}, bf16[128,2048]{1,0:T(8,128)(2,1)}, bf16[128,2048]{1,0:T(8,128)(2,1)}, bf16[128,2048]{1,0:T(8,128)(2,1)}, bf...) custom-call(s32[1]{0:T(128)} %bitcast._.flip_ref, ...), custom_call_target="tpu_custom_call" | custom-call | flops 1 | bytes 1 | tf_op jit(solution)/shard_map/pallas_call | solution.py:468
  450.7 6.8 collective-permute-done.56.refs_7_
  467.1 8.7 %shard_map.252.grad_ref = bf16[1024,1024]{1,0:T(8,128)(2,1)} custom-call(s32[1]{0:T(128)} %bitcast._.flip_ref, bf16[1024,2048]{1,0:T(8,128)(2,1)} %copy-done.3, bf16[1024,2048]{1,0:T(8,128)(2,1)} %all-gather.9.cloned.1.call-done.refs_1_), custom_call_target="tpu_custom_call" | custom-call | flops 1 | bytes 1 | tf_op jit(solution)/shard_map/pallas_call | solution.py:468
  475.9 15.1 %shard_map.253 = (bf16[1024,1024]{1,0:T(8,128)(2,1)}, f32[1024,256]{1,0:T(8,128)S(1)}, f32[1024,256]{1,0:T(8,128)S(1)}) custom-call(s32[1]{0:T(128)} %bitcast.24.length_ref, s32[1]{0:T(128)} %bitcast._.flip_ref, bf16[1024,1024]{1,0:T(8,128)(2,1)} %copy-done.16, bf16[1024,1024]{1,0:T(8,128)(2,1)} %shard_map.252.grad_ref, ...), custom_call_target="tpu_custom_call" | custom-call | flops 1 | bytes 1 | tf_op jit(solution)/shard_map/pallas_call | solution.py:374
  495.8 6.3 shard_map.254
  502.1 8.8 %shard_map.255 = bf16[1024,2048]{1,0:T(8,128)(2,1)} custom-call(s32[1]{0:T(128)} %bitcast._.flip_ref, bf16[1024,1024]{1,0:T(8,128)(2,1)} %get-tuple-element.367.refs_0_, bf16[1024,2048]{1,0:T(8,128)(2,1)} %copy-done.3), custom_call_target="tpu_custom_call" | custom-call | flops 1 | bytes 1 | tf_op jit(solution)/shard_map/pallas_call | solution.py:468
  518.7 6.1 collective-permute-done.62
  528.7 4.2 collective-permute-done.64
  534.0 8.2 %shard_map.256 = bf16[2,4,4,32,1024]{4,3,2,1,0:T(8,128)(2,1)} custom-call(s32[1]{0:T(128)} %constant.139.clone.1._, bf16[1024,1024]{1,0:T(8,128)(2,1)} %bitcast.236, bf16[1024,1024]{1,0:T(8,128)(2,1)} %get-tuple-element.375.grad_ref.refs_1_), custom_call_target="tpu_custom_call" | custom-call | flops 1 | bytes 1 | tf_op jit(solution)/shard_map/pallas_call | solution.py:468
  547.6 8.8 %collective-permute-done.68 = bf16[512,384]{1,0:T(8,128)(2,1)S(1)} collective-permute-done((bf16[512,384]{1,0:T(8,128)(2,1)S(1)}, bf16[512,384]{1,0:T(8,128)(2,1)S(1)}, u32[]{:S(2)}, u32[]{:S(2)}) %collective-permute-start.68) | collective-permute-done | bytes 393248 | tf_op jit(solution)/shard_map/ppermute | solution.py:72
  569.9 7.5 %shard_map.257 = (bf16[128,2048]{1,0:T(8,128)(2,1)}, bf16[128,2048]{1,0:T(8,128)(2,1)}, bf16[128,2048]{1,0:T(8,128)(2,1)}, bf16[128,2048]{1,0:T(8,128)(2,1)}, bf...) custom-call(s32[1]{0:T(128)} %bitcast._.flip_ref, ...), custom_call_target="tpu_custom_call" | custom-call | flops 1 | bytes 1 | tf_op jit(solution)/shard_map/pallas_call | solution.py:540
  580.4 7.3 %reduce-scatter.13.cloned.1.call-done = bf16[128,2048]{1,0:T(8,128)(2,1)} async-done(((bf16[512,2048]{1,0:T(8,128)(2,1)}), bf16[128,2048]{1,0:T(8,128)(2,1)}) %reduce-scatter.13.cloned.1.call-update) | async-done | bytes 524304 | tf_op jit(solution)/shard_map/reduce_scatter | solution.py:200
  594.1 8.2 %shard_map.258 = bf16[2,4,4,64,384]{4,3,2,1,0:T(8,128)(2,1)} custom-call(s32[1]{0:T(128)} %bitcast._.flip_ref, bf16[1024,2048]{1,0:T(8,128)(2,1)} %get-tuple-element.407.refs_0_, bf16[1024,384]{1,0:T(8,128)(2,1)} %pad_maximum_fusion.6.refs_0_.refs_1_), custom_call_target="tpu_custom_call" | custom-call | flops 1 | bytes 1 | tf_op jit(solution)/shard_map/pallas_call | solution.py:468
  606.6 6.0 collective-permute-done.77
  627.9 7.8 %collective-permute-done.91 = bf16[64,1408]{1,0:T(8,128)(2,1)S(1)} collective-permute-done((bf16[64,1408]{1,0:T(8,128)(2,1)}, bf16[64,1408]{1,0:T(8,128)(2,1)S(1)}, u32[]{:S(2)}, u32[]{:S(2)}) %collective-permute-start.91) | collective-permute-done | bytes 180256 | tf_op jit(solution)/shard_map/ppermute | solution.py:72
  666.6 10.2 %reduce-scatter.17.cloned.1.call-done = bf16[1,256,384]{1,2,0:T(8,128)(2,1)} async-done(((bf16[4,256,384]{1,2,0:T(8,128)(2,1)}), bf16[1,256,384]{1,2,0:T(8,128)(2,1)}) %reduce-scatter.17.cloned.1.call-update) | async-done | bytes 196624 | tf_op jit(solution)/shard_map/reduce_scatter | solution.py:200
  (562 shorter events, 262.6 us)
Async XLA Ops:
  7.3 49.0 %all-gather.13.cloned.1.call-start = ((), (), s32[]{:S(2)}) async-start(), calls=%async_computation.14 | async-start | bytes 2359296 | tf_op jit(solution)/shard_map/all_gather | solution.py:181
  25.1 121.5 %all-gather.15.cloned.1.call-start = ((), (), s32[]{:S(2)}) async-start(), calls=%async_computation.15 | async-start | bytes 2359296 | tf_op jit(solution)/shard_map/all_gather | solution.py:181
  32.2 136.5 %all-gather.9.cloned.1.call-start = ((), (), s32[]{:S(2)}) async-start(), calls=%async_computation.6 | async-start | bytes 4718592 | tf_op jit(solution)/shard_map/all_gather | solution.py:186
  35.5 19.8 %collective-permute-start.6 = (bf16[128,2048]{1,0:T(8,128)(2,1)S(1)}, bf16[128,2048]{1,0:T(8,128)(2,1)S(1)}, u32[]{:S(2)}, u32[]{:S(2)}) collective-permute-start(bf16[128,2048]{1,0:T(8,128)(2,1)S(1)} %get-tuple-element.232.refs_0_), channel_id=1, source_target_pairs={{0,16},{8,24},{16,0},{24,8},{1,17},{9,25},{17,1},{25,9},{2,18},{10... | collective-permute-start | bytes 1572872 | tf_op jit(solution)/shard_map/ppermute | solution.py:72
  36.0 20.3 %collective-permute-start.4 = (bf16[128,2048]{1,0:T(8,128)(2,1)S(1)}, bf16[128,2048]{1,0:T(8,128)(2,1)}, u32[]{:S(2)}, u32[]{:S(2)}) collective-permute-start(bf16[128,2048]{1,0:T(8,128)(2,1)S(1)} %get-tuple-element.232.refs_0_), channel_id=1, source_target_pairs={{0,8},{8,0},{16,24},{24,16},{1,9},{9,1},{17,25},{25,17},{2,10},{10... | collective-permute-start | bytes 1572872 | tf_op jit(solution)/shard_map/ppermute | solution.py:72
  56.3 212.6 %all-gather.17.cloned.1.call-start = ((), (), s32[]{:S(2)}) async-start(), calls=%async_computation.16 | async-start | bytes 12976128 | tf_op jit(solution)/shard_map/all_gather | solution.py:181
  74.9 228.9 %all-gather.11.cloned.1.call-start = ((), (), s32[]{:S(2)}) async-start(), calls=%async_computation.7 | async-start | bytes 6488064 | tf_op jit(solution)/shard_map/all_gather | solution.py:186
  75.5 336.2 %reduce-scatter.7.cloned.1.call-start = ((), (), s32[]{:S(2)}) async-start(), calls=%async_computation.8 | async-start | bytes 3604480 | tf_op jit(solution)/shard_map/reduce_scatter | solution.py:200
  87.4 39.8 %collective-permute-start.18 = (bf16[128,2048]{1,0:T(8,128)(2,1)S(1)}, bf16[128,2048]{1,0:T(8,128)(2,1)S(1)}, u32[]{:S(2)}, u32[]{:S(2)}) collective-permute-start(bf16[128,2048]{1,0:T(8,128)(2,1)S(1)} %get-tuple-element.493), channel_id=1, source_target_pairs={{0,4},{4,0},{1,5},{5,1},{2,6},{6,2},{3,7},{7,3},{8,12},{12,8},{9,1... | collective-permute-start | bytes 1572872 | tf_op jit(solution)/shard_map/ppermute | solution.py:67
  116.3 15.8 %collective-permute-start.13 = (bf16[512,384]{1,0:T(8,128)(2,1)S(1)}, bf16[512,384]{1,0:T(8,128)(2,1)S(1)}, u32[]{:S(2)}, u32[]{:S(2)}) collective-permute-start(bf16[512,384]{1,0:T(8,128)(2,1)S(1)} %get-tuple-element.502.refs_1_), channel_id=1, source_target_pairs={{0,8},{8,0},{16,24},{24,16},{1,9},{9,1},{17,25},{25,17},{2,10},{10... | collective-permute-start | bytes 1179656 | tf_op jit(solution)/shard_map/ppermute | solution.py:72
  138.5 40.1 %collective-permute-start.25 = (bf16[128,2048]{1,0:T(8,128)(2,1)}, bf16[128,2048]{1,0:T(8,128)(2,1)}, u32[]{:S(2)}, u32[]{:S(2)}) collective-permute-start(bf16[128,2048]{1,0:T(8,128)(2,1)} %get-tuple-element.279.refs_1_), channel_id=1, source_target_pairs={{0,16},{8,24},{16,0},{24,8},{1,17},{9,25},{17,1},{25,9},{2,18},{10... | collective-permute-start | bytes 1572872 | tf_op jit(solution)/shard_map/ppermute | solution.py:72
  140.1 38.5 %collective-permute-start.23 = (bf16[128,2048]{1,0:T(8,128)(2,1)}, bf16[128,2048]{1,0:T(8,128)(2,1)}, u32[]{:S(2)}, u32[]{:S(2)}) collective-permute-start(bf16[128,2048]{1,0:T(8,128)(2,1)} %get-tuple-element.279.refs_1_), channel_id=1, source_target_pairs={{0,8},{8,0},{16,24},{24,16},{1,9},{9,1},{17,25},{25,17},{2,10},{10... | collective-permute-start | bytes 1572872 | tf_op jit(solution)/shard_map/ppermute | solution.py:72
  141.9 36.7 %collective-permute-start.24 = (bf16[128,2048]{1,0:T(8,128)(2,1)}, bf16[128,2048]{1,0:T(8,128)(2,1)}, u32[]{:S(2)}, u32[]{:S(2)}) collective-permute-start(bf16[128,2048]{1,0:T(8,128)(2,1)} %get-tuple-element.278.refs_0_), channel_id=1, source_target_pairs={{0,16},{8,24},{16,0},{24,8},{1,17},{9,25},{17,1},{25,9},{2,18},{10... | collective-permute-start | bytes 1572872 | tf_op jit(solution)/shard_map/ppermute | solution.py:72
  142.3 36.3 %collective-permute-start.22 = (bf16[128,2048]{1,0:T(8,128)(2,1)}, bf16[128,2048]{1,0:T(8,128)(2,1)}, u32[]{:S(2)}, u32[]{:S(2)}) collective-permute-start(bf16[128,2048]{1,0:T(8,128)(2,1)} %get-tuple-element.278.refs_0_), channel_id=1, source_target_pairs={{0,8},{8,0},{16,24},{24,16},{1,9},{9,1},{17,25},{25,17},{2,10},{10... | collective-permute-start | bytes 1572872 | tf_op jit(solution)/shard_map/ppermute | solution.py:72
  182.2 18.5 %collective-permute-start.28 = (bf16[128,2048]{1,0:T(8,128)(2,1)}, bf16[128,2048]{1,0:T(8,128)(2,1)S(1)}, u32[]{:S(2)}, u32[]{:S(2)}) collective-permute-start(bf16[128,2048]{1,0:T(8,128)(2,1)} %get-tuple-element.263), channel_id=1, source_target_pairs={{0,8},{8,0},{16,24},{24,16},{1,9},{9,1},{17,25},{25,17},{2,10},{10... | collective-permute-start | bytes 1572872 | tf_op jit(solution)/shard_map/ppermute | solution.py:72
  182.4 21.6 %collective-permute-start.29 = (bf16[128,2048]{1,0:T(8,128)(2,1)}, bf16[128,2048]{1,0:T(8,128)(2,1)S(1)}, u32[]{:S(2)}, u32[]{:S(2)}) collective-permute-start(bf16[128,2048]{1,0:T(8,128)(2,1)} %get-tuple-element.265), channel_id=1, source_target_pairs={{0,16},{8,24},{16,0},{24,8},{1,17},{9,25},{17,1},{25,9},{2,18},{10... | collective-permute-start | bytes 1572872 | tf_op jit(solution)/shard_map/ppermute | solution.py:72
  220.7 22.2 %collective-permute-start.33 = (bf16[128,2048]{1,0:T(8,128)(2,1)S(1)}, bf16[128,2048]{1,0:T(8,128)(2,1)S(1)}, u32[]{:S(2)}, u32[]{:S(2)}) collective-permute-start(bf16[128,2048]{1,0:T(8,128)(2,1)S(1)} %get-tuple-element.488.refs_1_), channel_id=1, source_target_pairs={{0,8},{8,0},{16,24},{24,16},{1,9},{9,1},{17,25},{25,17},{2,10},{10... | collective-permute-start | bytes 1572872 | tf_op jit(solution)/shard_map/ppermute | solution.py:72
  222.7 20.2 %collective-permute-start.34 = (bf16[128,2048]{1,0:T(8,128)(2,1)S(1)}, bf16[128,2048]{1,0:T(8,128)(2,1)S(1)}, u32[]{:S(2)}, u32[]{:S(2)}) collective-permute-start(bf16[128,2048]{1,0:T(8,128)(2,1)S(1)} %get-tuple-element.489.refs_0_), channel_id=1, source_target_pairs={{0,16},{8,24},{16,0},{24,8},{1,17},{9,25},{17,1},{25,9},{2,18},{10... | collective-permute-start | bytes 1572872 | tf_op jit(solution)/shard_map/ppermute | solution.py:72
  235.5 16.9 %collective-permute-start.37 = (bf16[128,2048]{1,0:T(8,128)(2,1)S(1)}, bf16[128,2048]{1,0:T(8,128)(2,1)S(1)}, u32[]{:S(2)}, u32[]{:S(2)}) collective-permute-start(bf16[128,2048]{1,0:T(8,128)(2,1)S(1)} %collective-permute-done.35.refs_5_), channel_id=1, source_target_pairs={{0,8},{8,0},{16,24},{24,16},{1,9},{9,1},{17,25},{25,17},{2,10},{10... | collective-permute-start | bytes 1572872 | tf_op jit(solution)/shard_map/ppermute | solution.py:72
  235.6 16.8 %collective-permute-start.36 = (bf16[128,2048]{1,0:T(8,128)(2,1)S(1)}, bf16[128,2048]{1,0:T(8,128)(2,1)S(1)}, u32[]{:S(2)}, u32[]{:S(2)}) collective-permute-start(bf16[128,2048]{1,0:T(8,128)(2,1)S(1)} %collective-permute-done.32.refs_2_), channel_id=1, source_target_pairs={{0,16},{8,24},{16,0},{24,8},{1,17},{9,25},{17,1},{25,9},{2,18},{10... | collective-permute-start | bytes 1572872 | tf_op jit(solution)/shard_map/ppermute | solution.py:72
  327.3 132.8 %reduce-scatter.9.cloned.1.call-start = ((), (), s32[]{:S(2)}) async-start(), calls=%async_computation.9 | async-start | bytes 3604480 | tf_op jit(solution)/shard_map/reduce_scatter | solution.py:200
  348.8 28.4 %collective-permute-start.44 = (bf16[128,2048]{1,0:T(8,128)(2,1)}, bf16[128,2048]{1,0:T(8,128)(2,1)S(1)}, u32[]{:S(2)}, u32[]{:S(2)}) collective-permute-start(bf16[128,2048]{1,0:T(8,128)(2,1)} %get-tuple-element.307), channel_id=1, source_target_pairs={{0,8},{8,0},{16,24},{24,16},{1,9},{9,1},{17,25},{25,17},{2,10},{10... | collective-permute-start | bytes 1572872 | tf_op jit(solution)/shard_map/ppermute | solution.py:72
  348.8 29.3 %collective-permute-start.45 = (bf16[128,2048]{1,0:T(8,128)(2,1)}, bf16[128,2048]{1,0:T(8,128)(2,1)S(1)}, u32[]{:S(2)}, u32[]{:S(2)}) collective-permute-start(bf16[128,2048]{1,0:T(8,128)(2,1)} %get-tuple-element.309), channel_id=1, source_target_pairs={{0,16},{8,24},{16,0},{24,8},{1,17},{9,25},{17,1},{25,9},{2,18},{10... | collective-permute-start | bytes 1572872 | tf_op jit(solution)/shard_map/ppermute | solution.py:72
  350.9 28.2 %collective-permute-start.46 = (bf16[128,2048]{1,0:T(8,128)(2,1)}, bf16[128,2048]{1,0:T(8,128)(2,1)S(1)}, u32[]{:S(2)}, u32[]{:S(2)}) collective-permute-start(bf16[128,2048]{1,0:T(8,128)(2,1)} %get-tuple-element.311), channel_id=1, source_target_pairs={{0,8},{8,0},{16,24},{24,16},{1,9},{9,1},{17,25},{25,17},{2,10},{10... | collective-permute-start | bytes 1572872 | tf_op jit(solution)/shard_map/ppermute | solution.py:72
  352.9 26.2 %collective-permute-start.47 = (bf16[128,2048]{1,0:T(8,128)(2,1)}, bf16[128,2048]{1,0:T(8,128)(2,1)S(1)}, u32[]{:S(2)}, u32[]{:S(2)}) collective-permute-start(bf16[128,2048]{1,0:T(8,128)(2,1)} %get-tuple-element.313), channel_id=1, source_target_pairs={{0,16},{8,24},{16,0},{24,8},{1,17},{9,25},{17,1},{25,9},{2,18},{10... | collective-permute-start | bytes 1572872 | tf_op jit(solution)/shard_map/ppermute | solution.py:72
  389.3 143.7 %reduce-scatter.11.cloned.1.call-start = ((), (), s32[]{:S(2)}) async-start(), calls=%async_computation.10 | async-start | bytes 3604480 | tf_op jit(solution)/shard_map/reduce_scatter | solution.py:200
  391.6 17.8 %collective-permute-start.50 = (bf16[4,256,1408]{2,1,0:T(8,128)(2,1)S(1)}, bf16[4,256,1408]{2,1,0:T(8,128)(2,1)S(1)}, u32[]{:S(2)}, u32[]{:S(2)}) collective-permute-start(bf16[4,256,1408]{2,1,0:T(8,128)(2,1)S(1)} %dynamic-slice_bitcast_fusion.1), channel_id=1, source_target_pairs={{0,4},{4,0},{1,5},{5,1},{2,6},{6,2},{3,7},{7,3},{8,12},{12,8},{9,1... | collective-permute-start | bytes 8650760 | tf_op jit(solution)/shard_map/ppermute | solution.py:67
  419.7 168.1 %reduce-scatter.13.cloned.1.call-start = ((), (), s32[]{:S(2)}) async-start(), calls=%async_computation.11 | async-start | bytes 2621440 | tf_op jit(solution)/shard_map/reduce_scatter | solution.py:200
  421.9 28.9 %collective-permute-start.52 = (bf16[128,2048]{1,0:T(8,128)(2,1)S(1)}, bf16[128,2048]{1,0:T(8,128)(2,1)S(1)}, u32[]{:S(2)}, u32[]{:S(2)}) collective-permute-start(bf16[128,2048]{1,0:T(8,128)(2,1)S(1)} %get-tuple-element.486.refs_1_), channel_id=1, source_target_pairs={{0,8},{8,0},{16,24},{24,16},{1,9},{9,1},{17,25},{25,17},{2,10},{10... | collective-permute-start | bytes 1572872 | tf_op jit(solution)/shard_map/ppermute | solution.py:72
  423.9 26.9 %collective-permute-start.53 = (bf16[128,2048]{1,0:T(8,128)(2,1)S(1)}, bf16[128,2048]{1,0:T(8,128)(2,1)S(1)}, u32[]{:S(2)}, u32[]{:S(2)}) collective-permute-start(bf16[128,2048]{1,0:T(8,128)(2,1)S(1)} %get-tuple-element.487.refs_0_), channel_id=1, source_target_pairs={{0,16},{8,24},{16,0},{24,8},{1,17},{9,25},{17,1},{25,9},{2,18},{10... | collective-permute-start | bytes 1572872 | tf_op jit(solution)/shard_map/ppermute | solution.py:72
  435.9 21.6 %collective-permute-start.56 = (bf16[128,2048]{1,0:T(8,128)(2,1)S(1)}, bf16[128,2048]{1,0:T(8,128)(2,1)S(1)}, u32[]{:S(2)}, u32[]{:S(2)}) collective-permute-start(bf16[128,2048]{1,0:T(8,128)(2,1)S(1)} %collective-permute-done.54.refs_5_), channel_id=1, source_target_pairs={{0,8},{8,0},{16,24},{24,16},{1,9},{9,1},{17,25},{25,17},{2,10},{10... | collective-permute-start | bytes 1572872 | tf_op jit(solution)/shard_map/ppermute | solution.py:72
  436.7 20.8 %collective-permute-start.55 = (bf16[128,2048]{1,0:T(8,128)(2,1)S(1)}, bf16[128,2048]{1,0:T(8,128)(2,1)S(1)}, u32[]{:S(2)}, u32[]{:S(2)}) collective-permute-start(bf16[128,2048]{1,0:T(8,128)(2,1)S(1)} %collective-permute-done.51.refs_2_), channel_id=1, source_target_pairs={{0,16},{8,24},{16,0},{24,8},{1,17},{9,25},{17,1},{25,9},{2,18},{10... | collective-permute-start | bytes 1572872 | tf_op jit(solution)/shard_map/ppermute | solution.py:72
  460.1 30.8 %collective-permute-start.58 = (bf16[128,2048]{1,0:T(8,128)(2,1)}, bf16[128,2048]{1,0:T(8,128)(2,1)}, u32[]{:S(2)}, u32[]{:S(2)}) collective-permute-start(bf16[128,2048]{1,0:T(8,128)(2,1)} %get-tuple-element.340), channel_id=1, source_target_pairs={{0,8},{8,0},{16,24},{24,16},{1,9},{9,1},{17,25},{25,17},{2,10},{10... | collective-permute-start | bytes 1572872 | tf_op jit(solution)/shard_map/ppermute | solution.py:72
  460.4 32.6 %collective-permute-start.59 = (bf16[128,2048]{1,0:T(8,128)(2,1)}, bf16[128,2048]{1,0:T(8,128)(2,1)}, u32[]{:S(2)}, u32[]{:S(2)}) collective-permute-start(bf16[128,2048]{1,0:T(8,128)(2,1)} %get-tuple-element.342), channel_id=1, source_target_pairs={{0,16},{8,24},{16,0},{24,8},{1,17},{9,25},{17,1},{25,9},{2,18},{10... | collective-permute-start | bytes 1572872 | tf_op jit(solution)/shard_map/ppermute | solution.py:72
  464.6 30.5 %collective-permute-start.60 = (bf16[128,2048]{1,0:T(8,128)(2,1)}, bf16[128,2048]{1,0:T(8,128)(2,1)}, u32[]{:S(2)}, u32[]{:S(2)}) collective-permute-start(bf16[128,2048]{1,0:T(8,128)(2,1)} %get-tuple-element.344), channel_id=1, source_target_pairs={{0,8},{8,0},{16,24},{24,16},{1,9},{9,1},{17,25},{25,17},{2,10},{10... | collective-permute-start | bytes 1572872 | tf_op jit(solution)/shard_map/ppermute | solution.py:72
  466.1 29.0 %collective-permute-start.61 = (bf16[128,2048]{1,0:T(8,128)(2,1)}, bf16[128,2048]{1,0:T(8,128)(2,1)S(1)}, u32[]{:S(2)}, u32[]{:S(2)}) collective-permute-start(bf16[128,2048]{1,0:T(8,128)(2,1)} %get-tuple-element.346), channel_id=1, source_target_pairs={{0,16},{8,24},{16,0},{24,8},{1,17},{9,25},{17,1},{25,9},{2,18},{10... | collective-permute-start | bytes 1572872 | tf_op jit(solution)/shard_map/ppermute | solution.py:72
  516.0 16.9 %collective-permute-start.64 = (bf16[512,384]{1,0:T(8,128)(2,1)S(1)}, bf16[512,384]{1,0:T(8,128)(2,1)}, u32[]{:S(2)}, u32[]{:S(2)}) collective-permute-start(bf16[512,384]{1,0:T(8,128)(2,1)S(1)} %get-tuple-element.363), channel_id=1, source_target_pairs={{0,8},{8,0},{16,24},{24,16},{1,9},{9,1},{17,25},{25,17},{2,10},{10... | collective-permute-start | bytes 1179656 | tf_op jit(solution)/shard_map/ppermute | solution.py:72
  544.5 110.1 %reduce-scatter.15.cloned.1.call-start = ((), (), s32[]{:S(2)}) async-start(), calls=%async_computation.12 | async-start | bytes 1310720 | tf_op jit(solution)/shard_map/reduce_scatter | solution.py:200
  587.7 15.6 %collective-permute-start.75 = (bf16[128,2048]{1,0:T(8,128)(2,1)}, bf16[128,2048]{1,0:T(8,128)(2,1)}, u32[]{:S(2)}, u32[]{:S(2)}) collective-permute-start(bf16[128,2048]{1,0:T(8,128)(2,1)} %get-tuple-element.400), channel_id=1, source_target_pairs={{0,8},{8,0},{16,24},{24,16},{1,9},{9,1},{17,25},{25,17},{2,10},{10... | collective-permute-start | bytes 1572872 | tf_op jit(solution)/shard_map/ppermute | solution.py:72
  590.5 86.3 %reduce-scatter.17.cloned.1.call-start = ((), (), s32[]{:S(2)}) async-start(), calls=%async_computation.13 | async-start | bytes 983040 | tf_op jit(solution)/shard_map/reduce_scatter | solution.py:200
  593.0 30.9 %collective-permute-start.74 = (bf16[128,2048]{1,0:T(8,128)(2,1)}, bf16[128,2048]{1,0:T(8,128)(2,1)}, u32[]{:S(2)}, u32[]{:S(2)}) collective-permute-start(bf16[128,2048]{1,0:T(8,128)(2,1)} %get-tuple-element.481), channel_id=1, source_target_pairs={{0,4},{4,0},{1,5},{5,1},{2,6},{6,2},{3,7},{7,3},{8,12},{12,8},{9,1... | collective-permute-start | bytes 1572872 | tf_op jit(solution)/shard_map/ppermute | solution.py:67
  593.0 19.7 %collective-permute-start.77 = (bf16[128,2048]{1,0:T(8,128)(2,1)}, bf16[128,2048]{1,0:T(8,128)(2,1)S(1)}, u32[]{:S(2)}, u32[]{:S(2)}) collective-permute-start(bf16[128,2048]{1,0:T(8,128)(2,1)} %get-tuple-element.404), channel_id=1, source_target_pairs={{0,8},{8,0},{16,24},{24,16},{1,9},{9,1},{17,25},{25,17},{2,10},{10... | collective-permute-start | bytes 1572872 | tf_op jit(solution)/shard_map/ppermute | solution.py:72
  593.5 21.8 %collective-permute-start.78 = (bf16[128,2048]{1,0:T(8,128)(2,1)}, bf16[128,2048]{1,0:T(8,128)(2,1)S(1)}, u32[]{:S(2)}, u32[]{:S(2)}) collective-permute-start(bf16[128,2048]{1,0:T(8,128)(2,1)} %get-tuple-element.406), channel_id=1, source_target_pairs={{0,16},{8,24},{16,0},{24,8},{1,17},{9,25},{17,1},{25,9},{2,18},{10... | collective-permute-start | bytes 1572872 | tf_op jit(solution)/shard_map/ppermute | solution.py:72
  615.3 34.5 %collective-permute-start.79 = (bf16[128,2048]{1,0:T(8,128)(2,1)}, bf16[128,2048]{1,0:T(8,128)(2,1)}, u32[]{:S(2)}, u32[]{:S(2)}) collective-permute-start(bf16[128,2048]{1,0:T(8,128)(2,1)} %add_convert_fusion.1), channel_id=1, source_target_pairs={{0,16},{8,24},{16,0},{24,8},{1,17},{9,25},{17,1},{25,9},{2,18},{10... | collective-permute-start | bytes 1572872 | tf_op jit(solution)/shard_map/ppermute | solution.py:72
  616.7 34.4 %collective-permute-start.80 = (bf16[128,2048]{1,0:T(8,128)(2,1)}, bf16[128,2048]{1,0:T(8,128)(2,1)}, u32[]{:S(2)}, u32[]{:S(2)}) collective-permute-start(bf16[128,2048]{1,0:T(8,128)(2,1)} %add_convert_fusion), channel_id=1, source_target_pairs={{0,8},{8,0},{16,24},{24,16},{1,9},{9,1},{17,25},{25,17},{2,10},{10... | collective-permute-start | bytes 1572872 | tf_op jit(solution)/shard_map/ppermute | solution.py:72
  619.5 16.1 %collective-permute-start.91 = (bf16[64,1408]{1,0:T(8,128)(2,1)}, bf16[64,1408]{1,0:T(8,128)(2,1)S(1)}, u32[]{:S(2)}, u32[]{:S(2)}) collective-permute-start(bf16[64,1408]{1,0:T(8,128)(2,1)} %get-tuple-element.507), channel_id=1, source_target_pairs={{0,8},{8,0},{16,24},{24,16},{1,9},{9,1},{17,25},{25,17},{2,10},{10... | collective-permute-start | bytes 540680 | tf_op jit(solution)/shard_map/ppermute | solution.py:72
  623.9 15.6 %collective-permute-start.89 = (bf16[64,1408]{1,0:T(8,128)(2,1)S(1)}, bf16[64,1408]{1,0:T(8,128)(2,1)S(1)}, u32[]{:S(2)}, u32[]{:S(2)}) collective-permute-start(bf16[64,1408]{1,0:T(8,128)(2,1)S(1)} %copy-done.90), channel_id=1, source_target_pairs={{0,24},{8,16},{16,8},{24,0},{1,25},{9,17},{17,9},{25,1},{2,26},{10... | collective-permute-start | bytes 540680 | tf_op jit(solution)/shard_map/ppermute | solution.py:72
  657.1 24.4 %collective-permute-start.81 = (f32[128,2048]{1,0:T(8,128)S(1)}, f32[128,2048]{1,0:T(8,128)S(1)}, u32[]{:S(2)}, u32[]{:S(2)}) collective-permute-start(f32[128,2048]{1,0:T(8,128)S(1)} %get-tuple-element.469), channel_id=1, source_target_pairs={{0,4},{4,0},{1,5},{5,1},{2,6},{6,2},{3,7},{7,3},{8,12},{12,8},{9,1... | collective-permute-start | bytes 3145736 | tf_op jit(solution)/shard_map/ppermute | solution.py:67
  (168 other events, 1509.9 us)
Sparse Core Ops, SparseCore 0:
  25.2 28.4 all-gather.12
  55.3 28.5 all-gather.14
  85.6 46.6 all-gather.8
  134.3 106.7 all-gather.16
  242.6 58.6 all-gather.10
  327.4 56.0 reduce-scatter.6
  389.4 55.7 reduce-scatter.8
  447.5 56.0 reduce-scatter.10
  544.6 43.0 reduce-scatter.12
  590.6 25.8 reduce-scatter.14
  654.7 21.9 reduce-scatter.16

commit v3 on v2

--- a/solution.py
+++ b/solution.py
@@ -92,6 +92,8 @@
 def join_rows(pieces):
     rows, width = pieces[0].shape
     count = len(pieces)
+    if count == 1:
+        return pieces[0]
     return pl.pallas_call(
         join_kernel,
         grid=(count,),
@@ -104,13 +106,13 @@
 
 
 def gather_far(near):
+    return join_rows(far_pieces(near))
+
+
+def far_pieces(near):
     if lax.axis_size("chip") != 4:
-        return lax.all_gather(near[0], "chip", axis=0, tiled=True)
-    return join_rows(list(near) + list(far_halves(near)))
-
-
-def far_halves(near):
-    return to_chip(near[2], 2), to_chip(near[5], 1)
+        return [lax.all_gather(near[0], "chip", axis=0, tiled=True)]
+    return list(near) + [to_chip(near[2], 2), to_chip(near[5], 1)]
 
 
 def chip_flip():
@@ -138,17 +140,16 @@
     if lax.axis_size("chip") != 4:
         return tuple(pieces)
     top, low = pieces[::2], pieces[1::2]
-    top_far = add(top[2], to_chip(top[3], 1)).astype(bf16)
-    low_far = add(low[1], to_chip(low[3], 2)).astype(bf16)
-    return top_far, low_far, top[0], to_chip(top[1], 1), low[0], to_chip(low[2], 2)
+    far = (top[2], to_chip(top[3], 1), low[1], to_chip(low[3], 2))
+    return far + (top[0], to_chip(top[1], 1), low[0], to_chip(low[2], 2))
 
 
 def scatter_far(near):
     if lax.axis_size("chip") != 4:
         return lax.psum_scatter(near[0], "chip", scatter_dimension=0, tiled=True).astype(f32)
-    top_far, low_far, top, top_x, low, low_y = near
-    top = add(top, top_x) + to_chip(top_far, 2).astype(f32)
-    low = add(low, low_y) + to_chip(low_far, 1).astype(f32)
+    top_far, low_far = add(near[0], near[1]).astype(bf16), add(near[2], near[3]).astype(bf16)
+    top = add(near[4], near[5]) + to_chip(top_far, 2).astype(f32)
+    low = add(near[6], near[7]) + to_chip(low_far, 1).astype(f32)
     return jnp.concatenate([top, low], 0)
 
 
@@ -176,42 +177,34 @@
     return weight.reshape(rows, count, width // count).transpose(1, 0, 2)
 
 
+def gather_blocks(blocks):
+    mine = jnp.stack(blocks)[:, None]
+    return lax.all_gather(mine, ("core", "dp"), axis=1, tiled=True)
+
+
 def gather_columns(parts):
-    mine = jnp.stack(exchange(parts))[:, None]
-    whole = lax.all_gather(mine, ("core", "dp"), axis=1, tiled=True)
-    return whole
+    return gather_blocks(exchange(parts))
 
 
 def gather_rows(weight):
     return lax.all_gather(weight, ("core", "dp"), axis=0, tiled=True)
 
 
-def sum_cores(terms):
-    me = lax.axis_index("core")
-    return add(take(terms, me), swap_cores(take(terms, 1 - me))).astype(bf16)
-
-
-def halve_rows(terms):
-    rows, width = terms.shape
-    return sum_cores(terms.reshape(CORES, rows // CORES, width))
+def sum_cores(own, other):
+    return add(own, swap_cores(other)).astype(bf16)
 
 
 def scatter_dp(half):
+    half = half.reshape(lax.axis_size("dp"), -1, half.shape[-1])
     return lax.psum_scatter(half, "dp", scatter_dimension=0, tiled=True)
 
 
-def halve_columns(terms):
-    cores, dp, chips, own, width = terms.shape
-    return sum_cores(terms.reshape(cores, dp, chips * own, width))
-
-
-def join_blocks(mine):
-    blocks = exchange(jnp.split(mine.reshape(-1, mine.shape[-1]), lax.axis_size("chip"), 0))
-    return reordered(blocks, chip_flip())
-
-
-def join_columns(mine):
-    return jnp.concatenate(join_blocks(mine), 1).astype(f32)
+def trade_blocks(mine):
+    return exchange(jnp.split(mine.reshape(-1, mine.shape[-1]), lax.axis_size("chip"), 0))
+
+
+def join_columns(blocks):
+    return jnp.concatenate(reordered(blocks, chip_flip()), 1).astype(f32)
 
 
 def sum_chips(values):
@@ -406,75 +399,130 @@
             out_refs[2 * k + 1][...] = value[rows:]
 
 
-def product_kernel(kind, scale, layout, count, _, *refs):
-    inputs, out_refs = refs[: 2 * count], refs[2 * count :]
-    total = 0.0
-    for left, right in zip(inputs[::2], inputs[1::2]):
-        total = total + lax.dot_general(
-            left[...], right[...], (CONTRACT[kind], ((), ())), preferred_element_type=f32
-        )
-    out_ref = out_refs[0]
-    total = (total * scale).astype(bf16)
-    if layout == "split":
-        out_ref[0, :, 0] = total.reshape(out_ref.shape[1], out_ref.shape[3], out_ref.shape[4])
-    elif layout == "pieces":
+def product_kernel(kind, pieces, left_ref, right_ref, *out_refs):
+    total = lax.dot_general(
+        left_ref[...], right_ref[...], (CONTRACT[kind], ((), ())), preferred_element_type=f32
+    ).astype(bf16)
+    if pieces:
         write_halves(out_refs, pl.program_id(0), total)
     else:
-        out_ref[...] = total
-
-
-def product(kind, *pairs, scale=1.0, layout=None, plain=False):
-    left, right = pairs[0]
-    rows = left.shape[1] if kind == "tn" else left.shape[0]
-    width = right.shape[0] if kind == "nt" else right.shape[1]
-    chips, dp = lax.axis_size("chip"), lax.axis_size("dp")
-    own = rows // (chips * CORES * dp)
-    tiles = [t for t in (256, 128) if rows % t == 0]
-    if layout == "split":
-        tiles = [dp * own]
-    elif layout == "pieces":
-        tiles = [rows // chips] if chips == 4 else []
-    if not tiles or tiles[0] % 128 or width % 128:
-        total = sum(
-            lax.dot_general(a, b, (CONTRACT[kind], ((), ())), preferred_element_type=f32)
-            for a, b in pairs
-        )
-        total = (total * scale).astype(bf16)
-        if layout == "split":
-            total = total.reshape(chips, CORES, dp, own, width).transpose(1, 2, 0, 3, 4)
-        return as_pieces(total) if layout == "pieces" else total
-    tile = tiles[0]
-    inputs, specs = [], []
-    for left, right in pairs:
-        inputs += [left, right]
-        if kind == "tn":
-            specs.append(pl.BlockSpec((left.shape[0], tile), lambda i, f: (0, i)))
-        else:
-            specs.append(pl.BlockSpec((tile, left.shape[1]), lambda i, f: (i, 0)))
-        specs.append(pl.BlockSpec(right.shape, lambda i, f: (0, 0)))
-    if layout == "split":
-        shapes = [(CORES, dp, chips, own, width)]
-        outs = [
-            pl.BlockSpec(
-                (1, dp, 1, own, width), lambda i, f: (i % CORES, 0, (i // CORES) ^ f[0], 0, 0)
-            )
-        ]
-    elif layout == "pieces":
+        out_refs[0][...] = total
+
+
+def product(kind, left, right, pieces=False):
+    rows, width = left.shape[0], right.shape[0] if kind == "nt" else right.shape[1]
+    chips = lax.axis_size("chip")
+    tile = rows // chips if pieces else TILE
+    if (pieces and chips != 4) or rows % tile or tile % 128 or width % 128 or right.shape[0] % 128:
+        total = lax.dot_general(
+            left, right, (CONTRACT[kind], ((), ())), preferred_element_type=f32
+        ).astype(bf16)
+        return as_pieces(total) if pieces else total
+    if pieces:
         shapes = [(tile // 2, width)] * (2 * chips)
-        outs = [pl.BlockSpec(shape, lambda i, f: (0, 0)) for shape in shapes]
+        outs = [pl.BlockSpec(shape, lambda i: (0, 0)) for shape in shapes]
     else:
         shapes = [(rows, width)]
-        outs = [pl.BlockSpec((tile, width), lambda i, f: (i, 0))]
+        outs = [pl.BlockSpec((tile, width), lambda i: (i, 0))]
     results = pl.pallas_call(
-        functools.partial(product_kernel, kind, scale, layout, len(pairs)),
-        grid_spec=pltpu.PrefetchScalarGridSpec(
-            num_scalar_prefetch=1, grid=(rows // tile,), in_specs=specs, out_specs=outs
-        ),
+        functools.partial(product_kernel, kind, pieces),
+        grid=(rows // tile,),
+        in_specs=[
+            pl.BlockSpec((tile, left.shape[1]), lambda i: (i, 0)),
+            pl.BlockSpec(right.shape, lambda i: (0, 0)),
+        ],
+        out_specs=outs,
         out_shape=[jax.ShapeDtypeStruct(shape, bf16) for shape in shapes],
         compiler_params=pltpu.CompilerParams(vmem_limit_bytes=56 << 20),
         cost_estimate=BESIDE,
-    )(jnp.zeros(1, jnp.int32) if plain else chip_flip()[None], *inputs)
-    return results if layout == "pieces" else results[0]
+    )(left, right)
+    return results if pieces else results[0]
+
+
+def terms_kernel(scale, place_ref, left_ref, right_ref, own_ref, other_ref):
+    total = lax.dot_general(
+        left_ref[...], right_ref[...], (CONTRACT["tn"], ((), ())), preferred_element_type=f32
+    )
+    total = (total * scale).astype(bf16).reshape(own_ref.shape)
+
+    @pl.when(pl.program_id(0) == 0)
+    def _():
+        other_ref[...] = total
+
+    @pl.when(pl.program_id(0) == 1)
+    def _():
+        own_ref[...] = total
+
+
+def uneven_kernel(scale, place_ref, left_ref, right_ref, own_ref, other_ref, total_ref):
+    total = lax.dot_general(
+        left_ref[...], right_ref[...], (CONTRACT["tn"], ((), ())), preferred_element_type=f32
+    )
+    total_ref[...] = (total * scale).astype(bf16)
+    half, core = own_ref.shape[0], place_ref[1]
+    own_ref[...] = total_ref[pl.ds(pl.multiple_of(core * half, half), half), :]
+    other_ref[...] = total_ref[pl.ds(pl.multiple_of((1 - core) * half, half), half), :]
+
+
+def weight_terms(left, right, scale, flip=None):
+    depth, rows = left.shape
+    width = right.shape[1]
+    chips, dp = lax.axis_size("chip"), lax.axis_size("dp")
+    core = lax.axis_index("core")
+    own = rows // (CORES * dp) if flip is None else rows // (chips * CORES * dp)
+    half = (dp, chips, own, width) if flip is not None else (dp * own, width)
+    tile = dp * own if flip is not None else TILE
+    steps = rows // CORES // tile
+    whole = lambda array: pl.BlockSpec(array.shape, lambda *_: (0, 0))
+    place = jnp.stack([jnp.int32(0) if flip is None else flip, core])
+    params = dict(
+        out_shape=[jax.ShapeDtypeStruct(half, bf16)] * 2,
+        compiler_params=pltpu.CompilerParams(vmem_limit_bytes=56 << 20),
+        cost_estimate=BESIDE,
+    )
+    if tile % 128 == 0 and width % 128 == 0 and rows % (CORES * tile) == 0:
+        if flip is not None:
+            source = lambda j, k, p: (0, k * CORES + (p[1] ^ 1 ^ j))
+            block = (dp, 1, own, width)
+            target = lambda k, p: (0, k ^ p[0], 0, 0)
+        else:
+            source = lambda j, k, p: (0, (p[1] ^ 1 ^ j) * steps + k)
+            block = (tile, width)
+            target = lambda k, p: (k, 0)
+        return pl.pallas_call(
+            functools.partial(terms_kernel, scale),
+            grid_spec=pltpu.PrefetchScalarGridSpec(
+                num_scalar_prefetch=1,
+                grid=(CORES, steps),
+                in_specs=[pl.BlockSpec((depth, tile), source), whole(right)],
+                out_specs=[
+                    pl.BlockSpec(block, lambda j, k, p: target(jnp.where(j == 1, k, 0), p)),
+                    pl.BlockSpec(
+                        block, lambda j, k, p: target(jnp.where(j == 0, k, steps - 1), p)
+                    ),
+                ],
+            ),
+            **params,
+        )(place, left, right)
+    if flip is None and rows % 128 == 0 and width % 512 == 0:
+        columns = lambda size: pl.BlockSpec((size, 512), lambda i, p: (0, i))
+        return pl.pallas_call(
+            functools.partial(uneven_kernel, scale),
+            grid_spec=pltpu.PrefetchScalarGridSpec(
+                num_scalar_prefetch=1,
+                grid=(width // 512,),
+                in_specs=[whole(left), columns(depth)],
+                out_specs=[columns(rows // CORES)] * 2,
+                scratch_shapes=[pltpu.VMEM((rows, 512), bf16)],
+            ),
+            **params,
+        )(place, left, right)
+    total = (inner_rows(left, right) * scale).astype(bf16)
+    if flip is not None:
+        total = total.reshape(chips, CORES, dp, own, width).transpose(1, 2, 0, 3, 4)
+    else:
+        total = total.reshape((CORES,) + half)
+    return take(total, core), take(total, 1 - core)
 
 
 def as_pieces(terms):
@@ -511,34 +559,34 @@
     )(grad_q, up_q, grad_k, grad_v, place)
 
 
-def spread_kernel(flip_rows, count, flip_ref, *refs):
+def spread_kernel(flip_rows, count, own, flip_ref, *refs):
     left_refs, weight_ref, out_refs = refs[:count], refs[count], refs[count + 1 :]
-    chips, groups, _, own, _ = weight_ref.shape
+    chips, groups, _, _, width = weight_ref.shape
     depth = groups * own
     columns = []
     for place in range(chips):
         total = 0.0
         for j, left_ref in enumerate(left_refs):
-            block = weight_ref[place ^ flip_ref[0], :, j].reshape(depth, weight_ref.shape[4])
-            total = total + outer_cols(left_ref[...], block[:, : left_ref.shape[1]])
+            block = weight_ref[place ^ flip_ref[0], :, j, :own].reshape(depth, width)
+            total = total + outer_cols(left_ref[...], block)
         columns.append(total.astype(bf16))
     block = pl.program_id(0) ^ flip_ref[0] if flip_rows else pl.program_id(0)
     write_halves(out_refs, block, jnp.concatenate(columns, 1))
 
 
-def spread(lefts, weight, flip_rows=False):
-    chips, groups, _, own, width = weight.shape
+def spread(lefts, weight, own, flip_rows=False):
+    chips, groups, _, _, width = weight.shape
     rows, depth = lefts[0].shape[0], chips * groups * own
     if chips != 4 or lefts[0].shape[1] % 128:
         total = sum(
-            outer_cols(left, weight[:, :, j].reshape(depth, width)[:, : left.shape[1]])
+            outer_cols(left, weight[:, :, j, :own].reshape(depth, width))
             for j, left in enumerate(lefts)
         )
         return as_pieces(total.astype(bf16))
     tile = rows // chips
     shape = (tile // 2, depth)
     return pl.pallas_call(
-        functools.partial(spread_kernel, flip_rows, len(lefts)),
+        functools.partial(spread_kernel, flip_rows, len(lefts), own),
         grid_spec=pltpu.PrefetchScalarGridSpec(
             num_scalar_prefetch=1,
             grid=(chips,),
@@ -607,23 +655,24 @@
             rows = jnp.concatenate(pieces, 0).astype(f32)
             normed = (rows * rms_scale(rows) * gain_ref[...]).astype(bf16)
             normed_ref[...] = normed
-            depth = small_ref.shape[1]
+            chips, groups, _, width = small_ref.shape
+            depth = normed.shape[1] // chips
+            own = depth // groups
             raw = 0.0
-            for place in range(small_ref.shape[0]):
-                weight = small_ref[place ^ flip_ref[0]][:, : raw_ref.shape[1]]
+            for place in range(chips):
+                weight = small_ref[place ^ flip_ref[0], :, :own].reshape(depth, width)
                 columns = normed[:, place * depth : (place + 1) * depth]
                 raw = raw + matmul(columns, weight)
             raw_ref[...] = raw
 
 
-def normed_rows(near, gain, small, width_out):
+def normed_rows(pieces, gain, small, own):
     chips = lax.axis_size("chip")
     if chips != 4:
-        rows = lax.all_gather(near[0], "chip", axis=0, tiled=True).astype(f32)
+        rows = pieces[0].astype(f32)
         normed = (rows * rms_scale(rows) * gain).astype(bf16)
-        small = small.reshape(normed.shape[1], -1)[:, :width_out]
+        small = small[:, :, :own].reshape(normed.shape[1], -1)
         return normed, matmul(normed, small)
-    pieces = list(near) + list(far_halves(near))
     half, width = pieces[0].shape
     whole = lambda array: pl.BlockSpec(array.shape, lambda k, f: (0,) * array.ndim)
     block = lambda size: pl.BlockSpec((2 * half, size), lambda k, f: (k ^ f[0], 0))
@@ -635,11 +684,11 @@
             num_scalar_prefetch=1,
             grid=(chips,),
             in_specs=[whole(piece) for piece in pieces] + [whole(gain), whole(small)],
-            out_specs=[block(width), block(width_out)],
+            out_specs=[block(width), block(small.shape[-1])],
         ),
         out_shape=[
             jax.ShapeDtypeStruct((rows, width), bf16),
-            jax.ShapeDtypeStruct((rows, width_out), f32),
+            jax.ShapeDtypeStruct((rows, small.shape[-1]), f32),
         ],
         compiler_params=pltpu.CompilerParams(vmem_limit_bytes=48 << 20),
         cost_estimate=BESIDE,
@@ -743,6 +792,7 @@
     span = chips * row_count
     head_width = w_key.shape[1]
     q_width = w_qdown.shape[1]
+    down_shape = w_down.shape
     score_scale = 1.0 / math.sqrt(head_width)
     grad_scale = 1.0 / math.sqrt(slot_count * seq_span * devices)
 
@@ -757,43 +807,47 @@
     inputs = tokens_own.astype(f32)
     flip = chip_flip()[None]
 
-    gains = jnp.stack([attn_gain, ffn_gain, jnp.pad(q_gain, (0, own_rows - own_q))], 1)
-    gains = jnp.pad(gains, ((0, 0), (0, 125)))
     key_pairs = w_key.reshape(own_rows, 2, chips, k_cols).transpose(2, 0, 1, 3)
     small = jnp.concatenate(
         [
             by_columns(w_qdown),
             key_pairs.reshape(chips, own_rows, 2 * k_cols),
             by_columns(w_value),
-            jnp.broadcast_to(gains, (chips,) + gains.shape),
         ],
         2,
     )
+    gains = [jnp.pad(gain, (0, small_cols - gain.shape[0])) for gain in (attn_gain, ffn_gain, q_gain)]
+    gains = jnp.pad(jnp.stack(gains), ((0, 13), (0, 0)))
+    small = jnp.concatenate([small, jnp.broadcast_to(gains, (chips,) + gains.shape)], 1)
     small, up_q, gate_up = split_columns(small, w_qup, w_gate, w_up)
     tokens_own, small = tie(tokens_own, small)
     tokens_near = gather_near(tokens_own)
-    small = gather_columns(small)
-    small, w_out, cotangent, tokens_near, gate_up = tie(
-        small, w_out, cotangent, tokens_near, gate_up
-    )
-    up_q, gate_up = gather_columns(up_q), gather_columns(gate_up)
-    seed_grad = (pair_in(cotangent[0]).astype(f32) * valid_mask).astype(bf16)
-    gains = small.reshape(chips, -1, small.shape[-1])[:, :, small_cols : small_cols + 3]
-    gains = jnp.concatenate(reordered(list(gains.astype(f32)), flip[0]), 0)
-    gain_one, gain_two = gains[:, 0], gains[:, 1]
-    gain_q = gains[:, 2].reshape(devices, own_rows)[:, :own_q].reshape(-1)
-    gain_q = lax.dynamic_slice_in_dim(gain_q, chip * q_cols, q_cols, 0)
-    out_proj = gather_rows(w_out)
-    up_q = up_q.reshape(chips, q_cols, -1)
-    gate_up = gate_up.reshape(chips, CORES * dp, 2, own_rows, -1)
-    down_proj = gather_rows(w_down)
-
     cos_all, sin_all = rotary(jnp.arange(span, dtype=jnp.int32), head_width)
     cos_own = lax.dynamic_slice_in_dim(cos_all, chip * k_cols, k_cols, 1)
     sin_own = lax.dynamic_slice_in_dim(sin_all, chip * k_cols, k_cols, 1)
+    out_proj, small, tokens_near, tables = tie(
+        gather_rows(w_out), exchange(small), tokens_near, (cos_all, sin_all, cos_own, sin_own)
+    )
+    cos_all, sin_all, cos_own, sin_own = tables
+    small = gather_blocks(small)
+    tokens_pieces, up_q, gate_up = tie(far_pieces(tokens_near), up_q, gate_up)
+    up_q = gather_columns(up_q)
+    small, cotangent, gate_up = tie(small, cotangent, gate_up)
+    seed_grad = (pair_in(cotangent[0]).astype(f32) * valid_mask).astype(bf16)
+    gains = small[:, :, own_rows : own_rows + 3].astype(f32)
+    gains = jnp.stack(reordered(list(gains), flip[0]))
+    gain_one = gains[:, :, 0, :own_rows].reshape(-1)
+    gain_two = gains[:, :, 1, :own_rows].reshape(-1)
+    gain_q = gains[:, :, 2, :own_q].reshape(chips, -1)[chip]
+    up_q = up_q.reshape(chips, q_cols, -1)
+
     normed_all, raw = normed_rows(
-        tokens_near, gain_one, small.reshape(chips, -1, small.shape[-1]), small_cols
-    )
+        tokens_pieces, gain_one, small, own_rows
+    )
+    raw, gate_up = tie(raw, exchange(gate_up))
+    gate_up = gather_blocks(gate_up)
+    down_proj = gather_rows(w_down)
+    gate_up = gate_up.reshape(chips, CORES * dp, 2, own_rows, -1)
     q_down = raw[:, :q_cols]
     scale_q = lax.rsqrt(row_sums(q_down * q_down) / q_width + epsilon)
     q_normed = (q_down * scale_q * gain_q).astype(bf16)
@@ -819,55 +873,57 @@
     queries, mixed, log_total = attend(
         length[None], flip, shared, up_q, keys, values, cos_all, sin_all, score_scale
     )
-    part, *seed_near = tie(product("nn", (mixed, out_proj), layout="pieces"), *seed_near)
+    part, *seed_near = tie(product("nn", mixed, out_proj, pieces=True), *seed_near)
     middle = inputs + scatter_chips(part)
     scale_two = rms_scale(middle)
     normed2 = gather_chips((middle * scale_two * gain_two).astype(bf16))
 
     normed2, *seed_near = tie(normed2, *seed_near)
-    seed_all = gather_far(seed_near)
     activated, silu, slope = gated(normed2, gate_up)
-    down_terms = product("tn", (activated, seed_all), scale=grad_scale)
+    activated, seed_pieces = tie(activated, far_pieces(seed_near))
+    seed_all = join_rows(seed_pieces)
+    down_terms = weight_terms(activated, seed_all, grad_scale)
     down_terms, down_proj = tie(down_terms, down_proj)
-    down_half = halve_rows(down_terms)
+    down_half = sum_cores(*down_terms)
     gate_grad, up_grad = gated_back(seed_all, down_proj, silu, slope)
-    gate_tied, up_tied, down_half = tie(gate_grad, up_grad, down_half)
+    gate_grad, up_grad, down_half = tie(gate_grad, up_grad, down_half)
     grad_w_down = scatter_dp(down_half)
-    part = spread([gate_tied, up_tied], gate_up)
-    part, gate_grad, up_grad = tie(part, gate_grad, up_grad)
-    gate_part, up_part = [
-        product("tn", (normed2, grad), scale=grad_scale, layout="split")
-        for grad in (gate_grad, up_grad)
-    ]
-    grad_normed2, gate_sum, up_sum = scatter_chips(part, (gate_part, up_part))
-    gate_half, up_half = halve_columns(gate_sum), halve_columns(up_sum)
+    gate_part = weight_terms(normed2, gate_grad, grad_scale, flip[0])
+    gate_tied, up_tied, gate_part = tie(gate_grad, up_grad, gate_part)
+    part = spread([gate_tied, up_tied], gate_up, own_rows)
+    part, up_grad, gate_half = tie(part, up_grad, sum_cores(*gate_part))
     grad_w_gate = scatter_dp(gate_half)
+    up_part = weight_terms(normed2, up_grad, grad_scale, flip[0])
+    grad_normed2, up_part = scatter_chips(part, (up_part,))
+    up_half = sum_cores(*up_part)
     grad_normed2, grad_w_down, up_half = tie(grad_normed2, grad_w_down, up_half)
     grad_w_up = scatter_dp(up_half)
     grad_middle = seed_grad.astype(f32) + norm_back(grad_normed2, middle, scale_two, gain_two)
     grad_branch, activated = tie(grad_middle.astype(bf16), activated)
-    grad_branch, grad_w_gate, out_part = tie(
-        gather_chips(grad_branch), grad_w_gate, product("nn", (activated, down_proj), layout="pieces")
+    q_rows = shared[:, :, :q_cols].transpose(1, 0, 2).reshape(span, q_width)
+    grad_branch, out_part, q_rows = tie(
+        gather_chips(grad_branch), product("nn", activated, down_proj, pieces=True), q_rows
     )
     out_near = scatter_near(out_part)
-    grad_mixed = product("nt", (grad_branch, out_proj))
+    out_terms = weight_terms(mixed, grad_branch, grad_scale)
+    out_terms, grad_branch, grad_w_gate = tie(out_terms, grad_branch, grad_w_gate)
+    grad_mixed, out_half = tie(product("nt", grad_branch, out_proj), sum_cores(*out_terms))
+    grad_w_out = scatter_dp(out_half)
     grad_q, grad_k, grad_v = attend_back(
         length[None], flip, queries, grad_mixed, log_total, keys, values, cos_all, sin_all, score_scale
     )
     grad_q, out_near = tie(grad_q, out_near)
-    back = back_terms(grad_q, up_q, grad_k, grad_v, place)
-    back, mixed, grad_q = tie(back, mixed, grad_q)
-    out_half = halve_rows(product("tn", (mixed, grad_branch), scale=grad_scale))
-    back, grad_q, out_half, grad_w_up = scatter_chips(back, (grad_q, out_half, grad_w_up))
-    grad_w_out = scatter_dp(out_half)
-    q_rows = shared[:, :, :q_cols].transpose(1, 0, 2).reshape(span, q_width)
-    qup_half = halve_columns(
-        product("tn", (q_rows, grad_q), scale=grad_scale, layout="split", plain=True)
-    )
-    back, qup_half, out_near = tie(back, qup_half, out_near)
+    output = middle + scatter_far(out_near)
+    back, grad_q = tie(back_terms(grad_q, up_q, grad_k, grad_v, place), grad_q)
+    qup_part = weight_terms(q_rows, grad_q, grad_scale, jnp.int32(0))
+    back, qup_part, grad_w_up, output = scatter_chips(back, (qup_part, grad_w_up, output))
+    back, qup_half = tie(back, sum_cores(*qup_part))
     grad_w_qup = scatter_dp(qup_half)
     weighted = back[:, :q_cols] * gain_q
     mean = row_sums(weighted * q_down) / q_width
+    pair = jnp.concatenate([grad_w_gate, grad_w_up], 2)
+    mean, pair = tie(mean, pair)
+    pair = trade_blocks(pair)
     grad_q_down = scale_q * weighted - q_down * scale_q**3 * mean
     k_one, k_two = back[:, q_cols : q_cols + k_cols], back[:, q_cols + k_cols : q_cols + 2 * k_cols]
     back = jnp.concatenate(
@@ -879,24 +935,22 @@
         ],
         1,
     ).astype(bf16)
-    output = middle + scatter_far(out_near)
-    terms, back, grad_w_out, output = tie(
-        spread([back], small[:, :, None], flip_rows=True), back, grad_w_out, output
-    )
-    small_sum = product("tn", (normed_all, back), scale=grad_scale, layout="split")
-    grad_normed, small_sum, grad_w_gate, grad_w_up = scatter_chips(
-        terms, (small_sum, grad_w_gate, grad_w_up)
-    )
-    small_half, grad_w_qup = tie(halve_columns(small_sum), grad_w_qup)
+    small_half = sum_cores(*weight_terms(normed_all, back, grad_scale, flip[0]))
+    back, small_half, grad_w_out = tie(back, small_half, grad_w_out)
     grad_small = scatter_dp(small_half)
+    terms = spread([back], small[:, :, None], own_rows, flip_rows=True)
+    grad_normed, pair, grad_w_qup = scatter_chips(terms, (pair, grad_w_qup))
+    grad_w_qup = trade_blocks(grad_w_qup)
+    grad_normed, grad_small = tie(grad_normed, grad_small)
     out_tokens = pair_out(output.astype(bf16))[None]
     grad_inputs = grad_middle + norm_back(grad_normed, inputs, rms_scale(inputs), gain_one)
     grad_tokens = pair_out(grad_inputs)[None]
     grad_w_qup = join_columns(grad_w_qup)
-    parts = jnp.stack(join_blocks(grad_small), 1).astype(f32)
+    parts = jnp.stack(reordered(trade_blocks(grad_small), flip[0]), 1).astype(f32)
     grad_w_key = parts[:, :, q_cols : q_cols + v_cols].reshape(own_rows, chips, 2, k_cols)
     grad_w_key = grad_w_key.transpose(0, 2, 1, 3).reshape(own_rows, head_width)
-    grad_w_gate, grad_w_up = join_columns(grad_w_gate), join_columns(grad_w_up)
+    pairs = [jnp.split(block, 2, 1) for block in pair]
+    grad_w_gate, grad_w_up = [join_columns([pair[j] for pair in pairs]) for j in range(2)]
     grad_w_qdown = parts[:, :, :q_cols].reshape(own_rows, q_width)
     grad_w_value = parts[:, :, q_cols + v_cols :].reshape(own_rows, head_width)
     overlap = lambda weight, grad: jnp.sum(weight.astype(f32) * grad, axis=1)
@@ -912,11 +966,11 @@
         grad_w_qup,
         grad_w_key,
         grad_w_value,
-        grad_w_out.astype(f32),
+        grad_w_out.astype(f32).reshape(w_out.shape),
         ffn_terms / ffn_gain.astype(f32),
         grad_w_gate,
         grad_w_up,
-        grad_w_down.astype(f32),
+        grad_w_down.astype(f32).reshape(down_shape),
     )
 
 

time: 701 us -> 665 us (0.949)
  waiting for transfers between devices: 239 us -> 204 us
  local copies, waits for them, and re-layouts: 62 us -> 41.4 us
  other arithmetic: 78.5 us -> 88.1 us
    ppermute x85 -> x82, waiting for transfers between devices: 216 us -> 195 us  [to_chip(): return lax.ppermute(block, 'chip', [(i, i ^ bits) for i in range(count)])]
    reduce_scatter x6, waiting for transfers between devices: 17.5 us -> 0.05 us  [scatter_dp(): return lax.psum_scatter(half, 'dp', scatter_dimension=0, tiled=True)]
    squeeze x7 -> x2, local copies, waits for them, and re-layouts: 15.4 us -> 3.36 us  [take(): return lax.dynamic_index_in_dim(blocks, index, 0, keepdims=False)]
    convert_element_type x20 -> x18, other arithmetic: 32.1 us -> 29.3 us  [the longest x6 15.8 us: sum_cores(): return add(own, swap_cores(other)).astype(bf16)]
    unnamed x225 -> x205, local copies, waits for them, and re-layouts: 28.4 us -> 25.8 us
    ppermute x85 -> x82, starting transfers between devices: 89.6 us -> 91.4 us  [to_chip(): return lax.ppermute(block, 'chip', [(i, i ^ bits) for i in range(count)])]
  transfers between devices with their start and end apart: 106 -> 103, of which waited for: 57 -> 46; matrix products, arithmetic and copies ran while one was open for 15% -> 15% of each run, Pallas kernels for 30% -> 32%
where the time goes in v3:
time: 665 us; the launch traced here: 655 us
  Pallas kernels  212 us (32%)
  waiting for transfers between devices  204 us (31%)
  starting transfers between devices  93.4 us (14%)
  other arithmetic  88.1 us (13%)
  local copies, waits for them, and re-layouts  41.4 us (6%)
  between operations  15.7 us (2%)
    ppermute x82, waiting for transfers between devices, to_chip(): return lax.ppermute(block, 'chip', [(i, i ^ bits) for i in range(count)])  195 us
    ppermute x82, starting transfers between devices, to_chip(): return lax.ppermute(block, 'chip', [(i, i ^ bits) for i in range(count)])  91.4 us
    pallas_call x5, Pallas kernels, weight_terms(): pl.pallas_call(functools.partial(terms_kernel, scale), grid_spec=pltpu.Pr...  55.7 us
    pallas_call x3, Pallas kernels, product(): pl.pallas_call(functools.partial(product_kernel, kind, pieces), grid=(row...  31.2 us
    pallas_call x2, Pallas kernels, spread(): pl.pallas_call(functools.partial(spread_kernel, flip_rows, len(lefts), ow...  28.6 us
    unnamed x205, local copies, waits for them, and re-layouts  25.8 us
    pallas_call x1, Pallas kernels, gated(): pl.pallas_call(gate_kernel, grid_spec=pltpu.PrefetchScalarGridSpec(num_sc...  18.4 us
    pallas_call x1, Pallas kernels, attend(): pl.pallas_call(functools.partial(attend_kernel, score_scale), grid=(heads...  18.2 us
  transfers between devices with their start and end apart: 103, of which 46 were waited for; matrix products, arithmetic and copies ran while one was open for 15% of the time, Pallas kernels for 32%

profile of v3, /device:TPU:0, one launch (start us, length us, event | category | flops | bytes accessed | tf_op | source)
XLA Modules:
  0.0 655.0 jit_solution(801395577434361157)
XLA Ops:
  11.2 3.7 shard_map.237
  16.2 2.5 collective-permute-start.4
  24.7 19.2 %collective-permute-done.1 = bf16[80,384]{1,0:T(8,128)(2,1)S(1)} collective-permute-done((bf16[80,384]{1,0:T(8,128)(2,1)S(1)}, bf16[80,384]{1,0:T(8,128)(2,1)S(1)}, u32[]{:S(2)}, u32[]{:S(2)}) %collective-permute-start.1) | collective-permute-done | bytes 61472 | tf_op jit(solution)/shard_map/ppermute | solution.py:72
  48.3 2.7 collective-permute-start.3
  51.0 2.8 fusion.7
  54.4 5.2 all-gather.9.cloned.1.call-done.right_ref
  64.2 11.1 %collective-permute-done.8.refs_6_ = bf16[128,2048]{1,0:T(8,128)(2,1)S(1)} collective-permute-done((bf16[128,2048]{1,0:T(8,128)(2,1)S(1)}, bf16[128,2048]{1,0:T(8,128)(2,1)S(1)}, u32[]{:S(2)}, u32[]{:S(2)}) %collective-permute-start.8) | collective-permute-done | bytes 524320 | tf_op jit(solution)/shard_map/ppermute | solution.py:72
  99.1 6.6 %shard_map.238 = (bf16[1024,2048]{1,0:T(8,128)(2,1)}, f32[1024,384]{1,0:T(8,128)S(1)}) custom-call(s32[1]{0:T(128)} %bitcast.1._.flip_ref, bf16[128,2048]{1,0:T(8,128)(2,1)S(1)} %get-tuple-element.303.refs_0_, bf16[128,2048]{1,0:T(8,128)(2,1)S(1)} %get-tuple-element.304.refs_1_, bf16[128,2048]{1,0:T(8,128)(2,1)S(1)} %collective-permute-done.4.refs_2_, ...), custom_call_target="tpu_custom_call" | custom-call | flops 1 | bytes 1 | tf_op jit(solution)/shard_map/pallas_call | solution.py:681
  107.8 2.5 pad_maximum_fusion.3
  127.0 7.3 %collective-permute-done.15.refs_2_ = bf16[512,384]{1,0:T(8,128)(2,1)S(1)} collective-permute-done((bf16[512,384]{1,0:T(8,128)(2,1)S(1)}, bf16[512,384]{1,0:T(8,128)(2,1)S(1)}, u32[]{:S(2)}, u32[]{:S(2)}) %collective-permute-start.15) | collective-permute-done | bytes 393248 | tf_op jit(solution)/shard_map/ppermute | solution.py:72
  137.9 4.8 collective-permute-done.16.refs_3_
  143.9 5.7 collective-permute-done.19.refs_6_
  161.3 18.2 %shard_map.240 = (bf16[1024,1024]{1,0:T(8,128)(2,1)S(1)}, bf16[1024,1024]{1,0:T(8,128)(2,1)}, f32[4,1,1024]{2,1,0:T(1,128)S(1)}) custom-call(s32[1]{0:T(128)} %bitcast.length_ref, s32[1]{0:T(128)} %bitcast.1._.flip_ref, bf16[4,1024,384]{2,1,0:T(8,128)(2,1)} %bitcast.149, bf16[4,256,1024]{2,1,0:T(8,128)(2,1)} %all-gather.15.cloned.1.call-done.up_ref, ...), custom_call_target="tpu_custom_call" | custom-call | flops 1 | bytes 1 | tf_op jit(solution)/shard_map/pallas_call | solution.py:290
  180.9 10.0 %shard_map.241 = (bf16[128,2048]{1,0:T(8,128)(2,1)}, bf16[128,2048]{1,0:T(8,128)(2,1)}, bf16[128,2048]{1,0:T(8,128)(2,1)}, bf16[128,2048]{1,0:T(8,128)(2,1)}, bf...) custom-call(bf16[1024,1024]{1,0:T(8,128)(2,1)} %get-tuple-element.33, ...), custom_call_target="tpu_custom_call" | custom-call | flops 1 | bytes 1 | tf_op jit(solution)/shard_map/pallas_call | solution.py:427
  195.0 11.0 %collective-permute-done.29 = bf16[128,2048]{1,0:T(8,128)(2,1)S(1)} collective-permute-done((bf16[128,2048]{1,0:T(8,128)(2,1)}, bf16[128,2048]{1,0:T(8,128)(2,1)S(1)}, u32[]{:S(2)}, u32[]{:S(2)}) %collective-permute-start.29) | collective-permute-done | bytes 524320 | tf_op jit(solution)/shard_map/ppermute | solution.py:72
  206.9 5.8 collective-permute-done.31
  219.5 5.3 collective-permute-done.33
  226.3 2.8 collective-permute-done.34
  235.5 10.8 %collective-permute-done.35.refs_2_ = bf16[128,2048]{1,0:T(8,128)(2,1)S(1)} collective-permute-done((bf16[128,2048]{1,0:T(8,128)(2,1)S(1)}, bf16[128,2048]{1,0:T(8,128)(2,1)S(1)}, u32[]{:S(2)}, u32[]{:S(2)}) %collective-permute-start.35) | collective-permute-done | bytes 524320 | tf_op jit(solution)/shard_map/ppermute | solution.py:72
  248.4 7.9 %collective-permute-done.36.refs_3_ = bf16[128,2048]{1,0:T(8,128)(2,1)S(1)} collective-permute-done((bf16[128,2048]{1,0:T(8,128)(2,1)S(1)}, bf16[128,2048]{1,0:T(8,128)(2,1)S(1)}, u32[]{:S(2)}, u32[]{:S(2)}) %collective-permute-start.36) | collective-permute-done | bytes 524320 | tf_op jit(solution)/shard_map/ppermute | solution.py:72
  256.3 6.1 collective-permute-done.39.refs_6_
  267.6 18.4 %shard_map.243 = (bf16[1024,1408]{1,0:T(8,128)(2,1)S(1)}, bf16[1024,1408]{1,0:T(8,128)(2,1)S(1)}, bf16[1024,1408]{1,0:T(8,128)(2,1)}) custom-call(s32[1]{0:T(128)} %bitcast.1._.flip_ref, bf16[1024,2048]{1,0:T(8,128)(2,1)} %copy-done.2, bf16[4,8,2,64,1408]{4,3,2,1,0:T(8,128)(2,1)} %bitcast.151), custom_call_target="tpu_custom_call" | custom-call | flops 1 | bytes 1 | tf_op jit(solution)/shard_map/pallas_call | solution.py:725
  289.1 2.6 shard_map.244.right_ref.seed_ref
  293.8 11.2 %shard_map.245 = (bf16[704,2048]{1,0:T(8,128)(2,1)}, bf16[704,2048]{1,0:T(8,128)(2,1)}) custom-call(s32[2]{0:T(128)} %pad_add_fusion.place_ref, bf16[1024,1408]{1,0:T(8,128)(2,1)} %copy-done.11, bf16[1024,2048]{1,0:T(8,128)(2,1)} %copy-done.4), custom_call_target="tpu_custom_call" | custom-call | flops 1 | bytes 1 | tf_op jit(solution)/shard_map/pallas_call | solution.py:509
  305.0 11.9 %shard_map.246 = (bf16[1024,1408]{1,0:T(8,128)(2,1)S(1)}, bf16[1024,1408]{1,0:T(8,128)(2,1)S(1)}) custom-call(bf16[1024,2048]{1,0:T(8,128)(2,1)} %copy-done.4, bf16[1408,2048]{1,0:T(8,128)(2,1)} %all-gather.11.cloned.1.call-done.down_ref.right_ref, bf16[1024,1408]{1,0:T(8,128)(2,1)} %copy-done.18, bf16[1024,1408]{1,0:T(8,128)(2,1)} %get-tuple-element.395.slope_ref), custom_call_target="tpu_custom_call" | custom-call | flops 1 | bytes 1 | tf_op jit(solution)/shard_map/pallas_call | solution.py:754
  316.9 3.3 add_convert_fusion.2
  320.9 13.6 %shard_map.247 = (bf16[4,4,64,1408]{3,2,1,0:T(8,128)(2,1)}, bf16[4,4,64,1408]{3,2,1,0:T(8,128)(2,1)}) custom-call(s32[2]{0:T(128)} %pad_add_fusion.1.place_ref, bf16[1024,2048]{1,0:T(8,128)(2,1)} %copy-done.2, bf16[1024,1408]{1,0:T(8,128)(2,1)} %copy-done.10), custom_call_target="tpu_custom_call" | custom-call | flops 1 | bytes 1 | tf_op jit(solution)/shard_map/pallas_call | solution.py:492
  335.0 21.3 %shard_map.248 = (bf16[128,2048]{1,0:T(8,128)(2,1)}, bf16[128,2048]{1,0:T(8,128)(2,1)}, bf16[128,2048]{1,0:T(8,128)(2,1)}, bf16[128,2048]{1,0:T(8,128)(2,1)}, bf...) custom-call(s32[1]{0:T(128)} %bitcast.1._.flip_ref, ...), custom_call_target="tpu_custom_call" | custom-call | flops 1 | bytes 1 | tf_op jit(solution)/shard_map/pallas_call | solution.py:588
  356.3 4.5 add_convert_fusion.1
  365.0 13.5 %shard_map.249 = (bf16[4,4,64,1408]{3,2,1,0:T(8,128)(2,1)}, bf16[4,4,64,1408]{3,2,1,0:T(8,128)(2,1)}) custom-call(s32[2]{0:T(128)} %pad_add_fusion.1.place_ref, bf16[1024,2048]{1,0:T(8,128)(2,1)} %copy-done.2, bf16[1024,1408]{1,0:T(8,128)(2,1)} %copy-done.9), custom_call_target="tpu_custom_call" | custom-call | flops 1 | bytes 1 | tf_op jit(solution)/shard_map/pallas_call | solution.py:492
  378.5 7.7 %collective-permute-done.47 = bf16[128,2048]{1,0:T(8,128)(2,1)S(1)} collective-permute-done((bf16[128,2048]{1,0:T(8,128)(2,1)}, bf16[128,2048]{1,0:T(8,128)(2,1)S(1)}, u32[]{:S(2)}, u32[]{:S(2)}) %collective-permute-start.47) | collective-permute-done | bytes 524320 | tf_op jit(solution)/shard_map/ppermute | solution.py:72
  390.2 12.0 %collective-permute-done.49 = bf16[128,2048]{1,0:T(8,128)(2,1)S(1)} collective-permute-done((bf16[128,2048]{1,0:T(8,128)(2,1)S(1)}, bf16[128,2048]{1,0:T(8,128)(2,1)S(1)}, u32[]{:S(2)}, u32[]{:S(2)}) %collective-permute-start.49) | collective-permute-done | bytes 524320 | tf_op jit(solution)/shard_map/ppermute | solution.py:72
  410.3 4.2 fusion.18
  418.7 10.8 %collective-permute-done.52.refs_2_ = bf16[128,2048]{1,0:T(8,128)(2,1)S(1)} collective-permute-done((bf16[128,2048]{1,0:T(8,128)(2,1)S(1)}, bf16[128,2048]{1,0:T(8,128)(2,1)S(1)}, u32[]{:S(2)}, u32[]{:S(2)}) %collective-permute-start.52) | collective-permute-done | bytes 524320 | tf_op jit(solution)/shard_map/ppermute | solution.py:72
  433.3 12.6 %shard_map.251 = (bf16[128,2048]{1,0:T(8,128)(2,1)}, bf16[128,2048]{1,0:T(8,128)(2,1)}, bf16[128,2048]{1,0:T(8,128)(2,1)}, bf16[128,2048]{1,0:T(8,128)(2,1)}, bf...) custom-call(bf16[1024,1408]{1,0:T(8,128)(2,1)} %copy-done.11, ...), custom_call_target="tpu_custom_call" | custom-call | flops 1 | bytes 1 | tf_op jit(solution)/shard_map/pallas_call | solution.py:427
  446.0 6.0 collective-permute-done.56.refs_6_
  454.6 10.5 %shard_map.252 = (bf16[512,2048]{1,0:T(8,128)(2,1)}, bf16[512,2048]{1,0:T(8,128)(2,1)}) custom-call(s32[2]{0:T(128)} %pad_add_fusion.place_ref, bf16[1024,1024]{1,0:T(8,128)(2,1)} %get-tuple-element.337.left_ref, bf16[1024,2048]{1,0:T(8,128)(2,1)} %copy-done.3), custom_call_target="tpu_custom_call" | custom-call | flops 1 | bytes 1 | tf_op jit(solution)/shard_map/pallas_call | solution.py:492
  469.7 8.7 %shard_map.253.grad_ref = bf16[1024,1024]{1,0:T(8,128)(2,1)} custom-call(bf16[1024,2048]{1,0:T(8,128)(2,1)} %copy-done.3, bf16[1024,2048]{1,0:T(8,128)(2,1)} %all-gather.9.cloned.1.call-done.right_ref), custom_call_target="tpu_custom_call" | custom-call | flops 1 | bytes 1 | tf_op jit(solution)/shard_map/pallas_call | solution.py:427
  478.4 4.0 add_convert_fusion.3
  482.4 15.0 %shard_map.254 = (bf16[1024,1024]{1,0:T(8,128)(2,1)}, f32[1024,256]{1,0:T(8,128)S(1)}, f32[1024,256]{1,0:T(8,128)S(1)}) custom-call(s32[1]{0:T(128)} %bitcast.length_ref, s32[1]{0:T(128)} %bitcast.1._.flip_ref, bf16[1024,1024]{1,0:T(8,128)(2,1)} %copy-done.20, bf16[1024,1024]{1,0:T(8,128)(2,1)} %shard_map.253.grad_ref, ...), custom_call_target="tpu_custom_call" | custom-call | flops 1 | bytes 1 | tf_op jit(solution)/shard_map/pallas_call | solution.py:367
  504.0 7.0 %shard_map.255 = (bf16[512,384]{1,0:T(8,128)(2,1)S(1)}, bf16[512,384]{1,0:T(8,128)(2,1)S(1)}, bf16[512,384]{1,0:T(8,128)(2,1)S(1)}, bf16[512,384]{1,0:T(8,128)(2...) custom-call(bf16[1024,1024]{1,0:T(8,128)(2,1)} %get-tuple-element.48, ...), custom_call_target="tpu_custom_call" | custom-call | flops 1 | bytes 1 | tf_op jit(solution)/shard_map/pallas_call | solution.py:551
  513.8 9.1 %shard_map.256 = (bf16[4,4,32,1024]{3,2,1,0:T(8,128)(2,1)}, bf16[4,4,32,1024]{3,2,1,0:T(8,128)(2,1)}) custom-call(s32[2]{0:T(128)} %pad_add_fusion.place_ref, bf16[1024,1024]{1,0:T(8,128)(2,1)} %bitcast.158, bf16[1024,1024]{1,0:T(8,128)(2,1)} %get-tuple-element.487.grad_ref.right_ref), custom_call_target="tpu_custom_call" | custom-call | flops 1 | bytes 1 | tf_op jit(solution)/shard_map/pallas_call | solution.py:492
  537.8 7.2 %collective-permute-done.70 = bf16[512,384]{1,0:T(8,128)(2,1)S(1)} collective-permute-done((bf16[512,384]{1,0:T(8,128)(2,1)S(1)}, bf16[512,384]{1,0:T(8,128)(2,1)S(1)}, u32[]{:S(2)}, u32[]{:S(2)}) %collective-permute-start.70) | collective-permute-done | bytes 393248 | tf_op jit(solution)/shard_map/ppermute | solution.py:72
  559.2 9.0 %shard_map.257 = (bf16[4,4,64,384]{3,2,1,0:T(8,128)(2,1)}, bf16[4,4,64,384]{3,2,1,0:T(8,128)(2,1)}) custom-call(s32[2]{0:T(128)} %pad_add_fusion.1.place_ref, bf16[1024,2048]{1,0:T(8,128)(2,1)} %get-tuple-element.514.left_ref, bf16[1024,384]{1,0:T(8,128)(2,1)} %pad_maximum_fusion.8.right_ref.refs_0_), custom_call_target="tpu_custom_call" | custom-call | flops 1 | bytes 1 | tf_op jit(solution)/shard_map/pallas_call | solution.py:492
  571.5 7.2 %shard_map.258 = (bf16[128,2048]{1,0:T(8,128)(2,1)}, bf16[128,2048]{1,0:T(8,128)(2,1)}, bf16[128,2048]{1,0:T(8,128)(2,1)}, bf16[128,2048]{1,0:T(8,128)(2,1)}, bf...) custom-call(s32[1]{0:T(128)} %bitcast.1._.flip_ref, ...), custom_call_target="tpu_custom_call" | custom-call | flops 1 | bytes 1 | tf_op jit(solution)/shard_map/pallas_call | solution.py:588
  588.9 23.2 %collective-permute-done.82 = bf16[64,2816]{1,0:T(8,128)(2,1)S(1)} collective-permute-done((bf16[64,2816]{1,0:T(8,128)(2,1)S(1)}, bf16[64,2816]{1,0:T(8,128)(2,1)S(1)}, u32[]{:S(2)}, u32[]{:S(2)}) %collective-permute-start.82) | collective-permute-done | bytes 360480 | tf_op jit(solution)/shard_map/ppermute | solution.py:72
  626.4 4.0 collective-permute-done.83
  645.0 3.2 maximum_select_fusion
  (535 shorter events, 225.7 us)
Async XLA Ops:
  7.3 52.3 %all-gather.9.cloned.1.call-start = ((), (), s32[]{:S(2)}) async-start(), calls=%async_computation.6 | async-start | bytes 4718592 | tf_op jit(solution)/shard_map/all_gather | solution.py:190
  8.0 80.0 %all-gather.13.cloned.1.call-start = ((), (), s32[]{:S(2)}) async-start(), calls=%async_computation.14 | async-start | bytes 2211840 | tf_op jit(solution)/shard_map/all_gather | solution.py:182
  16.2 37.6 %collective-permute-start.4 = (bf16[128,2048]{1,0:T(8,128)(2,1)S(1)}, bf16[128,2048]{1,0:T(8,128)(2,1)S(1)}, u32[]{:S(2)}, u32[]{:S(2)}) collective-permute-start(bf16[128,2048]{1,0:T(8,128)(2,1)S(1)} %get-tuple-element.303.refs_0_), channel_id=1, source_target_pairs={{0,8},{8,0},{16,24},{24,16},{1,9},{9,1},{17,25},{25,17},{2,10},{10... | collective-permute-start | bytes 1572872 | tf_op jit(solution)/shard_map/ppermute | solution.py:72
  18.7 35.1 %collective-permute-start.6 = (bf16[128,2048]{1,0:T(8,128)(2,1)S(1)}, bf16[128,2048]{1,0:T(8,128)(2,1)S(1)}, u32[]{:S(2)}, u32[]{:S(2)}) collective-permute-start(bf16[128,2048]{1,0:T(8,128)(2,1)S(1)} %get-tuple-element.303.refs_0_), channel_id=1, source_target_pairs={{0,16},{8,24},{16,0},{24,8},{1,17},{9,25},{17,1},{25,9},{2,18},{10... | collective-permute-start | bytes 1572872 | tf_op jit(solution)/shard_map/ppermute | solution.py:72
  20.2 33.6 %collective-permute-start.5 = (bf16[128,2048]{1,0:T(8,128)(2,1)S(1)}, bf16[128,2048]{1,0:T(8,128)(2,1)S(1)}, u32[]{:S(2)}, u32[]{:S(2)}) collective-permute-start(bf16[128,2048]{1,0:T(8,128)(2,1)S(1)} %get-tuple-element.304.refs_1_), channel_id=1, source_target_pairs={{0,8},{8,0},{16,24},{24,16},{1,9},{9,1},{17,25},{25,17},{2,10},{10... | collective-permute-start | bytes 1572872 | tf_op jit(solution)/shard_map/ppermute | solution.py:72
  20.8 33.6 %collective-permute-start.7 = (bf16[128,2048]{1,0:T(8,128)(2,1)S(1)}, bf16[128,2048]{1,0:T(8,128)(2,1)S(1)}, u32[]{:S(2)}, u32[]{:S(2)}) collective-permute-start(bf16[128,2048]{1,0:T(8,128)(2,1)S(1)} %get-tuple-element.304.refs_1_), channel_id=1, source_target_pairs={{0,16},{8,24},{16,0},{24,8},{1,17},{9,25},{17,1},{25,9},{2,18},{10... | collective-permute-start | bytes 1572872 | tf_op jit(solution)/shard_map/ppermute | solution.py:72
  20.8 23.1 %collective-permute-start.1 = (bf16[80,384]{1,0:T(8,128)(2,1)S(1)}, bf16[80,384]{1,0:T(8,128)(2,1)S(1)}, u32[]{:S(2)}, u32[]{:S(2)}) collective-permute-start(bf16[80,384]{1,0:T(8,128)(2,1)S(1)} %copy-done.100), channel_id=1, source_target_pairs={{0,8},{8,0},{16,24},{24,16},{1,9},{9,1},{17,25},{25,17},{2,10},{10... | collective-permute-start | bytes 184328 | tf_op jit(solution)/shard_map/ppermute | solution.py:72
  61.2 96.6 %all-gather.15.cloned.1.call-start = ((), (), s32[]{:S(2)}) async-start(), calls=%async_computation.15 | async-start | bytes 2359296 | tf_op jit(solution)/shard_map/all_gather | solution.py:182
  86.0 181.6 %all-gather.17.cloned.1.call-start = ((), (), s32[]{:S(2)}) async-start(), calls=%async_computation.16 | async-start | bytes 12976128 | tf_op jit(solution)/shard_map/all_gather | solution.py:182
  89.5 18.3 %collective-permute-start.11 = (bf16[128,1408]{1,0:T(8,128)(2,1)}, bf16[128,1408]{1,0:T(8,128)(2,1)}, u32[]{:S(2)}, u32[]{:S(2)}) collective-permute-start(bf16[128,1408]{1,0:T(8,128)(2,1)} %get-tuple-element.323), channel_id=1, source_target_pairs={{0,16},{8,24},{16,0},{24,8},{1,17},{9,25},{17,1},{25,9},{2,18},{10... | collective-permute-start | bytes 1081352 | tf_op jit(solution)/shard_map/ppermute | solution.py:72
  110.4 194.6 %all-gather.11.cloned.1.call-start = ((), (), s32[]{:S(2)}) async-start(), calls=%async_computation.7 | async-start | bytes 6488064 | tf_op jit(solution)/shard_map/all_gather | solution.py:190
  111.0 296.9 %reduce-scatter.7.cloned.1.call-start = ((), (), s32[]{:S(2)}) async-start(), calls=%async_computation.8 | async-start | bytes 3604480 | tf_op jit(solution)/shard_map/reduce_scatter | solution.py:199
  113.9 22.4 %collective-permute-start.21 = (bf16[128,2048]{1,0:T(8,128)(2,1)}, bf16[128,2048]{1,0:T(8,128)(2,1)}, u32[]{:S(2)}, u32[]{:S(2)}) collective-permute-start(bf16[128,2048]{1,0:T(8,128)(2,1)} %get-tuple-element.605), channel_id=1, source_target_pairs={{0,4},{4,0},{1,5},{5,1},{2,6},{6,2},{3,7},{7,3},{8,12},{12,8},{9,1... | collective-permute-start | bytes 1572872 | tf_op jit(solution)/shard_map/ppermute | solution.py:67
  151.4 39.4 %collective-permute-start.25 = (bf16[128,2048]{1,0:T(8,128)(2,1)}, bf16[128,2048]{1,0:T(8,128)(2,1)}, u32[]{:S(2)}, u32[]{:S(2)}) collective-permute-start(bf16[128,2048]{1,0:T(8,128)(2,1)} %get-tuple-element.382.refs_0_), channel_id=1, source_target_pairs={{0,8},{8,0},{16,24},{24,16},{1,9},{9,1},{17,25},{25,17},{2,10},{10... | collective-permute-start | bytes 1572872 | tf_op jit(solution)/shard_map/ppermute | solution.py:72
  152.2 38.7 %collective-permute-start.27 = (bf16[128,2048]{1,0:T(8,128)(2,1)}, bf16[128,2048]{1,0:T(8,128)(2,1)}, u32[]{:S(2)}, u32[]{:S(2)}) collective-permute-start(bf16[128,2048]{1,0:T(8,128)(2,1)} %get-tuple-element.382.refs_0_), channel_id=1, source_target_pairs={{0,16},{8,24},{16,0},{24,8},{1,17},{9,25},{17,1},{25,9},{2,18},{10... | collective-permute-start | bytes 1572872 | tf_op jit(solution)/shard_map/ppermute | solution.py:72
  153.7 37.2 %collective-permute-start.26 = (bf16[128,2048]{1,0:T(8,128)(2,1)}, bf16[128,2048]{1,0:T(8,128)(2,1)}, u32[]{:S(2)}, u32[]{:S(2)}) collective-permute-start(bf16[128,2048]{1,0:T(8,128)(2,1)} %get-tuple-element.383.refs_1_), channel_id=1, source_target_pairs={{0,8},{8,0},{16,24},{24,16},{1,9},{9,1},{17,25},{25,17},{2,10},{10... | collective-permute-start | bytes 1572872 | tf_op jit(solution)/shard_map/ppermute | solution.py:72
  154.3 36.6 %collective-permute-start.28 = (bf16[128,2048]{1,0:T(8,128)(2,1)}, bf16[128,2048]{1,0:T(8,128)(2,1)}, u32[]{:S(2)}, u32[]{:S(2)}) collective-permute-start(bf16[128,2048]{1,0:T(8,128)(2,1)} %get-tuple-element.383.refs_1_), channel_id=1, source_target_pairs={{0,16},{8,24},{16,0},{24,8},{1,17},{9,25},{17,1},{25,9},{2,18},{10... | collective-permute-start | bytes 1572872 | tf_op jit(solution)/shard_map/ppermute | solution.py:72
  193.3 19.4 %collective-permute-start.31 = (bf16[128,2048]{1,0:T(8,128)(2,1)}, bf16[128,2048]{1,0:T(8,128)(2,1)S(1)}, u32[]{:S(2)}, u32[]{:S(2)}) collective-permute-start(bf16[128,2048]{1,0:T(8,128)(2,1)} %get-tuple-element.353), channel_id=1, source_target_pairs={{0,8},{8,0},{16,24},{24,16},{1,9},{9,1},{17,25},{25,17},{2,10},{10... | collective-permute-start | bytes 1572872 | tf_op jit(solution)/shard_map/ppermute | solution.py:72
  193.9 19.2 %collective-permute-start.32 = (bf16[128,2048]{1,0:T(8,128)(2,1)}, bf16[128,2048]{1,0:T(8,128)(2,1)S(1)}, u32[]{:S(2)}, u32[]{:S(2)}) collective-permute-start(bf16[128,2048]{1,0:T(8,128)(2,1)} %get-tuple-element.355), channel_id=1, source_target_pairs={{0,16},{8,24},{16,0},{24,8},{1,17},{9,25},{17,1},{25,9},{2,18},{10... | collective-permute-start | bytes 1572872 | tf_op jit(solution)/shard_map/ppermute | solution.py:72
  233.2 23.1 %collective-permute-start.36 = (bf16[128,2048]{1,0:T(8,128)(2,1)S(1)}, bf16[128,2048]{1,0:T(8,128)(2,1)S(1)}, u32[]{:S(2)}, u32[]{:S(2)}) collective-permute-start(bf16[128,2048]{1,0:T(8,128)(2,1)S(1)} %get-tuple-element.600.refs_1_), channel_id=1, source_target_pairs={{0,8},{8,0},{16,24},{24,16},{1,9},{9,1},{17,25},{25,17},{2,10},{10... | collective-permute-start | bytes 1572872 | tf_op jit(solution)/shard_map/ppermute | solution.py:72
  234.0 22.3 %collective-permute-start.37 = (bf16[128,2048]{1,0:T(8,128)(2,1)S(1)}, bf16[128,2048]{1,0:T(8,128)(2,1)S(1)}, u32[]{:S(2)}, u32[]{:S(2)}) collective-permute-start(bf16[128,2048]{1,0:T(8,128)(2,1)S(1)} %get-tuple-element.601.refs_0_), channel_id=1, source_target_pairs={{0,16},{8,24},{16,0},{24,8},{1,17},{9,25},{17,1},{25,9},{2,18},{10... | collective-permute-start | bytes 1572872 | tf_op jit(solution)/shard_map/ppermute | solution.py:72
  265.4 23.8 %collective-permute-start.41 = (bf16[128,2048]{1,0:T(8,128)(2,1)}, bf16[128,2048]{1,0:T(8,128)(2,1)S(1)}, u32[]{:S(2)}, u32[]{:S(2)}) collective-permute-start(bf16[128,2048]{1,0:T(8,128)(2,1)} %collective-permute-done.25.refs_2_), channel_id=1, source_target_pairs={{0,16},{8,24},{16,0},{24,8},{1,17},{9,25},{17,1},{25,9},{2,18},{10... | collective-permute-start | bytes 1572872 | tf_op jit(solution)/shard_map/ppermute | solution.py:72
  266.8 22.4 %collective-permute-start.42 = (bf16[128,2048]{1,0:T(8,128)(2,1)}, bf16[128,2048]{1,0:T(8,128)(2,1)S(1)}, u32[]{:S(2)}, u32[]{:S(2)}) collective-permute-start(bf16[128,2048]{1,0:T(8,128)(2,1)} %collective-permute-done.28.refs_5_), channel_id=1, source_target_pairs={{0,8},{8,0},{16,24},{24,16},{1,9},{9,1},{17,25},{25,17},{2,10},{10... | collective-permute-start | bytes 1572872 | tf_op jit(solution)/shard_map/ppermute | solution.py:72
  320.2 144.9 %reduce-scatter.9.cloned.1.call-start = ((), (), s32[]{:S(2)}) async-start(), calls=%async_computation.9 | async-start | bytes 3604480 | tf_op jit(solution)/shard_map/reduce_scatter | solution.py:199
  334.5 21.8 %collective-permute-start.44 = (bf16[4,4,64,1408]{3,2,1,0:T(8,128)(2,1)}, bf16[4,4,64,1408]{3,2,1,0:T(8,128)(2,1)}, u32[]{:S(2)}, u32[]{:S(2)}) collective-permute-start(bf16[4,4,64,1408]{3,2,1,0:T(8,128)(2,1)} %get-tuple-element.415), channel_id=1, source_target_pairs={{0,4},{4,0},{1,5},{5,1},{2,6},{6,2},{3,7},{7,3},{8,12},{12,8},{9,1... | collective-permute-start | bytes 8650760 | tf_op jit(solution)/shard_map/ppermute | solution.py:67
  360.8 171.5 %reduce-scatter.11.cloned.1.call-start = ((), (), s32[]{:S(2)}) async-start(), calls=%async_computation.10 | async-start | bytes 3604480 | tf_op jit(solution)/shard_map/reduce_scatter | solution.py:199
  363.1 23.1 %collective-permute-start.47 = (bf16[128,2048]{1,0:T(8,128)(2,1)}, bf16[128,2048]{1,0:T(8,128)(2,1)S(1)}, u32[]{:S(2)}, u32[]{:S(2)}) collective-permute-start(bf16[128,2048]{1,0:T(8,128)(2,1)} %get-tuple-element.421), channel_id=1, source_target_pairs={{0,8},{8,0},{16,24},{24,16},{1,9},{9,1},{17,25},{25,17},{2,10},{10... | collective-permute-start | bytes 1572872 | tf_op jit(solution)/shard_map/ppermute | solution.py:72
  364.8 22.9 %collective-permute-start.48 = (bf16[128,2048]{1,0:T(8,128)(2,1)}, bf16[128,2048]{1,0:T(8,128)(2,1)S(1)}, u32[]{:S(2)}, u32[]{:S(2)}) collective-permute-start(bf16[128,2048]{1,0:T(8,128)(2,1)} %get-tuple-element.423), channel_id=1, source_target_pairs={{0,16},{8,24},{16,0},{24,8},{1,17},{9,25},{17,1},{25,9},{2,18},{10... | collective-permute-start | bytes 1572872 | tf_op jit(solution)/shard_map/ppermute | solution.py:72
  410.1 161.4 %reduce-scatter.13.cloned.1.call-start = ((), (), s32[]{:S(2)}) async-start(), calls=%async_computation.11 | async-start | bytes 2621440 | tf_op jit(solution)/shard_map/reduce_scatter | solution.py:199
  416.6 29.3 %collective-permute-start.53 = (bf16[128,2048]{1,0:T(8,128)(2,1)S(1)}, bf16[128,2048]{1,0:T(8,128)(2,1)S(1)}, u32[]{:S(2)}, u32[]{:S(2)}) collective-permute-start(bf16[128,2048]{1,0:T(8,128)(2,1)S(1)} %get-tuple-element.598.refs_1_), channel_id=1, source_target_pairs={{0,8},{8,0},{16,24},{24,16},{1,9},{9,1},{17,25},{25,17},{2,10},{10... | collective-permute-start | bytes 1572872 | tf_op jit(solution)/shard_map/ppermute | solution.py:72
  418.3 27.6 %collective-permute-start.54 = (bf16[128,2048]{1,0:T(8,128)(2,1)S(1)}, bf16[128,2048]{1,0:T(8,128)(2,1)S(1)}, u32[]{:S(2)}, u32[]{:S(2)}) collective-permute-start(bf16[128,2048]{1,0:T(8,128)(2,1)S(1)} %get-tuple-element.599.refs_0_), channel_id=1, source_target_pairs={{0,16},{8,24},{16,0},{24,8},{1,17},{9,25},{17,1},{25,9},{2,18},{10... | collective-permute-start | bytes 1572872 | tf_op jit(solution)/shard_map/ppermute | solution.py:72
  429.5 22.4 %collective-permute-start.56 = (bf16[128,2048]{1,0:T(8,128)(2,1)S(1)}, bf16[128,2048]{1,0:T(8,128)(2,1)S(1)}, u32[]{:S(2)}, u32[]{:S(2)}) collective-permute-start(bf16[128,2048]{1,0:T(8,128)(2,1)S(1)} %collective-permute-done.52.refs_2_), channel_id=1, source_target_pairs={{0,16},{8,24},{16,0},{24,8},{1,17},{9,25},{17,1},{25,9},{2,18},{10... | collective-permute-start | bytes 1572872 | tf_op jit(solution)/shard_map/ppermute | solution.py:72
  431.2 20.7 %collective-permute-start.57 = (bf16[128,2048]{1,0:T(8,128)(2,1)S(1)}, bf16[128,2048]{1,0:T(8,128)(2,1)S(1)}, u32[]{:S(2)}, u32[]{:S(2)}) collective-permute-start(bf16[128,2048]{1,0:T(8,128)(2,1)S(1)} %collective-permute-done.55.refs_5_), channel_id=1, source_target_pairs={{0,8},{8,0},{16,24},{24,16},{1,9},{9,1},{17,25},{25,17},{2,10},{10... | collective-permute-start | bytes 1572872 | tf_op jit(solution)/shard_map/ppermute | solution.py:72
  465.6 31.8 %collective-permute-start.59 = (bf16[128,2048]{1,0:T(8,128)(2,1)}, bf16[128,2048]{1,0:T(8,128)(2,1)}, u32[]{:S(2)}, u32[]{:S(2)}) collective-permute-start(bf16[128,2048]{1,0:T(8,128)(2,1)} %get-tuple-element.460), channel_id=1, source_target_pairs={{0,8},{8,0},{16,24},{24,16},{1,9},{9,1},{17,25},{25,17},{2,10},{10... | collective-permute-start | bytes 1572872 | tf_op jit(solution)/shard_map/ppermute | solution.py:72
  466.2 31.2 %collective-permute-start.60 = (bf16[128,2048]{1,0:T(8,128)(2,1)}, bf16[128,2048]{1,0:T(8,128)(2,1)S(1)}, u32[]{:S(2)}, u32[]{:S(2)}) collective-permute-start(bf16[128,2048]{1,0:T(8,128)(2,1)} %get-tuple-element.462), channel_id=1, source_target_pairs={{0,16},{8,24},{16,0},{24,8},{1,17},{9,25},{17,1},{25,9},{2,18},{10... | collective-permute-start | bytes 1572872 | tf_op jit(solution)/shard_map/ppermute | solution.py:72
  467.6 29.9 %collective-permute-start.61 = (bf16[128,2048]{1,0:T(8,128)(2,1)}, bf16[128,2048]{1,0:T(8,128)(2,1)S(1)}, u32[]{:S(2)}, u32[]{:S(2)}) collective-permute-start(bf16[128,2048]{1,0:T(8,128)(2,1)} %get-tuple-element.464), channel_id=1, source_target_pairs={{0,8},{8,0},{16,24},{24,16},{1,9},{9,1},{17,25},{25,17},{2,10},{10... | collective-permute-start | bytes 1572872 | tf_op jit(solution)/shard_map/ppermute | solution.py:72
  468.2 29.2 %collective-permute-start.62 = (bf16[128,2048]{1,0:T(8,128)(2,1)}, bf16[128,2048]{1,0:T(8,128)(2,1)S(1)}, u32[]{:S(2)}, u32[]{:S(2)}) collective-permute-start(bf16[128,2048]{1,0:T(8,128)(2,1)} %get-tuple-element.466), channel_id=1, source_target_pairs={{0,16},{8,24},{16,0},{24,8},{1,17},{9,25},{17,1},{25,9},{2,18},{10... | collective-permute-start | bytes 1572872 | tf_op jit(solution)/shard_map/ppermute | solution.py:72
  499.9 23.2 %collective-permute-start.67 = (bf16[128,2048]{1,0:T(8,128)(2,1)}, bf16[128,2048]{1,0:T(8,128)(2,1)}, u32[]{:S(2)}, u32[]{:S(2)}) collective-permute-start(bf16[128,2048]{1,0:T(8,128)(2,1)} %add_convert_fusion.9), channel_id=1, source_target_pairs={{0,16},{8,24},{16,0},{24,8},{1,17},{9,25},{17,1},{25,9},{2,18},{10... | collective-permute-start | bytes 1572872 | tf_op jit(solution)/shard_map/ppermute | solution.py:72
  501.4 24.7 %collective-permute-start.68 = (bf16[128,2048]{1,0:T(8,128)(2,1)}, bf16[128,2048]{1,0:T(8,128)(2,1)}, u32[]{:S(2)}, u32[]{:S(2)}) collective-permute-start(bf16[128,2048]{1,0:T(8,128)(2,1)} %add_convert_fusion.8), channel_id=1, source_target_pairs={{0,8},{8,0},{16,24},{24,16},{1,9},{9,1},{17,25},{25,17},{2,10},{10... | collective-permute-start | bytes 1572872 | tf_op jit(solution)/shard_map/ppermute | solution.py:72
  513.2 18.3 %collective-permute-start.65 = (bf16[512,384]{1,0:T(8,128)(2,1)S(1)}, bf16[512,384]{1,0:T(8,128)(2,1)}, u32[]{:S(2)}, u32[]{:S(2)}) collective-permute-start(bf16[512,384]{1,0:T(8,128)(2,1)S(1)} %get-tuple-element.483), channel_id=1, source_target_pairs={{0,8},{8,0},{16,24},{24,16},{1,9},{9,1},{17,25},{25,17},{2,10},{10... | collective-permute-start | bytes 1179656 | tf_op jit(solution)/shard_map/ppermute | solution.py:72
  522.8 89.3 %reduce-scatter.15.cloned.1.call-start = ((), (), s32[]{:S(2)}) async-start(), calls=%async_computation.12 | async-start | bytes 1310720 | tf_op jit(solution)/shard_map/reduce_scatter | solution.py:199
  537.8 42.9 %collective-permute-start.69 = (bf16[128,2048]{1,0:T(8,128)(2,1)}, bf16[128,2048]{1,0:T(8,128)(2,1)}, u32[]{:S(2)}, u32[]{:S(2)}) collective-permute-start(bf16[128,2048]{1,0:T(8,128)(2,1)} %get-tuple-element.593), channel_id=1, source_target_pairs={{0,4},{4,0},{1,5},{5,1},{2,6},{6,2},{3,7},{7,3},{8,12},{12,8},{9,1... | collective-permute-start | bytes 1572872 | tf_op jit(solution)/shard_map/ppermute | solution.py:67
  556.4 77.3 %reduce-scatter.17.cloned.1.call-start = ((), (), s32[]{:S(2)}) async-start(), calls=%async_computation.13 | async-start | bytes 983040 | tf_op jit(solution)/shard_map/reduce_scatter | solution.py:199
  578.8 33.3 %collective-permute-start.76 = (bf16[128,2048]{1,0:T(8,128)(2,1)}, bf16[128,2048]{1,0:T(8,128)(2,1)}, u32[]{:S(2)}, u32[]{:S(2)}) collective-permute-start(bf16[128,2048]{1,0:T(8,128)(2,1)} %get-tuple-element.520), channel_id=1, source_target_pairs={{0,8},{8,0},{16,24},{24,16},{1,9},{9,1},{17,25},{25,17},{2,10},{10... | collective-permute-start | bytes 1572872 | tf_op jit(solution)/shard_map/ppermute | solution.py:72
  579.5 32.7 %collective-permute-start.77 = (bf16[128,2048]{1,0:T(8,128)(2,1)}, bf16[128,2048]{1,0:T(8,128)(2,1)}, u32[]{:S(2)}, u32[]{:S(2)}) collective-permute-start(bf16[128,2048]{1,0:T(8,128)(2,1)} %get-tuple-element.522), channel_id=1, source_target_pairs={{0,16},{8,24},{16,0},{24,8},{1,17},{9,25},{17,1},{25,9},{2,18},{10... | collective-permute-start | bytes 1572872 | tf_op jit(solution)/shard_map/ppermute | solution.py:72
  580.6 31.5 %collective-permute-start.78 = (bf16[128,2048]{1,0:T(8,128)(2,1)}, bf16[128,2048]{1,0:T(8,128)(2,1)}, u32[]{:S(2)}, u32[]{:S(2)}) collective-permute-start(bf16[128,2048]{1,0:T(8,128)(2,1)} %get-tuple-element.524), channel_id=1, source_target_pairs={{0,8},{8,0},{16,24},{24,16},{1,9},{9,1},{17,25},{25,17},{2,10},{10... | collective-permute-start | bytes 1572872 | tf_op jit(solution)/shard_map/ppermute | solution.py:72
  581.6 30.6 %collective-permute-start.79 = (bf16[128,2048]{1,0:T(8,128)(2,1)}, bf16[128,2048]{1,0:T(8,128)(2,1)}, u32[]{:S(2)}, u32[]{:S(2)}) collective-permute-start(bf16[128,2048]{1,0:T(8,128)(2,1)} %get-tuple-element.526), channel_id=1, source_target_pairs={{0,16},{8,24},{16,0},{24,8},{1,17},{9,25},{17,1},{25,9},{2,18},{10... | collective-permute-start | bytes 1572872 | tf_op jit(solution)/shard_map/ppermute | solution.py:72
  586.5 25.6 %collective-permute-start.82 = (bf16[64,2816]{1,0:T(8,128)(2,1)S(1)}, bf16[64,2816]{1,0:T(8,128)(2,1)S(1)}, u32[]{:S(2)}, u32[]{:S(2)}) collective-permute-start(bf16[64,2816]{1,0:T(8,128)(2,1)S(1)} %get-tuple-element.588), channel_id=1, source_target_pairs={{0,24},{8,16},{16,8},{24,0},{1,25},{9,17},{17,9},{25,1},{2,26},{10... | collective-permute-start | bytes 1081352 | tf_op jit(solution)/shard_map/ppermute | solution.py:72
  (156 other events, 1723.0 us)
Sparse Core Ops, SparseCore 0:
  9.7 49.8 all-gather.8
  61.3 26.7 all-gather.12
  90.2 28.6 all-gather.14
  120.9 107.5 all-gather.16
  230.0 58.6 all-gather.10
  320.3 55.1 reduce-scatter.6
  377.9 56.0 reduce-scatter.8
  436.3 56.0 reduce-scatter.10
  523.0 42.3 reduce-scatter.12
  568.2 26.4 reduce-scatter.14
  597.6 21.9 reduce-scatter.16

commit v4 on v3

--- a/solution.py
+++ b/solution.py
@@ -310,7 +310,7 @@
             jax.ShapeDtypeStruct((span, heads * head_width), bf16),
             jax.ShapeDtypeStruct((heads, 1, span), f32),
         ],
-        compiler_params=pltpu.CompilerParams(vmem_limit_bytes=48 << 20),
+        compiler_params=pltpu.CompilerParams(vmem_limit_bytes=62 << 20),
         cost_estimate=BESIDE,
     )(length, flip, rows, up, keys, values_t, cos_table, sin_table)
 
@@ -381,7 +381,7 @@
         ],
         out_specs=[head, whole(keys), whole(keys)],
         out_shape=[jax.ShapeDtypeStruct(queries.shape, bf16), summed, summed],
-        compiler_params=pltpu.CompilerParams(vmem_limit_bytes=48 << 20),
+        compiler_params=pltpu.CompilerParams(vmem_limit_bytes=62 << 20),
         cost_estimate=BESIDE,
     )(length, flip, queries, grads, total, keys, keys_t, values, cos_table, sin_table)
 
@@ -600,6 +600,45 @@
     )(chip_flip()[None], *lefts, weight)
 
 
+def whole_kernel(own, place_ref, *refs):
+    *left_refs, mine_ref, other_ref, out_ref = refs
+    chips = len(left_refs)
+    groups, width = mine_ref.shape[2], mine_ref.shape[4]
+    half = chips // CORES
+    total = 0.0
+    for k in range(chips):
+        block = pl.program_id(0) ^ k ^ place_ref[0]
+        mine = mine_ref[k, block % half, :, :own].reshape(groups * own, width)
+        other = other_ref[k, block % half, :, :own].reshape(groups * own, width)
+        weight = jnp.where(block // half == place_ref[1], mine, other)
+        total = total + outer_cols(left_refs[k][...], weight)
+    out_ref[...] = total
+
+
+def whole_products(lefts, mine, other, weights, own):
+    chips = len(lefts)
+    rows = lefts[0].shape[0]
+    if chips != 4:
+        every = lax.all_gather(weights[:, :, :own], "chip", axis=0)
+        return sum(
+            outer_cols(lefts[k], every[k].reshape(-1, every.shape[-1])) for k in range(chips)
+        )
+    depth = mine.shape[2] * own
+    whole = lambda array: pl.BlockSpec(array.shape, lambda i, p: (0,) * array.ndim)
+    return pl.pallas_call(
+        functools.partial(whole_kernel, own),
+        grid_spec=pltpu.PrefetchScalarGridSpec(
+            num_scalar_prefetch=1,
+            grid=(chips,),
+            in_specs=[whole(left) for left in lefts] + [whole(mine), whole(other)],
+            out_specs=pl.BlockSpec((rows, depth), lambda i, p: (0, i)),
+        ),
+        out_shape=jax.ShapeDtypeStruct((rows, chips * depth), f32),
+        compiler_params=pltpu.CompilerParams(vmem_limit_bytes=48 << 20),
+        cost_estimate=BESIDE,
+    )(jnp.stack([chip_flip(), lax.axis_index("core")]), *lefts, mine, other)
+
+
 def split_kernel(_, small_ref, qup_ref, gate_ref, up_ref, *out_refs):
     chips = len(out_refs) // 3
     own = gate_ref.shape[0]
@@ -645,7 +684,7 @@
 
 
 def normed_kernel(flip_ref, *refs):
-    *piece_refs, gain_ref, small_ref, normed_ref, raw_ref = refs
+    *piece_refs, gain_ref, small_ref, normed_ref, query_ref, pair_ref = refs
     per_step = len(piece_refs) // pl.num_programs(0)
     for k in range(pl.num_programs(0)):
 
@@ -663,16 +702,18 @@
                 weight = small_ref[place ^ flip_ref[0], :, :own].reshape(depth, width)
                 columns = normed[:, place * depth : (place + 1) * depth]
                 raw = raw + matmul(columns, weight)
-            raw_ref[...] = raw
-
-
-def normed_rows(pieces, gain, small, own):
+            split = query_ref.shape[1]
+            query_ref[...], pair_ref[...] = raw[:, :split], raw[:, split:]
+
+
+def normed_rows(pieces, gain, small, own, split):
     chips = lax.axis_size("chip")
     if chips != 4:
         rows = pieces[0].astype(f32)
         normed = (rows * rms_scale(rows) * gain).astype(bf16)
         small = small[:, :, :own].reshape(normed.shape[1], -1)
-        return normed, matmul(normed, small)
+        raw = matmul(normed, small)
+        return normed, raw[:, :split], raw[:, split:]
     half, width = pieces[0].shape
     whole = lambda array: pl.BlockSpec(array.shape, lambda k, f: (0,) * array.ndim)
     block = lambda size: pl.BlockSpec((2 * half, size), lambda k, f: (k ^ f[0], 0))
@@ -684,13 +725,14 @@
             num_scalar_prefetch=1,
             grid=(chips,),
             in_specs=[whole(piece) for piece in pieces] + [whole(gain), whole(small)],
-            out_specs=[block(width), block(small.shape[-1])],
+            out_specs=[block(width), block(split), block(small.shape[-1] - split)],
         ),
         out_shape=[
             jax.ShapeDtypeStruct((rows, width), bf16),
-            jax.ShapeDtypeStruct((rows, small.shape[-1]), f32),
+            jax.ShapeDtypeStruct((rows, split), f32),
+            jax.ShapeDtypeStruct((rows, small.shape[-1] - split), f32),
         ],
-        compiler_params=pltpu.CompilerParams(vmem_limit_bytes=48 << 20),
+        compiler_params=pltpu.CompilerParams(vmem_limit_bytes=62 << 20),
         cost_estimate=BESIDE,
     )(chip_flip()[None], *pieces, gain, small)
 
@@ -832,7 +874,7 @@
     small = gather_blocks(small)
     tokens_pieces, up_q, gate_up = tie(far_pieces(tokens_near), up_q, gate_up)
     up_q = gather_columns(up_q)
-    small, cotangent, gate_up = tie(small, cotangent, gate_up)
+    small, cotangent = tie(small, cotangent)
     seed_grad = (pair_in(cotangent[0]).astype(f32) * valid_mask).astype(bf16)
     gains = small[:, :, own_rows : own_rows + 3].astype(f32)
     gains = jnp.stack(reordered(list(gains), flip[0]))
@@ -841,19 +883,18 @@
     gain_q = gains[:, :, 2, :own_q].reshape(chips, -1)[chip]
     up_q = up_q.reshape(chips, q_cols, -1)
 
-    normed_all, raw = normed_rows(
-        tokens_pieces, gain_one, small, own_rows
-    )
-    raw, gate_up = tie(raw, exchange(gate_up))
+    normed_all, q_down, kv_raw = normed_rows(
+        tokens_pieces, gain_one, small, own_rows, q_cols
+    )
+    q_down, kv_raw, gate_up = tie(q_down, kv_raw, exchange(gate_up))
+    scale_q = lax.rsqrt(row_sums(q_down * q_down) / q_width + epsilon)
     gate_up = gather_blocks(gate_up)
     down_proj = gather_rows(w_down)
     gate_up = gate_up.reshape(chips, CORES * dp, 2, own_rows, -1)
-    q_down = raw[:, :q_cols]
-    scale_q = lax.rsqrt(row_sums(q_down * q_down) / q_width + epsilon)
     q_normed = (q_down * scale_q * gain_q).astype(bf16)
-    k_one, k_two = raw[:, q_cols : q_cols + k_cols], raw[:, q_cols + k_cols : q_cols + 2 * k_cols]
+    k_one, k_two = kv_raw[:, :k_cols], kv_raw[:, k_cols:v_cols]
     key_cols = [k_one * cos_own - k_two * sin_own, k_two * cos_own + k_one * sin_own]
-    shared = jnp.concatenate(key_cols + [raw[:, q_cols + v_cols :]], 1).astype(bf16)
+    shared = jnp.concatenate(key_cols + [kv_raw[:, v_cols:]], 1).astype(bf16)
     shared = gather_chips(jnp.concatenate([q_normed, shared], 1))
     shared, seed_tied = tie(shared, seed_grad)
     seed_near = gather_near(seed_tied)
@@ -878,7 +919,9 @@
     scale_two = rms_scale(middle)
     normed2 = gather_chips((middle * scale_two * gain_two).astype(bf16))
 
-    normed2, *seed_near = tie(normed2, *seed_near)
+    small_rows = small.reshape(CORES, -1, small_cols)
+    small_rows = take(small_rows, core) if chips == 4 else small_rows[0]
+    normed2, seed_near = tie(normed2, seed_near)
     activated, silu, slope = gated(normed2, gate_up)
     activated, seed_pieces = tie(activated, far_pieces(seed_near))
     seed_all = join_rows(seed_pieces)
@@ -886,16 +929,19 @@
     down_terms, down_proj = tie(down_terms, down_proj)
     down_half = sum_cores(*down_terms)
     gate_grad, up_grad = gated_back(seed_all, down_proj, silu, slope)
-    gate_grad, up_grad, down_half = tie(gate_grad, up_grad, down_half)
+    gate_grad, up_grad, down_half, small_rows = tie(gate_grad, up_grad, down_half, small_rows)
+    small_near = gather_near(small_rows) if chips == 4 else (small_rows,)
     grad_w_down = scatter_dp(down_half)
+    part, gate_grad, up_grad = tie(
+        spread([gate_grad, up_grad], gate_up, own_rows), gate_grad, up_grad
+    )
     gate_part = weight_terms(normed2, gate_grad, grad_scale, flip[0])
-    gate_tied, up_tied, gate_part = tie(gate_grad, up_grad, gate_part)
-    part = spread([gate_tied, up_tied], gate_up, own_rows)
-    part, up_grad, gate_half = tie(part, up_grad, sum_cores(*gate_part))
+    up_part = weight_terms(normed2, up_grad, grad_scale, flip[0])
+    part, small_near = tie(part, small_near)
+    near, gate_part, up_part = tie(scatter_near(part), gate_part, up_part)
+    near, gate_half = tie(near, sum_cores(*gate_part))
     grad_w_gate = scatter_dp(gate_half)
-    up_part = weight_terms(normed2, up_grad, grad_scale, flip[0])
-    grad_normed2, up_part = scatter_chips(part, (up_part,))
-    up_half = sum_cores(*up_part)
+    grad_normed2, up_half = scatter_far(near), sum_cores(*up_part)
     grad_normed2, grad_w_down, up_half = tie(grad_normed2, grad_w_down, up_half)
     grad_w_up = scatter_dp(up_half)
     grad_middle = seed_grad.astype(f32) + norm_back(grad_normed2, middle, scale_two, gain_two)
@@ -907,17 +953,22 @@
     out_near = scatter_near(out_part)
     out_terms = weight_terms(mixed, grad_branch, grad_scale)
     out_terms, grad_branch, grad_w_gate = tie(out_terms, grad_branch, grad_w_gate)
-    grad_mixed, out_half = tie(product("nt", grad_branch, out_proj), sum_cores(*out_terms))
+    grad_mixed, out_half, small_near = tie(
+        product("nt", grad_branch, out_proj), sum_cores(*out_terms), small_near
+    )
+    small_pieces = far_pieces(small_near) if chips == 4 else list(small_near)
     grad_w_out = scatter_dp(out_half)
     grad_q, grad_k, grad_v = attend_back(
         length[None], flip, queries, grad_mixed, log_total, keys, values, cos_all, sin_all, score_scale
     )
-    grad_q, out_near = tie(grad_q, out_near)
+    grad_q, out_near, small_pieces = tie(grad_q, out_near, small_pieces)
     output = middle + scatter_far(out_near)
     back, grad_q = tie(back_terms(grad_q, up_q, grad_k, grad_v, place), grad_q)
     qup_part = weight_terms(q_rows, grad_q, grad_scale, jnp.int32(0))
-    back, qup_part, grad_w_up, output = scatter_chips(back, (qup_part, grad_w_up, output))
-    back, qup_half = tie(back, sum_cores(*qup_part))
+    back, qup_part, grad_w_up, output, small_pieces = scatter_chips(
+        back, (qup_part, grad_w_up, output, small_pieces)
+    )
+    back, qup_half, grad_w_out = tie(back, sum_cores(*qup_part), grad_w_out)
     grad_w_qup = scatter_dp(qup_half)
     weighted = back[:, :q_cols] * gain_q
     mean = row_sums(weighted * q_down) / q_width
@@ -935,13 +986,19 @@
         ],
         1,
     ).astype(bf16)
-    small_half = sum_cores(*weight_terms(normed_all, back, grad_scale, flip[0]))
-    back, small_half, grad_w_out = tie(back, small_half, grad_w_out)
+    small_mine = join_rows(small_pieces)
+    small_other = swap_cores(small_mine)
+    back_parts = exchange(reordered(jnp.split(back, chips, 0), flip[0]))
+    small_part = weight_terms(normed_all, back, grad_scale, flip[0])
+    back_parts, small_part, small_pair = tie(back_parts, small_part, (small_mine, small_other))
+    small_half = sum_cores(*small_part)
     grad_small = scatter_dp(small_half)
-    terms = spread([back], small[:, :, None], own_rows, flip_rows=True)
-    grad_normed, pair, grad_w_qup = scatter_chips(terms, (pair, grad_w_qup))
-    grad_w_qup = trade_blocks(grad_w_qup)
-    grad_normed, grad_small = tie(grad_normed, grad_small)
+    if chips == 4:
+        shape = (chips, -1, CORES * dp, small.shape[2], small_cols)
+        small_pair = [array.reshape(shape) for array in small_pair]
+    grad_normed = whole_products(back_parts, *small_pair, small, own_rows)
+    grad_normed, grad_w_qup = tie(grad_normed, grad_w_qup)
+    grad_w_qup, pair = tie(trade_blocks(grad_w_qup), pair)
     out_tokens = pair_out(output.astype(bf16))[None]
     grad_inputs = grad_middle + norm_back(grad_normed, inputs, rms_scale(inputs), gain_one)
     grad_tokens = pair_out(grad_inputs)[None]

time: 665 us -> 643 us (0.967)
  waiting for transfers between devices: 204 us -> 180 us
  Pallas kernels: 212 us -> 220 us
    ppermute x82 -> x85, waiting for transfers between devices: 195 us -> 163 us  [to_chip(): return lax.ppermute(block, 'chip', [(i, i ^ bits) for i in range(count)])]
    unnamed x205 -> x249, local copies, waits for them, and re-layouts: 25.8 us -> 16.2 us
    pallas_call x2 -> x1, Pallas kernels: 28.6 us -> 21.1 us  [spread(): pl.pallas_call(functools.partial(spread_kernel, flip_rows, len(lefts), ow...]
    pallas_call x0 -> x1, Pallas kernels: none -> 7.16 us  [whole_products(): pl.pallas_call(functools.partial(whole_kernel, own), grid_spec=pltpu.Pref...]
    ppermute x82 -> x85, starting transfers between devices: 91.4 us -> 93.6 us  [to_chip(): return lax.ppermute(block, 'chip', [(i, i ^ bits) for i in range(count)])]
  transfers between devices with their start and end apart: 103 -> 107, of which waited for: 46 -> 48; matrix products, arithmetic and copies ran while one was open for 15% -> 16% of each run, Pallas kernels for 32% -> 35%
where the time goes in v4:
time: 643 us; the launch traced here: 634 us
  Pallas kernels  220 us (34%)
  waiting for transfers between devices  180 us (28%)
  starting transfers between devices  96.4 us (15%)
  other arithmetic  84.4 us (13%)
  local copies, waits for them, and re-layouts  35.5 us (6%)
  between operations  16 us (2%)
    ppermute x85, waiting for transfers between devices, to_chip(): return lax.ppermute(block, 'chip', [(i, i ^ bits) for i in range(count)])  163 us
    ppermute x85, starting transfers between devices, to_chip(): return lax.ppermute(block, 'chip', [(i, i ^ bits) for i in range(count)])  93.6 us
    pallas_call x5, Pallas kernels, weight_terms(): pl.pallas_call(functools.partial(terms_kernel, scale), grid_spec=pltpu.Pr...  55.9 us
    pallas_call x3, Pallas kernels, product(): pl.pallas_call(functools.partial(product_kernel, kind, pieces), grid=(row...  31.1 us
    pallas_call x1, Pallas kernels, spread(): pl.pallas_call(functools.partial(spread_kernel, flip_rows, len(lefts), ow...  21.1 us
    pallas_call x1, Pallas kernels, attend(): pl.pallas_call(functools.partial(attend_kernel, score_scale), grid=(heads...  18.8 us
    pallas_call x1, Pallas kernels, gated(): pl.pallas_call(gate_kernel, grid_spec=pltpu.PrefetchScalarGridSpec(num_sc...  18.4 us
    convert_element_type x6, other arithmetic, sum_cores(): return add(own, swap_cores(other)).astype(bf16)  16.6 us
  transfers between devices with their start and end apart: 107, of which 48 were waited for; matrix products, arithmetic and copies ran while one was open for 16% of the time, Pallas kernels for 35%

profile of v4, /device:TPU:0, one launch (start us, length us, event | category | flops | bytes accessed | tf_op | source)
XLA Modules:
  0.0 633.8 jit_solution(2193075805520995793)
XLA Ops:
  11.2 3.8 shard_map.237
  17.1 2.5 collective-permute-start.4
  25.6 19.4 %collective-permute-done.1 = bf16[80,384]{1,0:T(8,128)(2,1)S(1)} collective-permute-done((bf16[80,384]{1,0:T(8,128)(2,1)S(1)}, bf16[80,384]{1,0:T(8,128)(2,1)S(1)}, u32[]{:S(2)}, u32[]{:S(2)}) %collective-permute-start.1) | collective-permute-done | bytes 61472 | tf_op jit(solution)/shard_map/ppermute | solution.py:72
  49.2 2.7 collective-permute-start.3
  54.3 5.3 all-gather.9.cloned.1.call-done.right_ref
  63.4 11.3 %collective-permute-done.8.refs_6_ = bf16[128,2048]{1,0:T(8,128)(2,1)S(1)} collective-permute-done((bf16[128,2048]{1,0:T(8,128)(2,1)}, bf16[128,2048]{1,0:T(8,128)(2,1)S(1)}, u32[]{:S(2)}, u32[]{:S(2)}) %collective-permute-start.8) | collective-permute-done | bytes 524320 | tf_op jit(solution)/shard_map/ppermute | solution.py:72
  91.5 8.2 %shard_map.238 = (bf16[1024,2048]{1,0:T(8,128)(2,1)}, f32[1024,256]{1,0:T(8,128)}, f32[1024,128]{1,0:T(8,128)}) custom-call(s32[1]{0:T(128)} %bitcast.1._.flip_ref, bf16[128,2048]{1,0:T(8,128)(2,1)} %get-tuple-element.338.refs_0_, bf16[128,2048]{1,0:T(8,128)(2,1)} %copy-done.55, bf16[128,2048]{1,0:T(8,128)(2,1)} %collective-permute-done.4.refs_2_, ...), custom_call_target="tpu_custom_call" | custom-call | flops 1 | bytes 1 | tf_op jit(solution)/shard_map/pallas_call | solution.py:722
  101.4 2.6 pad_maximum_fusion.2
  122.5 7.2 %collective-permute-done.15.refs_2_ = bf16[512,384]{1,0:T(8,128)(2,1)S(1)} collective-permute-done((bf16[512,384]{1,0:T(8,128)(2,1)S(1)}, bf16[512,384]{1,0:T(8,128)(2,1)S(1)}, u32[]{:S(2)}, u32[]{:S(2)}) %collective-permute-start.15) | collective-permute-done | bytes 393248 | tf_op jit(solution)/shard_map/ppermute | solution.py:72
  133.7 4.5 collective-permute-done.16.refs_3_
  139.0 6.1 collective-permute-done.19.refs_6_
  153.1 18.8 %shard_map.240 = (bf16[1024,1024]{1,0:T(8,128)(2,1)}, bf16[1024,1024]{1,0:T(8,128)(2,1)}, f32[4,1,1024]{2,1,0:T(1,128)}) custom-call(s32[1]{0:T(128)} %bitcast.length_ref, s32[1]{0:T(128)} %bitcast.1._.flip_ref, bf16[4,1024,384]{2,1,0:T(8,128)(2,1)} %bitcast.147, bf16[4,256,1024]{2,1,0:T(8,128)(2,1)} %all-gather.15.cloned.1.call-done.up_ref, ...), custom_call_target="tpu_custom_call" | custom-call | flops 1 | bytes 1 | tf_op jit(solution)/shard_map/pallas_call | solution.py:290
  171.9 9.9 %shard_map.241 = (bf16[128,2048]{1,0:T(8,128)(2,1)}, bf16[128,2048]{1,0:T(8,128)(2,1)}, bf16[128,2048]{1,0:T(8,128)(2,1)}, bf16[128,2048]{1,0:T(8,128)(2,1)}, bf...) custom-call(bf16[1024,1024]{1,0:T(8,128)(2,1)} %get-tuple-element.37, ...), custom_call_target="tpu_custom_call" | custom-call | flops 1 | bytes 1 | tf_op jit(solution)/shard_map/pallas_call | solution.py:427
  185.9 11.0 %collective-permute-done.29 = bf16[128,2048]{1,0:T(8,128)(2,1)S(1)} collective-permute-done((bf16[128,2048]{1,0:T(8,128)(2,1)}, bf16[128,2048]{1,0:T(8,128)(2,1)S(1)}, u32[]{:S(2)}, u32[]{:S(2)}) %collective-permute-start.29) | collective-permute-done | bytes 524320 | tf_op jit(solution)/shard_map/ppermute | solution.py:72
  198.1 6.0 collective-permute-done.31
  211.6 5.6 collective-permute-done.33
  227.1 10.8 %collective-permute-done.35.refs_2_ = bf16[128,2048]{1,0:T(8,128)(2,1)S(1)} collective-permute-done((bf16[128,2048]{1,0:T(8,128)(2,1)S(1)}, bf16[128,2048]{1,0:T(8,128)(2,1)S(1)}, u32[]{:S(2)}, u32[]{:S(2)}) %collective-permute-start.35) | collective-permute-done | bytes 524320 | tf_op jit(solution)/shard_map/ppermute | solution.py:72
  239.9 8.3 %collective-permute-done.36.refs_3_ = bf16[128,2048]{1,0:T(8,128)(2,1)S(1)} collective-permute-done((bf16[128,2048]{1,0:T(8,128)(2,1)S(1)}, bf16[128,2048]{1,0:T(8,128)(2,1)S(1)}, u32[]{:S(2)}, u32[]{:S(2)}) %collective-permute-start.36) | collective-permute-done | bytes 524320 | tf_op jit(solution)/shard_map/ppermute | solution.py:72
  249.1 7.0 %collective-permute-done.39.refs_6_ = bf16[128,2048]{1,0:T(8,128)(2,1)S(1)} collective-permute-done((bf16[128,2048]{1,0:T(8,128)(2,1)S(1)}, bf16[128,2048]{1,0:T(8,128)(2,1)S(1)}, u32[]{:S(2)}, u32[]{:S(2)}) %collective-permute-start.39) | collective-permute-done | bytes 524320 | tf_op jit(solution)/shard_map/ppermute | solution.py:72
  261.1 18.4 %shard_map.243 = (bf16[1024,1408]{1,0:T(8,128)(2,1)S(1)}, bf16[1024,1408]{1,0:T(8,128)(2,1)S(1)}, bf16[1024,1408]{1,0:T(8,128)(2,1)}) custom-call(s32[1]{0:T(128)} %bitcast.1._.flip_ref, bf16[1024,2048]{1,0:T(8,128)(2,1)} %copy-done.2, bf16[4,8,2,64,1408]{4,3,2,1,0:T(8,128)(2,1)} %bitcast.149), custom_call_target="tpu_custom_call" | custom-call | flops 1 | bytes 1 | tf_op jit(solution)/shard_map/pallas_call | solution.py:767
  286.8 11.3 %shard_map.245 = (bf16[704,2048]{1,0:T(8,128)(2,1)}, bf16[704,2048]{1,0:T(8,128)(2,1)}) custom-call(s32[2]{0:T(128)} %pad_add_fusion.place_ref, bf16[1024,1408]{1,0:T(8,128)(2,1)} %copy-done.9, bf16[1024,2048]{1,0:T(8,128)(2,1)} %copy-done.4), custom_call_target="tpu_custom_call" | custom-call | flops 1 | bytes 1 | tf_op jit(solution)/shard_map/pallas_call | solution.py:509
  298.2 11.6 %shard_map.246 = (bf16[1024,1408]{1,0:T(8,128)(2,1)S(1)}, bf16[1024,1408]{1,0:T(8,128)(2,1)S(1)}) custom-call(bf16[1024,2048]{1,0:T(8,128)(2,1)} %copy-done.4, bf16[1408,2048]{1,0:T(8,128)(2,1)} %all-gather.11.cloned.1.call-done.down_ref.right_ref, bf16[1024,1408]{1,0:T(8,128)(2,1)} %copy-done.10, bf16[1024,1408]{1,0:T(8,128)(2,1)} %get-tuple-element.428.slope_ref), custom_call_target="tpu_custom_call" | custom-call | flops 1 | bytes 1 | tf_op jit(solution)/shard_map/pallas_call | solution.py:796
  309.9 3.4 add_convert_fusion.2
  317.7 21.1 %shard_map.247 = (bf16[128,2048]{1,0:T(8,128)(2,1)}, bf16[128,2048]{1,0:T(8,128)(2,1)}, bf16[128,2048]{1,0:T(8,128)(2,1)}, bf16[128,2048]{1,0:T(8,128)(2,1)}, bf...) custom-call(s32[1]{0:T(128)} %bitcast.1._.flip_ref, ...), custom_call_target="tpu_custom_call" | custom-call | flops 1 | bytes 1 | tf_op jit(solution)/shard_map/pallas_call | solution.py:588
  344.0 13.6 %shard_map.249 = (bf16[4,4,64,1408]{3,2,1,0:T(8,128)(2,1)}, bf16[4,4,64,1408]{3,2,1,0:T(8,128)(2,1)}) custom-call(s32[2]{0:T(128)} %pad_add_fusion.1.place_ref, bf16[1024,2048]{1,0:T(8,128)(2,1)} %copy-done.2, bf16[1024,1408]{1,0:T(8,128)(2,1)} %copy-done.8), custom_call_target="tpu_custom_call" | custom-call | flops 1 | bytes 1 | tf_op jit(solution)/shard_map/pallas_call | solution.py:492
  357.6 13.5 %shard_map.248 = (bf16[4,4,64,1408]{3,2,1,0:T(8,128)(2,1)}, bf16[4,4,64,1408]{3,2,1,0:T(8,128)(2,1)}) custom-call(s32[2]{0:T(128)} %pad_add_fusion.1.place_ref, bf16[1024,2048]{1,0:T(8,128)(2,1)} %copy-done.2, bf16[1024,1408]{1,0:T(8,128)(2,1)} %copy-done.7), custom_call_target="tpu_custom_call" | custom-call | flops 1 | bytes 1 | tf_op jit(solution)/shard_map/pallas_call | solution.py:492
  371.2 5.5 collective-permute-done.52
  376.7 4.1 add_convert_fusion.1
  386.9 2.6 add_convert_fusion
  389.5 7.8 %collective-permute-done.53 = bf16[128,2048]{1,0:T(8,128)(2,1)S(1)} collective-permute-done((bf16[128,2048]{1,0:T(8,128)(2,1)S(1)}, bf16[128,2048]{1,0:T(8,128)(2,1)S(1)}, u32[]{:S(2)}, u32[]{:S(2)}) %collective-permute-start.53) | collective-permute-done | bytes 524320 | tf_op jit(solution)/shard_map/ppermute | solution.py:72
  402.3 3.5 fusion
  412.6 10.8 %collective-permute-done.56.refs_2_ = bf16[128,2048]{1,0:T(8,128)(2,1)S(1)} collective-permute-done((bf16[128,2048]{1,0:T(8,128)(2,1)S(1)}, bf16[128,2048]{1,0:T(8,128)(2,1)S(1)}, u32[]{:S(2)}, u32[]{:S(2)}) %collective-permute-start.56) | collective-permute-done | bytes 524320 | tf_op jit(solution)/shard_map/ppermute | solution.py:72
  427.1 12.6 %shard_map.251 = (bf16[128,2048]{1,0:T(8,128)(2,1)}, bf16[128,2048]{1,0:T(8,128)(2,1)}, bf16[128,2048]{1,0:T(8,128)(2,1)}, bf16[128,2048]{1,0:T(8,128)(2,1)}, bf...) custom-call(bf16[1024,1408]{1,0:T(8,128)(2,1)} %copy-done.9, ...), custom_call_target="tpu_custom_call" | custom-call | flops 1 | bytes 1 | tf_op jit(solution)/shard_map/pallas_call | solution.py:427
  439.8 5.1 collective-permute-done.60.refs_6_
  447.4 10.5 %shard_map.252 = (bf16[512,2048]{1,0:T(8,128)(2,1)}, bf16[512,2048]{1,0:T(8,128)(2,1)}) custom-call(s32[2]{0:T(128)} %pad_add_fusion.place_ref, bf16[1024,1024]{1,0:T(8,128)(2,1)} %get-tuple-element.370.left_ref, bf16[1024,2048]{1,0:T(8,128)(2,1)} %copy-done.3), custom_call_target="tpu_custom_call" | custom-call | flops 1 | bytes 1 | tf_op jit(solution)/shard_map/pallas_call | solution.py:492
  463.2 8.7 %shard_map.253.grad_ref = bf16[1024,1024]{1,0:T(8,128)(2,1)} custom-call(bf16[1024,2048]{1,0:T(8,128)(2,1)} %copy-done.3, bf16[1024,2048]{1,0:T(8,128)(2,1)} %all-gather.9.cloned.1.call-done.right_ref), custom_call_target="tpu_custom_call" | custom-call | flops 1 | bytes 1 | tf_op jit(solution)/shard_map/pallas_call | solution.py:427
  471.9 4.0 add_convert_fusion.3
  479.2 16.4 %shard_map.254 = (bf16[1024,1024]{1,0:T(8,128)(2,1)}, f32[1024,256]{1,0:T(8,128)}, f32[1024,256]{1,0:T(8,128)}) custom-call(s32[1]{0:T(128)} %bitcast.length_ref, s32[1]{0:T(128)} %bitcast.1._.flip_ref, bf16[1024,1024]{1,0:T(8,128)(2,1)} %get-tuple-element.369.queries_ref, bf16[1024,1024]{1,0:T(8,128)(2,1)} %shard_map.253.grad_ref, ...), custom_call_target="tpu_custom_call" | custom-call | flops 1 | bytes 1 | tf_op jit(solution)/shard_map/pallas_call | solution.py:367
  501.4 7.6 %shard_map.255 = (bf16[512,384]{1,0:T(8,128)(2,1)S(1)}, bf16[512,384]{1,0:T(8,128)(2,1)S(1)}, bf16[512,384]{1,0:T(8,128)(2,1)}, bf16[512,384]{1,0:T(8,128)(2,1)S...) custom-call(bf16[1024,1024]{1,0:T(8,128)(2,1)} %get-tuple-element.54, ...), custom_call_target="tpu_custom_call" | custom-call | flops 1 | bytes 1 | tf_op jit(solution)/shard_map/pallas_call | solution.py:551
  514.8 9.2 %shard_map.256 = (bf16[4,4,32,1024]{3,2,1,0:T(8,128)(2,1)}, bf16[4,4,32,1024]{3,2,1,0:T(8,128)(2,1)}) custom-call(s32[2]{0:T(128)} %pad_add_fusion.place_ref, bf16[1024,1024]{1,0:T(8,128)(2,1)} %bitcast.156, bf16[1024,1024]{1,0:T(8,128)(2,1)} %get-tuple-element.548.grad_ref.right_ref), custom_call_target="tpu_custom_call" | custom-call | flops 1 | bytes 1 | tf_op jit(solution)/shard_map/pallas_call | solution.py:492
  529.8 3.4 collective-permute-done.72
  533.2 5.1 shard_map.258
  542.9 8.2 %collective-permute-done.76 = bf16[512,384]{1,0:T(8,128)(2,1)S(1)} collective-permute-done((bf16[512,384]{1,0:T(8,128)(2,1)S(1)}, bf16[512,384]{1,0:T(8,128)(2,1)S(1)}, u32[]{:S(2)}, u32[]{:S(2)}) %collective-permute-start.76) | collective-permute-done | bytes 393248 | tf_op jit(solution)/shard_map/ppermute | solution.py:72
  569.4 9.0 %shard_map.257 = (bf16[4,4,64,384]{3,2,1,0:T(8,128)(2,1)}, bf16[4,4,64,384]{3,2,1,0:T(8,128)(2,1)}) custom-call(s32[2]{0:T(128)} %pad_add_fusion.1.place_ref, bf16[1024,2048]{1,0:T(8,128)(2,1)} %get-tuple-element.584.left_ref, bf16[1024,384]{1,0:T(8,128)(2,1)} %copy-done.41), custom_call_target="tpu_custom_call" | custom-call | flops 1 | bytes 1 | tf_op jit(solution)/shard_map/pallas_call | solution.py:492
  584.2 7.2 %shard_map.259 = f32[256,2048]{1,0:T(8,128)S(1)} custom-call(s32[2]{0:T(128)S(1)} %copy-done.23, bf16[256,384]{1,0:T(8,128)(2,1)S(1)} %get-tuple-element.595.refs_0_, bf16[256,384]{1,0:T(8,128)(2,1)S(1)} %collective-permute-done.81.refs_1_, bf16[256,384]{1,0:T(8,128)(2,1)S(1)} %collective-permute-done.82.refs_2_, ...), custom_call_target="tpu_custom_call" | custom-call | flops 1 | bytes 1 | tf_op jit(solution)/shard_map/pallas_call | solution.py:628
  601.4 2.7 collective-permute-done.92
  611.9 4.0 reduce-scatter.17.cloned.1.call-done
  617.0 2.4 collective-permute-start.87
  (586 shorter events, 223.7 us)
Async XLA Ops:
  7.3 52.3 %all-gather.9.cloned.1.call-start = ((), (), s32[]{:S(2)}) async-start(), calls=%async_computation.6 | async-start | bytes 4718592 | tf_op jit(solution)/shard_map/all_gather | solution.py:190
  8.0 80.5 %all-gather.13.cloned.1.call-start = ((), (), s32[]{:S(2)}) async-start(), calls=%async_computation.14 | async-start | bytes 2211840 | tf_op jit(solution)/shard_map/all_gather | solution.py:182
  17.1 37.2 %collective-permute-start.4 = (bf16[128,2048]{1,0:T(8,128)(2,1)}, bf16[128,2048]{1,0:T(8,128)(2,1)}, u32[]{:S(2)}, u32[]{:S(2)}) collective-permute-start(bf16[128,2048]{1,0:T(8,128)(2,1)} %get-tuple-element.338.refs_0_), channel_id=1, source_target_pairs={{0,8},{8,0},{16,24},{24,16},{1,9},{9,1},{17,25},{25,17},{2,10},{10... | collective-permute-start | bytes 1572872 | tf_op jit(solution)/shard_map/ppermute | solution.py:72
  19.6 34.7 %collective-permute-start.6 = (bf16[128,2048]{1,0:T(8,128)(2,1)}, bf16[128,2048]{1,0:T(8,128)(2,1)}, u32[]{:S(2)}, u32[]{:S(2)}) collective-permute-start(bf16[128,2048]{1,0:T(8,128)(2,1)} %get-tuple-element.338.refs_0_), channel_id=1, source_target_pairs={{0,16},{8,24},{16,0},{24,8},{1,17},{9,25},{17,1},{25,9},{2,18},{10... | collective-permute-start | bytes 1572872 | tf_op jit(solution)/shard_map/ppermute | solution.py:72
  21.1 33.2 %collective-permute-start.5 = (bf16[128,2048]{1,0:T(8,128)(2,1)S(1)}, bf16[128,2048]{1,0:T(8,128)(2,1)}, u32[]{:S(2)}, u32[]{:S(2)}) collective-permute-start(bf16[128,2048]{1,0:T(8,128)(2,1)S(1)} %get-tuple-element.339.refs_1_), channel_id=1, source_target_pairs={{0,8},{8,0},{16,24},{24,16},{1,9},{9,1},{17,25},{25,17},{2,10},{10... | collective-permute-start | bytes 1572872 | tf_op jit(solution)/shard_map/ppermute | solution.py:72
  21.7 32.6 %collective-permute-start.7 = (bf16[128,2048]{1,0:T(8,128)(2,1)S(1)}, bf16[128,2048]{1,0:T(8,128)(2,1)}, u32[]{:S(2)}, u32[]{:S(2)}) collective-permute-start(bf16[128,2048]{1,0:T(8,128)(2,1)S(1)} %get-tuple-element.339.refs_1_), channel_id=1, source_target_pairs={{0,16},{8,24},{16,0},{24,8},{1,17},{9,25},{17,1},{25,9},{2,18},{10... | collective-permute-start | bytes 1572872 | tf_op jit(solution)/shard_map/ppermute | solution.py:72
  21.7 23.3 %collective-permute-start.1 = (bf16[80,384]{1,0:T(8,128)(2,1)S(1)}, bf16[80,384]{1,0:T(8,128)(2,1)S(1)}, u32[]{:S(2)}, u32[]{:S(2)}) collective-permute-start(bf16[80,384]{1,0:T(8,128)(2,1)S(1)} %copy-done.122), channel_id=1, source_target_pairs={{0,8},{8,0},{16,24},{24,16},{1,9},{9,1},{17,25},{25,17},{2,10},{10... | collective-permute-start | bytes 184328 | tf_op jit(solution)/shard_map/ppermute | solution.py:72
  60.3 92.7 %all-gather.15.cloned.1.call-start = ((), (), s32[]{:S(2)}) async-start(), calls=%async_computation.15 | async-start | bytes 2359296 | tf_op jit(solution)/shard_map/all_gather | solution.py:182
  84.0 177.2 %all-gather.17.cloned.1.call-start = ((), (), s32[]{:S(2)}) async-start(), calls=%async_computation.16 | async-start | bytes 12976128 | tf_op jit(solution)/shard_map/all_gather | solution.py:182
  104.0 194.1 %all-gather.11.cloned.1.call-start = ((), (), s32[]{:S(2)}) async-start(), calls=%async_computation.7 | async-start | bytes 6488064 | tf_op jit(solution)/shard_map/all_gather | solution.py:190
  104.6 296.4 %reduce-scatter.7.cloned.1.call-start = ((), (), s32[]{:S(2)}) async-start(), calls=%async_computation.8 | async-start | bytes 3604480 | tf_op jit(solution)/shard_map/reduce_scatter | solution.py:199
  108.9 23.2 %collective-permute-start.21 = (bf16[128,2048]{1,0:T(8,128)(2,1)}, bf16[128,2048]{1,0:T(8,128)(2,1)}, u32[]{:S(2)}, u32[]{:S(2)}) collective-permute-start(bf16[128,2048]{1,0:T(8,128)(2,1)} %get-tuple-element.675), channel_id=1, source_target_pairs={{0,4},{4,0},{1,5},{5,1},{2,6},{6,2},{3,7},{7,3},{8,12},{12,8},{9,1... | collective-permute-start | bytes 1572872 | tf_op jit(solution)/shard_map/ppermute | solution.py:67
  145.9 35.9 %collective-permute-start.25 = (bf16[128,2048]{1,0:T(8,128)(2,1)S(1)}, bf16[128,2048]{1,0:T(8,128)(2,1)S(1)}, u32[]{:S(2)}, u32[]{:S(2)}) collective-permute-start(bf16[128,2048]{1,0:T(8,128)(2,1)S(1)} %get-tuple-element.415.refs_0_), channel_id=1, source_target_pairs={{0,8},{8,0},{16,24},{24,16},{1,9},{9,1},{17,25},{25,17},{2,10},{10... | collective-permute-start | bytes 1572872 | tf_op jit(solution)/shard_map/ppermute | solution.py:72
  147.1 34.6 %collective-permute-start.27 = (bf16[128,2048]{1,0:T(8,128)(2,1)S(1)}, bf16[128,2048]{1,0:T(8,128)(2,1)}, u32[]{:S(2)}, u32[]{:S(2)}) collective-permute-start(bf16[128,2048]{1,0:T(8,128)(2,1)S(1)} %get-tuple-element.415.refs_0_), channel_id=1, source_target_pairs={{0,16},{8,24},{16,0},{24,8},{1,17},{9,25},{17,1},{25,9},{2,18},{10... | collective-permute-start | bytes 1572872 | tf_op jit(solution)/shard_map/ppermute | solution.py:72
  148.2 33.6 %collective-permute-start.26 = (bf16[128,2048]{1,0:T(8,128)(2,1)S(1)}, bf16[128,2048]{1,0:T(8,128)(2,1)}, u32[]{:S(2)}, u32[]{:S(2)}) collective-permute-start(bf16[128,2048]{1,0:T(8,128)(2,1)S(1)} %get-tuple-element.416.refs_1_), channel_id=1, source_target_pairs={{0,8},{8,0},{16,24},{24,16},{1,9},{9,1},{17,25},{25,17},{2,10},{10... | collective-permute-start | bytes 1572872 | tf_op jit(solution)/shard_map/ppermute | solution.py:72
  149.4 32.4 %collective-permute-start.28 = (bf16[128,2048]{1,0:T(8,128)(2,1)S(1)}, bf16[128,2048]{1,0:T(8,128)(2,1)}, u32[]{:S(2)}, u32[]{:S(2)}) collective-permute-start(bf16[128,2048]{1,0:T(8,128)(2,1)S(1)} %get-tuple-element.416.refs_1_), channel_id=1, source_target_pairs={{0,16},{8,24},{16,0},{24,8},{1,17},{9,25},{17,1},{25,9},{2,18},{10... | collective-permute-start | bytes 1572872 | tf_op jit(solution)/shard_map/ppermute | solution.py:72
  184.2 20.0 %collective-permute-start.31 = (bf16[128,2048]{1,0:T(8,128)(2,1)}, bf16[128,2048]{1,0:T(8,128)(2,1)}, u32[]{:S(2)}, u32[]{:S(2)}) collective-permute-start(bf16[128,2048]{1,0:T(8,128)(2,1)} %get-tuple-element.386), channel_id=1, source_target_pairs={{0,8},{8,0},{16,24},{24,16},{1,9},{9,1},{17,25},{25,17},{2,10},{10... | collective-permute-start | bytes 1572872 | tf_op jit(solution)/shard_map/ppermute | solution.py:72
  185.4 19.8 %collective-permute-start.32 = (bf16[128,2048]{1,0:T(8,128)(2,1)}, bf16[128,2048]{1,0:T(8,128)(2,1)}, u32[]{:S(2)}, u32[]{:S(2)}) collective-permute-start(bf16[128,2048]{1,0:T(8,128)(2,1)} %get-tuple-element.388), channel_id=1, source_target_pairs={{0,16},{8,24},{16,0},{24,8},{1,17},{9,25},{17,1},{25,9},{2,18},{10... | collective-permute-start | bytes 1572872 | tf_op jit(solution)/shard_map/ppermute | solution.py:72
  224.8 23.4 %collective-permute-start.36 = (bf16[128,2048]{1,0:T(8,128)(2,1)S(1)}, bf16[128,2048]{1,0:T(8,128)(2,1)S(1)}, u32[]{:S(2)}, u32[]{:S(2)}) collective-permute-start(bf16[128,2048]{1,0:T(8,128)(2,1)S(1)} %get-tuple-element.670.refs_1_), channel_id=1, source_target_pairs={{0,8},{8,0},{16,24},{24,16},{1,9},{9,1},{17,25},{25,17},{2,10},{10... | collective-permute-start | bytes 1572872 | tf_op jit(solution)/shard_map/ppermute | solution.py:72
  226.1 23.0 %collective-permute-start.37 = (bf16[128,2048]{1,0:T(8,128)(2,1)S(1)}, bf16[128,2048]{1,0:T(8,128)(2,1)S(1)}, u32[]{:S(2)}, u32[]{:S(2)}) collective-permute-start(bf16[128,2048]{1,0:T(8,128)(2,1)S(1)} %get-tuple-element.671.refs_0_), channel_id=1, source_target_pairs={{0,16},{8,24},{16,0},{24,8},{1,17},{9,25},{17,1},{25,9},{2,18},{10... | collective-permute-start | bytes 1572872 | tf_op jit(solution)/shard_map/ppermute | solution.py:72
  258.7 24.0 %collective-permute-start.41 = (bf16[128,2048]{1,0:T(8,128)(2,1)S(1)}, bf16[128,2048]{1,0:T(8,128)(2,1)S(1)}, u32[]{:S(2)}, u32[]{:S(2)}) collective-permute-start(bf16[128,2048]{1,0:T(8,128)(2,1)S(1)} %collective-permute-done.25.refs_2_), channel_id=1, source_target_pairs={{0,16},{8,24},{16,0},{24,8},{1,17},{9,25},{17,1},{25,9},{2,18},{10... | collective-permute-start | bytes 1572872 | tf_op jit(solution)/shard_map/ppermute | solution.py:72
  259.2 23.5 %collective-permute-start.42 = (bf16[128,2048]{1,0:T(8,128)(2,1)}, bf16[128,2048]{1,0:T(8,128)(2,1)S(1)}, u32[]{:S(2)}, u32[]{:S(2)}) collective-permute-start(bf16[128,2048]{1,0:T(8,128)(2,1)} %collective-permute-done.28.refs_5_), channel_id=1, source_target_pairs={{0,8},{8,0},{16,24},{24,16},{1,9},{9,1},{17,25},{25,17},{2,10},{10... | collective-permute-start | bytes 1572872 | tf_op jit(solution)/shard_map/ppermute | solution.py:72
  313.4 144.5 %reduce-scatter.9.cloned.1.call-start = ((), (), s32[]{:S(2)}) async-start(), calls=%async_computation.9 | async-start | bytes 3604480 | tf_op jit(solution)/shard_map/reduce_scatter | solution.py:199
  313.5 25.2 %collective-permute-start.44 = (bf16[640,384]{1,0:T(8,128)(2,1)S(1)}, bf16[640,384]{1,0:T(8,128)(2,1)S(1)}, u32[]{:S(2)}, u32[]{:S(2)}) collective-permute-start(bf16[640,384]{1,0:T(8,128)(2,1)S(1)} %get-tuple-element.587.refs_0_), channel_id=1, source_target_pairs={{0,8},{8,0},{16,24},{24,16},{1,9},{9,1},{17,25},{25,17},{2,10},{10... | collective-permute-start | bytes 1474568 | tf_op jit(solution)/shard_map/ppermute | solution.py:72
  314.3 24.5 %collective-permute-start.45 = (bf16[640,384]{1,0:T(8,128)(2,1)S(1)}, bf16[640,384]{1,0:T(8,128)(2,1)S(1)}, u32[]{:S(2)}, u32[]{:S(2)}) collective-permute-start(bf16[640,384]{1,0:T(8,128)(2,1)S(1)} %get-tuple-element.588.refs_1_), channel_id=1, source_target_pairs={{0,8},{8,0},{16,24},{24,16},{1,9},{9,1},{17,25},{25,17},{2,10},{10... | collective-permute-start | bytes 1474568 | tf_op jit(solution)/shard_map/ppermute | solution.py:72
  315.6 23.2 %collective-permute-start.46 = (bf16[640,384]{1,0:T(8,128)(2,1)S(1)}, bf16[640,384]{1,0:T(8,128)(2,1)S(1)}, u32[]{:S(2)}, u32[]{:S(2)}) collective-permute-start(bf16[640,384]{1,0:T(8,128)(2,1)S(1)} %get-tuple-element.587.refs_0_), channel_id=1, source_target_pairs={{0,16},{8,24},{16,0},{24,8},{1,17},{9,25},{17,1},{25,9},{2,18},{10... | collective-permute-start | bytes 1474568 | tf_op jit(solution)/shard_map/ppermute | solution.py:72
  316.7 22.7 %collective-permute-start.47 = (bf16[640,384]{1,0:T(8,128)(2,1)S(1)}, bf16[640,384]{1,0:T(8,128)(2,1)}, u32[]{:S(2)}, u32[]{:S(2)}) collective-permute-start(bf16[640,384]{1,0:T(8,128)(2,1)S(1)} %get-tuple-element.588.refs_1_), channel_id=1, source_target_pairs={{0,16},{8,24},{16,0},{24,8},{1,17},{9,25},{17,1},{25,9},{2,18},{10... | collective-permute-start | bytes 1474568 | tf_op jit(solution)/shard_map/ppermute | solution.py:72
  339.3 31.8 %collective-permute-start.48 = (bf16[128,2048]{1,0:T(8,128)(2,1)}, bf16[128,2048]{1,0:T(8,128)(2,1)S(1)}, u32[]{:S(2)}, u32[]{:S(2)}) collective-permute-start(bf16[128,2048]{1,0:T(8,128)(2,1)} %get-tuple-element.453), channel_id=1, source_target_pairs={{0,8},{8,0},{16,24},{24,16},{1,9},{9,1},{17,25},{25,17},{2,10},{10... | collective-permute-start | bytes 1572872 | tf_op jit(solution)/shard_map/ppermute | solution.py:72
  340.0 31.1 %collective-permute-start.49 = (bf16[128,2048]{1,0:T(8,128)(2,1)}, bf16[128,2048]{1,0:T(8,128)(2,1)S(1)}, u32[]{:S(2)}, u32[]{:S(2)}) collective-permute-start(bf16[128,2048]{1,0:T(8,128)(2,1)} %get-tuple-element.455), channel_id=1, source_target_pairs={{0,16},{8,24},{16,0},{24,8},{1,17},{9,25},{17,1},{25,9},{2,18},{10... | collective-permute-start | bytes 1572872 | tf_op jit(solution)/shard_map/ppermute | solution.py:72
  341.5 29.6 %collective-permute-start.50 = (bf16[128,2048]{1,0:T(8,128)(2,1)}, bf16[128,2048]{1,0:T(8,128)(2,1)S(1)}, u32[]{:S(2)}, u32[]{:S(2)}) collective-permute-start(bf16[128,2048]{1,0:T(8,128)(2,1)} %get-tuple-element.457), channel_id=1, source_target_pairs={{0,8},{8,0},{16,24},{24,16},{1,9},{9,1},{17,25},{25,17},{2,10},{10... | collective-permute-start | bytes 1572872 | tf_op jit(solution)/shard_map/ppermute | solution.py:72
  342.4 28.8 %collective-permute-start.51 = (bf16[128,2048]{1,0:T(8,128)(2,1)}, bf16[128,2048]{1,0:T(8,128)(2,1)S(1)}, u32[]{:S(2)}, u32[]{:S(2)}) collective-permute-start(bf16[128,2048]{1,0:T(8,128)(2,1)} %get-tuple-element.459), channel_id=1, source_target_pairs={{0,16},{8,24},{16,0},{24,8},{1,17},{9,25},{17,1},{25,9},{2,18},{10... | collective-permute-start | bytes 1572872 | tf_op jit(solution)/shard_map/ppermute | solution.py:72
  380.9 148.2 %reduce-scatter.11.cloned.1.call-start = ((), (), s32[]{:S(2)}) async-start(), calls=%async_computation.10 | async-start | bytes 3604480 | tf_op jit(solution)/shard_map/reduce_scatter | solution.py:199
  401.1 154.0 %reduce-scatter.13.cloned.1.call-start = ((), (), s32[]{:S(2)}) async-start(), calls=%async_computation.11 | async-start | bytes 2621440 | tf_op jit(solution)/shard_map/reduce_scatter | solution.py:199
  410.1 29.6 %collective-permute-start.57 = (bf16[128,2048]{1,0:T(8,128)(2,1)S(1)}, bf16[128,2048]{1,0:T(8,128)(2,1)S(1)}, u32[]{:S(2)}, u32[]{:S(2)}) collective-permute-start(bf16[128,2048]{1,0:T(8,128)(2,1)S(1)} %get-tuple-element.668.refs_1_), channel_id=1, source_target_pairs={{0,8},{8,0},{16,24},{24,16},{1,9},{9,1},{17,25},{25,17},{2,10},{10... | collective-permute-start | bytes 1572872 | tf_op jit(solution)/shard_map/ppermute | solution.py:72
  411.5 28.3 %collective-permute-start.58 = (bf16[128,2048]{1,0:T(8,128)(2,1)S(1)}, bf16[128,2048]{1,0:T(8,128)(2,1)S(1)}, u32[]{:S(2)}, u32[]{:S(2)}) collective-permute-start(bf16[128,2048]{1,0:T(8,128)(2,1)S(1)} %get-tuple-element.669.refs_0_), channel_id=1, source_target_pairs={{0,16},{8,24},{16,0},{24,8},{1,17},{9,25},{17,1},{25,9},{2,18},{10... | collective-permute-start | bytes 1572872 | tf_op jit(solution)/shard_map/ppermute | solution.py:72
  423.4 21.4 %collective-permute-start.60 = (bf16[128,2048]{1,0:T(8,128)(2,1)S(1)}, bf16[128,2048]{1,0:T(8,128)(2,1)S(1)}, u32[]{:S(2)}, u32[]{:S(2)}) collective-permute-start(bf16[128,2048]{1,0:T(8,128)(2,1)S(1)} %collective-permute-done.56.refs_2_), channel_id=1, source_target_pairs={{0,16},{8,24},{16,0},{24,8},{1,17},{9,25},{17,1},{25,9},{2,18},{10... | collective-permute-start | bytes 1572872 | tf_op jit(solution)/shard_map/ppermute | solution.py:72
  424.6 20.2 %collective-permute-start.61 = (bf16[128,2048]{1,0:T(8,128)(2,1)S(1)}, bf16[128,2048]{1,0:T(8,128)(2,1)S(1)}, u32[]{:S(2)}, u32[]{:S(2)}) collective-permute-start(bf16[128,2048]{1,0:T(8,128)(2,1)S(1)} %collective-permute-done.59.refs_5_), channel_id=1, source_target_pairs={{0,8},{8,0},{16,24},{24,16},{1,9},{9,1},{17,25},{25,17},{2,10},{10... | collective-permute-start | bytes 1572872 | tf_op jit(solution)/shard_map/ppermute | solution.py:72
  459.8 35.8 %collective-permute-start.64 = (bf16[128,2048]{1,0:T(8,128)(2,1)}, bf16[128,2048]{1,0:T(8,128)(2,1)}, u32[]{:S(2)}, u32[]{:S(2)}) collective-permute-start(bf16[128,2048]{1,0:T(8,128)(2,1)} %get-tuple-element.517), channel_id=1, source_target_pairs={{0,16},{8,24},{16,0},{24,8},{1,17},{9,25},{17,1},{25,9},{2,18},{10... | collective-permute-start | bytes 1572872 | tf_op jit(solution)/shard_map/ppermute | solution.py:72
  461.0 34.7 %collective-permute-start.65 = (bf16[128,2048]{1,0:T(8,128)(2,1)}, bf16[128,2048]{1,0:T(8,128)(2,1)}, u32[]{:S(2)}, u32[]{:S(2)}) collective-permute-start(bf16[128,2048]{1,0:T(8,128)(2,1)} %get-tuple-element.519), channel_id=1, source_target_pairs={{0,8},{8,0},{16,24},{24,16},{1,9},{9,1},{17,25},{25,17},{2,10},{10... | collective-permute-start | bytes 1572872 | tf_op jit(solution)/shard_map/ppermute | solution.py:72
  461.6 34.1 %collective-permute-start.66 = (bf16[128,2048]{1,0:T(8,128)(2,1)}, bf16[128,2048]{1,0:T(8,128)(2,1)}, u32[]{:S(2)}, u32[]{:S(2)}) collective-permute-start(bf16[128,2048]{1,0:T(8,128)(2,1)} %get-tuple-element.521), channel_id=1, source_target_pairs={{0,16},{8,24},{16,0},{24,8},{1,17},{9,25},{17,1},{25,9},{2,18},{10... | collective-permute-start | bytes 1572872 | tf_op jit(solution)/shard_map/ppermute | solution.py:72
  475.9 20.1 %collective-permute-start.67 = (bf16[640,384]{1,0:T(8,128)(2,1)S(1)}, bf16[640,384]{1,0:T(8,128)(2,1)}, u32[]{:S(2)}, u32[]{:S(2)}) collective-permute-start(bf16[640,384]{1,0:T(8,128)(2,1)S(1)} %collective-permute-done.44.refs_2_), channel_id=1, source_target_pairs={{0,16},{8,24},{16,0},{24,8},{1,17},{9,25},{17,1},{25,9},{2,18},{10... | collective-permute-start | bytes 1474568 | tf_op jit(solution)/shard_map/ppermute | solution.py:72
  479.0 115.8 %reduce-scatter.15.cloned.1.call-start = ((), (), s32[]{:S(2)}) async-start(), calls=%async_computation.12 | async-start | bytes 1310720 | tf_op jit(solution)/shard_map/reduce_scatter | solution.py:199
  497.4 26.6 %collective-permute-start.73 = (bf16[128,2048]{1,0:T(8,128)(2,1)S(1)}, bf16[128,2048]{1,0:T(8,128)(2,1)S(1)}, u32[]{:S(2)}, u32[]{:S(2)}) collective-permute-start(bf16[128,2048]{1,0:T(8,128)(2,1)S(1)} %add_convert_fusion.7), channel_id=1, source_target_pairs={{0,16},{8,24},{16,0},{24,8},{1,17},{9,25},{17,1},{25,9},{2,18},{10... | collective-permute-start | bytes 1572872 | tf_op jit(solution)/shard_map/ppermute | solution.py:72
  499.9 26.3 %collective-permute-start.74 = (bf16[128,2048]{1,0:T(8,128)(2,1)S(1)}, bf16[128,2048]{1,0:T(8,128)(2,1)S(1)}, u32[]{:S(2)}, u32[]{:S(2)}) collective-permute-start(bf16[128,2048]{1,0:T(8,128)(2,1)S(1)} %add_convert_fusion.6), channel_id=1, source_target_pairs={{0,8},{8,0},{16,24},{24,16},{1,9},{9,1},{17,25},{25,17},{2,10},{10... | collective-permute-start | bytes 1572872 | tf_op jit(solution)/shard_map/ppermute | solution.py:72
  538.3 40.2 %collective-permute-start.84 = (bf16[5120,384]{1,0:T(8,128)(2,1)}, bf16[5120,384]{1,0:T(8,128)(2,1)}, u32[]{:S(2)}, u32[]{:S(2)}) collective-permute-start(bf16[5120,384]{1,0:T(8,128)(2,1)} %shard_map.258), channel_id=1, source_target_pairs={{0,4},{4,0},{1,5},{5,1},{2,6},{6,2},{3,7},{7,3},{8,12},{12,8},{9,1... | collective-permute-start | bytes 11796488 | tf_op jit(solution)/shard_map/ppermute | solution.py:67
  542.9 24.2 %collective-permute-start.75 = (bf16[128,2048]{1,0:T(8,128)(2,1)}, bf16[128,2048]{1,0:T(8,128)(2,1)}, u32[]{:S(2)}, u32[]{:S(2)}) collective-permute-start(bf16[128,2048]{1,0:T(8,128)(2,1)} %get-tuple-element.663), channel_id=1, source_target_pairs={{0,4},{4,0},{1,5},{5,1},{2,6},{6,2},{3,7},{7,3},{8,12},{12,8},{9,1... | collective-permute-start | bytes 1572872 | tf_op jit(solution)/shard_map/ppermute | solution.py:67
  560.9 55.0 %reduce-scatter.17.cloned.1.call-start = ((), (), s32[]{:S(2)}) async-start(), calls=%async_computation.13 | async-start | bytes 983040 | tf_op jit(solution)/shard_map/reduce_scatter | solution.py:199
  600.8 19.7 %collective-permute-start.85 = (f32[128,2048]{1,0:T(8,128)S(1)}, f32[128,2048]{1,0:T(8,128)S(1)}, u32[]{:S(2)}, u32[]{:S(2)}) collective-permute-start(f32[128,2048]{1,0:T(8,128)S(1)} %get-tuple-element.647), channel_id=1, source_target_pairs={{0,4},{4,0},{1,5},{5,1},{2,6},{6,2},{3,7},{7,3},{8,12},{12,8},{9,1... | collective-permute-start | bytes 3145736 | tf_op jit(solution)/shard_map/ppermute | solution.py:67
  (182 other events, 1804.2 us)
Sparse Core Ops, SparseCore 0:
  9.7 49.8 all-gather.8
  61.8 26.7 all-gather.12
  90.7 28.6 all-gather.14
  121.4 107.5 all-gather.16
  230.4 58.6 all-gather.10
  313.5 54.2 reduce-scatter.6
  381.0 54.2 reduce-scatter.8
  437.6 56.0 reduce-scatter.10
  495.9 43.6 reduce-scatter.12
  561.0 25.0 reduce-scatter.14
  595.0 20.8 reduce-scatter.16

commit v5 on v4

--- a/solution.py
+++ b/solution.py
@@ -381,7 +381,7 @@
         ],
         out_specs=[head, whole(keys), whole(keys)],
         out_shape=[jax.ShapeDtypeStruct(queries.shape, bf16), summed, summed],
-        compiler_params=pltpu.CompilerParams(vmem_limit_bytes=62 << 20),
+        compiler_params=pltpu.CompilerParams(vmem_limit_bytes=48 << 20),
         cost_estimate=BESIDE,
     )(length, flip, queries, grads, total, keys, keys_t, values, cos_table, sin_table)
 
@@ -399,40 +399,39 @@
             out_refs[2 * k + 1][...] = value[rows:]
 
 
-def product_kernel(kind, pieces, left_ref, right_ref, *out_refs):
+def write_rows(out_refs, value):
+    rows = value.shape[0] // len(out_refs)
+    for k, out_ref in enumerate(out_refs):
+        out_ref[...] = value[k * rows : (k + 1) * rows]
+
+
+def product_kernel(kind, left_ref, right_ref, *out_refs):
     total = lax.dot_general(
         left_ref[...], right_ref[...], (CONTRACT[kind], ((), ())), preferred_element_type=f32
-    ).astype(bf16)
-    if pieces:
-        write_halves(out_refs, pl.program_id(0), total)
-    else:
-        out_refs[0][...] = total
+    )
+    write_rows(out_refs, total.astype(bf16))
 
 
 def product(kind, left, right, pieces=False):
     rows, width = left.shape[0], right.shape[0] if kind == "nt" else right.shape[1]
     chips = lax.axis_size("chip")
-    tile = rows // chips if pieces else TILE
-    if (pieces and chips != 4) or rows % tile or tile % 128 or width % 128 or right.shape[0] % 128:
+    count = 2 * chips if pieces else 1
+    if (pieces and chips != 4) or width % TILE or left.shape[1] % 128 or rows % (16 * count):
         total = lax.dot_general(
             left, right, (CONTRACT[kind], ((), ())), preferred_element_type=f32
         ).astype(bf16)
         return as_pieces(total) if pieces else total
-    if pieces:
-        shapes = [(tile // 2, width)] * (2 * chips)
-        outs = [pl.BlockSpec(shape, lambda i: (0, 0)) for shape in shapes]
+    shape = (rows // count, width)
+    if kind == "nt":
+        source = pl.BlockSpec((TILE, right.shape[1]), lambda i: (i, 0))
     else:
-        shapes = [(rows, width)]
-        outs = [pl.BlockSpec((tile, width), lambda i: (i, 0))]
+        source = pl.BlockSpec((right.shape[0], TILE), lambda i: (0, i))
     results = pl.pallas_call(
-        functools.partial(product_kernel, kind, pieces),
-        grid=(rows // tile,),
-        in_specs=[
-            pl.BlockSpec((tile, left.shape[1]), lambda i: (i, 0)),
-            pl.BlockSpec(right.shape, lambda i: (0, 0)),
-        ],
-        out_specs=outs,
-        out_shape=[jax.ShapeDtypeStruct(shape, bf16) for shape in shapes],
+        functools.partial(product_kernel, kind),
+        grid=(width // TILE,),
+        in_specs=[pl.BlockSpec(left.shape, lambda i: (0, 0)), source],
+        out_specs=[pl.BlockSpec((shape[0], TILE), lambda i: (0, i))] * count,
+        out_shape=[jax.ShapeDtypeStruct(shape, bf16)] * count,
         compiler_params=pltpu.CompilerParams(vmem_limit_bytes=56 << 20),
         cost_estimate=BESIDE,
     )(left, right)
@@ -559,40 +558,34 @@
     )(grad_q, up_q, grad_k, grad_v, place)
 
 
-def spread_kernel(flip_rows, count, own, flip_ref, *refs):
+def spread_kernel(count, _, *refs):
     left_refs, weight_ref, out_refs = refs[:count], refs[count], refs[count + 1 :]
-    chips, groups, _, _, width = weight_ref.shape
-    depth = groups * own
-    columns = []
-    for place in range(chips):
-        total = 0.0
-        for j, left_ref in enumerate(left_refs):
-            block = weight_ref[place ^ flip_ref[0], :, j, :own].reshape(depth, width)
-            total = total + outer_cols(left_ref[...], block)
-        columns.append(total.astype(bf16))
-    block = pl.program_id(0) ^ flip_ref[0] if flip_rows else pl.program_id(0)
-    write_halves(out_refs, block, jnp.concatenate(columns, 1))
-
-
-def spread(lefts, weight, own, flip_rows=False):
-    chips, groups, _, _, width = weight.shape
-    rows, depth = lefts[0].shape[0], chips * groups * own
-    if chips != 4 or lefts[0].shape[1] % 128:
+    _, groups, _, own, width = weight_ref.shape
+    total = 0.0
+    for j, left_ref in enumerate(left_refs):
+        block = weight_ref[0, :, j].reshape(groups * own, width)
+        total = total + outer_cols(left_ref[...], block)
+    write_rows(out_refs, total.astype(bf16))
+
+
+def spread(lefts, weight):
+    chips, groups, _, own, width = weight.shape
+    rows, depth = lefts[0].shape[0], groups * own
+    if chips != 4 or width % 128:
         total = sum(
-            outer_cols(left, weight[:, :, j, :own].reshape(depth, width))
+            outer_cols(left, weight[:, :, j].reshape(chips * depth, width))
             for j, left in enumerate(lefts)
         )
         return as_pieces(total.astype(bf16))
-    tile = rows // chips
-    shape = (tile // 2, depth)
+    shape = (rows // (2 * chips), chips * depth)
     return pl.pallas_call(
-        functools.partial(spread_kernel, flip_rows, len(lefts), own),
+        functools.partial(spread_kernel, len(lefts)),
         grid_spec=pltpu.PrefetchScalarGridSpec(
             num_scalar_prefetch=1,
             grid=(chips,),
-            in_specs=[pl.BlockSpec((tile, left.shape[1]), lambda i, f: (i, 0)) for left in lefts]
-            + [pl.BlockSpec(weight.shape, lambda i, f: (0, 0, 0, 0, 0))],
-            out_specs=[pl.BlockSpec(shape, lambda i, f: (0, 0))] * (2 * chips),
+            in_specs=[pl.BlockSpec(left.shape, lambda i, f: (0, 0)) for left in lefts]
+            + [pl.BlockSpec((1,) + weight.shape[1:], lambda i, f: (i ^ f[0], 0, 0, 0, 0))],
+            out_specs=[pl.BlockSpec((shape[0], depth), lambda i, f: (0, i))] * (2 * chips),
         ),
         out_shape=[jax.ShapeDtypeStruct(shape, bf16)] * (2 * chips),
         compiler_params=pltpu.CompilerParams(vmem_limit_bytes=56 << 20),
@@ -933,7 +926,7 @@
     small_near = gather_near(small_rows) if chips == 4 else (small_rows,)
     grad_w_down = scatter_dp(down_half)
     part, gate_grad, up_grad = tie(
-        spread([gate_grad, up_grad], gate_up, own_rows), gate_grad, up_grad
+        spread([gate_grad, up_grad], gate_up), gate_grad, up_grad
     )
     gate_part = weight_terms(normed2, gate_grad, grad_scale, flip[0])
     up_part = weight_terms(normed2, up_grad, grad_scale, flip[0])

time: 643 us -> 639 us (level)
    unnamed x249 -> x247, local copies, waits for them, and re-layouts: 16.2 us -> 14.5 us
  transfers between devices with their start and end apart: 107 -> 107, of which waited for: 48 -> 50; matrix products, arithmetic and copies ran while one was open for 16% -> 15% of each run, Pallas kernels for 35% -> 34%
where the time goes in v5:
time: 639 us; the launch traced here: 629 us
  Pallas kernels  215 us (34%)
  waiting for transfers between devices  186 us (29%)
  starting transfers between devices  98.1 us (15%)
  other arithmetic  81 us (13%)
  local copies, waits for them, and re-layouts  33 us (5%)
  between operations  16 us (3%)
    ppermute x85, waiting for transfers between devices, to_chip(): return lax.ppermute(block, 'chip', [(i, i ^ bits) for i in range(count)])  169 us
    ppermute x85, starting transfers between devices, to_chip(): return lax.ppermute(block, 'chip', [(i, i ^ bits) for i in range(count)])  95.3 us
    pallas_call x5, Pallas kernels, weight_terms(): pl.pallas_call(functools.partial(terms_kernel, scale), grid_spec=pltpu.Pr...  56 us
    pallas_call x3, Pallas kernels, product(): pl.pallas_call(functools.partial(product_kernel, kind), grid=(width // TI...  29.6 us
    pallas_call x1, Pallas kernels, attend(): pl.pallas_call(functools.partial(attend_kernel, score_scale), grid=(heads...  18.8 us
    pallas_call x1, Pallas kernels, gated(): pl.pallas_call(gate_kernel, grid_spec=pltpu.PrefetchScalarGridSpec(num_sc...  18.4 us
    pallas_call x1, Pallas kernels, spread(): pl.pallas_call(functools.partial(spread_kernel, len(lefts)), grid_spec=pl...  18.2 us
    pallas_call x1, Pallas kernels, attend_back(): pl.pallas_call(functools.partial(attend_back_kernel, score_scale), grid=(...  15 us
  transfers between devices with their start and end apart: 107, of which 50 were waited for; matrix products, arithmetic and copies ran while one was open for 15% of the time, Pallas kernels for 34%

profile of v5, /device:TPU:0, one launch (start us, length us, event | category | flops | bytes accessed | tf_op | source)
XLA Modules:
  0.0 629.5 jit_solution(13810377975212632194)
XLA Ops:
  11.2 3.8 shard_map.237
  17.1 2.5 collective-permute-start.4
  25.6 19.4 %collective-permute-done.1 = bf16[80,384]{1,0:T(8,128)(2,1)S(1)} collective-permute-done((bf16[80,384]{1,0:T(8,128)(2,1)S(1)}, bf16[80,384]{1,0:T(8,128)(2,1)S(1)}, u32[]{:S(2)}, u32[]{:S(2)}) %collective-permute-start.1) | collective-permute-done | bytes 61472 | tf_op jit(solution)/shard_map/ppermute | solution.py:72
  49.2 2.7 collective-permute-start.3
  54.3 5.3 all-gather.9.cloned.1.call-done.right_ref
  63.4 11.3 %collective-permute-done.8.refs_6_ = bf16[128,2048]{1,0:T(8,128)(2,1)S(1)} collective-permute-done((bf16[128,2048]{1,0:T(8,128)(2,1)}, bf16[128,2048]{1,0:T(8,128)(2,1)S(1)}, u32[]{:S(2)}, u32[]{:S(2)}) %collective-permute-start.8) | collective-permute-done | bytes 524320 | tf_op jit(solution)/shard_map/ppermute | solution.py:72
  91.5 8.2 %shard_map.238 = (bf16[1024,2048]{1,0:T(8,128)(2,1)}, f32[1024,256]{1,0:T(8,128)}, f32[1024,128]{1,0:T(8,128)}) custom-call(s32[1]{0:T(128)} %bitcast.1._.flip_ref, bf16[128,2048]{1,0:T(8,128)(2,1)} %get-tuple-element.338.refs_0_, bf16[128,2048]{1,0:T(8,128)(2,1)} %copy-done.57, bf16[128,2048]{1,0:T(8,128)(2,1)} %collective-permute-done.4.refs_2_, ...), custom_call_target="tpu_custom_call" | custom-call | flops 1 | bytes 1 | tf_op jit(solution)/shard_map/pallas_call | solution.py:715
  101.4 2.6 pad_maximum_fusion.2
  114.0 2.4 collective-permute-done.14
  122.5 7.2 %collective-permute-done.15.refs_2_ = bf16[512,384]{1,0:T(8,128)(2,1)S(1)} collective-permute-done((bf16[512,384]{1,0:T(8,128)(2,1)S(1)}, bf16[512,384]{1,0:T(8,128)(2,1)S(1)}, u32[]{:S(2)}, u32[]{:S(2)}) %collective-permute-start.15) | collective-permute-done | bytes 393248 | tf_op jit(solution)/shard_map/ppermute | solution.py:72
  133.6 4.5 collective-permute-done.16.refs_3_
  139.0 6.1 collective-permute-done.19.refs_6_
  153.1 18.8 %shard_map.240 = (bf16[1024,1024]{1,0:T(8,128)(2,1)}, bf16[1024,1024]{1,0:T(8,128)(2,1)}, f32[4,1,1024]{2,1,0:T(1,128)}) custom-call(s32[1]{0:T(128)} %bitcast.length_ref, s32[1]{0:T(128)} %bitcast.1._.flip_ref, bf16[4,1024,384]{2,1,0:T(8,128)(2,1)} %bitcast.147, bf16[4,256,1024]{2,1,0:T(8,128)(2,1)} %all-gather.15.cloned.1.call-done.up_ref, ...), custom_call_target="tpu_custom_call" | custom-call | flops 1 | bytes 1 | tf_op jit(solution)/shard_map/pallas_call | solution.py:290
  171.9 9.5 %shard_map.241 = (bf16[128,2048]{1,0:T(8,128)(2,1)}, bf16[128,2048]{1,0:T(8,128)(2,1)}, bf16[128,2048]{1,0:T(8,128)(2,1)}, bf16[128,2048]{1,0:T(8,128)(2,1)}, bf...) custom-call(bf16[1024,1024]{1,0:T(8,128)(2,1)} %get-tuple-element.37, ...), custom_call_target="tpu_custom_call" | custom-call | flops 1 | bytes 1 | tf_op jit(solution)/shard_map/pallas_call | solution.py:429
  185.6 11.0 %collective-permute-done.29 = bf16[128,2048]{1,0:T(8,128)(2,1)S(1)} collective-permute-done((bf16[128,2048]{1,0:T(8,128)(2,1)}, bf16[128,2048]{1,0:T(8,128)(2,1)S(1)}, u32[]{:S(2)}, u32[]{:S(2)}) %collective-permute-start.29) | collective-permute-done | bytes 524320 | tf_op jit(solution)/shard_map/ppermute | solution.py:72
  197.8 6.0 collective-permute-done.31
  211.2 5.6 collective-permute-done.33
  226.4 10.8 %collective-permute-done.35.refs_2_ = bf16[128,2048]{1,0:T(8,128)(2,1)S(1)} collective-permute-done((bf16[128,2048]{1,0:T(8,128)(2,1)S(1)}, bf16[128,2048]{1,0:T(8,128)(2,1)S(1)}, u32[]{:S(2)}, u32[]{:S(2)}) %collective-permute-start.35) | collective-permute-done | bytes 524320 | tf_op jit(solution)/shard_map/ppermute | solution.py:72
  239.3 8.3 %collective-permute-done.36.refs_3_ = bf16[128,2048]{1,0:T(8,128)(2,1)S(1)} collective-permute-done((bf16[128,2048]{1,0:T(8,128)(2,1)S(1)}, bf16[128,2048]{1,0:T(8,128)(2,1)S(1)}, u32[]{:S(2)}, u32[]{:S(2)}) %collective-permute-start.36) | collective-permute-done | bytes 524320 | tf_op jit(solution)/shard_map/ppermute | solution.py:72
  248.7 6.9 %collective-permute-done.39.refs_6_ = bf16[128,2048]{1,0:T(8,128)(2,1)S(1)} collective-permute-done((bf16[128,2048]{1,0:T(8,128)(2,1)S(1)}, bf16[128,2048]{1,0:T(8,128)(2,1)S(1)}, u32[]{:S(2)}, u32[]{:S(2)}) %collective-permute-start.39) | collective-permute-done | bytes 524320 | tf_op jit(solution)/shard_map/ppermute | solution.py:72
  260.6 18.4 %shard_map.243 = (bf16[1024,1408]{1,0:T(8,128)(2,1)S(1)}, bf16[1024,1408]{1,0:T(8,128)(2,1)S(1)}, bf16[1024,1408]{1,0:T(8,128)(2,1)}) custom-call(s32[1]{0:T(128)} %bitcast.1._.flip_ref, bf16[1024,2048]{1,0:T(8,128)(2,1)} %copy-done.2, bf16[4,8,2,64,1408]{4,3,2,1,0:T(8,128)(2,1)} %bitcast.149), custom_call_target="tpu_custom_call" | custom-call | flops 1 | bytes 1 | tf_op jit(solution)/shard_map/pallas_call | solution.py:760
  286.2 11.4 %shard_map.245 = (bf16[704,2048]{1,0:T(8,128)(2,1)}, bf16[704,2048]{1,0:T(8,128)(2,1)}) custom-call(s32[2]{0:T(128)} %pad_add_fusion.place_ref, bf16[1024,1408]{1,0:T(8,128)(2,1)} %copy-done.9, bf16[1024,2048]{1,0:T(8,128)(2,1)} %copy-done.4), custom_call_target="tpu_custom_call" | custom-call | flops 1 | bytes 1 | tf_op jit(solution)/shard_map/pallas_call | solution.py:508
  297.7 11.6 %shard_map.246 = (bf16[1024,1408]{1,0:T(8,128)(2,1)S(1)}, bf16[1024,1408]{1,0:T(8,128)(2,1)S(1)}) custom-call(bf16[1024,2048]{1,0:T(8,128)(2,1)} %copy-done.4, bf16[1408,2048]{1,0:T(8,128)(2,1)} %all-gather.11.cloned.1.call-done.down_ref.right_ref, bf16[1024,1408]{1,0:T(8,128)(2,1)} %copy-done.13, bf16[1024,1408]{1,0:T(8,128)(2,1)} %get-tuple-element.428.slope_ref), custom_call_target="tpu_custom_call" | custom-call | flops 1 | bytes 1 | tf_op jit(solution)/shard_map/pallas_call | solution.py:789
  309.4 3.4 add_convert_fusion.2
  317.1 18.2 %shard_map.247 = (bf16[128,2048]{1,0:T(8,128)(2,1)}, bf16[128,2048]{1,0:T(8,128)(2,1)}, bf16[128,2048]{1,0:T(8,128)(2,1)}, bf16[128,2048]{1,0:T(8,128)(2,1)}, bf...) custom-call(s32[1]{0:T(128)} %bitcast.1._.flip_ref, ...), custom_call_target="tpu_custom_call" | custom-call | flops 1 | bytes 1 | tf_op jit(solution)/shard_map/pallas_call | solution.py:581
  343.5 13.6 %shard_map.249 = (bf16[4,4,64,1408]{3,2,1,0:T(8,128)(2,1)}, bf16[4,4,64,1408]{3,2,1,0:T(8,128)(2,1)}) custom-call(s32[2]{0:T(128)} %pad_add_fusion.1.place_ref, bf16[1024,2048]{1,0:T(8,128)(2,1)} %copy-done.2, bf16[1024,1408]{1,0:T(8,128)(2,1)} %copy-done.8), custom_call_target="tpu_custom_call" | custom-call | flops 1 | bytes 1 | tf_op jit(solution)/shard_map/pallas_call | solution.py:491
  357.1 13.6 %shard_map.248 = (bf16[4,4,64,1408]{3,2,1,0:T(8,128)(2,1)}, bf16[4,4,64,1408]{3,2,1,0:T(8,128)(2,1)}) custom-call(s32[2]{0:T(128)} %pad_add_fusion.1.place_ref, bf16[1024,2048]{1,0:T(8,128)(2,1)} %copy-done.2, bf16[1024,1408]{1,0:T(8,128)(2,1)} %copy-done.7), custom_call_target="tpu_custom_call" | custom-call | flops 1 | bytes 1 | tf_op jit(solution)/shard_map/pallas_call | solution.py:491
  370.8 5.5 collective-permute-done.52
  376.3 4.1 add_convert_fusion.1
  386.1 2.6 add_convert_fusion
  388.7 7.9 %collective-permute-done.53 = bf16[128,2048]{1,0:T(8,128)(2,1)S(1)} collective-permute-done((bf16[128,2048]{1,0:T(8,128)(2,1)S(1)}, bf16[128,2048]{1,0:T(8,128)(2,1)S(1)}, u32[]{:S(2)}, u32[]{:S(2)}) %collective-permute-start.53) | collective-permute-done | bytes 524320 | tf_op jit(solution)/shard_map/ppermute | solution.py:72
  410.6 10.8 %collective-permute-done.56.refs_2_ = bf16[128,2048]{1,0:T(8,128)(2,1)S(1)} collective-permute-done((bf16[128,2048]{1,0:T(8,128)(2,1)S(1)}, bf16[128,2048]{1,0:T(8,128)(2,1)S(1)}, u32[]{:S(2)}, u32[]{:S(2)}) %collective-permute-start.56) | collective-permute-done | bytes 524320 | tf_op jit(solution)/shard_map/ppermute | solution.py:72
  425.2 11.3 %shard_map.251 = (bf16[128,2048]{1,0:T(8,128)(2,1)}, bf16[128,2048]{1,0:T(8,128)(2,1)}, bf16[128,2048]{1,0:T(8,128)(2,1)}, bf16[128,2048]{1,0:T(8,128)(2,1)}, bf...) custom-call(bf16[1024,1408]{1,0:T(8,128)(2,1)} %copy-done.9, ...), custom_call_target="tpu_custom_call" | custom-call | flops 1 | bytes 1 | tf_op jit(solution)/shard_map/pallas_call | solution.py:429
  436.6 6.9 %collective-permute-done.60.refs_6_ = bf16[128,2048]{1,0:T(8,128)(2,1)S(1)} collective-permute-done((bf16[128,2048]{1,0:T(8,128)(2,1)S(1)}, bf16[128,2048]{1,0:T(8,128)(2,1)S(1)}, u32[]{:S(2)}, u32[]{:S(2)}) %collective-permute-start.60) | collective-permute-done | bytes 524320 | tf_op jit(solution)/shard_map/ppermute | solution.py:72
  446.0 10.5 %shard_map.252 = (bf16[512,2048]{1,0:T(8,128)(2,1)}, bf16[512,2048]{1,0:T(8,128)(2,1)}) custom-call(s32[2]{0:T(128)} %pad_add_fusion.place_ref, bf16[1024,1024]{1,0:T(8,128)(2,1)} %get-tuple-element.370.left_ref, bf16[1024,2048]{1,0:T(8,128)(2,1)} %copy-done.3), custom_call_target="tpu_custom_call" | custom-call | flops 1 | bytes 1 | tf_op jit(solution)/shard_map/pallas_call | solution.py:491
  461.8 8.8 %shard_map.253.grad_ref = bf16[1024,1024]{1,0:T(8,128)(2,1)} custom-call(bf16[1024,2048]{1,0:T(8,128)(2,1)} %copy-done.3, bf16[1024,2048]{1,0:T(8,128)(2,1)} %all-gather.9.cloned.1.call-done.right_ref), custom_call_target="tpu_custom_call" | custom-call | flops 1 | bytes 1 | tf_op jit(solution)/shard_map/pallas_call | solution.py:429
  477.3 15.0 %shard_map.254 = (bf16[1024,1024]{1,0:T(8,128)(2,1)}, f32[1024,256]{1,0:T(8,128)S(1)}, f32[1024,256]{1,0:T(8,128)S(1)}) custom-call(s32[1]{0:T(128)} %bitcast.length_ref, s32[1]{0:T(128)} %bitcast.1._.flip_ref, bf16[1024,1024]{1,0:T(8,128)(2,1)} %get-tuple-element.369.queries_ref, bf16[1024,1024]{1,0:T(8,128)(2,1)} %shard_map.253.grad_ref, ...), custom_call_target="tpu_custom_call" | custom-call | flops 1 | bytes 1 | tf_op jit(solution)/shard_map/pallas_call | solution.py:367
  498.4 7.4 %shard_map.255 = (bf16[512,384]{1,0:T(8,128)(2,1)S(1)}, bf16[512,384]{1,0:T(8,128)(2,1)S(1)}, bf16[512,384]{1,0:T(8,128)(2,1)}, bf16[512,384]{1,0:T(8,128)(2,1)S...) custom-call(bf16[1024,1024]{1,0:T(8,128)(2,1)} %get-tuple-element.54, ...), custom_call_target="tpu_custom_call" | custom-call | flops 1 | bytes 1 | tf_op jit(solution)/shard_map/pallas_call | solution.py:550
  509.5 9.2 %shard_map.256 = (bf16[4,4,32,1024]{3,2,1,0:T(8,128)(2,1)}, bf16[4,4,32,1024]{3,2,1,0:T(8,128)(2,1)}) custom-call(s32[2]{0:T(128)} %pad_add_fusion.place_ref, bf16[1024,1024]{1,0:T(8,128)(2,1)} %bitcast.156, bf16[1024,1024]{1,0:T(8,128)(2,1)} %get-tuple-element.548.grad_ref.right_ref), custom_call_target="tpu_custom_call" | custom-call | flops 1 | bytes 1 | tf_op jit(solution)/shard_map/pallas_call | solution.py:491
  523.6 3.7 collective-permute-done.71
  528.2 5.1 shard_map.258
  539.2 6.9 %collective-permute-done.76 = bf16[512,384]{1,0:T(8,128)(2,1)S(1)} collective-permute-done((bf16[512,384]{1,0:T(8,128)(2,1)S(1)}, bf16[512,384]{1,0:T(8,128)(2,1)S(1)}, u32[]{:S(2)}, u32[]{:S(2)}) %collective-permute-start.76) | collective-permute-done | bytes 393248 | tf_op jit(solution)/shard_map/ppermute | solution.py:72
  562.4 2.4 maximum_select_fusion.3
  564.9 9.1 %shard_map.257 = (bf16[4,4,64,384]{3,2,1,0:T(8,128)(2,1)}, bf16[4,4,64,384]{3,2,1,0:T(8,128)(2,1)}) custom-call(s32[2]{0:T(128)} %pad_add_fusion.1.place_ref, bf16[1024,2048]{1,0:T(8,128)(2,1)} %get-tuple-element.584.left_ref, bf16[1024,384]{1,0:T(8,128)(2,1)} %copy-done.43), custom_call_target="tpu_custom_call" | custom-call | flops 1 | bytes 1 | tf_op jit(solution)/shard_map/pallas_call | solution.py:491
  579.6 7.2 %shard_map.259 = f32[256,2048]{1,0:T(8,128)S(1)} custom-call(s32[2]{0:T(128)S(1)} %copy-done.25, bf16[256,384]{1,0:T(8,128)(2,1)S(1)} %get-tuple-element.595.refs_0_, bf16[256,384]{1,0:T(8,128)(2,1)S(1)} %collective-permute-done.81.refs_1_, bf16[256,384]{1,0:T(8,128)(2,1)S(1)} %collective-permute-done.82.refs_2_, ...), custom_call_target="tpu_custom_call" | custom-call | flops 1 | bytes 1 | tf_op jit(solution)/shard_map/pallas_call | solution.py:621
  597.2 2.7 collective-permute-done.92
  607.7 3.8 reduce-scatter.17.cloned.1.call-done
  612.7 2.4 collective-permute-start.87
  (584 shorter events, 226.9 us)
Async XLA Ops:
  7.3 52.3 %all-gather.9.cloned.1.call-start = ((), (), s32[]{:S(2)}) async-start(), calls=%async_computation.6 | async-start | bytes 4718592 | tf_op jit(solution)/shard_map/all_gather | solution.py:190
  8.0 80.5 %all-gather.13.cloned.1.call-start = ((), (), s32[]{:S(2)}) async-start(), calls=%async_computation.14 | async-start | bytes 2211840 | tf_op jit(solution)/shard_map/all_gather | solution.py:182
  17.1 37.2 %collective-permute-start.4 = (bf16[128,2048]{1,0:T(8,128)(2,1)}, bf16[128,2048]{1,0:T(8,128)(2,1)}, u32[]{:S(2)}, u32[]{:S(2)}) collective-permute-start(bf16[128,2048]{1,0:T(8,128)(2,1)} %get-tuple-element.338.refs_0_), channel_id=1, source_target_pairs={{0,8},{8,0},{16,24},{24,16},{1,9},{9,1},{17,25},{25,17},{2,10},{10... | collective-permute-start | bytes 1572872 | tf_op jit(solution)/shard_map/ppermute | solution.py:72
  19.6 34.7 %collective-permute-start.6 = (bf16[128,2048]{1,0:T(8,128)(2,1)}, bf16[128,2048]{1,0:T(8,128)(2,1)}, u32[]{:S(2)}, u32[]{:S(2)}) collective-permute-start(bf16[128,2048]{1,0:T(8,128)(2,1)} %get-tuple-element.338.refs_0_), channel_id=1, source_target_pairs={{0,16},{8,24},{16,0},{24,8},{1,17},{9,25},{17,1},{25,9},{2,18},{10... | collective-permute-start | bytes 1572872 | tf_op jit(solution)/shard_map/ppermute | solution.py:72
  21.1 33.2 %collective-permute-start.5 = (bf16[128,2048]{1,0:T(8,128)(2,1)S(1)}, bf16[128,2048]{1,0:T(8,128)(2,1)}, u32[]{:S(2)}, u32[]{:S(2)}) collective-permute-start(bf16[128,2048]{1,0:T(8,128)(2,1)S(1)} %get-tuple-element.339.refs_1_), channel_id=1, source_target_pairs={{0,8},{8,0},{16,24},{24,16},{1,9},{9,1},{17,25},{25,17},{2,10},{10... | collective-permute-start | bytes 1572872 | tf_op jit(solution)/shard_map/ppermute | solution.py:72
  21.7 32.6 %collective-permute-start.7 = (bf16[128,2048]{1,0:T(8,128)(2,1)S(1)}, bf16[128,2048]{1,0:T(8,128)(2,1)}, u32[]{:S(2)}, u32[]{:S(2)}) collective-permute-start(bf16[128,2048]{1,0:T(8,128)(2,1)S(1)} %get-tuple-element.339.refs_1_), channel_id=1, source_target_pairs={{0,16},{8,24},{16,0},{24,8},{1,17},{9,25},{17,1},{25,9},{2,18},{10... | collective-permute-start | bytes 1572872 | tf_op jit(solution)/shard_map/ppermute | solution.py:72
  21.7 23.3 %collective-permute-start.1 = (bf16[80,384]{1,0:T(8,128)(2,1)S(1)}, bf16[80,384]{1,0:T(8,128)(2,1)S(1)}, u32[]{:S(2)}, u32[]{:S(2)}) collective-permute-start(bf16[80,384]{1,0:T(8,128)(2,1)S(1)} %copy-done.121), channel_id=1, source_target_pairs={{0,8},{8,0},{16,24},{24,16},{1,9},{9,1},{17,25},{25,17},{2,10},{10... | collective-permute-start | bytes 184328 | tf_op jit(solution)/shard_map/ppermute | solution.py:72
  60.3 92.7 %all-gather.15.cloned.1.call-start = ((), (), s32[]{:S(2)}) async-start(), calls=%async_computation.15 | async-start | bytes 2359296 | tf_op jit(solution)/shard_map/all_gather | solution.py:182
  84.0 176.6 %all-gather.17.cloned.1.call-start = ((), (), s32[]{:S(2)}) async-start(), calls=%async_computation.16 | async-start | bytes 12976128 | tf_op jit(solution)/shard_map/all_gather | solution.py:182
  104.0 193.5 %all-gather.11.cloned.1.call-start = ((), (), s32[]{:S(2)}) async-start(), calls=%async_computation.7 | async-start | bytes 6488064 | tf_op jit(solution)/shard_map/all_gather | solution.py:190
  104.6 295.5 %reduce-scatter.7.cloned.1.call-start = ((), (), s32[]{:S(2)}) async-start(), calls=%async_computation.8 | async-start | bytes 3604480 | tf_op jit(solution)/shard_map/reduce_scatter | solution.py:199
  108.9 23.2 %collective-permute-start.21 = (bf16[128,2048]{1,0:T(8,128)(2,1)}, bf16[128,2048]{1,0:T(8,128)(2,1)}, u32[]{:S(2)}, u32[]{:S(2)}) collective-permute-start(bf16[128,2048]{1,0:T(8,128)(2,1)} %get-tuple-element.675), channel_id=1, source_target_pairs={{0,4},{4,0},{1,5},{5,1},{2,6},{6,2},{3,7},{7,3},{8,12},{12,8},{9,1... | collective-permute-start | bytes 1572872 | tf_op jit(solution)/shard_map/ppermute | solution.py:67
  145.9 35.6 %collective-permute-start.25 = (bf16[128,2048]{1,0:T(8,128)(2,1)S(1)}, bf16[128,2048]{1,0:T(8,128)(2,1)S(1)}, u32[]{:S(2)}, u32[]{:S(2)}) collective-permute-start(bf16[128,2048]{1,0:T(8,128)(2,1)S(1)} %get-tuple-element.415.refs_0_), channel_id=1, source_target_pairs={{0,8},{8,0},{16,24},{24,16},{1,9},{9,1},{17,25},{25,17},{2,10},{10... | collective-permute-start | bytes 1572872 | tf_op jit(solution)/shard_map/ppermute | solution.py:72
  147.1 34.3 %collective-permute-start.27 = (bf16[128,2048]{1,0:T(8,128)(2,1)S(1)}, bf16[128,2048]{1,0:T(8,128)(2,1)}, u32[]{:S(2)}, u32[]{:S(2)}) collective-permute-start(bf16[128,2048]{1,0:T(8,128)(2,1)S(1)} %get-tuple-element.415.refs_0_), channel_id=1, source_target_pairs={{0,16},{8,24},{16,0},{24,8},{1,17},{9,25},{17,1},{25,9},{2,18},{10... | collective-permute-start | bytes 1572872 | tf_op jit(solution)/shard_map/ppermute | solution.py:72
  148.2 33.2 %collective-permute-start.26 = (bf16[128,2048]{1,0:T(8,128)(2,1)S(1)}, bf16[128,2048]{1,0:T(8,128)(2,1)}, u32[]{:S(2)}, u32[]{:S(2)}) collective-permute-start(bf16[128,2048]{1,0:T(8,128)(2,1)S(1)} %get-tuple-element.416.refs_1_), channel_id=1, source_target_pairs={{0,8},{8,0},{16,24},{24,16},{1,9},{9,1},{17,25},{25,17},{2,10},{10... | collective-permute-start | bytes 1572872 | tf_op jit(solution)/shard_map/ppermute | solution.py:72
  149.4 32.0 %collective-permute-start.28 = (bf16[128,2048]{1,0:T(8,128)(2,1)S(1)}, bf16[128,2048]{1,0:T(8,128)(2,1)}, u32[]{:S(2)}, u32[]{:S(2)}) collective-permute-start(bf16[128,2048]{1,0:T(8,128)(2,1)S(1)} %get-tuple-element.416.refs_1_), channel_id=1, source_target_pairs={{0,16},{8,24},{16,0},{24,8},{1,17},{9,25},{17,1},{25,9},{2,18},{10... | collective-permute-start | bytes 1572872 | tf_op jit(solution)/shard_map/ppermute | solution.py:72
  183.8 20.0 %collective-permute-start.31 = (bf16[128,2048]{1,0:T(8,128)(2,1)}, bf16[128,2048]{1,0:T(8,128)(2,1)}, u32[]{:S(2)}, u32[]{:S(2)}) collective-permute-start(bf16[128,2048]{1,0:T(8,128)(2,1)} %get-tuple-element.386), channel_id=1, source_target_pairs={{0,8},{8,0},{16,24},{24,16},{1,9},{9,1},{17,25},{25,17},{2,10},{10... | collective-permute-start | bytes 1572872 | tf_op jit(solution)/shard_map/ppermute | solution.py:72
  224.2 23.4 %collective-permute-start.36 = (bf16[128,2048]{1,0:T(8,128)(2,1)S(1)}, bf16[128,2048]{1,0:T(8,128)(2,1)S(1)}, u32[]{:S(2)}, u32[]{:S(2)}) collective-permute-start(bf16[128,2048]{1,0:T(8,128)(2,1)S(1)} %get-tuple-element.670.refs_1_), channel_id=1, source_target_pairs={{0,8},{8,0},{16,24},{24,16},{1,9},{9,1},{17,25},{25,17},{2,10},{10... | collective-permute-start | bytes 1572872 | tf_op jit(solution)/shard_map/ppermute | solution.py:72
  225.5 23.1 %collective-permute-start.37 = (bf16[128,2048]{1,0:T(8,128)(2,1)S(1)}, bf16[128,2048]{1,0:T(8,128)(2,1)S(1)}, u32[]{:S(2)}, u32[]{:S(2)}) collective-permute-start(bf16[128,2048]{1,0:T(8,128)(2,1)S(1)} %get-tuple-element.671.refs_0_), channel_id=1, source_target_pairs={{0,16},{8,24},{16,0},{24,8},{1,17},{9,25},{17,1},{25,9},{2,18},{10... | collective-permute-start | bytes 1572872 | tf_op jit(solution)/shard_map/ppermute | solution.py:72
  258.1 24.0 %collective-permute-start.41 = (bf16[128,2048]{1,0:T(8,128)(2,1)S(1)}, bf16[128,2048]{1,0:T(8,128)(2,1)S(1)}, u32[]{:S(2)}, u32[]{:S(2)}) collective-permute-start(bf16[128,2048]{1,0:T(8,128)(2,1)S(1)} %collective-permute-done.25.refs_2_), channel_id=1, source_target_pairs={{0,16},{8,24},{16,0},{24,8},{1,17},{9,25},{17,1},{25,9},{2,18},{10... | collective-permute-start | bytes 1572872 | tf_op jit(solution)/shard_map/ppermute | solution.py:72
  258.6 23.5 %collective-permute-start.42 = (bf16[128,2048]{1,0:T(8,128)(2,1)}, bf16[128,2048]{1,0:T(8,128)(2,1)S(1)}, u32[]{:S(2)}, u32[]{:S(2)}) collective-permute-start(bf16[128,2048]{1,0:T(8,128)(2,1)} %collective-permute-done.28.refs_5_), channel_id=1, source_target_pairs={{0,8},{8,0},{16,24},{24,16},{1,9},{9,1},{17,25},{25,17},{2,10},{10... | collective-permute-start | bytes 1572872 | tf_op jit(solution)/shard_map/ppermute | solution.py:72
  312.8 143.7 %reduce-scatter.9.cloned.1.call-start = ((), (), s32[]{:S(2)}) async-start(), calls=%async_computation.9 | async-start | bytes 3604480 | tf_op jit(solution)/shard_map/reduce_scatter | solution.py:199
  313.0 22.3 %collective-permute-start.44 = (bf16[640,384]{1,0:T(8,128)(2,1)S(1)}, bf16[640,384]{1,0:T(8,128)(2,1)}, u32[]{:S(2)}, u32[]{:S(2)}) collective-permute-start(bf16[640,384]{1,0:T(8,128)(2,1)S(1)} %get-tuple-element.587.refs_0_), channel_id=1, source_target_pairs={{0,8},{8,0},{16,24},{24,16},{1,9},{9,1},{17,25},{25,17},{2,10},{10... | collective-permute-start | bytes 1474568 | tf_op jit(solution)/shard_map/ppermute | solution.py:72
  313.6 23.6 %collective-permute-start.45 = (bf16[640,384]{1,0:T(8,128)(2,1)S(1)}, bf16[640,384]{1,0:T(8,128)(2,1)S(1)}, u32[]{:S(2)}, u32[]{:S(2)}) collective-permute-start(bf16[640,384]{1,0:T(8,128)(2,1)S(1)} %get-tuple-element.588.refs_1_), channel_id=1, source_target_pairs={{0,8},{8,0},{16,24},{24,16},{1,9},{9,1},{17,25},{25,17},{2,10},{10... | collective-permute-start | bytes 1474568 | tf_op jit(solution)/shard_map/ppermute | solution.py:72
  315.1 22.1 %collective-permute-start.46 = (bf16[640,384]{1,0:T(8,128)(2,1)S(1)}, bf16[640,384]{1,0:T(8,128)(2,1)S(1)}, u32[]{:S(2)}, u32[]{:S(2)}) collective-permute-start(bf16[640,384]{1,0:T(8,128)(2,1)S(1)} %get-tuple-element.587.refs_0_), channel_id=1, source_target_pairs={{0,16},{8,24},{16,0},{24,8},{1,17},{9,25},{17,1},{25,9},{2,18},{10... | collective-permute-start | bytes 1474568 | tf_op jit(solution)/shard_map/ppermute | solution.py:72
  315.9 22.9 %collective-permute-start.47 = (bf16[640,384]{1,0:T(8,128)(2,1)S(1)}, bf16[640,384]{1,0:T(8,128)(2,1)}, u32[]{:S(2)}, u32[]{:S(2)}) collective-permute-start(bf16[640,384]{1,0:T(8,128)(2,1)S(1)} %get-tuple-element.588.refs_1_), channel_id=1, source_target_pairs={{0,16},{8,24},{16,0},{24,8},{1,17},{9,25},{17,1},{25,9},{2,18},{10... | collective-permute-start | bytes 1474568 | tf_op jit(solution)/shard_map/ppermute | solution.py:72
  338.8 31.9 %collective-permute-start.48 = (bf16[128,2048]{1,0:T(8,128)(2,1)}, bf16[128,2048]{1,0:T(8,128)(2,1)S(1)}, u32[]{:S(2)}, u32[]{:S(2)}) collective-permute-start(bf16[128,2048]{1,0:T(8,128)(2,1)} %get-tuple-element.453), channel_id=1, source_target_pairs={{0,8},{8,0},{16,24},{24,16},{1,9},{9,1},{17,25},{25,17},{2,10},{10... | collective-permute-start | bytes 1572872 | tf_op jit(solution)/shard_map/ppermute | solution.py:72
  339.3 31.4 %collective-permute-start.49 = (bf16[128,2048]{1,0:T(8,128)(2,1)}, bf16[128,2048]{1,0:T(8,128)(2,1)S(1)}, u32[]{:S(2)}, u32[]{:S(2)}) collective-permute-start(bf16[128,2048]{1,0:T(8,128)(2,1)} %get-tuple-element.455), channel_id=1, source_target_pairs={{0,16},{8,24},{16,0},{24,8},{1,17},{9,25},{17,1},{25,9},{2,18},{10... | collective-permute-start | bytes 1572872 | tf_op jit(solution)/shard_map/ppermute | solution.py:72
  340.9 29.8 %collective-permute-start.50 = (bf16[128,2048]{1,0:T(8,128)(2,1)}, bf16[128,2048]{1,0:T(8,128)(2,1)S(1)}, u32[]{:S(2)}, u32[]{:S(2)}) collective-permute-start(bf16[128,2048]{1,0:T(8,128)(2,1)} %get-tuple-element.457), channel_id=1, source_target_pairs={{0,8},{8,0},{16,24},{24,16},{1,9},{9,1},{17,25},{25,17},{2,10},{10... | collective-permute-start | bytes 1572872 | tf_op jit(solution)/shard_map/ppermute | solution.py:72
  341.6 29.1 %collective-permute-start.51 = (bf16[128,2048]{1,0:T(8,128)(2,1)}, bf16[128,2048]{1,0:T(8,128)(2,1)S(1)}, u32[]{:S(2)}, u32[]{:S(2)}) collective-permute-start(bf16[128,2048]{1,0:T(8,128)(2,1)} %get-tuple-element.459), channel_id=1, source_target_pairs={{0,16},{8,24},{16,0},{24,8},{1,17},{9,25},{17,1},{25,9},{2,18},{10... | collective-permute-start | bytes 1572872 | tf_op jit(solution)/shard_map/ppermute | solution.py:72
  380.5 143.1 %reduce-scatter.11.cloned.1.call-start = ((), (), s32[]{:S(2)}) async-start(), calls=%async_computation.10 | async-start | bytes 3604480 | tf_op jit(solution)/shard_map/reduce_scatter | solution.py:199
  400.2 150.2 %reduce-scatter.13.cloned.1.call-start = ((), (), s32[]{:S(2)}) async-start(), calls=%async_computation.11 | async-start | bytes 2621440 | tf_op jit(solution)/shard_map/reduce_scatter | solution.py:199
  408.3 28.3 %collective-permute-start.57 = (bf16[128,2048]{1,0:T(8,128)(2,1)S(1)}, bf16[128,2048]{1,0:T(8,128)(2,1)S(1)}, u32[]{:S(2)}, u32[]{:S(2)}) collective-permute-start(bf16[128,2048]{1,0:T(8,128)(2,1)S(1)} %get-tuple-element.668.refs_1_), channel_id=1, source_target_pairs={{0,8},{8,0},{16,24},{24,16},{1,9},{9,1},{17,25},{25,17},{2,10},{10... | collective-permute-start | bytes 1572872 | tf_op jit(solution)/shard_map/ppermute | solution.py:72
  409.9 26.7 %collective-permute-start.58 = (bf16[128,2048]{1,0:T(8,128)(2,1)S(1)}, bf16[128,2048]{1,0:T(8,128)(2,1)S(1)}, u32[]{:S(2)}, u32[]{:S(2)}) collective-permute-start(bf16[128,2048]{1,0:T(8,128)(2,1)S(1)} %get-tuple-element.669.refs_0_), channel_id=1, source_target_pairs={{0,16},{8,24},{16,0},{24,8},{1,17},{9,25},{17,1},{25,9},{2,18},{10... | collective-permute-start | bytes 1572872 | tf_op jit(solution)/shard_map/ppermute | solution.py:72
  421.4 22.0 %collective-permute-start.60 = (bf16[128,2048]{1,0:T(8,128)(2,1)S(1)}, bf16[128,2048]{1,0:T(8,128)(2,1)S(1)}, u32[]{:S(2)}, u32[]{:S(2)}) collective-permute-start(bf16[128,2048]{1,0:T(8,128)(2,1)S(1)} %collective-permute-done.56.refs_2_), channel_id=1, source_target_pairs={{0,16},{8,24},{16,0},{24,8},{1,17},{9,25},{17,1},{25,9},{2,18},{10... | collective-permute-start | bytes 1572872 | tf_op jit(solution)/shard_map/ppermute | solution.py:72
  422.8 20.6 %collective-permute-start.61 = (bf16[128,2048]{1,0:T(8,128)(2,1)S(1)}, bf16[128,2048]{1,0:T(8,128)(2,1)S(1)}, u32[]{:S(2)}, u32[]{:S(2)}) collective-permute-start(bf16[128,2048]{1,0:T(8,128)(2,1)S(1)} %collective-permute-done.59.refs_5_), channel_id=1, source_target_pairs={{0,8},{8,0},{16,24},{24,16},{1,9},{9,1},{17,25},{25,17},{2,10},{10... | collective-permute-start | bytes 1572872 | tf_op jit(solution)/shard_map/ppermute | solution.py:72
  458.5 33.8 %collective-permute-start.64 = (bf16[128,2048]{1,0:T(8,128)(2,1)}, bf16[128,2048]{1,0:T(8,128)(2,1)}, u32[]{:S(2)}, u32[]{:S(2)}) collective-permute-start(bf16[128,2048]{1,0:T(8,128)(2,1)} %get-tuple-element.517), channel_id=1, source_target_pairs={{0,16},{8,24},{16,0},{24,8},{1,17},{9,25},{17,1},{25,9},{2,18},{10... | collective-permute-start | bytes 1572872 | tf_op jit(solution)/shard_map/ppermute | solution.py:72
  459.7 32.6 %collective-permute-start.65 = (bf16[128,2048]{1,0:T(8,128)(2,1)}, bf16[128,2048]{1,0:T(8,128)(2,1)}, u32[]{:S(2)}, u32[]{:S(2)}) collective-permute-start(bf16[128,2048]{1,0:T(8,128)(2,1)} %get-tuple-element.519), channel_id=1, source_target_pairs={{0,8},{8,0},{16,24},{24,16},{1,9},{9,1},{17,25},{25,17},{2,10},{10... | collective-permute-start | bytes 1572872 | tf_op jit(solution)/shard_map/ppermute | solution.py:72
  460.2 32.1 %collective-permute-start.66 = (bf16[128,2048]{1,0:T(8,128)(2,1)}, bf16[128,2048]{1,0:T(8,128)(2,1)}, u32[]{:S(2)}, u32[]{:S(2)}) collective-permute-start(bf16[128,2048]{1,0:T(8,128)(2,1)} %get-tuple-element.521), channel_id=1, source_target_pairs={{0,16},{8,24},{16,0},{24,8},{1,17},{9,25},{17,1},{25,9},{2,18},{10... | collective-permute-start | bytes 1572872 | tf_op jit(solution)/shard_map/ppermute | solution.py:72
  472.8 21.9 %collective-permute-start.67 = (bf16[640,384]{1,0:T(8,128)(2,1)}, bf16[640,384]{1,0:T(8,128)(2,1)}, u32[]{:S(2)}, u32[]{:S(2)}) collective-permute-start(bf16[640,384]{1,0:T(8,128)(2,1)} %collective-permute-done.44.refs_2_), channel_id=1, source_target_pairs={{0,16},{8,24},{16,0},{24,8},{1,17},{9,25},{17,1},{25,9},{2,18},{10... | collective-permute-start | bytes 1474568 | tf_op jit(solution)/shard_map/ppermute | solution.py:72
  473.1 21.5 %collective-permute-start.68 = (bf16[640,384]{1,0:T(8,128)(2,1)}, bf16[640,384]{1,0:T(8,128)(2,1)}, u32[]{:S(2)}, u32[]{:S(2)}) collective-permute-start(bf16[640,384]{1,0:T(8,128)(2,1)} %collective-permute-done.47.refs_5_), channel_id=1, source_target_pairs={{0,8},{8,0},{16,24},{24,16},{1,9},{9,1},{17,25},{25,17},{2,10},{10... | collective-permute-start | bytes 1474568 | tf_op jit(solution)/shard_map/ppermute | solution.py:72
  476.0 114.3 %reduce-scatter.15.cloned.1.call-start = ((), (), s32[]{:S(2)}) async-start(), calls=%async_computation.12 | async-start | bytes 1310720 | tf_op jit(solution)/shard_map/reduce_scatter | solution.py:199
  494.8 24.0 %collective-permute-start.73 = (bf16[128,2048]{1,0:T(8,128)(2,1)S(1)}, bf16[128,2048]{1,0:T(8,128)(2,1)S(1)}, u32[]{:S(2)}, u32[]{:S(2)}) collective-permute-start(bf16[128,2048]{1,0:T(8,128)(2,1)S(1)} %add_convert_fusion.7), channel_id=1, source_target_pairs={{0,16},{8,24},{16,0},{24,8},{1,17},{9,25},{17,1},{25,9},{2,18},{10... | collective-permute-start | bytes 1572872 | tf_op jit(solution)/shard_map/ppermute | solution.py:72
  497.3 23.5 %collective-permute-start.74 = (bf16[128,2048]{1,0:T(8,128)(2,1)S(1)}, bf16[128,2048]{1,0:T(8,128)(2,1)S(1)}, u32[]{:S(2)}, u32[]{:S(2)}) collective-permute-start(bf16[128,2048]{1,0:T(8,128)(2,1)S(1)} %add_convert_fusion.6), channel_id=1, source_target_pairs={{0,8},{8,0},{16,24},{24,16},{1,9},{9,1},{17,25},{25,17},{2,10},{10... | collective-permute-start | bytes 1572872 | tf_op jit(solution)/shard_map/ppermute | solution.py:72
  533.3 40.6 %collective-permute-start.84 = (bf16[5120,384]{1,0:T(8,128)(2,1)}, bf16[5120,384]{1,0:T(8,128)(2,1)}, u32[]{:S(2)}, u32[]{:S(2)}) collective-permute-start(bf16[5120,384]{1,0:T(8,128)(2,1)} %shard_map.258), channel_id=1, source_target_pairs={{0,4},{4,0},{1,5},{5,1},{2,6},{6,2},{3,7},{7,3},{8,12},{12,8},{9,1... | collective-permute-start | bytes 11796488 | tf_op jit(solution)/shard_map/ppermute | solution.py:67
  539.2 23.3 %collective-permute-start.75 = (bf16[128,2048]{1,0:T(8,128)(2,1)}, bf16[128,2048]{1,0:T(8,128)(2,1)}, u32[]{:S(2)}, u32[]{:S(2)}) collective-permute-start(bf16[128,2048]{1,0:T(8,128)(2,1)} %get-tuple-element.663), channel_id=1, source_target_pairs={{0,4},{4,0},{1,5},{5,1},{2,6},{6,2},{3,7},{7,3},{8,12},{12,8},{9,1... | collective-permute-start | bytes 1572872 | tf_op jit(solution)/shard_map/ppermute | solution.py:67
  556.8 54.7 %reduce-scatter.17.cloned.1.call-start = ((), (), s32[]{:S(2)}) async-start(), calls=%async_computation.13 | async-start | bytes 983040 | tf_op jit(solution)/shard_map/reduce_scatter | solution.py:199
  596.2 20.0 %collective-permute-start.85 = (f32[128,2048]{1,0:T(8,128)S(1)}, f32[128,2048]{1,0:T(8,128)S(1)}, u32[]{:S(2)}, u32[]{:S(2)}) collective-permute-start(f32[128,2048]{1,0:T(8,128)S(1)} %get-tuple-element.647), channel_id=1, source_target_pairs={{0,4},{4,0},{1,5},{5,1},{2,6},{6,2},{3,7},{7,3},{8,12},{12,8},{9,1... | collective-permute-start | bytes 3145736 | tf_op jit(solution)/shard_map/ppermute | solution.py:67
  (181 other events, 1843.7 us)
Sparse Core Ops, SparseCore 0:
  9.7 49.8 all-gather.8
  61.8 26.7 all-gather.12
  90.7 28.6 all-gather.14
  121.4 107.5 all-gather.16
  230.4 58.6 all-gather.10
  312.9 54.0 reduce-scatter.6
  380.6 53.9 reduce-scatter.8
  436.9 56.0 reduce-scatter.10
  495.3 43.7 reduce-scatter.12
  557.0 24.6 reduce-scatter.14
  590.4 21.1 reduce-scatter.16

commit v6 on v5

--- a/solution.py
+++ b/solution.py
@@ -432,7 +432,7 @@
         in_specs=[pl.BlockSpec(left.shape, lambda i: (0, 0)), source],
         out_specs=[pl.BlockSpec((shape[0], TILE), lambda i: (0, i))] * count,
         out_shape=[jax.ShapeDtypeStruct(shape, bf16)] * count,
-        compiler_params=pltpu.CompilerParams(vmem_limit_bytes=56 << 20),
+        compiler_params=pltpu.CompilerParams(vmem_limit_bytes=34 << 20),
         cost_estimate=BESIDE,
     )(left, right)
     return results if pieces else results[0]
@@ -476,7 +476,7 @@
     place = jnp.stack([jnp.int32(0) if flip is None else flip, core])
     params = dict(
         out_shape=[jax.ShapeDtypeStruct(half, bf16)] * 2,
-        compiler_params=pltpu.CompilerParams(vmem_limit_bytes=56 << 20),
+        compiler_params=pltpu.CompilerParams(vmem_limit_bytes=34 << 20),
         cost_estimate=BESIDE,
     )
     if tile % 128 == 0 and width % 128 == 0 and rows % (CORES * tile) == 0:
@@ -588,7 +588,7 @@
             out_specs=[pl.BlockSpec((shape[0], depth), lambda i, f: (0, i))] * (2 * chips),
         ),
         out_shape=[jax.ShapeDtypeStruct(shape, bf16)] * (2 * chips),
-        compiler_params=pltpu.CompilerParams(vmem_limit_bytes=56 << 20),
+        compiler_params=pltpu.CompilerParams(vmem_limit_bytes=34 << 20),
         cost_estimate=BESIDE,
     )(chip_flip()[None], *lefts, weight)
 

time: 639 us -> 630 us (0.986)
  Pallas kernels: 215 us -> 188 us
  local copies, waits for them, and re-layouts: 33 us -> 51.9 us
    unnamed x247 -> x303, local copies, waits for them, and re-layouts: 14.5 us -> 31.1 us
    pallas_call x5, Pallas kernels: 56 us -> 40.2 us  [weight_terms(): pl.pallas_call(functools.partial(terms_kernel, scale), grid_spec=pltpu.Pr...]
    pallas_call x3, Pallas kernels: 29.6 us -> 22 us  [product(): pl.pallas_call(functools.partial(product_kernel, kind), grid=(width // TI...]
  transfers between devices with their start and end apart: 107 -> 107, of which waited for: 50 -> 47; matrix products, arithmetic and copies ran while one was open for 15% -> 16% of each run, Pallas kernels for 34% -> 30%
where the time goes in v6:
time: 630 us; the launch traced here: 622 us
  Pallas kernels  188 us (30%)
  waiting for transfers between devices  183 us (29%)
  starting transfers between devices  99.2 us (16%)
  other arithmetic  82.4 us (13%)
  local copies, waits for them, and re-layouts  51.9 us (8%)
  between operations  16.3 us (3%)
    ppermute x85, waiting for transfers between devices, to_chip(): return lax.ppermute(block, 'chip', [(i, i ^ bits) for i in range(count)])  165 us
    ppermute x85, starting transfers between devices, to_chip(): return lax.ppermute(block, 'chip', [(i, i ^ bits) for i in range(count)])  96.3 us
    pallas_call x5, Pallas kernels, weight_terms(): pl.pallas_call(functools.partial(terms_kernel, scale), grid_spec=pltpu.Pr...  40.2 us
    unnamed x303, local copies, waits for them, and re-layouts  31.1 us
    pallas_call x3, Pallas kernels, product(): pl.pallas_call(functools.partial(product_kernel, kind), grid=(width // TI...  22 us
    pallas_call x1, Pallas kernels, attend(): pl.pallas_call(functools.partial(attend_kernel, score_scale), grid=(heads...  18.8 us
    pallas_call x1, Pallas kernels, gated(): pl.pallas_call(gate_kernel, grid_spec=pltpu.PrefetchScalarGridSpec(num_sc...  18.3 us
    pallas_call x1, Pallas kernels, spread(): pl.pallas_call(functools.partial(spread_kernel, len(lefts)), grid_spec=pl...  16.1 us
  transfers between devices with their start and end apart: 107, of which 47 were waited for; matrix products, arithmetic and copies ran while one was open for 16% of the time, Pallas kernels for 30%

profile of v6, /device:TPU:0, one launch (start us, length us, event | category | flops | bytes accessed | tf_op | source)
XLA Modules:
  0.0 621.8 jit_solution(464834647257975970)
XLA Ops:
  11.2 3.8 shard_map.237
  17.1 2.5 collective-permute-start.4
  25.6 19.4 %collective-permute-done.1 = bf16[80,384]{1,0:T(8,128)(2,1)S(1)} collective-permute-done((bf16[80,384]{1,0:T(8,128)(2,1)S(1)}, bf16[80,384]{1,0:T(8,128)(2,1)S(1)}, u32[]{:S(2)}, u32[]{:S(2)}) %collective-permute-start.1) | collective-permute-done | bytes 61472 | tf_op jit(solution)/shard_map/ppermute | solution.py:72
  49.2 2.7 collective-permute-start.3
  54.3 5.3 all-gather.9.cloned.1.call-done.right_ref
  63.4 11.3 %collective-permute-done.8.refs_6_ = bf16[128,2048]{1,0:T(8,128)(2,1)S(1)} collective-permute-done((bf16[128,2048]{1,0:T(8,128)(2,1)}, bf16[128,2048]{1,0:T(8,128)(2,1)S(1)}, u32[]{:S(2)}, u32[]{:S(2)}) %collective-permute-start.8) | collective-permute-done | bytes 524320 | tf_op jit(solution)/shard_map/ppermute | solution.py:72
  91.5 8.2 %shard_map.238 = (bf16[1024,2048]{1,0:T(8,128)(2,1)}, f32[1024,256]{1,0:T(8,128)}, f32[1024,128]{1,0:T(8,128)}) custom-call(s32[1]{0:T(128)} %bitcast.1._.flip_ref, bf16[128,2048]{1,0:T(8,128)(2,1)} %get-tuple-element.338.refs_0_, bf16[128,2048]{1,0:T(8,128)(2,1)} %copy-done.91, bf16[128,2048]{1,0:T(8,128)(2,1)} %collective-permute-done.4.refs_2_, ...), custom_call_target="tpu_custom_call" | custom-call | flops 1 | bytes 1 | tf_op jit(solution)/shard_map/pallas_call | solution.py:715
  101.4 2.6 pad_maximum_fusion.2
  114.0 2.4 collective-permute-done.14
  122.5 7.2 %collective-permute-done.15.refs_2_ = bf16[512,384]{1,0:T(8,128)(2,1)S(1)} collective-permute-done((bf16[512,384]{1,0:T(8,128)(2,1)S(1)}, bf16[512,384]{1,0:T(8,128)(2,1)S(1)}, u32[]{:S(2)}, u32[]{:S(2)}) %collective-permute-start.15) | collective-permute-done | bytes 393248 | tf_op jit(solution)/shard_map/ppermute | solution.py:72
  133.6 4.5 collective-permute-done.16.refs_3_
  138.9 6.1 collective-permute-done.19.refs_6_
  153.0 18.8 %shard_map.240 = (bf16[1024,1024]{1,0:T(8,128)(2,1)}, bf16[1024,1024]{1,0:T(8,128)(2,1)}, f32[4,1,1024]{2,1,0:T(1,128)}) custom-call(s32[1]{0:T(128)} %bitcast.length_ref, s32[1]{0:T(128)} %bitcast.1._.flip_ref, bf16[4,1024,384]{2,1,0:T(8,128)(2,1)} %bitcast.149, bf16[4,256,1024]{2,1,0:T(8,128)(2,1)} %all-gather.15.cloned.1.call-done.up_ref, ...), custom_call_target="tpu_custom_call" | custom-call | flops 1 | bytes 1 | tf_op jit(solution)/shard_map/pallas_call | solution.py:290
  175.7 6.8 %shard_map.241 = (bf16[128,2048]{1,0:T(8,128)(2,1)S(1)}, bf16[128,2048]{1,0:T(8,128)(2,1)S(1)}, bf16[128,2048]{1,0:T(8,128)(2,1)S(1)}, bf16[128,2048]{1,0:T(8,12...) custom-call(bf16[1024,1024]{1,0:T(8,128)(2,1)S(1)} %copy-done.18, ...), custom_call_target="tpu_custom_call" | custom-call | flops 1 | bytes 1 | tf_op jit(solution)/shard_map/pallas_call | solution.py:429
  186.7 10.8 %collective-permute-done.29 = bf16[128,2048]{1,0:T(8,128)(2,1)S(1)} collective-permute-done((bf16[128,2048]{1,0:T(8,128)(2,1)S(1)}, bf16[128,2048]{1,0:T(8,128)(2,1)S(1)}, u32[]{:S(2)}, u32[]{:S(2)}) %collective-permute-start.29) | collective-permute-done | bytes 524320 | tf_op jit(solution)/shard_map/ppermute | solution.py:72
  198.7 5.9 collective-permute-done.31
  210.2 6.7 %collective-permute-done.33 = bf16[128,2048]{1,0:T(8,128)(2,1)} collective-permute-done((bf16[128,2048]{1,0:T(8,128)(2,1)}, bf16[128,2048]{1,0:T(8,128)(2,1)}, u32[]{:S(2)}, u32[]{:S(2)}) %collective-permute-start.33) | collective-permute-done | bytes 524320 | tf_op jit(solution)/shard_map/ppermute | solution.py:72
  225.6 10.8 %collective-permute-done.35.refs_2_ = bf16[128,2048]{1,0:T(8,128)(2,1)S(1)} collective-permute-done((bf16[128,2048]{1,0:T(8,128)(2,1)S(1)}, bf16[128,2048]{1,0:T(8,128)(2,1)S(1)}, u32[]{:S(2)}, u32[]{:S(2)}) %collective-permute-start.35) | collective-permute-done | bytes 524320 | tf_op jit(solution)/shard_map/ppermute | solution.py:72
  238.6 8.6 %collective-permute-done.36.refs_3_ = bf16[128,2048]{1,0:T(8,128)(2,1)S(1)} collective-permute-done((bf16[128,2048]{1,0:T(8,128)(2,1)S(1)}, bf16[128,2048]{1,0:T(8,128)(2,1)S(1)}, u32[]{:S(2)}, u32[]{:S(2)}) %collective-permute-start.36) | collective-permute-done | bytes 524320 | tf_op jit(solution)/shard_map/ppermute | solution.py:72
  247.7 6.5 %collective-permute-done.39.refs_6_ = bf16[128,2048]{1,0:T(8,128)(2,1)S(1)} collective-permute-done((bf16[128,2048]{1,0:T(8,128)(2,1)S(1)}, bf16[128,2048]{1,0:T(8,128)(2,1)S(1)}, u32[]{:S(2)}, u32[]{:S(2)}) %collective-permute-start.39) | collective-permute-done | bytes 524320 | tf_op jit(solution)/shard_map/ppermute | solution.py:72
  259.1 18.3 %shard_map.243 = (bf16[1024,1408]{1,0:T(8,128)(2,1)S(1)}, bf16[1024,1408]{1,0:T(8,128)(2,1)S(1)}, bf16[1024,1408]{1,0:T(8,128)(2,1)}) custom-call(s32[1]{0:T(128)} %bitcast.1._.flip_ref, bf16[1024,2048]{1,0:T(8,128)(2,1)} %copy-done.2, bf16[4,8,2,64,1408]{4,3,2,1,0:T(8,128)(2,1)} %bitcast.152), custom_call_target="tpu_custom_call" | custom-call | flops 1 | bytes 1 | tf_op jit(solution)/shard_map/pallas_call | solution.py:760
  277.4 3.2 shard_map.244.right_ref.seed_ref
  280.6 9.3 %shard_map.245 = (bf16[704,2048]{1,0:T(8,128)(2,1)S(1)}, bf16[704,2048]{1,0:T(8,128)(2,1)}) custom-call(s32[2]{0:T(128)S(1)} %pad_add_fusion.place_ref, bf16[1024,1408]{1,0:T(8,128)(2,1)S(1)} %get-tuple-element.489.left_ref, bf16[1024,2048]{1,0:T(8,128)(2,1)S(1)} %shard_map.244.right_ref.seed_ref), custom_call_target="tpu_custom_call" | custom-call | flops 1 | bytes 1 | tf_op jit(solution)/shard_map/pallas_call | solution.py:508
  294.6 11.6 %shard_map.246 = (bf16[1024,1408]{1,0:T(8,128)(2,1)S(1)}, bf16[1024,1408]{1,0:T(8,128)(2,1)S(1)}) custom-call(bf16[1024,2048]{1,0:T(8,128)(2,1)} %copy-done.6, bf16[1408,2048]{1,0:T(8,128)(2,1)} %all-gather.11.cloned.1.call-done.down_ref.right_ref, bf16[1024,1408]{1,0:T(8,128)(2,1)} %copy-done.29, bf16[1024,1408]{1,0:T(8,128)(2,1)} %get-tuple-element.428.slope_ref), custom_call_target="tpu_custom_call" | custom-call | flops 1 | bytes 1 | tf_op jit(solution)/shard_map/pallas_call | solution.py:789
  306.2 3.0 add_convert_fusion.2
  316.5 16.1 %shard_map.247 = (bf16[128,2048]{1,0:T(8,128)(2,1)S(1)}, bf16[128,2048]{1,0:T(8,128)(2,1)S(1)}, bf16[128,2048]{1,0:T(8,128)(2,1)S(1)}, bf16[128,2048]{1,0:T(8,12...) custom-call(s32[1]{0:T(128)} %bitcast.1._.flip_ref, ...), custom_call_target="tpu_custom_call" | custom-call | flops 1 | bytes 1 | tf_op jit(solution)/shard_map/pallas_call | solution.py:581
  340.5 10.9 %shard_map.249 = (bf16[4,4,64,1408]{3,2,1,0:T(8,128)(2,1)S(1)}, bf16[4,4,64,1408]{3,2,1,0:T(8,128)(2,1)S(1)}) custom-call(s32[2]{0:T(128)S(1)} %pad_add_fusion.1.place_ref, bf16[1024,2048]{1,0:T(8,128)(2,1)S(1)} %copy-done.3, bf16[1024,1408]{1,0:T(8,128)(2,1)S(1)} %copy-done.13), custom_call_target="tpu_custom_call" | custom-call | flops 1 | bytes 1 | tf_op jit(solution)/shard_map/pallas_call | solution.py:491
  353.1 11.0 %shard_map.248 = (bf16[4,4,64,1408]{3,2,1,0:T(8,128)(2,1)S(1)}, bf16[4,4,64,1408]{3,2,1,0:T(8,128)(2,1)S(1)}) custom-call(s32[2]{0:T(128)S(1)} %pad_add_fusion.1.place_ref, bf16[1024,2048]{1,0:T(8,128)(2,1)S(1)} %copy-done.3, bf16[1024,1408]{1,0:T(8,128)(2,1)S(1)} %get-tuple-element.460.refs_0_.right_ref), custom_call_target="tpu_custom_call" | custom-call | flops 1 | bytes 1 | tf_op jit(solution)/shard_map/pallas_call | solution.py:491
  364.3 5.3 collective-permute-done.52
  369.5 2.6 add_convert_fusion.1
  377.8 2.5 add_convert_fusion
  380.3 8.0 %collective-permute-done.53 = bf16[128,2048]{1,0:T(8,128)(2,1)S(1)} collective-permute-done((bf16[128,2048]{1,0:T(8,128)(2,1)S(1)}, bf16[128,2048]{1,0:T(8,128)(2,1)S(1)}, u32[]{:S(2)}, u32[]{:S(2)}) %collective-permute-start.53) | collective-permute-done | bytes 524320 | tf_op jit(solution)/shard_map/ppermute | solution.py:72
  402.7 10.8 %collective-permute-done.56.refs_2_ = bf16[128,2048]{1,0:T(8,128)(2,1)S(1)} collective-permute-done((bf16[128,2048]{1,0:T(8,128)(2,1)S(1)}, bf16[128,2048]{1,0:T(8,128)(2,1)S(1)}, u32[]{:S(2)}, u32[]{:S(2)}) %collective-permute-start.56) | collective-permute-done | bytes 524320 | tf_op jit(solution)/shard_map/ppermute | solution.py:72
  418.3 9.8 %shard_map.251 = (bf16[128,2048]{1,0:T(8,128)(2,1)S(1)}, bf16[128,2048]{1,0:T(8,128)(2,1)S(1)}, bf16[128,2048]{1,0:T(8,128)(2,1)}, bf16[128,2048]{1,0:T(8,128)(2...) custom-call(bf16[1024,1408]{1,0:T(8,128)(2,1)S(1)} %copy-done.15, ...), custom_call_target="tpu_custom_call" | custom-call | flops 1 | bytes 1 | tf_op jit(solution)/shard_map/pallas_call | solution.py:429
  428.1 6.7 %collective-permute-done.60.refs_6_ = bf16[128,2048]{1,0:T(8,128)(2,1)S(1)} collective-permute-done((bf16[128,2048]{1,0:T(8,128)(2,1)S(1)}, bf16[128,2048]{1,0:T(8,128)(2,1)S(1)}, u32[]{:S(2)}, u32[]{:S(2)}) %collective-permute-start.60) | collective-permute-done | bytes 524320 | tf_op jit(solution)/shard_map/ppermute | solution.py:72
  435.5 6.8 %shard_map.252 = (bf16[512,2048]{1,0:T(8,128)(2,1)S(1)}, bf16[512,2048]{1,0:T(8,128)(2,1)S(1)}) custom-call(s32[2]{0:T(128)S(1)} %pad_add_fusion.place_ref, bf16[1024,1024]{1,0:T(8,128)(2,1)S(1)} %copy-done.19, bf16[1024,2048]{1,0:T(8,128)(2,1)S(1)} %shard_map.250.right_ref.left_ref), custom_call_target="tpu_custom_call" | custom-call | flops 1 | bytes 1 | tf_op jit(solution)/shard_map/pallas_call | solution.py:491
  455.4 5.4 shard_map.253.grad_ref
  460.8 4.4 add_convert_fusion.3
  469.9 15.2 %shard_map.254 = (bf16[1024,1024]{1,0:T(8,128)(2,1)}, f32[1024,256]{1,0:T(8,128)S(1)}, f32[1024,256]{1,0:T(8,128)S(1)}) custom-call(s32[1]{0:T(128)} %bitcast.length_ref, s32[1]{0:T(128)} %bitcast.1._.flip_ref, bf16[1024,1024]{1,0:T(8,128)(2,1)} %get-tuple-element.369.queries_ref, bf16[1024,1024]{1,0:T(8,128)(2,1)} %copy-done.22, ...), custom_call_target="tpu_custom_call" | custom-call | flops 1 | bytes 1 | tf_op jit(solution)/shard_map/pallas_call | solution.py:367
  489.3 7.6 %shard_map.255 = (bf16[512,384]{1,0:T(8,128)(2,1)S(1)}, bf16[512,384]{1,0:T(8,128)(2,1)S(1)}, bf16[512,384]{1,0:T(8,128)(2,1)}, bf16[512,384]{1,0:T(8,128)(2,1)S...) custom-call(bf16[1024,1024]{1,0:T(8,128)(2,1)} %get-tuple-element.54, ...), custom_call_target="tpu_custom_call" | custom-call | flops 1 | bytes 1 | tf_op jit(solution)/shard_map/pallas_call | solution.py:550
  502.5 5.7 shard_map.256
  514.5 2.6 collective-permute-done.71
  518.1 5.2 shard_map.258
  529.4 6.7 %collective-permute-done.76 = bf16[512,384]{1,0:T(8,128)(2,1)S(1)} collective-permute-done((bf16[512,384]{1,0:T(8,128)(2,1)S(1)}, bf16[512,384]{1,0:T(8,128)(2,1)S(1)}, u32[]{:S(2)}, u32[]{:S(2)}) %collective-permute-start.76) | collective-permute-done | bytes 393248 | tf_op jit(solution)/shard_map/ppermute | solution.py:72
  560.4 5.7 shard_map.257
  572.0 7.2 %shard_map.259 = f32[256,2048]{1,0:T(8,128)S(1)} custom-call(s32[2]{0:T(128)S(1)} %pad_add_fusion.1.place_ref, bf16[256,384]{1,0:T(8,128)(2,1)S(1)} %get-tuple-element.595.refs_0_, bf16[256,384]{1,0:T(8,128)(2,1)S(1)} %collective-permute-done.81.refs_1_, bf16[256,384]{1,0:T(8,128)(2,1)S(1)} %collective-permute-done.82.refs_2_, ...), custom_call_target="tpu_custom_call" | custom-call | flops 1 | bytes 1 | tf_op jit(solution)/shard_map/pallas_call | solution.py:621
  599.8 4.1 reduce-scatter.17.cloned.1.call-done
  605.0 2.5 collective-permute-start.87
  (641 shorter events, 246.4 us)
Async XLA Ops:
  7.3 52.3 %all-gather.9.cloned.1.call-start = ((), (), s32[]{:S(2)}) async-start(), calls=%async_computation.6 | async-start | bytes 4718592 | tf_op jit(solution)/shard_map/all_gather | solution.py:190
  8.0 80.5 %all-gather.13.cloned.1.call-start = ((), (), s32[]{:S(2)}) async-start(), calls=%async_computation.14 | async-start | bytes 2211840 | tf_op jit(solution)/shard_map/all_gather | solution.py:182
  17.1 37.2 %collective-permute-start.4 = (bf16[128,2048]{1,0:T(8,128)(2,1)}, bf16[128,2048]{1,0:T(8,128)(2,1)}, u32[]{:S(2)}, u32[]{:S(2)}) collective-permute-start(bf16[128,2048]{1,0:T(8,128)(2,1)} %get-tuple-element.338.refs_0_), channel_id=1, source_target_pairs={{0,8},{8,0},{16,24},{24,16},{1,9},{9,1},{17,25},{25,17},{2,10},{10... | collective-permute-start | bytes 1572872 | tf_op jit(solution)/shard_map/ppermute | solution.py:72
  19.6 34.7 %collective-permute-start.6 = (bf16[128,2048]{1,0:T(8,128)(2,1)}, bf16[128,2048]{1,0:T(8,128)(2,1)}, u32[]{:S(2)}, u32[]{:S(2)}) collective-permute-start(bf16[128,2048]{1,0:T(8,128)(2,1)} %get-tuple-element.338.refs_0_), channel_id=1, source_target_pairs={{0,16},{8,24},{16,0},{24,8},{1,17},{9,25},{17,1},{25,9},{2,18},{10... | collective-permute-start | bytes 1572872 | tf_op jit(solution)/shard_map/ppermute | solution.py:72
  21.1 33.2 %collective-permute-start.5 = (bf16[128,2048]{1,0:T(8,128)(2,1)S(1)}, bf16[128,2048]{1,0:T(8,128)(2,1)}, u32[]{:S(2)}, u32[]{:S(2)}) collective-permute-start(bf16[128,2048]{1,0:T(8,128)(2,1)S(1)} %get-tuple-element.339.refs_1_), channel_id=1, source_target_pairs={{0,8},{8,0},{16,24},{24,16},{1,9},{9,1},{17,25},{25,17},{2,10},{10... | collective-permute-start | bytes 1572872 | tf_op jit(solution)/shard_map/ppermute | solution.py:72
  21.7 32.6 %collective-permute-start.7 = (bf16[128,2048]{1,0:T(8,128)(2,1)S(1)}, bf16[128,2048]{1,0:T(8,128)(2,1)}, u32[]{:S(2)}, u32[]{:S(2)}) collective-permute-start(bf16[128,2048]{1,0:T(8,128)(2,1)S(1)} %get-tuple-element.339.refs_1_), channel_id=1, source_target_pairs={{0,16},{8,24},{16,0},{24,8},{1,17},{9,25},{17,1},{25,9},{2,18},{10... | collective-permute-start | bytes 1572872 | tf_op jit(solution)/shard_map/ppermute | solution.py:72
  21.7 23.3 %collective-permute-start.1 = (bf16[80,384]{1,0:T(8,128)(2,1)S(1)}, bf16[80,384]{1,0:T(8,128)(2,1)S(1)}, u32[]{:S(2)}, u32[]{:S(2)}) collective-permute-start(bf16[80,384]{1,0:T(8,128)(2,1)S(1)} %copy-done.147), channel_id=1, source_target_pairs={{0,8},{8,0},{16,24},{24,16},{1,9},{9,1},{17,25},{25,17},{2,10},{10... | collective-permute-start | bytes 184328 | tf_op jit(solution)/shard_map/ppermute | solution.py:72
  60.3 92.7 %all-gather.15.cloned.1.call-start = ((), (), s32[]{:S(2)}) async-start(), calls=%async_computation.15 | async-start | bytes 2359296 | tf_op jit(solution)/shard_map/all_gather | solution.py:182
  84.0 175.1 %all-gather.17.cloned.1.call-start = ((), (), s32[]{:S(2)}) async-start(), calls=%async_computation.16 | async-start | bytes 12976128 | tf_op jit(solution)/shard_map/all_gather | solution.py:182
  104.0 189.5 %all-gather.11.cloned.1.call-start = ((), (), s32[]{:S(2)}) async-start(), calls=%async_computation.7 | async-start | bytes 6488064 | tf_op jit(solution)/shard_map/all_gather | solution.py:190
  104.6 287.6 %reduce-scatter.7.cloned.1.call-start = ((), (), s32[]{:S(2)}) async-start(), calls=%async_computation.8 | async-start | bytes 3604480 | tf_op jit(solution)/shard_map/reduce_scatter | solution.py:199
  108.8 23.2 %collective-permute-start.21 = (bf16[128,2048]{1,0:T(8,128)(2,1)}, bf16[128,2048]{1,0:T(8,128)(2,1)}, u32[]{:S(2)}, u32[]{:S(2)}) collective-permute-start(bf16[128,2048]{1,0:T(8,128)(2,1)} %get-tuple-element.675), channel_id=1, source_target_pairs={{0,4},{4,0},{1,5},{5,1},{2,6},{6,2},{3,7},{7,3},{8,12},{12,8},{9,1... | collective-permute-start | bytes 1572872 | tf_op jit(solution)/shard_map/ppermute | solution.py:67
  145.8 36.7 %collective-permute-start.25 = (bf16[128,2048]{1,0:T(8,128)(2,1)S(1)}, bf16[128,2048]{1,0:T(8,128)(2,1)S(1)}, u32[]{:S(2)}, u32[]{:S(2)}) collective-permute-start(bf16[128,2048]{1,0:T(8,128)(2,1)S(1)} %get-tuple-element.415.refs_0_), channel_id=1, source_target_pairs={{0,8},{8,0},{16,24},{24,16},{1,9},{9,1},{17,25},{25,17},{2,10},{10... | collective-permute-start | bytes 1572872 | tf_op jit(solution)/shard_map/ppermute | solution.py:72
  147.1 35.4 %collective-permute-start.27 = (bf16[128,2048]{1,0:T(8,128)(2,1)S(1)}, bf16[128,2048]{1,0:T(8,128)(2,1)}, u32[]{:S(2)}, u32[]{:S(2)}) collective-permute-start(bf16[128,2048]{1,0:T(8,128)(2,1)S(1)} %get-tuple-element.415.refs_0_), channel_id=1, source_target_pairs={{0,16},{8,24},{16,0},{24,8},{1,17},{9,25},{17,1},{25,9},{2,18},{10... | collective-permute-start | bytes 1572872 | tf_op jit(solution)/shard_map/ppermute | solution.py:72
  148.1 34.4 %collective-permute-start.26 = (bf16[128,2048]{1,0:T(8,128)(2,1)S(1)}, bf16[128,2048]{1,0:T(8,128)(2,1)}, u32[]{:S(2)}, u32[]{:S(2)}) collective-permute-start(bf16[128,2048]{1,0:T(8,128)(2,1)S(1)} %get-tuple-element.416.refs_1_), channel_id=1, source_target_pairs={{0,8},{8,0},{16,24},{24,16},{1,9},{9,1},{17,25},{25,17},{2,10},{10... | collective-permute-start | bytes 1572872 | tf_op jit(solution)/shard_map/ppermute | solution.py:72
  149.4 33.1 %collective-permute-start.28 = (bf16[128,2048]{1,0:T(8,128)(2,1)S(1)}, bf16[128,2048]{1,0:T(8,128)(2,1)}, u32[]{:S(2)}, u32[]{:S(2)}) collective-permute-start(bf16[128,2048]{1,0:T(8,128)(2,1)S(1)} %get-tuple-element.416.refs_1_), channel_id=1, source_target_pairs={{0,16},{8,24},{16,0},{24,8},{1,17},{9,25},{17,1},{25,9},{2,18},{10... | collective-permute-start | bytes 1572872 | tf_op jit(solution)/shard_map/ppermute | solution.py:72
  185.0 19.6 %collective-permute-start.31 = (bf16[128,2048]{1,0:T(8,128)(2,1)S(1)}, bf16[128,2048]{1,0:T(8,128)(2,1)S(1)}, u32[]{:S(2)}, u32[]{:S(2)}) collective-permute-start(bf16[128,2048]{1,0:T(8,128)(2,1)S(1)} %get-tuple-element.386), channel_id=1, source_target_pairs={{0,8},{8,0},{16,24},{24,16},{1,9},{9,1},{17,25},{25,17},{2,10},{10... | collective-permute-start | bytes 1572872 | tf_op jit(solution)/shard_map/ppermute | solution.py:72
  186.1 19.7 %collective-permute-start.32 = (bf16[128,2048]{1,0:T(8,128)(2,1)S(1)}, bf16[128,2048]{1,0:T(8,128)(2,1)S(1)}, u32[]{:S(2)}, u32[]{:S(2)}) collective-permute-start(bf16[128,2048]{1,0:T(8,128)(2,1)S(1)} %get-tuple-element.388), channel_id=1, source_target_pairs={{0,16},{8,24},{16,0},{24,8},{1,17},{9,25},{17,1},{25,9},{2,18},{10... | collective-permute-start | bytes 1572872 | tf_op jit(solution)/shard_map/ppermute | solution.py:72
  223.8 23.4 %collective-permute-start.36 = (bf16[128,2048]{1,0:T(8,128)(2,1)S(1)}, bf16[128,2048]{1,0:T(8,128)(2,1)S(1)}, u32[]{:S(2)}, u32[]{:S(2)}) collective-permute-start(bf16[128,2048]{1,0:T(8,128)(2,1)S(1)} %get-tuple-element.670.refs_1_), channel_id=1, source_target_pairs={{0,8},{8,0},{16,24},{24,16},{1,9},{9,1},{17,25},{25,17},{2,10},{10... | collective-permute-start | bytes 1572872 | tf_op jit(solution)/shard_map/ppermute | solution.py:72
  224.5 23.1 %collective-permute-start.37 = (bf16[128,2048]{1,0:T(8,128)(2,1)S(1)}, bf16[128,2048]{1,0:T(8,128)(2,1)S(1)}, u32[]{:S(2)}, u32[]{:S(2)}) collective-permute-start(bf16[128,2048]{1,0:T(8,128)(2,1)S(1)} %get-tuple-element.671.refs_0_), channel_id=1, source_target_pairs={{0,16},{8,24},{16,0},{24,8},{1,17},{9,25},{17,1},{25,9},{2,18},{10... | collective-permute-start | bytes 1572872 | tf_op jit(solution)/shard_map/ppermute | solution.py:72
  256.8 20.5 %collective-permute-start.41 = (bf16[128,2048]{1,0:T(8,128)(2,1)S(1)}, bf16[128,2048]{1,0:T(8,128)(2,1)S(1)}, u32[]{:S(2)}, u32[]{:S(2)}) collective-permute-start(bf16[128,2048]{1,0:T(8,128)(2,1)S(1)} %collective-permute-done.25.refs_2_), channel_id=1, source_target_pairs={{0,16},{8,24},{16,0},{24,8},{1,17},{9,25},{17,1},{25,9},{2,18},{10... | collective-permute-start | bytes 1572872 | tf_op jit(solution)/shard_map/ppermute | solution.py:72
  309.2 136.4 %reduce-scatter.9.cloned.1.call-start = ((), (), s32[]{:S(2)}) async-start(), calls=%async_computation.9 | async-start | bytes 3604480 | tf_op jit(solution)/shard_map/reduce_scatter | solution.py:199
  310.6 22.9 %collective-permute-start.44 = (bf16[640,384]{1,0:T(8,128)(2,1)S(1)}, bf16[640,384]{1,0:T(8,128)(2,1)}, u32[]{:S(2)}, u32[]{:S(2)}) collective-permute-start(bf16[640,384]{1,0:T(8,128)(2,1)S(1)} %get-tuple-element.587.refs_0_), channel_id=1, source_target_pairs={{0,8},{8,0},{16,24},{24,16},{1,9},{9,1},{17,25},{25,17},{2,10},{10... | collective-permute-start | bytes 1474568 | tf_op jit(solution)/shard_map/ppermute | solution.py:72
  311.9 22.9 %collective-permute-start.45 = (bf16[640,384]{1,0:T(8,128)(2,1)S(1)}, bf16[640,384]{1,0:T(8,128)(2,1)S(1)}, u32[]{:S(2)}, u32[]{:S(2)}) collective-permute-start(bf16[640,384]{1,0:T(8,128)(2,1)S(1)} %get-tuple-element.588.refs_1_), channel_id=1, source_target_pairs={{0,8},{8,0},{16,24},{24,16},{1,9},{9,1},{17,25},{25,17},{2,10},{10... | collective-permute-start | bytes 1474568 | tf_op jit(solution)/shard_map/ppermute | solution.py:72
  312.7 22.1 %collective-permute-start.46 = (bf16[640,384]{1,0:T(8,128)(2,1)S(1)}, bf16[640,384]{1,0:T(8,128)(2,1)S(1)}, u32[]{:S(2)}, u32[]{:S(2)}) collective-permute-start(bf16[640,384]{1,0:T(8,128)(2,1)S(1)} %get-tuple-element.587.refs_0_), channel_id=1, source_target_pairs={{0,16},{8,24},{16,0},{24,8},{1,17},{9,25},{17,1},{25,9},{2,18},{10... | collective-permute-start | bytes 1474568 | tf_op jit(solution)/shard_map/ppermute | solution.py:72
  313.7 22.7 %collective-permute-start.47 = (bf16[640,384]{1,0:T(8,128)(2,1)S(1)}, bf16[640,384]{1,0:T(8,128)(2,1)}, u32[]{:S(2)}, u32[]{:S(2)}) collective-permute-start(bf16[640,384]{1,0:T(8,128)(2,1)S(1)} %get-tuple-element.588.refs_1_), channel_id=1, source_target_pairs={{0,16},{8,24},{16,0},{24,8},{1,17},{9,25},{17,1},{25,9},{2,18},{10... | collective-permute-start | bytes 1474568 | tf_op jit(solution)/shard_map/ppermute | solution.py:72
  336.4 27.7 %collective-permute-start.48 = (bf16[128,2048]{1,0:T(8,128)(2,1)S(1)}, bf16[128,2048]{1,0:T(8,128)(2,1)S(1)}, u32[]{:S(2)}, u32[]{:S(2)}) collective-permute-start(bf16[128,2048]{1,0:T(8,128)(2,1)S(1)} %get-tuple-element.453), channel_id=1, source_target_pairs={{0,8},{8,0},{16,24},{24,16},{1,9},{9,1},{17,25},{25,17},{2,10},{10... | collective-permute-start | bytes 1572872 | tf_op jit(solution)/shard_map/ppermute | solution.py:72
  337.7 26.5 %collective-permute-start.49 = (bf16[128,2048]{1,0:T(8,128)(2,1)S(1)}, bf16[128,2048]{1,0:T(8,128)(2,1)S(1)}, u32[]{:S(2)}, u32[]{:S(2)}) collective-permute-start(bf16[128,2048]{1,0:T(8,128)(2,1)S(1)} %get-tuple-element.455), channel_id=1, source_target_pairs={{0,16},{8,24},{16,0},{24,8},{1,17},{9,25},{17,1},{25,9},{2,18},{10... | collective-permute-start | bytes 1572872 | tf_op jit(solution)/shard_map/ppermute | solution.py:72
  338.3 25.8 %collective-permute-start.50 = (bf16[128,2048]{1,0:T(8,128)(2,1)S(1)}, bf16[128,2048]{1,0:T(8,128)(2,1)S(1)}, u32[]{:S(2)}, u32[]{:S(2)}) collective-permute-start(bf16[128,2048]{1,0:T(8,128)(2,1)S(1)} %get-tuple-element.457), channel_id=1, source_target_pairs={{0,8},{8,0},{16,24},{24,16},{1,9},{9,1},{17,25},{25,17},{2,10},{10... | collective-permute-start | bytes 1572872 | tf_op jit(solution)/shard_map/ppermute | solution.py:72
  339.5 24.7 %collective-permute-start.51 = (bf16[128,2048]{1,0:T(8,128)(2,1)S(1)}, bf16[128,2048]{1,0:T(8,128)(2,1)S(1)}, u32[]{:S(2)}, u32[]{:S(2)}) collective-permute-start(bf16[128,2048]{1,0:T(8,128)(2,1)S(1)} %get-tuple-element.459), channel_id=1, source_target_pairs={{0,16},{8,24},{16,0},{24,8},{1,17},{9,25},{17,1},{25,9},{2,18},{10... | collective-permute-start | bytes 1572872 | tf_op jit(solution)/shard_map/ppermute | solution.py:72
  372.1 142.4 %reduce-scatter.11.cloned.1.call-start = ((), (), s32[]{:S(2)}) async-start(), calls=%async_computation.10 | async-start | bytes 3604480 | tf_op jit(solution)/shard_map/reduce_scatter | solution.py:199
  392.3 149.4 %reduce-scatter.13.cloned.1.call-start = ((), (), s32[]{:S(2)}) async-start(), calls=%async_computation.11 | async-start | bytes 2621440 | tf_op jit(solution)/shard_map/reduce_scatter | solution.py:199
  400.7 27.4 %collective-permute-start.57 = (bf16[128,2048]{1,0:T(8,128)(2,1)S(1)}, bf16[128,2048]{1,0:T(8,128)(2,1)S(1)}, u32[]{:S(2)}, u32[]{:S(2)}) collective-permute-start(bf16[128,2048]{1,0:T(8,128)(2,1)S(1)} %get-tuple-element.668.refs_1_), channel_id=1, source_target_pairs={{0,8},{8,0},{16,24},{24,16},{1,9},{9,1},{17,25},{25,17},{2,10},{10... | collective-permute-start | bytes 1572872 | tf_op jit(solution)/shard_map/ppermute | solution.py:72
  401.5 26.6 %collective-permute-start.58 = (bf16[128,2048]{1,0:T(8,128)(2,1)S(1)}, bf16[128,2048]{1,0:T(8,128)(2,1)S(1)}, u32[]{:S(2)}, u32[]{:S(2)}) collective-permute-start(bf16[128,2048]{1,0:T(8,128)(2,1)S(1)} %get-tuple-element.669.refs_0_), channel_id=1, source_target_pairs={{0,16},{8,24},{16,0},{24,8},{1,17},{9,25},{17,1},{25,9},{2,18},{10... | collective-permute-start | bytes 1572872 | tf_op jit(solution)/shard_map/ppermute | solution.py:72
  413.5 21.4 %collective-permute-start.60 = (bf16[128,2048]{1,0:T(8,128)(2,1)S(1)}, bf16[128,2048]{1,0:T(8,128)(2,1)S(1)}, u32[]{:S(2)}, u32[]{:S(2)}) collective-permute-start(bf16[128,2048]{1,0:T(8,128)(2,1)S(1)} %collective-permute-done.56.refs_2_), channel_id=1, source_target_pairs={{0,16},{8,24},{16,0},{24,8},{1,17},{9,25},{17,1},{25,9},{2,18},{10... | collective-permute-start | bytes 1572872 | tf_op jit(solution)/shard_map/ppermute | solution.py:72
  414.3 20.6 %collective-permute-start.61 = (bf16[128,2048]{1,0:T(8,128)(2,1)S(1)}, bf16[128,2048]{1,0:T(8,128)(2,1)S(1)}, u32[]{:S(2)}, u32[]{:S(2)}) collective-permute-start(bf16[128,2048]{1,0:T(8,128)(2,1)S(1)} %collective-permute-done.59.refs_5_), channel_id=1, source_target_pairs={{0,8},{8,0},{16,24},{24,16},{1,9},{9,1},{17,25},{25,17},{2,10},{10... | collective-permute-start | bytes 1572872 | tf_op jit(solution)/shard_map/ppermute | solution.py:72
  446.9 19.8 %collective-permute-start.63 = (bf16[128,2048]{1,0:T(8,128)(2,1)}, bf16[128,2048]{1,0:T(8,128)(2,1)S(1)}, u32[]{:S(2)}, u32[]{:S(2)}) collective-permute-start(bf16[128,2048]{1,0:T(8,128)(2,1)} %get-tuple-element.515), channel_id=1, source_target_pairs={{0,8},{8,0},{16,24},{24,16},{1,9},{9,1},{17,25},{25,17},{2,10},{10... | collective-permute-start | bytes 1572872 | tf_op jit(solution)/shard_map/ppermute | solution.py:72
  448.1 37.0 %collective-permute-start.64 = (bf16[128,2048]{1,0:T(8,128)(2,1)}, bf16[128,2048]{1,0:T(8,128)(2,1)}, u32[]{:S(2)}, u32[]{:S(2)}) collective-permute-start(bf16[128,2048]{1,0:T(8,128)(2,1)} %get-tuple-element.517), channel_id=1, source_target_pairs={{0,16},{8,24},{16,0},{24,8},{1,17},{9,25},{17,1},{25,9},{2,18},{10... | collective-permute-start | bytes 1572872 | tf_op jit(solution)/shard_map/ppermute | solution.py:72
  449.0 36.1 %collective-permute-start.65 = (bf16[128,2048]{1,0:T(8,128)(2,1)}, bf16[128,2048]{1,0:T(8,128)(2,1)}, u32[]{:S(2)}, u32[]{:S(2)}) collective-permute-start(bf16[128,2048]{1,0:T(8,128)(2,1)} %get-tuple-element.519), channel_id=1, source_target_pairs={{0,8},{8,0},{16,24},{24,16},{1,9},{9,1},{17,25},{25,17},{2,10},{10... | collective-permute-start | bytes 1572872 | tf_op jit(solution)/shard_map/ppermute | solution.py:72
  450.3 34.8 %collective-permute-start.66 = (bf16[128,2048]{1,0:T(8,128)(2,1)}, bf16[128,2048]{1,0:T(8,128)(2,1)}, u32[]{:S(2)}, u32[]{:S(2)}) collective-permute-start(bf16[128,2048]{1,0:T(8,128)(2,1)} %get-tuple-element.521), channel_id=1, source_target_pairs={{0,16},{8,24},{16,0},{24,8},{1,17},{9,25},{17,1},{25,9},{2,18},{10... | collective-permute-start | bytes 1572872 | tf_op jit(solution)/shard_map/ppermute | solution.py:72
  465.2 19.9 %collective-permute-start.67 = (bf16[640,384]{1,0:T(8,128)(2,1)}, bf16[640,384]{1,0:T(8,128)(2,1)}, u32[]{:S(2)}, u32[]{:S(2)}) collective-permute-start(bf16[640,384]{1,0:T(8,128)(2,1)} %collective-permute-done.44.refs_2_), channel_id=1, source_target_pairs={{0,16},{8,24},{16,0},{24,8},{1,17},{9,25},{17,1},{25,9},{2,18},{10... | collective-permute-start | bytes 1474568 | tf_op jit(solution)/shard_map/ppermute | solution.py:72
  468.6 114.1 %reduce-scatter.15.cloned.1.call-start = ((), (), s32[]{:S(2)}) async-start(), calls=%async_computation.12 | async-start | bytes 1310720 | tf_op jit(solution)/shard_map/reduce_scatter | solution.py:199
  485.3 24.0 %collective-permute-start.73 = (bf16[128,2048]{1,0:T(8,128)(2,1)S(1)}, bf16[128,2048]{1,0:T(8,128)(2,1)S(1)}, u32[]{:S(2)}, u32[]{:S(2)}) collective-permute-start(bf16[128,2048]{1,0:T(8,128)(2,1)S(1)} %add_convert_fusion.7), channel_id=1, source_target_pairs={{0,16},{8,24},{16,0},{24,8},{1,17},{9,25},{17,1},{25,9},{2,18},{10... | collective-permute-start | bytes 1572872 | tf_op jit(solution)/shard_map/ppermute | solution.py:72
  487.7 24.0 %collective-permute-start.74 = (bf16[128,2048]{1,0:T(8,128)(2,1)S(1)}, bf16[128,2048]{1,0:T(8,128)(2,1)S(1)}, u32[]{:S(2)}, u32[]{:S(2)}) collective-permute-start(bf16[128,2048]{1,0:T(8,128)(2,1)S(1)} %add_convert_fusion.6), channel_id=1, source_target_pairs={{0,8},{8,0},{16,24},{24,16},{1,9},{9,1},{17,25},{25,17},{2,10},{10... | collective-permute-start | bytes 1572872 | tf_op jit(solution)/shard_map/ppermute | solution.py:72
  523.3 42.9 %collective-permute-start.84 = (bf16[5120,384]{1,0:T(8,128)(2,1)}, bf16[5120,384]{1,0:T(8,128)(2,1)}, u32[]{:S(2)}, u32[]{:S(2)}) collective-permute-start(bf16[5120,384]{1,0:T(8,128)(2,1)} %shard_map.258), channel_id=1, source_target_pairs={{0,4},{4,0},{1,5},{5,1},{2,6},{6,2},{3,7},{7,3},{8,12},{12,8},{9,1... | collective-permute-start | bytes 11796488 | tf_op jit(solution)/shard_map/ppermute | solution.py:67
  529.4 28.6 %collective-permute-start.75 = (bf16[128,2048]{1,0:T(8,128)(2,1)}, bf16[128,2048]{1,0:T(8,128)(2,1)}, u32[]{:S(2)}, u32[]{:S(2)}) collective-permute-start(bf16[128,2048]{1,0:T(8,128)(2,1)} %get-tuple-element.663), channel_id=1, source_target_pairs={{0,4},{4,0},{1,5},{5,1},{2,6},{6,2},{3,7},{7,3},{8,12},{12,8},{9,1... | collective-permute-start | bytes 1572872 | tf_op jit(solution)/shard_map/ppermute | solution.py:67
  550.1 53.9 %reduce-scatter.17.cloned.1.call-start = ((), (), s32[]{:S(2)}) async-start(), calls=%async_computation.13 | async-start | bytes 983040 | tf_op jit(solution)/shard_map/reduce_scatter | solution.py:199
  588.7 19.9 %collective-permute-start.85 = (f32[128,2048]{1,0:T(8,128)S(1)}, f32[128,2048]{1,0:T(8,128)S(1)}, u32[]{:S(2)}, u32[]{:S(2)}) collective-permute-start(f32[128,2048]{1,0:T(8,128)S(1)} %get-tuple-element.647), channel_id=1, source_target_pairs={{0,4},{4,0},{1,5},{5,1},{2,6},{6,2},{3,7},{7,3},{8,12},{12,8},{9,1... | collective-permute-start | bytes 3145736 | tf_op jit(solution)/shard_map/ppermute | solution.py:67
  (209 other events, 2408.3 us)
Sparse Core Ops, SparseCore 0:
  9.7 49.8 all-gather.8
  61.8 26.7 all-gather.12
  90.7 28.6 all-gather.14
  121.4 107.5 all-gather.16
  230.4 58.6 all-gather.10
  309.4 54.0 reduce-scatter.6
  372.3 53.8 reduce-scatter.8
  428.5 56.0 reduce-scatter.10
  486.8 43.7 reduce-scatter.12
  550.2 25.1 reduce-scatter.14
  582.8 21.0 reduce-scatter.16

commit v7 on v6

--- a/solution.py
+++ b/solution.py
@@ -381,7 +381,7 @@
         ],
         out_specs=[head, whole(keys), whole(keys)],
         out_shape=[jax.ShapeDtypeStruct(queries.shape, bf16), summed, summed],
-        compiler_params=pltpu.CompilerParams(vmem_limit_bytes=48 << 20),
+        compiler_params=pltpu.CompilerParams(vmem_limit_bytes=36 << 20),
         cost_estimate=BESIDE,
     )(length, flip, queries, grads, total, keys, keys_t, values, cos_table, sin_table)
 
@@ -553,7 +553,7 @@
         in_specs=[whole(grad_q), block(up_q), whole(grad_k), whole(grad_v), block(place)],
         out_specs=[pl.BlockSpec(shape, lambda k: (0, 0))] * (2 * chips),
         out_shape=[jax.ShapeDtypeStruct(shape, bf16)] * (2 * chips),
-        compiler_params=pltpu.CompilerParams(vmem_limit_bytes=48 << 20),
+        compiler_params=pltpu.CompilerParams(vmem_limit_bytes=36 << 20),
         cost_estimate=BESIDE,
     )(grad_q, up_q, grad_k, grad_v, place)
 
@@ -627,7 +627,7 @@
             out_specs=pl.BlockSpec((rows, depth), lambda i, p: (0, i)),
         ),
         out_shape=jax.ShapeDtypeStruct((rows, chips * depth), f32),
-        compiler_params=pltpu.CompilerParams(vmem_limit_bytes=48 << 20),
+        compiler_params=pltpu.CompilerParams(vmem_limit_bytes=36 << 20),
         cost_estimate=BESIDE,
     )(jnp.stack([chip_flip(), lax.axis_index("core")]), *lefts, mine, other)
 
@@ -769,7 +769,7 @@
             out_specs=[out] * 3,
         ),
         out_shape=[jax.ShapeDtypeStruct((rows.shape[0], width), bf16)] * 3,
-        compiler_params=pltpu.CompilerParams(vmem_limit_bytes=48 << 20),
+        compiler_params=pltpu.CompilerParams(vmem_limit_bytes=36 << 20),
         cost_estimate=BESIDE,
     )(chip_flip()[None], rows, gate_up)
 
@@ -797,7 +797,7 @@
         ],
         out_specs=[rows(width)] * 2,
         out_shape=[jax.ShapeDtypeStruct(silu.shape, bf16)] * 2,
-        compiler_params=pltpu.CompilerParams(vmem_limit_bytes=48 << 20),
+        compiler_params=pltpu.CompilerParams(vmem_limit_bytes=36 << 20),
         cost_estimate=BESIDE,
     )(seed, down_proj, silu, slope)
 

time: 630 us -> 641 us (1.017)
  local copies, waits for them, and re-layouts: 51.9 us -> 64.6 us
    unnamed x303 -> x315, local copies, waits for them, and re-layouts: 31.1 us -> 43.3 us
  transfers between devices with their start and end apart: 107 -> 107, of which waited for: 47 -> 49; matrix products, arithmetic and copies ran while one was open for 16% -> 16% of each run, Pallas kernels for 30% -> 29%
where the time goes in v7:
time: 641 us; the launch traced here: 632 us
  waiting for transfers between devices  185 us (29%)
  Pallas kernels  183 us (29%)
  starting transfers between devices  99.3 us (15%)
  other arithmetic  83.1 us (13%)
  local copies, waits for them, and re-layouts  64.6 us (10%)
  between operations  16.3 us (3%)
    ppermute x85, waiting for transfers between devices, to_chip(): return lax.ppermute(block, 'chip', [(i, i ^ bits) for i in range(count)])  168 us
    ppermute x85, starting transfers between devices, to_chip(): return lax.ppermute(block, 'chip', [(i, i ^ bits) for i in range(count)])  96.5 us
    unnamed x315, local copies, waits for them, and re-layouts  43.3 us
    pallas_call x5, Pallas kernels, weight_terms(): pl.pallas_call(functools.partial(terms_kernel, scale), grid_spec=pltpu.Pr...  40.2 us
    pallas_call x3, Pallas kernels, product(): pl.pallas_call(functools.partial(product_kernel, kind), grid=(width // TI...  22 us
    pallas_call x1, Pallas kernels, attend(): pl.pallas_call(functools.partial(attend_kernel, score_scale), grid=(heads...  18.8 us
    pallas_call x1, Pallas kernels, gated(): pl.pallas_call(gate_kernel, grid_spec=pltpu.PrefetchScalarGridSpec(num_sc...  16.7 us
    pallas_call x1, Pallas kernels, spread(): pl.pallas_call(functools.partial(spread_kernel, len(lefts)), grid_spec=pl...  16.1 us
  transfers between devices with their start and end apart: 107, of which 49 were waited for; matrix products, arithmetic and copies ran while one was open for 16% of the time, Pallas kernels for 29%

profile of v7, /device:TPU:0, one launch (start us, length us, event | category | flops | bytes accessed | tf_op | source)
XLA Modules:
  0.0 632.2 jit_solution(10590145211787577189)
XLA Ops:
  11.2 3.8 shard_map.237
  17.1 2.5 collective-permute-start.4
  25.6 19.4 %collective-permute-done.1 = bf16[80,384]{1,0:T(8,128)(2,1)S(1)} collective-permute-done((bf16[80,384]{1,0:T(8,128)(2,1)S(1)}, bf16[80,384]{1,0:T(8,128)(2,1)S(1)}, u32[]{:S(2)}, u32[]{:S(2)}) %collective-permute-start.1) | collective-permute-done | bytes 61472 | tf_op jit(solution)/shard_map/ppermute | solution.py:72
  49.2 2.7 collective-permute-start.3
  54.3 5.3 all-gather.9.cloned.1.call-done.right_ref
  63.4 11.3 %collective-permute-done.8.refs_6_ = bf16[128,2048]{1,0:T(8,128)(2,1)S(1)} collective-permute-done((bf16[128,2048]{1,0:T(8,128)(2,1)}, bf16[128,2048]{1,0:T(8,128)(2,1)S(1)}, u32[]{:S(2)}, u32[]{:S(2)}) %collective-permute-start.8) | collective-permute-done | bytes 524320 | tf_op jit(solution)/shard_map/ppermute | solution.py:72
  91.5 8.2 %shard_map.238 = (bf16[1024,2048]{1,0:T(8,128)(2,1)}, f32[1024,256]{1,0:T(8,128)}, f32[1024,128]{1,0:T(8,128)}) custom-call(s32[1]{0:T(128)} %bitcast.1._.flip_ref, bf16[128,2048]{1,0:T(8,128)(2,1)} %get-tuple-element.338.refs_0_, bf16[128,2048]{1,0:T(8,128)(2,1)} %copy-done.98, bf16[128,2048]{1,0:T(8,128)(2,1)} %collective-permute-done.4.refs_2_, ...), custom_call_target="tpu_custom_call" | custom-call | flops 1 | bytes 1 | tf_op jit(solution)/shard_map/pallas_call | solution.py:715
  101.4 2.6 pad_maximum_fusion.2
  123.2 7.2 %collective-permute-done.15.refs_2_ = bf16[512,384]{1,0:T(8,128)(2,1)S(1)} collective-permute-done((bf16[512,384]{1,0:T(8,128)(2,1)S(1)}, bf16[512,384]{1,0:T(8,128)(2,1)S(1)}, u32[]{:S(2)}, u32[]{:S(2)}) %collective-permute-start.15) | collective-permute-done | bytes 393248 | tf_op jit(solution)/shard_map/ppermute | solution.py:72
  134.3 4.5 collective-permute-done.16.refs_3_
  139.6 6.1 collective-permute-done.19.refs_6_
  153.7 18.8 %shard_map.240 = (bf16[1024,1024]{1,0:T(8,128)(2,1)}, bf16[1024,1024]{1,0:T(8,128)(2,1)}, f32[4,1,1024]{2,1,0:T(1,128)}) custom-call(s32[1]{0:T(128)} %bitcast.length_ref, s32[1]{0:T(128)} %bitcast.1._.flip_ref, bf16[4,1024,384]{2,1,0:T(8,128)(2,1)} %bitcast.149, bf16[4,256,1024]{2,1,0:T(8,128)(2,1)} %all-gather.15.cloned.1.call-done.up_ref, ...), custom_call_target="tpu_custom_call" | custom-call | flops 1 | bytes 1 | tf_op jit(solution)/shard_map/pallas_call | solution.py:290
  176.4 6.9 %shard_map.241 = (bf16[128,2048]{1,0:T(8,128)(2,1)S(1)}, bf16[128,2048]{1,0:T(8,128)(2,1)S(1)}, bf16[128,2048]{1,0:T(8,128)(2,1)S(1)}, bf16[128,2048]{1,0:T(8,12...) custom-call(bf16[1024,1024]{1,0:T(8,128)(2,1)S(1)} %copy-done.20, ...), custom_call_target="tpu_custom_call" | custom-call | flops 1 | bytes 1 | tf_op jit(solution)/shard_map/pallas_call | solution.py:429
  187.4 10.8 %collective-permute-done.29 = bf16[128,2048]{1,0:T(8,128)(2,1)S(1)} collective-permute-done((bf16[128,2048]{1,0:T(8,128)(2,1)S(1)}, bf16[128,2048]{1,0:T(8,128)(2,1)S(1)}, u32[]{:S(2)}, u32[]{:S(2)}) %collective-permute-start.29) | collective-permute-done | bytes 524320 | tf_op jit(solution)/shard_map/ppermute | solution.py:72
  199.3 5.9 collective-permute-done.31
  210.9 6.6 %collective-permute-done.33 = bf16[128,2048]{1,0:T(8,128)(2,1)} collective-permute-done((bf16[128,2048]{1,0:T(8,128)(2,1)}, bf16[128,2048]{1,0:T(8,128)(2,1)}, u32[]{:S(2)}, u32[]{:S(2)}) %collective-permute-start.33) | collective-permute-done | bytes 524320 | tf_op jit(solution)/shard_map/ppermute | solution.py:72
  226.2 10.8 %collective-permute-done.35.refs_2_ = bf16[128,2048]{1,0:T(8,128)(2,1)S(1)} collective-permute-done((bf16[128,2048]{1,0:T(8,128)(2,1)S(1)}, bf16[128,2048]{1,0:T(8,128)(2,1)S(1)}, u32[]{:S(2)}, u32[]{:S(2)}) %collective-permute-start.35) | collective-permute-done | bytes 524320 | tf_op jit(solution)/shard_map/ppermute | solution.py:72
  239.3 8.5 %collective-permute-done.36.refs_3_ = bf16[128,2048]{1,0:T(8,128)(2,1)S(1)} collective-permute-done((bf16[128,2048]{1,0:T(8,128)(2,1)S(1)}, bf16[128,2048]{1,0:T(8,128)(2,1)S(1)}, u32[]{:S(2)}, u32[]{:S(2)}) %collective-permute-start.36) | collective-permute-done | bytes 524320 | tf_op jit(solution)/shard_map/ppermute | solution.py:72
  248.2 6.6 %collective-permute-done.39.refs_6_ = bf16[128,2048]{1,0:T(8,128)(2,1)S(1)} collective-permute-done((bf16[128,2048]{1,0:T(8,128)(2,1)S(1)}, bf16[128,2048]{1,0:T(8,128)(2,1)S(1)}, u32[]{:S(2)}, u32[]{:S(2)}) %collective-permute-start.39) | collective-permute-done | bytes 524320 | tf_op jit(solution)/shard_map/ppermute | solution.py:72
  261.9 16.7 %shard_map.243 = (bf16[1024,1408]{1,0:T(8,128)(2,1)S(1)}, bf16[1024,1408]{1,0:T(8,128)(2,1)S(1)}, bf16[1024,1408]{1,0:T(8,128)(2,1)S(1)}) custom-call(s32[1]{0:T(128)} %bitcast.1._.flip_ref, bf16[1024,2048]{1,0:T(8,128)(2,1)S(1)} %copy-done.3, bf16[4,8,2,64,1408]{4,3,2,1,0:T(8,128)(2,1)} %bitcast.152), custom_call_target="tpu_custom_call" | custom-call | flops 1 | bytes 1 | tf_op jit(solution)/shard_map/pallas_call | solution.py:760
  281.9 3.1 shard_map.244.right_ref.seed_ref
  285.0 9.3 %shard_map.245 = (bf16[704,2048]{1,0:T(8,128)(2,1)S(1)}, bf16[704,2048]{1,0:T(8,128)(2,1)}) custom-call(s32[2]{0:T(128)S(1)} %pad_add_fusion.place_ref, bf16[1024,1408]{1,0:T(8,128)(2,1)S(1)} %get-tuple-element.489.left_ref, bf16[1024,2048]{1,0:T(8,128)(2,1)S(1)} %shard_map.244.right_ref.seed_ref), custom_call_target="tpu_custom_call" | custom-call | flops 1 | bytes 1 | tf_op jit(solution)/shard_map/pallas_call | solution.py:508
  304.8 10.7 %shard_map.246 = (bf16[1024,1408]{1,0:T(8,128)(2,1)S(1)}, bf16[1024,1408]{1,0:T(8,128)(2,1)S(1)}) custom-call(bf16[1024,2048]{1,0:T(8,128)(2,1)S(1)} %copy-done.8, bf16[1408,2048]{1,0:T(8,128)(2,1)} %all-gather.11.cloned.1.call-done.down_ref.right_ref, bf16[1024,1408]{1,0:T(8,128)(2,1)S(1)} %copy-done.33, bf16[1024,1408]{1,0:T(8,128)(2,1)S(1)} %copy-done.35), custom_call_target="tpu_custom_call" | custom-call | flops 1 | bytes 1 | tf_op jit(solution)/shard_map/pallas_call | solution.py:789
  315.5 3.0 add_convert_fusion.2
  325.8 16.1 %shard_map.247 = (bf16[128,2048]{1,0:T(8,128)(2,1)S(1)}, bf16[128,2048]{1,0:T(8,128)(2,1)S(1)}, bf16[128,2048]{1,0:T(8,128)(2,1)S(1)}, bf16[128,2048]{1,0:T(8,12...) custom-call(s32[1]{0:T(128)} %bitcast.1._.flip_ref, ...), custom_call_target="tpu_custom_call" | custom-call | flops 1 | bytes 1 | tf_op jit(solution)/shard_map/pallas_call | solution.py:581
  349.8 11.0 %shard_map.249 = (bf16[4,4,64,1408]{3,2,1,0:T(8,128)(2,1)S(1)}, bf16[4,4,64,1408]{3,2,1,0:T(8,128)(2,1)S(1)}) custom-call(s32[2]{0:T(128)S(1)} %pad_add_fusion.1.place_ref, bf16[1024,2048]{1,0:T(8,128)(2,1)S(1)} %copy-done.4, bf16[1024,1408]{1,0:T(8,128)(2,1)S(1)} %copy-done.15), custom_call_target="tpu_custom_call" | custom-call | flops 1 | bytes 1 | tf_op jit(solution)/shard_map/pallas_call | solution.py:491
  362.4 11.0 %shard_map.248 = (bf16[4,4,64,1408]{3,2,1,0:T(8,128)(2,1)S(1)}, bf16[4,4,64,1408]{3,2,1,0:T(8,128)(2,1)S(1)}) custom-call(s32[2]{0:T(128)S(1)} %pad_add_fusion.1.place_ref, bf16[1024,2048]{1,0:T(8,128)(2,1)S(1)} %copy-done.4, bf16[1024,1408]{1,0:T(8,128)(2,1)S(1)} %get-tuple-element.460.refs_0_.right_ref), custom_call_target="tpu_custom_call" | custom-call | flops 1 | bytes 1 | tf_op jit(solution)/shard_map/pallas_call | solution.py:491
  373.5 5.3 collective-permute-done.52
  378.8 2.6 add_convert_fusion.1
  387.0 2.5 add_convert_fusion
  389.6 8.0 %collective-permute-done.53 = bf16[128,2048]{1,0:T(8,128)(2,1)S(1)} collective-permute-done((bf16[128,2048]{1,0:T(8,128)(2,1)S(1)}, bf16[128,2048]{1,0:T(8,128)(2,1)S(1)}, u32[]{:S(2)}, u32[]{:S(2)}) %collective-permute-start.53) | collective-permute-done | bytes 524320 | tf_op jit(solution)/shard_map/ppermute | solution.py:72
  411.8 10.8 %collective-permute-done.56.refs_2_ = bf16[128,2048]{1,0:T(8,128)(2,1)S(1)} collective-permute-done((bf16[128,2048]{1,0:T(8,128)(2,1)S(1)}, bf16[128,2048]{1,0:T(8,128)(2,1)S(1)}, u32[]{:S(2)}, u32[]{:S(2)}) %collective-permute-start.56) | collective-permute-done | bytes 524320 | tf_op jit(solution)/shard_map/ppermute | solution.py:72
  427.6 9.8 %shard_map.251 = (bf16[128,2048]{1,0:T(8,128)(2,1)S(1)}, bf16[128,2048]{1,0:T(8,128)(2,1)S(1)}, bf16[128,2048]{1,0:T(8,128)(2,1)}, bf16[128,2048]{1,0:T(8,128)(2...) custom-call(bf16[1024,1408]{1,0:T(8,128)(2,1)S(1)} %copy-done.17, ...), custom_call_target="tpu_custom_call" | custom-call | flops 1 | bytes 1 | tf_op jit(solution)/shard_map/pallas_call | solution.py:429
  437.4 6.6 %collective-permute-done.60.refs_6_ = bf16[128,2048]{1,0:T(8,128)(2,1)S(1)} collective-permute-done((bf16[128,2048]{1,0:T(8,128)(2,1)S(1)}, bf16[128,2048]{1,0:T(8,128)(2,1)S(1)}, u32[]{:S(2)}, u32[]{:S(2)}) %collective-permute-start.60) | collective-permute-done | bytes 524320 | tf_op jit(solution)/shard_map/ppermute | solution.py:72
  444.6 6.8 %shard_map.252 = (bf16[512,2048]{1,0:T(8,128)(2,1)S(1)}, bf16[512,2048]{1,0:T(8,128)(2,1)S(1)}) custom-call(s32[2]{0:T(128)S(1)} %pad_add_fusion.place_ref, bf16[1024,1024]{1,0:T(8,128)(2,1)S(1)} %copy-done.21, bf16[1024,2048]{1,0:T(8,128)(2,1)S(1)} %shard_map.250.right_ref.left_ref), custom_call_target="tpu_custom_call" | custom-call | flops 1 | bytes 1 | tf_op jit(solution)/shard_map/pallas_call | solution.py:491
  464.5 5.4 shard_map.253.grad_ref
  469.9 4.4 add_convert_fusion.3
  482.4 13.9 %shard_map.254 = (bf16[1024,1024]{1,0:T(8,128)(2,1)S(1)}, f32[1024,256]{1,0:T(8,128)S(1)}, f32[1024,256]{1,0:T(8,128)S(1)}) custom-call(s32[1]{0:T(128)} %bitcast.length_ref, s32[1]{0:T(128)} %bitcast.1._.flip_ref, bf16[1024,1024]{1,0:T(8,128)(2,1)S(1)} %copy-done.37, bf16[1024,1024]{1,0:T(8,128)(2,1)S(1)} %copy-done.25, f32[4,1,1024]{2,1,0:T(1,128)S(1)} %copy-done.65, ...), custom_call_target="tpu_custom_call" | custom-call | flops 1 | bytes 1 | tf_op jit(solution)/shard_map/pallas_call | solution.py:367
  500.4 5.7 shard_map.255
  509.6 5.8 shard_map.256
  522.3 5.9 collective-permute-done.71
  528.3 5.2 shard_map.258
  539.8 6.5 %collective-permute-done.76 = bf16[512,384]{1,0:T(8,128)(2,1)S(1)} collective-permute-done((bf16[512,384]{1,0:T(8,128)(2,1)S(1)}, bf16[512,384]{1,0:T(8,128)(2,1)S(1)}, u32[]{:S(2)}, u32[]{:S(2)}) %collective-permute-start.76) | collective-permute-done | bytes 393248 | tf_op jit(solution)/shard_map/ppermute | solution.py:72
  568.4 2.4 maximum_select_fusion.3
  570.8 5.7 shard_map.257
  582.4 7.2 %shard_map.259 = f32[256,2048]{1,0:T(8,128)S(1)} custom-call(s32[2]{0:T(128)S(1)} %pad_add_fusion.1.place_ref, bf16[256,384]{1,0:T(8,128)(2,1)S(1)} %get-tuple-element.595.refs_0_, bf16[256,384]{1,0:T(8,128)(2,1)S(1)} %collective-permute-done.81.refs_1_, bf16[256,384]{1,0:T(8,128)(2,1)S(1)} %collective-permute-done.82.refs_2_, ...), custom_call_target="tpu_custom_call" | custom-call | flops 1 | bytes 1 | tf_op jit(solution)/shard_map/pallas_call | solution.py:621
  600.0 2.5 collective-permute-done.92
  610.2 4.1 reduce-scatter.17.cloned.1.call-done
  (653 shorter events, 259.6 us)
Async XLA Ops:
  7.3 52.3 %all-gather.9.cloned.1.call-start = ((), (), s32[]{:S(2)}) async-start(), calls=%async_computation.6 | async-start | bytes 4718592 | tf_op jit(solution)/shard_map/all_gather | solution.py:190
  8.0 80.5 %all-gather.13.cloned.1.call-start = ((), (), s32[]{:S(2)}) async-start(), calls=%async_computation.14 | async-start | bytes 2211840 | tf_op jit(solution)/shard_map/all_gather | solution.py:182
  17.1 37.2 %collective-permute-start.4 = (bf16[128,2048]{1,0:T(8,128)(2,1)}, bf16[128,2048]{1,0:T(8,128)(2,1)}, u32[]{:S(2)}, u32[]{:S(2)}) collective-permute-start(bf16[128,2048]{1,0:T(8,128)(2,1)} %get-tuple-element.338.refs_0_), channel_id=1, source_target_pairs={{0,8},{8,0},{16,24},{24,16},{1,9},{9,1},{17,25},{25,17},{2,10},{10... | collective-permute-start | bytes 1572872 | tf_op jit(solution)/shard_map/ppermute | solution.py:72
  19.6 34.7 %collective-permute-start.6 = (bf16[128,2048]{1,0:T(8,128)(2,1)}, bf16[128,2048]{1,0:T(8,128)(2,1)}, u32[]{:S(2)}, u32[]{:S(2)}) collective-permute-start(bf16[128,2048]{1,0:T(8,128)(2,1)} %get-tuple-element.338.refs_0_), channel_id=1, source_target_pairs={{0,16},{8,24},{16,0},{24,8},{1,17},{9,25},{17,1},{25,9},{2,18},{10... | collective-permute-start | bytes 1572872 | tf_op jit(solution)/shard_map/ppermute | solution.py:72
  21.1 33.2 %collective-permute-start.5 = (bf16[128,2048]{1,0:T(8,128)(2,1)S(1)}, bf16[128,2048]{1,0:T(8,128)(2,1)}, u32[]{:S(2)}, u32[]{:S(2)}) collective-permute-start(bf16[128,2048]{1,0:T(8,128)(2,1)S(1)} %get-tuple-element.339.refs_1_), channel_id=1, source_target_pairs={{0,8},{8,0},{16,24},{24,16},{1,9},{9,1},{17,25},{25,17},{2,10},{10... | collective-permute-start | bytes 1572872 | tf_op jit(solution)/shard_map/ppermute | solution.py:72
  21.7 32.6 %collective-permute-start.7 = (bf16[128,2048]{1,0:T(8,128)(2,1)S(1)}, bf16[128,2048]{1,0:T(8,128)(2,1)}, u32[]{:S(2)}, u32[]{:S(2)}) collective-permute-start(bf16[128,2048]{1,0:T(8,128)(2,1)S(1)} %get-tuple-element.339.refs_1_), channel_id=1, source_target_pairs={{0,16},{8,24},{16,0},{24,8},{1,17},{9,25},{17,1},{25,9},{2,18},{10... | collective-permute-start | bytes 1572872 | tf_op jit(solution)/shard_map/ppermute | solution.py:72
  21.7 23.3 %collective-permute-start.1 = (bf16[80,384]{1,0:T(8,128)(2,1)S(1)}, bf16[80,384]{1,0:T(8,128)(2,1)S(1)}, u32[]{:S(2)}, u32[]{:S(2)}) collective-permute-start(bf16[80,384]{1,0:T(8,128)(2,1)S(1)} %copy-done.153), channel_id=1, source_target_pairs={{0,8},{8,0},{16,24},{24,16},{1,9},{9,1},{17,25},{25,17},{2,10},{10... | collective-permute-start | bytes 184328 | tf_op jit(solution)/shard_map/ppermute | solution.py:72
  60.3 93.3 %all-gather.15.cloned.1.call-start = ((), (), s32[]{:S(2)}) async-start(), calls=%async_computation.15 | async-start | bytes 2359296 | tf_op jit(solution)/shard_map/all_gather | solution.py:182
  84.0 175.7 %all-gather.17.cloned.1.call-start = ((), (), s32[]{:S(2)}) async-start(), calls=%async_computation.16 | async-start | bytes 12976128 | tf_op jit(solution)/shard_map/all_gather | solution.py:182
  104.0 193.8 %all-gather.11.cloned.1.call-start = ((), (), s32[]{:S(2)}) async-start(), calls=%async_computation.7 | async-start | bytes 6488064 | tf_op jit(solution)/shard_map/all_gather | solution.py:190
  104.6 296.8 %reduce-scatter.7.cloned.1.call-start = ((), (), s32[]{:S(2)}) async-start(), calls=%async_computation.8 | async-start | bytes 3604480 | tf_op jit(solution)/shard_map/reduce_scatter | solution.py:199
  108.9 23.8 %collective-permute-start.21 = (bf16[128,2048]{1,0:T(8,128)(2,1)}, bf16[128,2048]{1,0:T(8,128)(2,1)}, u32[]{:S(2)}, u32[]{:S(2)}) collective-permute-start(bf16[128,2048]{1,0:T(8,128)(2,1)} %get-tuple-element.675), channel_id=1, source_target_pairs={{0,4},{4,0},{1,5},{5,1},{2,6},{6,2},{3,7},{7,3},{8,12},{12,8},{9,1... | collective-permute-start | bytes 1572872 | tf_op jit(solution)/shard_map/ppermute | solution.py:67
  146.5 36.7 %collective-permute-start.25 = (bf16[128,2048]{1,0:T(8,128)(2,1)S(1)}, bf16[128,2048]{1,0:T(8,128)(2,1)S(1)}, u32[]{:S(2)}, u32[]{:S(2)}) collective-permute-start(bf16[128,2048]{1,0:T(8,128)(2,1)S(1)} %get-tuple-element.415.refs_0_), channel_id=1, source_target_pairs={{0,8},{8,0},{16,24},{24,16},{1,9},{9,1},{17,25},{25,17},{2,10},{10... | collective-permute-start | bytes 1572872 | tf_op jit(solution)/shard_map/ppermute | solution.py:72
  147.8 35.5 %collective-permute-start.27 = (bf16[128,2048]{1,0:T(8,128)(2,1)S(1)}, bf16[128,2048]{1,0:T(8,128)(2,1)}, u32[]{:S(2)}, u32[]{:S(2)}) collective-permute-start(bf16[128,2048]{1,0:T(8,128)(2,1)S(1)} %get-tuple-element.415.refs_0_), channel_id=1, source_target_pairs={{0,16},{8,24},{16,0},{24,8},{1,17},{9,25},{17,1},{25,9},{2,18},{10... | collective-permute-start | bytes 1572872 | tf_op jit(solution)/shard_map/ppermute | solution.py:72
  148.8 34.4 %collective-permute-start.26 = (bf16[128,2048]{1,0:T(8,128)(2,1)S(1)}, bf16[128,2048]{1,0:T(8,128)(2,1)}, u32[]{:S(2)}, u32[]{:S(2)}) collective-permute-start(bf16[128,2048]{1,0:T(8,128)(2,1)S(1)} %get-tuple-element.416.refs_1_), channel_id=1, source_target_pairs={{0,8},{8,0},{16,24},{24,16},{1,9},{9,1},{17,25},{25,17},{2,10},{10... | collective-permute-start | bytes 1572872 | tf_op jit(solution)/shard_map/ppermute | solution.py:72
  150.1 33.2 %collective-permute-start.28 = (bf16[128,2048]{1,0:T(8,128)(2,1)S(1)}, bf16[128,2048]{1,0:T(8,128)(2,1)}, u32[]{:S(2)}, u32[]{:S(2)}) collective-permute-start(bf16[128,2048]{1,0:T(8,128)(2,1)S(1)} %get-tuple-element.416.refs_1_), channel_id=1, source_target_pairs={{0,16},{8,24},{16,0},{24,8},{1,17},{9,25},{17,1},{25,9},{2,18},{10... | collective-permute-start | bytes 1572872 | tf_op jit(solution)/shard_map/ppermute | solution.py:72
  224.4 23.4 %collective-permute-start.36 = (bf16[128,2048]{1,0:T(8,128)(2,1)S(1)}, bf16[128,2048]{1,0:T(8,128)(2,1)S(1)}, u32[]{:S(2)}, u32[]{:S(2)}) collective-permute-start(bf16[128,2048]{1,0:T(8,128)(2,1)S(1)} %get-tuple-element.670.refs_1_), channel_id=1, source_target_pairs={{0,8},{8,0},{16,24},{24,16},{1,9},{9,1},{17,25},{25,17},{2,10},{10... | collective-permute-start | bytes 1572872 | tf_op jit(solution)/shard_map/ppermute | solution.py:72
  225.2 23.0 %collective-permute-start.37 = (bf16[128,2048]{1,0:T(8,128)(2,1)S(1)}, bf16[128,2048]{1,0:T(8,128)(2,1)S(1)}, u32[]{:S(2)}, u32[]{:S(2)}) collective-permute-start(bf16[128,2048]{1,0:T(8,128)(2,1)S(1)} %get-tuple-element.671.refs_0_), channel_id=1, source_target_pairs={{0,16},{8,24},{16,0},{24,8},{1,17},{9,25},{17,1},{25,9},{2,18},{10... | collective-permute-start | bytes 1572872 | tf_op jit(solution)/shard_map/ppermute | solution.py:72
  257.3 24.5 %collective-permute-start.41 = (bf16[128,2048]{1,0:T(8,128)(2,1)S(1)}, bf16[128,2048]{1,0:T(8,128)(2,1)S(1)}, u32[]{:S(2)}, u32[]{:S(2)}) collective-permute-start(bf16[128,2048]{1,0:T(8,128)(2,1)S(1)} %collective-permute-done.25.refs_2_), channel_id=1, source_target_pairs={{0,16},{8,24},{16,0},{24,8},{1,17},{9,25},{17,1},{25,9},{2,18},{10... | collective-permute-start | bytes 1572872 | tf_op jit(solution)/shard_map/ppermute | solution.py:72
  258.9 23.0 %collective-permute-start.42 = (bf16[128,2048]{1,0:T(8,128)(2,1)}, bf16[128,2048]{1,0:T(8,128)(2,1)S(1)}, u32[]{:S(2)}, u32[]{:S(2)}) collective-permute-start(bf16[128,2048]{1,0:T(8,128)(2,1)} %collective-permute-done.28.refs_5_), channel_id=1, source_target_pairs={{0,8},{8,0},{16,24},{24,16},{1,9},{9,1},{17,25},{25,17},{2,10},{10... | collective-permute-start | bytes 1572872 | tf_op jit(solution)/shard_map/ppermute | solution.py:72
  318.5 136.2 %reduce-scatter.9.cloned.1.call-start = ((), (), s32[]{:S(2)}) async-start(), calls=%async_computation.9 | async-start | bytes 3604480 | tf_op jit(solution)/shard_map/reduce_scatter | solution.py:199
  319.9 22.9 %collective-permute-start.44 = (bf16[640,384]{1,0:T(8,128)(2,1)S(1)}, bf16[640,384]{1,0:T(8,128)(2,1)}, u32[]{:S(2)}, u32[]{:S(2)}) collective-permute-start(bf16[640,384]{1,0:T(8,128)(2,1)S(1)} %get-tuple-element.587.refs_0_), channel_id=1, source_target_pairs={{0,8},{8,0},{16,24},{24,16},{1,9},{9,1},{17,25},{25,17},{2,10},{10... | collective-permute-start | bytes 1474568 | tf_op jit(solution)/shard_map/ppermute | solution.py:72
  321.2 22.9 %collective-permute-start.45 = (bf16[640,384]{1,0:T(8,128)(2,1)S(1)}, bf16[640,384]{1,0:T(8,128)(2,1)S(1)}, u32[]{:S(2)}, u32[]{:S(2)}) collective-permute-start(bf16[640,384]{1,0:T(8,128)(2,1)S(1)} %get-tuple-element.588.refs_1_), channel_id=1, source_target_pairs={{0,8},{8,0},{16,24},{24,16},{1,9},{9,1},{17,25},{25,17},{2,10},{10... | collective-permute-start | bytes 1474568 | tf_op jit(solution)/shard_map/ppermute | solution.py:72
  322.0 22.1 %collective-permute-start.46 = (bf16[640,384]{1,0:T(8,128)(2,1)S(1)}, bf16[640,384]{1,0:T(8,128)(2,1)S(1)}, u32[]{:S(2)}, u32[]{:S(2)}) collective-permute-start(bf16[640,384]{1,0:T(8,128)(2,1)S(1)} %get-tuple-element.587.refs_0_), channel_id=1, source_target_pairs={{0,16},{8,24},{16,0},{24,8},{1,17},{9,25},{17,1},{25,9},{2,18},{10... | collective-permute-start | bytes 1474568 | tf_op jit(solution)/shard_map/ppermute | solution.py:72
  322.9 22.8 %collective-permute-start.47 = (bf16[640,384]{1,0:T(8,128)(2,1)S(1)}, bf16[640,384]{1,0:T(8,128)(2,1)}, u32[]{:S(2)}, u32[]{:S(2)}) collective-permute-start(bf16[640,384]{1,0:T(8,128)(2,1)S(1)} %get-tuple-element.588.refs_1_), channel_id=1, source_target_pairs={{0,16},{8,24},{16,0},{24,8},{1,17},{9,25},{17,1},{25,9},{2,18},{10... | collective-permute-start | bytes 1474568 | tf_op jit(solution)/shard_map/ppermute | solution.py:72
  345.7 27.7 %collective-permute-start.48 = (bf16[128,2048]{1,0:T(8,128)(2,1)S(1)}, bf16[128,2048]{1,0:T(8,128)(2,1)S(1)}, u32[]{:S(2)}, u32[]{:S(2)}) collective-permute-start(bf16[128,2048]{1,0:T(8,128)(2,1)S(1)} %get-tuple-element.453), channel_id=1, source_target_pairs={{0,8},{8,0},{16,24},{24,16},{1,9},{9,1},{17,25},{25,17},{2,10},{10... | collective-permute-start | bytes 1572872 | tf_op jit(solution)/shard_map/ppermute | solution.py:72
  346.9 26.5 %collective-permute-start.49 = (bf16[128,2048]{1,0:T(8,128)(2,1)S(1)}, bf16[128,2048]{1,0:T(8,128)(2,1)S(1)}, u32[]{:S(2)}, u32[]{:S(2)}) collective-permute-start(bf16[128,2048]{1,0:T(8,128)(2,1)S(1)} %get-tuple-element.455), channel_id=1, source_target_pairs={{0,16},{8,24},{16,0},{24,8},{1,17},{9,25},{17,1},{25,9},{2,18},{10... | collective-permute-start | bytes 1572872 | tf_op jit(solution)/shard_map/ppermute | solution.py:72
  347.4 26.0 %collective-permute-start.50 = (bf16[128,2048]{1,0:T(8,128)(2,1)S(1)}, bf16[128,2048]{1,0:T(8,128)(2,1)S(1)}, u32[]{:S(2)}, u32[]{:S(2)}) collective-permute-start(bf16[128,2048]{1,0:T(8,128)(2,1)S(1)} %get-tuple-element.457), channel_id=1, source_target_pairs={{0,8},{8,0},{16,24},{24,16},{1,9},{9,1},{17,25},{25,17},{2,10},{10... | collective-permute-start | bytes 1572872 | tf_op jit(solution)/shard_map/ppermute | solution.py:72
  348.6 24.8 %collective-permute-start.51 = (bf16[128,2048]{1,0:T(8,128)(2,1)S(1)}, bf16[128,2048]{1,0:T(8,128)(2,1)S(1)}, u32[]{:S(2)}, u32[]{:S(2)}) collective-permute-start(bf16[128,2048]{1,0:T(8,128)(2,1)S(1)} %get-tuple-element.459), channel_id=1, source_target_pairs={{0,16},{8,24},{16,0},{24,8},{1,17},{9,25},{17,1},{25,9},{2,18},{10... | collective-permute-start | bytes 1572872 | tf_op jit(solution)/shard_map/ppermute | solution.py:72
  381.4 140.1 %reduce-scatter.11.cloned.1.call-start = ((), (), s32[]{:S(2)}) async-start(), calls=%async_computation.10 | async-start | bytes 3604480 | tf_op jit(solution)/shard_map/reduce_scatter | solution.py:199
  401.5 150.6 %reduce-scatter.13.cloned.1.call-start = ((), (), s32[]{:S(2)}) async-start(), calls=%async_computation.11 | async-start | bytes 2621440 | tf_op jit(solution)/shard_map/reduce_scatter | solution.py:199
  410.0 27.4 %collective-permute-start.57 = (bf16[128,2048]{1,0:T(8,128)(2,1)S(1)}, bf16[128,2048]{1,0:T(8,128)(2,1)S(1)}, u32[]{:S(2)}, u32[]{:S(2)}) collective-permute-start(bf16[128,2048]{1,0:T(8,128)(2,1)S(1)} %get-tuple-element.668.refs_1_), channel_id=1, source_target_pairs={{0,8},{8,0},{16,24},{24,16},{1,9},{9,1},{17,25},{25,17},{2,10},{10... | collective-permute-start | bytes 1572872 | tf_op jit(solution)/shard_map/ppermute | solution.py:72
  410.8 26.6 %collective-permute-start.58 = (bf16[128,2048]{1,0:T(8,128)(2,1)S(1)}, bf16[128,2048]{1,0:T(8,128)(2,1)S(1)}, u32[]{:S(2)}, u32[]{:S(2)}) collective-permute-start(bf16[128,2048]{1,0:T(8,128)(2,1)S(1)} %get-tuple-element.669.refs_0_), channel_id=1, source_target_pairs={{0,16},{8,24},{16,0},{24,8},{1,17},{9,25},{17,1},{25,9},{2,18},{10... | collective-permute-start | bytes 1572872 | tf_op jit(solution)/shard_map/ppermute | solution.py:72
  422.6 21.3 %collective-permute-start.60 = (bf16[128,2048]{1,0:T(8,128)(2,1)S(1)}, bf16[128,2048]{1,0:T(8,128)(2,1)S(1)}, u32[]{:S(2)}, u32[]{:S(2)}) collective-permute-start(bf16[128,2048]{1,0:T(8,128)(2,1)S(1)} %collective-permute-done.56.refs_2_), channel_id=1, source_target_pairs={{0,16},{8,24},{16,0},{24,8},{1,17},{9,25},{17,1},{25,9},{2,18},{10... | collective-permute-start | bytes 1572872 | tf_op jit(solution)/shard_map/ppermute | solution.py:72
  423.6 20.4 %collective-permute-start.61 = (bf16[128,2048]{1,0:T(8,128)(2,1)S(1)}, bf16[128,2048]{1,0:T(8,128)(2,1)S(1)}, u32[]{:S(2)}, u32[]{:S(2)}) collective-permute-start(bf16[128,2048]{1,0:T(8,128)(2,1)S(1)} %collective-permute-done.59.refs_5_), channel_id=1, source_target_pairs={{0,8},{8,0},{16,24},{24,16},{1,9},{9,1},{17,25},{25,17},{2,10},{10... | collective-permute-start | bytes 1572872 | tf_op jit(solution)/shard_map/ppermute | solution.py:72
  456.0 19.9 %collective-permute-start.63 = (bf16[128,2048]{1,0:T(8,128)(2,1)}, bf16[128,2048]{1,0:T(8,128)(2,1)S(1)}, u32[]{:S(2)}, u32[]{:S(2)}) collective-permute-start(bf16[128,2048]{1,0:T(8,128)(2,1)} %get-tuple-element.515), channel_id=1, source_target_pairs={{0,8},{8,0},{16,24},{24,16},{1,9},{9,1},{17,25},{25,17},{2,10},{10... | collective-permute-start | bytes 1572872 | tf_op jit(solution)/shard_map/ppermute | solution.py:72
  457.3 39.1 %collective-permute-start.64 = (bf16[128,2048]{1,0:T(8,128)(2,1)}, bf16[128,2048]{1,0:T(8,128)(2,1)}, u32[]{:S(2)}, u32[]{:S(2)}) collective-permute-start(bf16[128,2048]{1,0:T(8,128)(2,1)} %get-tuple-element.517), channel_id=1, source_target_pairs={{0,16},{8,24},{16,0},{24,8},{1,17},{9,25},{17,1},{25,9},{2,18},{10... | collective-permute-start | bytes 1572872 | tf_op jit(solution)/shard_map/ppermute | solution.py:72
  458.3 38.1 %collective-permute-start.65 = (bf16[128,2048]{1,0:T(8,128)(2,1)}, bf16[128,2048]{1,0:T(8,128)(2,1)}, u32[]{:S(2)}, u32[]{:S(2)}) collective-permute-start(bf16[128,2048]{1,0:T(8,128)(2,1)} %get-tuple-element.519), channel_id=1, source_target_pairs={{0,8},{8,0},{16,24},{24,16},{1,9},{9,1},{17,25},{25,17},{2,10},{10... | collective-permute-start | bytes 1572872 | tf_op jit(solution)/shard_map/ppermute | solution.py:72
  459.6 36.8 %collective-permute-start.66 = (bf16[128,2048]{1,0:T(8,128)(2,1)}, bf16[128,2048]{1,0:T(8,128)(2,1)}, u32[]{:S(2)}, u32[]{:S(2)}) collective-permute-start(bf16[128,2048]{1,0:T(8,128)(2,1)} %get-tuple-element.521), channel_id=1, source_target_pairs={{0,16},{8,24},{16,0},{24,8},{1,17},{9,25},{17,1},{25,9},{2,18},{10... | collective-permute-start | bytes 1572872 | tf_op jit(solution)/shard_map/ppermute | solution.py:72
  474.3 22.1 %collective-permute-start.67 = (bf16[640,384]{1,0:T(8,128)(2,1)}, bf16[640,384]{1,0:T(8,128)(2,1)}, u32[]{:S(2)}, u32[]{:S(2)}) collective-permute-start(bf16[640,384]{1,0:T(8,128)(2,1)} %collective-permute-done.44.refs_2_), channel_id=1, source_target_pairs={{0,16},{8,24},{16,0},{24,8},{1,17},{9,25},{17,1},{25,9},{2,18},{10... | collective-permute-start | bytes 1474568 | tf_op jit(solution)/shard_map/ppermute | solution.py:72
  475.9 20.6 %collective-permute-start.68 = (bf16[640,384]{1,0:T(8,128)(2,1)}, bf16[640,384]{1,0:T(8,128)(2,1)}, u32[]{:S(2)}, u32[]{:S(2)}) collective-permute-start(bf16[640,384]{1,0:T(8,128)(2,1)} %collective-permute-done.47.refs_5_), channel_id=1, source_target_pairs={{0,8},{8,0},{16,24},{24,16},{1,9},{9,1},{17,25},{25,17},{2,10},{10... | collective-permute-start | bytes 1474568 | tf_op jit(solution)/shard_map/ppermute | solution.py:72
  477.9 115.2 %reduce-scatter.15.cloned.1.call-start = ((), (), s32[]{:S(2)}) async-start(), calls=%async_computation.12 | async-start | bytes 1310720 | tf_op jit(solution)/shard_map/reduce_scatter | solution.py:199
  498.9 19.8 %collective-permute-start.74 = (bf16[128,2048]{1,0:T(8,128)(2,1)S(1)}, bf16[128,2048]{1,0:T(8,128)(2,1)S(1)}, u32[]{:S(2)}, u32[]{:S(2)}) collective-permute-start(bf16[128,2048]{1,0:T(8,128)(2,1)S(1)} %add_convert_fusion.6), channel_id=1, source_target_pairs={{0,8},{8,0},{16,24},{24,16},{1,9},{9,1},{17,25},{25,17},{2,10},{10... | collective-permute-start | bytes 1572872 | tf_op jit(solution)/shard_map/ppermute | solution.py:72
  508.4 19.9 %collective-permute-start.71 = (bf16[512,384]{1,0:T(8,128)(2,1)}, bf16[512,384]{1,0:T(8,128)(2,1)}, u32[]{:S(2)}, u32[]{:S(2)}) collective-permute-start(bf16[512,384]{1,0:T(8,128)(2,1)} %get-tuple-element.544), channel_id=1, source_target_pairs={{0,8},{8,0},{16,24},{24,16},{1,9},{9,1},{17,25},{25,17},{2,10},{10... | collective-permute-start | bytes 1179656 | tf_op jit(solution)/shard_map/ppermute | solution.py:72
  533.5 43.0 %collective-permute-start.84 = (bf16[5120,384]{1,0:T(8,128)(2,1)}, bf16[5120,384]{1,0:T(8,128)(2,1)}, u32[]{:S(2)}, u32[]{:S(2)}) collective-permute-start(bf16[5120,384]{1,0:T(8,128)(2,1)} %shard_map.258), channel_id=1, source_target_pairs={{0,4},{4,0},{1,5},{5,1},{2,6},{6,2},{3,7},{7,3},{8,12},{12,8},{9,1... | collective-permute-start | bytes 11796488 | tf_op jit(solution)/shard_map/ppermute | solution.py:67
  539.8 28.6 %collective-permute-start.75 = (bf16[128,2048]{1,0:T(8,128)(2,1)}, bf16[128,2048]{1,0:T(8,128)(2,1)}, u32[]{:S(2)}, u32[]{:S(2)}) collective-permute-start(bf16[128,2048]{1,0:T(8,128)(2,1)} %get-tuple-element.663), channel_id=1, source_target_pairs={{0,4},{4,0},{1,5},{5,1},{2,6},{6,2},{3,7},{7,3},{8,12},{12,8},{9,1... | collective-permute-start | bytes 1572872 | tf_op jit(solution)/shard_map/ppermute | solution.py:67
  560.3 54.0 %reduce-scatter.17.cloned.1.call-start = ((), (), s32[]{:S(2)}) async-start(), calls=%async_computation.13 | async-start | bytes 983040 | tf_op jit(solution)/shard_map/reduce_scatter | solution.py:199
  599.1 19.9 %collective-permute-start.85 = (f32[128,2048]{1,0:T(8,128)S(1)}, f32[128,2048]{1,0:T(8,128)S(1)}, u32[]{:S(2)}, u32[]{:S(2)}) collective-permute-start(f32[128,2048]{1,0:T(8,128)S(1)} %get-tuple-element.647), channel_id=1, source_target_pairs={{0,4},{4,0},{1,5},{5,1},{2,6},{6,2},{3,7},{7,3},{8,12},{12,8},{9,1... | collective-permute-start | bytes 3145736 | tf_op jit(solution)/shard_map/ppermute | solution.py:67
  (215 other events, 2027.7 us)
Sparse Core Ops, SparseCore 0:
  9.7 49.8 all-gather.8
  61.8 26.7 all-gather.12
  90.7 28.6 all-gather.14
  121.4 107.5 all-gather.16
  230.4 58.6 all-gather.10
  318.6 53.9 reduce-scatter.6
  381.5 53.8 reduce-scatter.8
  437.7 56.0 reduce-scatter.10
  496.1 43.6 reduce-scatter.12
  560.4 25.1 reduce-scatter.14
  593.2 21.0 reduce-scatter.16
